TPU v7x, 32 devices: a whole 2x2x4 slice. The times are simulated.
32 devices in a mesh: img: 4 (over z), row: 8 (over y, x, core).
Axes of the slice: x: 2, y: 2, z: 4, core: 2. Of those that a mesh axis runs over, the one named last changes fastest.
Arguments:
- patches: bfloat16 [4, 64, 56, 256], P('img', 'row'), may hold values from -6 to 6
- cotangent: bfloat16 [4, 64, 56, 256], P('img', 'row'), may hold values from -6 to 6
- image_sizes: int32 [4, 2], P('img'), may hold values from 28 to 64, as said below
- weights: float32 [32, 32768], P(('img', 'row')), may hold values from -8 to 8
- first_moment: float32 [32, 32768], P(('img', 'row')), may hold values from -14336 to 14336
- second_moment: float32 [32, 32768], P(('img', 'row')), may hold values from 0 to 28672
- weight_ema: float32 [32, 32768], P(('img', 'row')), may hold values from -8 to 8
- vectors: float32 [25, 256], replicated, may hold values from -2 to 2
- vec_first: float32 [25, 256], replicated, may hold values from -14336 to 14336
- vec_second: float32 [25, 256], replicated, may hold values from 0 to 57344
- vec_ema: float32 [25, 256], replicated, may hold values from -2 to 2
- basis_narrow: float32 [8, 256, 256], replicated, may hold values from -0.375 to 0.375
- basis_pair: float32 [512, 512], replicated, may hold values from -0.25 to 0.25
- basis_wide: float32 [3, 1024, 1024], replicated, may hold values from -0.1875 to 0.1875
Outputs:
- layer_out: bfloat16 [4, 64, 56, 256], P('img', 'row')
- grad_input: float32 [4, 64, 56, 256], P('img', 'row')
- new_weights: float32 [32, 32768], P(('img', 'row'))
- new_first: float32 [32, 32768], P(('img', 'row'))
- new_second: float32 [32, 32768], P(('img', 'row'))
- new_ema: float32 [32, 32768], P(('img', 'row'))
- new_vectors: float32 [25, 256], replicated
- new_vec_first: float32 [25, 256], replicated
- new_vec_second: float32 [25, 256], replicated
- new_vec_ema: float32 [25, 256], replicated
Inputs may be any that keep to these rules, and one draw needn't show every extreme that they name: `image_sizes`: column 0 is an image's height in cells, from 57 to 64; column 1 its width, from 28 to 56; in every draw some image has height 64 and width 56.
All inputs are finite; a program needn't handle non-finite values.
Results may differ from a plain program's by a relative error of at most 0.014.
The roundings to bfloat16 on the way count: a program that leaves them out, or rounds other values in their place, can miss the bound.
Values may be sent and summed in bfloat16 or wider, within the bound.
No kernel may reach another device: no remote copies, remote signals or barrier semaphores. Data moves between devices by JAX's collectives and lax.ppermute only.
A program may use at most 192 MiB of HBM per device.

v0:
```python
from functools import partial

import jax
import jax.numpy as jnp
from jax import lax
from jax.sharding import PartitionSpec as P

HEADS = 8
FF = 1024
STEP = 5


NORM_EPS = 1e-05
ADAM_EPS = 1e-08
BETA = 0.5
WEIGHT_DECAY = 0.05
EMA_KEEP = 0.75
VECTOR_RATE = 0.06
MATRIX_RATES = (0.04, 0.02, 0.25, 0.02, 0.01, 0.01)
HIGH = lax.Precision.HIGHEST


def extended(cells, sides, width):
    for axis, dim in sides:
        count = lax.axis_size(axis)
        ends = count - 1
        head = lax.slice_in_dim(cells, 0, width, axis=dim)
        tail = lax.slice_in_dim(cells, cells.shape[dim] - width, cells.shape[dim], axis=dim)
        cells = jnp.concatenate(
            [
                lax.ppermute(tail, axis, [(i, (i + 1) % count) for i in range(ends)]),
                cells,
                lax.ppermute(head, axis, [((i + 1) % count, i) for i in range(ends)]),
            ],
            axis=dim,
        )
    return cells


def layer_norm(values, gain, shift):
    centred = values - jnp.mean(values, axis=-1, keepdims=True)
    inverse = lax.rsqrt(jnp.mean(centred * centred, axis=-1, keepdims=True) + NORM_EPS)
    return centred * inverse * gain + shift


def peg_mix(padded, peg_taps, peg_bias):
    framed = jnp.pad(padded, ((0, 0), (1, 1), (0, 0)))
    cell_rows = padded.shape[0] - 2
    cell_cols = padded.shape[1]
    mixed_sum = padded[1:-1] + peg_bias
    for tap_index in range(9):
        row_shift = tap_index // 3
        col_shift = tap_index % 3
        mixed_sum = (
            mixed_sum
            + peg_taps[tap_index]
            * framed[row_shift : row_shift + cell_rows, col_shift : col_shift + cell_cols]
        )
    return mixed_sum


def matrix_shapes(model_width, hidden_width):
    return (
        (model_width, model_width),
        (model_width, 2 * model_width),
        (model_width, model_width),
        (model_width, hidden_width),
        (hidden_width, model_width),
        (4 * model_width, model_width),
    )


def basis_pairs(narrow, paired, wide):
    return (
        (narrow[0], narrow[1]),
        (narrow[2], paired),
        (narrow[3], narrow[4]),
        (narrow[5], wide[0]),
        (wide[1], narrow[6]),
        (wide[2], narrow[7]),
    )


def low_dot(left_side, right_side):
    return jnp.dot(left_side, right_side, preferred_element_type=jnp.float32)


def high_dot(left_side, right_side):
    return jnp.dot(left_side, right_side, precision=HIGH, preferred_element_type=jnp.float32)


def on_device(
    patches,
    cotangent,
    image_sizes,
    weights,
    first_moment,
    second_moment,
    weight_ema,
    vectors,
    vec_first,
    vec_second,
    vec_ema,
    basis_narrow,
    basis_pair,
    basis_wide,
):
    patch_tile = patches[0]
    tile_rows, tile_cols, model_width = patch_tile.shape
    token_count = tile_rows * tile_cols
    shard_count = lax.axis_size(("img", "row"))
    shard_rank = lax.axis_index(("img", "row"))
    tile_count = lax.axis_size("row")
    tile_rank = lax.axis_index("row")
    head_width = model_width // HEADS
    score_scale = head_width ** (-0.5)
    matrix_dims = matrix_shapes(model_width, FF)
    shard_spans = [dim_rows * dim_cols // shard_count for dim_rows, dim_cols in matrix_dims]
    gathered = lax.all_gather(weights.astype(jnp.bfloat16), ("img", "row"), axis=0, tiled=True)
    matrices = []
    column_start = 0
    for (dim_rows, dim_cols), shard_span in zip(matrix_dims, shard_spans):
        matrices.append(
            gathered[:, column_start : column_start + shard_span].reshape(dim_rows, dim_cols)
        )
        column_start = column_start + shard_span
    w_query, w_keyval, w_out, w_up, w_down, w_reduce = matrices
    peg_taps = vectors[0:9]
    peg_bias = vectors[9]
    gain_one, shift_one = (vectors[10], vectors[11])
    query_bias, reduce_bias = (vectors[12], vectors[13])
    gain_red, shift_red = (vectors[14], vectors[15])
    value_bias, out_bias = (vectors[16], vectors[17])
    gain_two, shift_two = (vectors[18], vectors[19])
    down_bias = vectors[20]
    up_bias = vectors[21:].reshape(-1)
    image_height = image_sizes[0, 0]
    image_width = image_sizes[0, 1]
    cell_rows = tile_rank * tile_rows + jnp.arange(tile_rows, dtype=jnp.int32)
    cell_index = jnp.arange(tile_cols, dtype=jnp.int32)
    inside = (cell_rows[:, None] < image_height) & (cell_index[None, :] < image_width)
    key_rows = jnp.arange(tile_count * tile_rows // 2, dtype=jnp.int32)
    key_cols = jnp.arange(tile_cols // 2, dtype=jnp.int32)
    key_inside = (
        (2 * key_rows[:, None] < image_height) & (2 * key_cols[None, :] < image_width)
    ).reshape(-1)
    padded = extended(patch_tile, (("row", 0),), 1).astype(jnp.float32)
    mixed_in = peg_mix(padded, peg_taps, peg_bias)
    normed = layer_norm(mixed_in, gain_one, shift_one).astype(jnp.bfloat16)
    flat_normed = normed.reshape(token_count, model_width)
    queries = (low_dot(flat_normed, w_query) + query_bias).astype(jnp.bfloat16)
    masked = normed * inside[:, :, None].astype(jnp.bfloat16)
    blocks = (
        masked.reshape(tile_rows // 2, 2, tile_cols // 2, 2, model_width)
        .transpose(0, 2, 1, 3, 4)
        .reshape(-1, 4 * model_width)
    )
    reduced = low_dot(blocks, w_reduce) + reduce_bias
    red_norm = layer_norm(reduced, gain_red, shift_red).astype(jnp.bfloat16)
    projected = low_dot(red_norm, w_keyval)
    own_keys = projected[:, :model_width].astype(jnp.bfloat16)
    own_values = (projected[:, model_width:] + value_bias).astype(jnp.bfloat16)
    all_keys, all_values = (
        lax.all_gather(own_keys, "row", axis=0, tiled=True),
        lax.all_gather(own_values, "row", axis=0, tiled=True),
    )
    key_heads = all_keys.reshape(-1, HEADS, head_width).transpose(1, 0, 2)
    value_heads = all_values.reshape(-1, HEADS, head_width).transpose(1, 0, 2)
    query_heads = queries.reshape(token_count, HEADS, head_width).transpose(1, 0, 2)

    def head_forward(operands):
        q_part, k_part, v_part = operands
        scores = (
            jnp.einsum("qd,kd->qk", q_part, k_part, preferred_element_type=jnp.float32)
            * score_scale
        )
        scores = jnp.where(key_inside[None, :], scores, -1e30)
        row_top = jnp.max(scores, axis=1, keepdims=True)
        exponent = jnp.exp(scores - row_top)
        row_total = jnp.sum(exponent, axis=1, keepdims=True)
        softmax_rows = (exponent / row_total).astype(jnp.bfloat16)
        head_out = jnp.einsum("qk,kd->qd", softmax_rows, v_part, preferred_element_type=jnp.float32)
        return (head_out, (row_top + jnp.log(row_total))[:, 0])

    head_out, log_totals = lax.map(head_forward, (query_heads, key_heads, value_heads))
    attended = head_out.transpose(1, 0, 2).reshape(token_count, model_width).astype(jnp.bfloat16)
    residual = mixed_in.reshape(token_count, model_width) + (low_dot(attended, w_out) + out_bias)
    second_in = layer_norm(residual, gain_two, shift_two).astype(jnp.bfloat16)
    up_input = low_dot(second_in, w_up) + up_bias
    activated = jax.nn.gelu(up_input, approximate=False).astype(jnp.bfloat16)
    result = residual + low_dot(activated, w_down) + down_bias
    layer_out = result.astype(jnp.bfloat16).reshape(1, tile_rows, tile_cols, model_width)
    grad_out = cotangent[0].reshape(token_count, model_width)
    grad_result = grad_out.astype(jnp.float32)
    g_down = jnp.einsum("tf,td->fd", activated, grad_out, preferred_element_type=jnp.float32)
    g_down_bias = jnp.sum(grad_result, axis=0)
    grad_act = jnp.einsum("td,fd->tf", grad_out, w_down, preferred_element_type=jnp.float32)
    ignored, gelu_pull = jax.vjp(partial(jax.nn.gelu, approximate=False), up_input)
    grad_upper = gelu_pull(grad_act)[0].astype(jnp.bfloat16)
    g_up = jnp.einsum("td,tf->df", second_in, grad_upper, preferred_element_type=jnp.float32)
    g_up_bias = jnp.sum(grad_upper.astype(jnp.float32), axis=0)
    grad_second = jnp.einsum("tf,df->td", grad_upper, w_up, preferred_element_type=jnp.float32)
    ignored, second_pull = jax.vjp(layer_norm, residual, gain_two, shift_two)
    grad_resid, g_gain_two, g_shift_two = second_pull(grad_second)
    grad_resid = grad_resid + grad_result
    grad_branch = grad_resid.astype(jnp.bfloat16)
    g_out = jnp.einsum("td,te->de", attended, grad_branch, preferred_element_type=jnp.float32)
    g_out_bias = jnp.sum(grad_branch.astype(jnp.float32), axis=0)
    grad_att = jnp.einsum(
        "te,de->td", grad_branch, w_out, preferred_element_type=jnp.float32
    ).astype(jnp.bfloat16)
    grad_heads = grad_att.reshape(token_count, HEADS, head_width).transpose(1, 0, 2)

    def head_backward(operands):
        q_part, k_part, v_part, g_part, log_total = operands
        scores = (
            jnp.einsum("qd,kd->qk", q_part, k_part, preferred_element_type=jnp.float32)
            * score_scale
        )
        scores = jnp.where(key_inside[None, :], scores, -1e30)
        softmax_rows = jnp.exp(scores - log_total[:, None])
        grad_probs = jnp.einsum("qd,kd->qk", g_part, v_part, preferred_element_type=jnp.float32)
        inner_sum = jnp.sum(softmax_rows * grad_probs, axis=1, keepdims=True)
        grad_scores = (softmax_rows * (grad_probs - inner_sum)).astype(jnp.bfloat16)
        grad_q = (
            jnp.einsum("qk,kd->qd", grad_scores, k_part, preferred_element_type=jnp.float32)
            * score_scale
        )
        grad_k = (
            jnp.einsum("qk,qd->kd", grad_scores, q_part, preferred_element_type=jnp.float32)
            * score_scale
        )
        grad_v = jnp.einsum(
            "qk,qd->kd",
            softmax_rows.astype(jnp.bfloat16),
            g_part,
            preferred_element_type=jnp.float32,
        )
        return (grad_q, grad_k, grad_v)

    grad_qh, grad_kh, grad_vh = lax.map(
        head_backward, (query_heads, key_heads, value_heads, grad_heads, log_totals)
    )
    grad_query = grad_qh.transpose(1, 0, 2).reshape(token_count, model_width).astype(jnp.bfloat16)
    grad_keys_all = grad_kh.transpose(1, 0, 2).reshape(-1, model_width)
    grad_vals_all = grad_vh.transpose(1, 0, 2).reshape(-1, model_width)
    keyval_wide = w_keyval.astype(jnp.float32)
    own_grad_keys, own_grad_vals = (
        lax.psum_scatter(grad_keys_all, "row", scatter_dimension=0, tiled=True),
        lax.psum_scatter(grad_vals_all, "row", scatter_dimension=0, tiled=True),
    )
    grad_keyval = jnp.concatenate([own_grad_keys, own_grad_vals], axis=1)
    g_keyval = high_dot(red_norm.astype(jnp.float32).T, grad_keyval)
    g_value_bias = jnp.sum(own_grad_vals, axis=0)
    grad_red_norm = high_dot(grad_keyval, keyval_wide.T)
    g_query = jnp.einsum("td,te->de", flat_normed, grad_query, preferred_element_type=jnp.float32)
    g_query_bias = jnp.sum(grad_query.astype(jnp.float32), axis=0)
    ignored, reduced_pull = jax.vjp(layer_norm, reduced, gain_red, shift_red)
    grad_reduced_full, g_gain_red, g_shift_red = reduced_pull(grad_red_norm)
    grad_reduced = grad_reduced_full.astype(jnp.bfloat16)
    g_reduce = jnp.einsum("kc,kd->cd", blocks, grad_reduced, preferred_element_type=jnp.float32)
    g_reduce_bias = jnp.sum(grad_reduced.astype(jnp.float32), axis=0)
    grad_blocks = jnp.einsum(
        "kd,cd->kc", grad_reduced, w_reduce, preferred_element_type=jnp.float32
    )
    grad_masked = (
        grad_blocks.reshape(tile_rows // 2, tile_cols // 2, 2, 2, model_width)
        .transpose(0, 2, 1, 3, 4)
        .reshape(tile_rows, tile_cols, model_width)
    )
    grad_from_query = jnp.einsum(
        "te,de->td", grad_query, w_query, preferred_element_type=jnp.float32
    )
    grad_normed = grad_from_query.reshape(tile_rows, tile_cols, model_width) + grad_masked * inside[
        :, :, None
    ].astype(jnp.float32)
    ignored, first_pull = jax.vjp(layer_norm, mixed_in, gain_one, shift_one)
    grad_mixed, g_gain_one, g_shift_one = first_pull(grad_normed)
    grad_mixed = grad_mixed + grad_resid.reshape(tile_rows, tile_cols, model_width)
    framed = jnp.pad(padded, ((0, 0), (1, 1), (0, 0)))
    g_peg_bias = jnp.sum(grad_mixed, axis=(0, 1))
    tap_grads = []
    for tap_index in range(9):
        row_shift = tap_index // 3
        col_shift = tap_index % 3
        tap_grads.append(
            jnp.sum(
                framed[row_shift : row_shift + tile_rows, col_shift : col_shift + tile_cols]
                * grad_mixed,
                axis=(0, 1),
            )
        )
    grad_frame = extended(grad_mixed.astype(jnp.bfloat16), (("row", 0),), 1).astype(
        grad_mixed.dtype
    )
    grad_frame = jnp.pad(grad_frame, ((0, 0), (1, 1), (0, 0)))
    grad_input = grad_mixed
    for tap_index in range(9):
        row_shift = 2 - tap_index // 3
        col_shift = 2 - tap_index % 3
        grad_input = (
            grad_input
            + peg_taps[tap_index]
            * grad_frame[row_shift : row_shift + tile_rows, col_shift : col_shift + tile_cols]
        )
    grad_input = grad_input.reshape(1, tile_rows, tile_cols, model_width)
    vec_grads = jnp.concatenate(
        [
            jnp.stack(tap_grads),
            jnp.stack(
                [
                    g_peg_bias,
                    g_gain_one,
                    g_shift_one,
                    g_query_bias,
                    g_reduce_bias,
                    g_gain_red,
                    g_shift_red,
                    g_value_bias,
                    g_out_bias,
                    g_gain_two,
                    g_shift_two,
                    g_down_bias,
                ]
            ),
            g_up_bias.reshape(-1, model_width),
        ],
        axis=0,
    )
    vec_total = lax.psum(vec_grads, ("img", "row"))
    bases = basis_pairs(basis_narrow, basis_pair, basis_wide)
    local_grads = (g_query, g_keyval, g_out, g_up, g_down, g_reduce)
    rotated_terms = []
    for local_grad, (basis_left, basis_right) in zip(local_grads, bases):
        rotated_terms.append(
            high_dot(high_dot(basis_left.T, local_grad), basis_right).reshape(shard_count, -1)
        )
    summed = (
        lax.psum_scatter(rotated_terms[0], ("img", "row"), scatter_dimension=0, tiled=True),
        lax.psum_scatter(rotated_terms[1], ("img", "row"), scatter_dimension=0, tiled=True),
        lax.psum_scatter(rotated_terms[2], ("img", "row"), scatter_dimension=0, tiled=True),
        lax.psum_scatter(rotated_terms[3], ("img", "row"), scatter_dimension=0, tiled=True),
        lax.psum_scatter(rotated_terms[4], ("img", "row"), scatter_dimension=0, tiled=True),
        lax.psum_scatter(rotated_terms[5], ("img", "row"), scatter_dimension=0, tiled=True),
    )
    rotated = jnp.concatenate(summed, axis=1)
    correction = 1.0 - BETA**STEP
    new_first = BETA * first_moment + (1.0 - BETA) * rotated
    new_second = BETA * second_moment + (1.0 - BETA) * rotated * rotated
    direction = new_first / correction / (jnp.sqrt(new_second / correction) + ADAM_EPS)
    all_steps = lax.all_gather(direction, ("img", "row"), axis=0, tiled=True)
    turned_rows = []
    column_start = 0
    for (dim_rows, dim_cols), shard_span, (basis_left, basis_right) in zip(
        matrix_dims, shard_spans, bases
    ):
        step_matrix = all_steps[:, column_start : column_start + shard_span].reshape(
            dim_rows, dim_cols
        )
        rows_count = max(1, shard_span // dim_cols)
        entry_first = shard_rank * shard_span
        left_rows = lax.dynamic_slice_in_dim(basis_left, entry_first // dim_cols, rows_count, 0)
        turned = high_dot(high_dot(left_rows, step_matrix), basis_right.T).reshape(-1)
        turned_rows.append(turned.reshape(1, shard_span))
        column_start = column_start + shard_span
    turned_all = jnp.concatenate(turned_rows, axis=1)
    rate_row = jnp.concatenate(
        [
            jnp.full((shard_span,), rate_value, jnp.float32)
            for shard_span, rate_value in zip(shard_spans, MATRIX_RATES)
        ]
    )
    new_weights = weights - rate_row[None, :] * (turned_all + WEIGHT_DECAY * weights)
    new_ema = EMA_KEEP * weight_ema + (1.0 - EMA_KEEP) * new_weights
    vec_moment = BETA * vec_first + (1.0 - BETA) * vec_total
    vec_square = BETA * vec_second + (1.0 - BETA) * vec_total * vec_total
    vec_direction = vec_moment / correction / (jnp.sqrt(vec_square / correction) + ADAM_EPS)
    new_vectors = vectors - VECTOR_RATE * vec_direction
    new_vec_ema = EMA_KEEP * vec_ema + (1.0 - EMA_KEEP) * new_vectors
    return (
        layer_out,
        grad_input,
        new_weights,
        new_first,
        new_second,
        new_ema,
        new_vectors,
        vec_moment,
        vec_square,
        new_vec_ema,
    )


def solution(mesh):
    placed = (
        P("img", "row", None, None),
        P("img", "row", None, None),
        P("img", None),
        P(("img", "row"), None),
        P(("img", "row"), None),
        P(("img", "row"), None),
        P(("img", "row"), None),
        P(),
        P(),
        P(),
        P(),
        P(),
        P(),
        P(),
    )
    return jax.shard_map(
        on_device,
        mesh=mesh,
        in_specs=placed,
        out_specs=(
            P("img", "row", None, None),
            P("img", "row", None, None),
            P(("img", "row"), None),
            P(("img", "row"), None),
            P(("img", "row"), None),
            P(("img", "row"), None),
            P(),
            P(),
            P(),
            P(),
        ),
        check_vma=False,
    )
```

profile of v0, /device:TPU:0, one launch (start us, length us, event | category | flops | bytes accessed | tf_op | source)
XLA Modules:
  0.0 608.7 jit_solution(17747054788299024773)
XLA Ops:
  11.1 3.0 collective-permute-start
  25.9 50.4 %all-gather.5.cloned.1.call-done = bf16[32,1,32768]{2,1,0:T(2,128)(2,1)} async-done(((bf16[1,1,32768]{2,1,0:T(2,128)(2,1)}), bf16[32,1,32768]{2,1,0:T(2,128)(2,1)}) %all-gather.5.cloned.1.call-update) | async-done | bytes 2097168 | tf_op jit(solution)/shard_map/all_gather | solution.py:119
  76.2 4.5 copy.96
  92.7 9.7 %all_gather.13 = bf16[896,256]{1,0:T(8,128)(2,1)S(1)} all-gather(bf16[112,256]{1,0:T(8,128)(2,1)S(1)} %slice.516), channel_id=1, replica_groups=mesh['img'=4,'row'=8] {'row'}, dimensions={0}, use_global_device_ids=true | all-gather | bytes 516096 | tf_op jit(solution)/shard_map/all_gather | solution.py:164
  103.4 2.6 copy.63
  106.0 9.0 %all_gather.14 = bf16[896,256]{1,0:T(8,128)(2,1)S(1)} all-gather(bf16[112,256]{1,0:T(8,128)(2,1)S(1)} %fusion.118), channel_id=1, replica_groups=mesh['img'=4,'row'=8] {'row'}, dimensions={0}, use_global_device_ids=true | all-gather | bytes 516096 | tf_op jit(solution)/shard_map/all_gather | solution.py:165
  116.0 2.5 copy.64
  118.5 39.6 %while.28 = (s32[]{:T(128)}, bf16[8,448,32]{1,2,0:T(8,128)(2,1)S(1)}, f32[8,448]{1,0:T(8,128)}, bf16[8,448,32]{2,1,0:T(8,128)(2,1)S(1)}, bf16[8,896,32]{2,1,0:T(...) while((s32[]{:T(128)}, ...), condition=%wide.region_7.8_spmd.clone, body=%wide.region_4.7_spmd.clone.sunk | while | flops 54591936 | bytes 5480237 | solution.py:185
  163.5 6.4 %multiply_convert_fusion.1 = (bf16[448,1024]{1,0:T(8,128)(2,1)}, f32[448,1024]{1,0:T(8,128)S(1)}, f32[448,1024]{1,0:T(8,128)S(1)}) fusion(f32[1024]{0:T(1024)S(1)} %bitcast.419, bf16[256,1024]{1,0:T(8,128)(2,1)} %reshape.576, f32[448,256]{1,0:T(8,128)S(1)} %get-tuple-element.350, f32[256]{0:T(256)S(1)} %bitcast.412, f32[256]{0:T(256)S(1)} %bitcast.396, ...), kind=kOutput, calls=%fused_computation.68 | convolution fusion | flops 265732096 | bytes 5580288 | tf_op jit(solution)/shard_map/dot_general | solution.py:85
  175.6 73.1 %while.29 = (s32[]{:T(128)}, bf16[8,448,32]{1,2,0:T(8,128)(2,1)S(1)}, f32[8,896,32]{1,2,0:T(8,128)}, f32[8,896,32]{1,2,0:T(8,128)}, bf16[8,448,32]{2,1,0:T(8,128...) while((s32[]{:T(128)}, ...), condition=%wide.region_14.15_spmd.clone, body=%wide.region_12.14_spmd.clone.sunk | while | flops 132106688 | bytes 13338045 | solution.py:241
  253.6 2.5 copy.73
  260.9 3.8 fusion.86
  269.4 7.2 %fusion.46 = f32[256,1024]{1,0:T(8,128)} fusion(f32[1024,256]{1,0:T(8,128)} %fusion.86, f32[3,1024,1024]{2,1,0:T(8,128)} %param.31), kind=kOutput, calls=%fused_computation.59 | convolution fusion | flops 3221225472 | bytes 6291456 | tf_op jit(solution)/shard_map/dot_general | solution.py:89
  280.7 6.0 fusion.42
  286.8 3.8 fusion.84
  294.0 30.0 %reduce-scatter.7.cloned.1.call-done = f32[112,256]{1,0:T(8,128)} async-done(((f32[896,256]{1,0:T(8,128)}), f32[112,256]{1,0:T(8,128)}) %reduce-scatter.7.cloned.1.call-update) | async-done | bytes 114704
  335.0 5.8 fusion.40
  340.9 3.8 fusion.81
  347.4 144.3 %all-reduce.11.cloned.1.call-done = (f32[32,2048]{1,0:T(8,128)}, f32[32,4096]{1,0:T(8,128)}, f32[32,2048]{1,0:T(8,128)}, f32[32,8192]{1,0:T(8,128)}, f32[32,8192]{1,0:T(8,128)}, /*index=5*/f32[32,8192]{1,0:T(8,128)}) async-done(((f32[32,2048]{1,0:T(8,128)}, f32[32,4096]{1,0:T(8,128)}, f32[32,2048]{1,0:T(8,128)}, f32[32,8192]{1,0:T(8,128)}, f32[32,8192]{1,0:T(8,128)}, /*index=5*/f32[32,8192]{1,0:T(8,128)}), ...) | async-done | bytes 4194320
  501.7 8.4 %fusion.165 = (f32[1,1024,1024]{2,1,0:T(8,128)}, f32[1,1024,1024]{2,1,0:T(8,128)}) fusion(f32[3,1024,1024]{2,1,0:T(8,128)} %param.31), kind=kLoop, calls=%fused_computation.295 | loop fusion | bytes 16777216 | tf_op jit(solution)/shard_map/slice | solution.py:80
  524.6 3.0 collective-permute-start.2
  528.0 40.3 %psum.7 = f32[25,256]{1,0:T(8,128)S(1)} all-reduce(f32[25,256]{1,0:T(8,128)S(1)} %concatenate.43), channel_id=1, replica_groups=mesh['img'=4,'row'=8] {'img','row'}, use_global_device_ids=true, to_apply=%region_49.50 | all-reduce | flops 6400 | bytes 51200 | tf_op jit(solution)/shard_map/psum | solution.py:330
  570.2 4.6 copy.95
  586.3 5.7 fusion.60
  (480 shorter events, 235.2 us)
Async XLA Ops:
  7.2 323.9 %copy-start = (f32[512,512]{1,0:T(8,128)S(1)}, f32[512,512]{1,0:T(8,128)}, u32[]{:S(2)}) copy-start(f32[512,512]{1,0:T(8,128)} %param.30) | copy-start | bytes 3145732
  7.2 69.0 %all-gather.5.cloned.1.call-start = ((), (), s32[]{:S(2)}) async-start(), calls=%async_computation.2 | async-start | bytes 4325376 | tf_op jit(solution)/shard_map/all_gather | solution.py:119
  9.0 284.0 %reduce-scatter.9.cloned.1.call-start = ((), (), s32[]{:S(2)}) async-start(), calls=%async_computation.5 | async-start | bytes 1032192
  9.8 12.8 %collective-permute-start.1 = (bf16[1,56,256]{2,1,0:T(8,128)(2,1)S(1)}, bf16[1,56,256]{2,1,0:T(8,128)(2,1)S(1)}, u32[]{:S(2)}, u32[]{:S(2)}) collective-permute-start(bf16[1,56,256]{2,1,0:T(8,128)(2,1)S(1)} %get-tuple-element.321), channel_id=1, source_target_pairs={{1,0},{2,1},{3,2},{4,3},{5,4},{6,5},{7,6},{9,8},{10,9},{11,10},{12... | collective-permute-start | bytes 86024 | tf_op jit(solution)/shard_map/ppermute | solution.py:33
  11.1 11.5 %collective-permute-start = (bf16[1,56,256]{2,1,0:T(8,128)(2,1)S(1)}, bf16[1,56,256]{2,1,0:T(8,128)(2,1)S(1)}, u32[]{:S(2)}, u32[]{:S(2)}) collective-permute-start(bf16[1,56,256]{2,1,0:T(8,128)(2,1)S(1)} %get-tuple-element.320), channel_id=1, source_target_pairs={{0,1},{1,2},{2,3},{3,4},{4,5},{5,6},{6,7},{8,9},{9,10},{10,11},{11... | collective-permute-start | bytes 86024 | tf_op jit(solution)/shard_map/ppermute | solution.py:31
  21.3 69.1 %copy-start.70 = (f32[1,256]{1,0:T(1,128)}, f32[1,256]{1,0:T(1,128)S(1)}, u32[]{:S(2)}) copy-start(f32[1,256]{1,0:T(1,128)S(1)} %get-tuple-element.327) | copy-start | bytes 3076
  24.1 136.6 %copy-start.1 = (f32[8,56,256]{2,1,0:T(8,128)}, f32[8,56,256]{2,1,0:T(8,128)S(1)}, u32[]{:S(2)}) copy-start(f32[8,56,256]{2,1,0:T(8,128)S(1)} %get-tuple-element.297) | copy-start | bytes 1376260
  24.5 56.2 %copy-start.40 = (f32[8,56]{1,0:T(8,128)}, f32[8,56]{1,0:T(8,128)S(1)}, u32[]{:S(2)}) copy-start(f32[8,56]{1,0:T(8,128)S(1)} %multiply_reduce_fusion.15) | copy-start | bytes 5380
  24.8 58.5 %copy-start.19 = (bf16[8,56,256]{2,1,0:T(8,128)(2,1)}, bf16[8,56,256]{2,1,0:T(8,128)(2,1)S(1)}, u32[]{:S(2)}) copy-start(bf16[8,56,256]{2,1,0:T(8,128)(2,1)S(1)} %get-tuple-element.295) | copy-start | bytes 688132
  251.2 72.9 %reduce-scatter.7.cloned.1.call-start = ((), (), s32[]{:S(2)}) async-start(), calls=%async_computation.4 | async-start | bytes 1032192
  264.7 226.9 %all-reduce.11.cloned.1.call-start = ((), (), s32[]{:S(2)}) async-start(), calls=%async_computation.6 | async-start | bytes 8388608
  347.1 150.2 %copy-start.35 = (f32[1,32768]{1,0:T(1,128)S(1)}, f32[1,32768]{1,0:T(1,128)}, u32[]{:S(2)}) copy-start(f32[1,32768]{1,0:T(1,128)} %param.22) | copy-start | bytes 393220
  347.1 150.2 %copy-start.36 = (f32[1,32768]{1,0:T(1,128)S(1)}, f32[1,32768]{1,0:T(1,128)}, u32[]{:S(2)}) copy-start(f32[1,32768]{1,0:T(1,128)} %param.23) | copy-start | bytes 393220
  347.1 151.7 %copy-start.18 = (bf16[1,8,56,256]{3,2,1,0:T(8,128)(2,1)S(1)}, bf16[1,8,56,256]{3,2,1,0:T(8,128)(2,1)}, u32[]{:S(2)}) copy-start(bf16[1,8,56,256]{3,2,1,0:T(8,128)(2,1)} %param.19) | copy-start | bytes 688132
  347.1 223.1 %all-gather.7.cloned.1.call-start = ((), (), s32[]{:S(2)}) async-start(), calls=%async_computation.3 | async-start | bytes 4325376 | tf_op jit(solution)/shard_map/all_gather | solution.py:351
  523.2 45.8 %copy-start.52 = (f32[1,256]{1,0:T(1,128)S(1)}, f32[1,256]{1,0:T(1,128)}, u32[]{:S(2)}) copy-start(f32[1,256]{1,0:T(1,128)} %copy-done.51) | copy-start | bytes 3076
  523.2 45.8 %copy-start.54 = (f32[1,256]{1,0:T(1,128)S(1)}, f32[1,256]{1,0:T(1,128)}, u32[]{:S(2)}) copy-start(f32[1,256]{1,0:T(1,128)} %copy-done.53) | copy-start | bytes 3076
  523.2 45.8 %copy-start.56 = (f32[1,256]{1,0:T(1,128)S(1)}, f32[1,256]{1,0:T(1,128)}, u32[]{:S(2)}) copy-start(f32[1,256]{1,0:T(1,128)} %copy-done.55) | copy-start | bytes 3076
  523.2 45.8 %copy-start.58 = (f32[1,256]{1,0:T(1,128)S(1)}, f32[1,256]{1,0:T(1,128)}, u32[]{:S(2)}) copy-start(f32[1,256]{1,0:T(1,128)} %copy-done.57) | copy-start | bytes 3076
  523.2 45.8 %copy-start.60 = (f32[1,256]{1,0:T(1,128)S(1)}, f32[1,256]{1,0:T(1,128)}, u32[]{:S(2)}) copy-start(f32[1,256]{1,0:T(1,128)} %copy-done.59) | copy-start | bytes 3076
  523.2 45.8 %copy-start.62 = (f32[1,256]{1,0:T(1,128)S(1)}, f32[1,256]{1,0:T(1,128)}, u32[]{:S(2)}) copy-start(f32[1,256]{1,0:T(1,128)} %copy-done.61) | copy-start | bytes 3076
  523.2 45.8 %copy-start.64 = (f32[1,256]{1,0:T(1,128)S(1)}, f32[1,256]{1,0:T(1,128)}, u32[]{:S(2)}) copy-start(f32[1,256]{1,0:T(1,128)} %copy-done.63) | copy-start | bytes 3076
  523.3 45.6 %collective-permute-start.3 = (bf16[1,56,256]{2,1,0:T(8,128)(2,1)S(1)}, bf16[1,56,256]{2,1,0:T(8,128)(2,1)S(1)}, u32[]{:S(2)}, u32[]{:S(2)}) collective-permute-start(bf16[1,56,256]{2,1,0:T(8,128)(2,1)S(1)} %get-tuple-element.319), channel_id=1, source_target_pairs={{1,0},{2,1},{3,2},{4,3},{5,4},{6,5},{7,6},{9,8},{10,9},{11,10},{12... | collective-permute-start | bytes 86024 | tf_op jit(solution)/shard_map/ppermute | solution.py:33
  524.6 44.3 %collective-permute-start.2 = (bf16[1,56,256]{2,1,0:T(8,128)(2,1)S(1)}, bf16[1,56,256]{2,1,0:T(8,128)(2,1)S(1)}, u32[]{:S(2)}, u32[]{:S(2)}) collective-permute-start(bf16[1,56,256]{2,1,0:T(8,128)(2,1)S(1)} %get-tuple-element.318), channel_id=1, source_target_pairs={{0,1},{1,2},{2,3},{3,4},{4,5},{5,6},{6,7},{8,9},{9,10},{10,11},{11... | collective-permute-start | bytes 86024 | tf_op jit(solution)/shard_map/ppermute | solution.py:31
  (77 other events, 900.8 us)
Sparse Core Ops, SparseCore 0:
  11.5 64.7 all-gather.4
  251.3 34.0 reduce-scatter.8
  288.6 35.4 reduce-scatter.6
  347.2 144.3 all-reduce.10
  498.8 61.7 all-gather.6
where the time goes:
time: 619 us; the launch traced here: 609 us
  waiting for transfers between devices  225 us (36%)
  matrix products  172 us (28%)
  local copies, waits for them, and re-layouts  104 us (17%)
  blocking collectives  58.9 us (10%)
  other arithmetic  23.2 us (4%)
  between operations  15.9 us (3%)
  starting transfers between devices  9.46 us (2%)
    unnamed x8, waiting for transfers between devices  174 us
    dot_general x26, matrix products, high_dot(): jnp.dot(left_side, right_side, precision=HIGH, preferred_element_type=jnp...  62.6 us
    all_gather x1, waiting for transfers between devices, on_device(): lax.all_gather(weights.astype(jnp.bfloat16), ('img', 'row'), axis=0, tile...  50.4 us
    psum x1, blocking collectives, on_device(): vec_total = lax.psum(vec_grads, ('img', 'row'))  40.3 us
    unnamed x211, local copies, waits for them, and re-layouts  31.8 us
    dot_general x8, matrix products, head_backward(): jnp.einsum('qk,qd->kd', grad_scores, q_part, preferred_element_type=jnp.f...  14.7 us
    dot_general x8, matrix products, head_backward(): jnp.einsum('qd,kd->qk', q_part, k_part, preferred_element_type=jnp.float32)  13.6 us
    dot_general x8, matrix products, head_backward(): jnp.einsum('qk,qd->kd', softmax_rows.astype(jnp.bfloat16), g_part, prefer...  13.4 us
  transfers between devices with their start and end apart: 9, of which 3 were waited for; matrix products, arithmetic and copies ran while one was open for 13% of the time, Pallas kernels for 0%

commit v1 on v0

--- a/solution.py
+++ b/solution.py
@@ -18,6 +18,159 @@
 VECTOR_RATE = 0.06
 MATRIX_RATES = (0.04, 0.02, 0.25, 0.02, 0.01, 0.01)
 HIGH = lax.Precision.HIGHEST
+
+
+import functools
+import math
+from jax.experimental import pallas as pl
+from jax.experimental.pallas import tpu as pltpu
+LOG2E = math.log2(math.e)
+f32 = jnp.float32
+bf16 = jnp.bfloat16
+
+
+def contract(a, b, ca, cb, **kw):
+    return lax.dot_general(
+        a, b, (((ca,), (cb,)), ((), ())), preferred_element_type=f32, **kw
+    )
+
+
+def over_heads(body, heads, unroll):
+    if unroll:
+        for head in range(heads):
+            body(head)
+    else:
+
+        def step(head, carry):
+            body(head)
+            return carry
+
+        lax.fori_loop(0, heads, step, 0)
+
+
+def head_columns(head):
+    group = head // 4
+    if isinstance(head, int):
+        return slice(group * 128, group * 128 + 128)
+    return pl.ds(pl.multiple_of(group * 128, 128), 128)
+
+
+def head_rows(head, base=0):
+    if isinstance(head, int):
+        return slice(base + head * 32, base + head * 32 + 32)
+    return pl.ds(pl.multiple_of(base + head * 32, 32), 32)
+
+
+def attend_kernel(step, unroll, q_ref, k_ref, v_ref, mask_ref, o_ref, log_ref):
+    tokens = q_ref.shape[0]
+    scale = 32**-0.5 * LOG2E
+    lane = lax.broadcasted_iota(jnp.int32, (1, 128), 1) // 32
+    mask = mask_ref[...]
+
+    def one_head(head):
+        cols = head_columns(head)
+        mine = lane == head % 4
+        keys = jnp.where(mine, k_ref[:, cols], 0)
+        values = jnp.where(mine, v_ref[:, cols], 0)
+
+        def block(start):
+            rows = pl.ds(start, step)
+            scores = contract(q_ref[rows, cols], keys, 1, 1) * scale + mask
+            top = jnp.max(scores, axis=1, keepdims=True)
+            exponent = jnp.exp2(scores - top)
+            total = jnp.sum(exponent, axis=1, keepdims=True)
+            probs = (exponent * (1.0 / total)).astype(bf16)
+            out = contract(probs, values, 1, 0)
+            o_ref[rows, cols] = jnp.where(mine, out, o_ref[rows, cols])
+            log_ref[head, rows, :] = jnp.broadcast_to(top + jnp.log2(total), (step, 128))
+
+        over_blocks(block, tokens, step)
+
+    over_heads(one_head, HEADS, unroll)
+
+
+def over_blocks(block, tokens, step):
+    if tokens == step:
+        block(0)
+    else:
+
+        def go(index, carry):
+            block(pl.multiple_of(index * step, step))
+            return carry
+
+        lax.fori_loop(0, tokens // step, go, 0)
+
+
+def attend(q, k, v, mask):
+    tokens, width = q.shape
+    unroll = k.shape[0] <= 1024
+    return pl.pallas_call(
+        functools.partial(attend_kernel, tokens if unroll else 64, unroll),
+        out_shape=(
+            jax.ShapeDtypeStruct((tokens, width), f32),
+            jax.ShapeDtypeStruct((HEADS, tokens, 128), f32),
+        ),
+        compiler_params=pltpu.CompilerParams(vmem_limit_bytes=40 * 2**20),
+        name="attend",
+    )(q, k, v, mask)
+
+
+def attend_back_kernel(
+    step, unroll, q_ref, k_ref, v_ref, mask_ref, o_ref, log_ref, g_ref, dq_ref, dkv_ref, ps, dss, qt, gt
+):
+    tokens, width = q_ref.shape
+    scale = 32**-0.5
+    lane = lax.broadcasted_iota(jnp.int32, (1, 128), 1) // 32
+    mask = mask_ref[...]
+    qt[...] = q_ref[...].astype(f32).T.astype(bf16)
+    gt[...] = g_ref[...].astype(f32).T.astype(bf16)
+
+    def one_head(head):
+        cols = head_columns(head)
+        mine = lane == head % 4
+        keys = jnp.where(mine, k_ref[:, cols], 0)
+        values = jnp.where(mine, v_ref[:, cols], 0)
+
+        def block(start):
+            rows = pl.ds(start, step)
+            grad = g_ref[rows, cols]
+            inner = jnp.sum(
+                jnp.where(mine, grad.astype(f32) * o_ref[rows, cols], 0.0), axis=1, keepdims=True
+            )
+            scores = contract(q_ref[rows, cols], keys, 1, 1)
+            probs = jnp.exp2(scores * (scale * LOG2E) + mask - log_ref[head, rows, 0:1])
+            grad_scores = (probs * (contract(grad, values, 1, 1) - inner)).astype(bf16)
+            ps[rows, :] = probs.astype(bf16)
+            dss[rows, :] = grad_scores
+            out = contract(grad_scores, keys, 1, 0) * scale
+            dq_ref[rows, cols] = jnp.where(mine, out, dq_ref[rows, cols])
+
+        over_blocks(block, tokens, step)
+        dkv_ref[head_rows(head), :] = contract(qt[head_rows(head), :], dss[...], 1, 0) * scale
+        dkv_ref[head_rows(head, width), :] = contract(gt[head_rows(head), :], ps[...], 1, 0)
+
+    over_heads(one_head, HEADS, unroll)
+
+
+def attend_back(q, k, v, mask, o, log, grad):
+    tokens, width = q.shape
+    keys = k.shape[0]
+    unroll = keys <= 1024
+    return pl.pallas_call(
+        functools.partial(attend_back_kernel, tokens if unroll else 64, unroll),
+        out_shape=(
+            jax.ShapeDtypeStruct((tokens, width), f32),
+            jax.ShapeDtypeStruct((2 * width, keys), f32),
+        ),
+        scratch_shapes=[
+            pltpu.VMEM((tokens, keys), bf16),
+            pltpu.VMEM((tokens, keys), bf16),
+            pltpu.VMEM((width, tokens), bf16),
+            pltpu.VMEM((width, tokens), bf16),
+        ],
+        compiler_params=pltpu.CompilerParams(vmem_limit_bytes=56 * 2**20),
+        name="attend_back",
+    )(q, k, v, mask, o, log, grad)
 
 
 def extended(cells, sides, width):
@@ -164,26 +317,9 @@
         lax.all_gather(own_keys, "row", axis=0, tiled=True),
         lax.all_gather(own_values, "row", axis=0, tiled=True),
     )
-    key_heads = all_keys.reshape(-1, HEADS, head_width).transpose(1, 0, 2)
-    value_heads = all_values.reshape(-1, HEADS, head_width).transpose(1, 0, 2)
-    query_heads = queries.reshape(token_count, HEADS, head_width).transpose(1, 0, 2)
-
-    def head_forward(operands):
-        q_part, k_part, v_part = operands
-        scores = (
-            jnp.einsum("qd,kd->qk", q_part, k_part, preferred_element_type=jnp.float32)
-            * score_scale
-        )
-        scores = jnp.where(key_inside[None, :], scores, -1e30)
-        row_top = jnp.max(scores, axis=1, keepdims=True)
-        exponent = jnp.exp(scores - row_top)
-        row_total = jnp.sum(exponent, axis=1, keepdims=True)
-        softmax_rows = (exponent / row_total).astype(jnp.bfloat16)
-        head_out = jnp.einsum("qk,kd->qd", softmax_rows, v_part, preferred_element_type=jnp.float32)
-        return (head_out, (row_top + jnp.log(row_total))[:, 0])
-
-    head_out, log_totals = lax.map(head_forward, (query_heads, key_heads, value_heads))
-    attended = head_out.transpose(1, 0, 2).reshape(token_count, model_width).astype(jnp.bfloat16)
+    key_mask = jnp.where(key_inside, 0.0, -1e30).astype(f32)[None, :]
+    o32, logs = attend(queries, all_keys, all_values, key_mask)
+    attended = o32.astype(jnp.bfloat16)
     residual = mixed_in.reshape(token_count, model_width) + (low_dot(attended, w_out) + out_bias)
     second_in = layer_norm(residual, gain_two, shift_two).astype(jnp.bfloat16)
     up_input = low_dot(second_in, w_up) + up_bias
@@ -209,41 +345,10 @@
     grad_att = jnp.einsum(
         "te,de->td", grad_branch, w_out, preferred_element_type=jnp.float32
     ).astype(jnp.bfloat16)
-    grad_heads = grad_att.reshape(token_count, HEADS, head_width).transpose(1, 0, 2)
-
-    def head_backward(operands):
-        q_part, k_part, v_part, g_part, log_total = operands
-        scores = (
-            jnp.einsum("qd,kd->qk", q_part, k_part, preferred_element_type=jnp.float32)
-            * score_scale
-        )
-        scores = jnp.where(key_inside[None, :], scores, -1e30)
-        softmax_rows = jnp.exp(scores - log_total[:, None])
-        grad_probs = jnp.einsum("qd,kd->qk", g_part, v_part, preferred_element_type=jnp.float32)
-        inner_sum = jnp.sum(softmax_rows * grad_probs, axis=1, keepdims=True)
-        grad_scores = (softmax_rows * (grad_probs - inner_sum)).astype(jnp.bfloat16)
-        grad_q = (
-            jnp.einsum("qk,kd->qd", grad_scores, k_part, preferred_element_type=jnp.float32)
-            * score_scale
-        )
-        grad_k = (
-            jnp.einsum("qk,qd->kd", grad_scores, q_part, preferred_element_type=jnp.float32)
-            * score_scale
-        )
-        grad_v = jnp.einsum(
-            "qk,qd->kd",
-            softmax_rows.astype(jnp.bfloat16),
-            g_part,
-            preferred_element_type=jnp.float32,
-        )
-        return (grad_q, grad_k, grad_v)
-
-    grad_qh, grad_kh, grad_vh = lax.map(
-        head_backward, (query_heads, key_heads, value_heads, grad_heads, log_totals)
-    )
-    grad_query = grad_qh.transpose(1, 0, 2).reshape(token_count, model_width).astype(jnp.bfloat16)
-    grad_keys_all = grad_kh.transpose(1, 0, 2).reshape(-1, model_width)
-    grad_vals_all = grad_vh.transpose(1, 0, 2).reshape(-1, model_width)
+    dq32, dkv_t = attend_back(queries, all_keys, all_values, key_mask, o32, logs, grad_att)
+    grad_query = dq32.astype(jnp.bfloat16)
+    grad_keys_all = dkv_t[:model_width].T
+    grad_vals_all = dkv_t[model_width:].T
     keyval_wide = w_keyval.astype(jnp.float32)
     own_grad_keys, own_grad_vals = (
         lax.psum_scatter(grad_keys_all, "row", scatter_dimension=0, tiled=True),

time: 619 us -> 508 us (0.82)
  matrix products: 172 us -> 84.1 us
  local copies, waits for them, and re-layouts: 104 us -> 73.6 us
  Pallas kernels: 0 us -> 18.7 us
    dot_general x56 -> x0, matrix products: 86.9 us -> none  [the longest x8 14.7 us: head_backward(): jnp.einsum('qk,qd->kd', grad_scores, q_part, preferred_element_type=jnp.f...]
    pallas_call x0 -> x2, Pallas kernels: none -> 18.7 us  [the longest x1 11.3 us: attend_back(): pl.pallas_call(functools.partial(attend_back_kernel, tokens if unroll els...]
    dynamic_update_slice x8 -> x0, local copies, waits for them, and re-layouts: 10.7 us -> none  [on_device(): lax.map(head_forward, (query_heads, key_heads, value_heads))]
    unnamed x211 -> x140, local copies, waits for them, and re-layouts: 31.8 us -> 25.6 us
  transfers between devices with their start and end apart: 9 -> 9, of which waited for: 3 -> 3; matrix products, arithmetic and copies ran while one was open for 13% -> 17% of each run, Pallas kernels for 0% -> 0%
where the time goes in v1:
time: 508 us; the launch traced here: 501 us
  waiting for transfers between devices  221 us (44%)
  matrix products  84.1 us (17%)
  local copies, waits for them, and re-layouts  73.6 us (14%)
  blocking collectives  59.1 us (12%)
  other arithmetic  20 us (4%)
  Pallas kernels  18.7 us (4%)
  between operations  15.2 us (3%)
  starting transfers between devices  9.31 us (2%)
    unnamed x8, waiting for transfers between devices  171 us
    dot_general x26, matrix products, high_dot(): jnp.dot(left_side, right_side, precision=HIGH, preferred_element_type=jnp...  62.5 us
    all_gather x1, waiting for transfers between devices, on_device(): lax.all_gather(weights.astype(jnp.bfloat16), ('img', 'row'), axis=0, tile...  50.4 us
    psum x1, blocking collectives, on_device(): vec_total = lax.psum(vec_grads, ('img', 'row'))  40.4 us
    unnamed x140, local copies, waits for them, and re-layouts  25.6 us
    dot_general x6, matrix products, low_dot(): return jnp.dot(left_side, right_side, preferred_element_type=jnp.float32)  12.6 us
    reshape x6, local copies, waits for them, and re-layouts, on_device(): high_dot(high_dot(basis_left.T, local_grad), basis_right)  11.6 us
    pallas_call x1, Pallas kernels, attend_back(): pl.pallas_call(functools.partial(attend_back_kernel, tokens if unroll els...  11.3 us
  transfers between devices with their start and end apart: 9, of which 3 were waited for; matrix products, arithmetic and copies ran while one was open for 17% of the time, Pallas kernels for 0%

profile of v1, /device:TPU:0, one launch (start us, length us, event | category | flops | bytes accessed | tf_op | source)
XLA Modules:
  0.0 501.0 jit_solution(3283420626958731331)
XLA Ops:
  11.1 3.0 collective-permute-start
  25.8 50.4 %all-gather.5.cloned.1.call-done = bf16[32,1,32768]{2,1,0:T(2,128)(2,1)} async-done(((bf16[1,1,32768]{2,1,0:T(2,128)(2,1)}), bf16[32,1,32768]{2,1,0:T(2,128)(2,1)}) %all-gather.5.cloned.1.call-update) | async-done | bytes 2097168 | tf_op jit(solution)/shard_map/all_gather | solution.py:272
  76.2 4.5 copy.50
  83.8 9.7 %all_gather.13.k_ref = bf16[896,256]{1,0:T(8,128)(2,1)S(1)} all-gather(bf16[112,256]{1,0:T(8,128)(2,1)S(1)} %slice.526), channel_id=1, replica_groups=mesh['img'=4,'row'=8] {'row'}, dimensions={0}, use_global_device_ids=true | all-gather | bytes 516096 | tf_op jit(solution)/shard_map/all_gather | solution.py:317
  93.5 8.9 %all_gather.14.v_ref = bf16[896,256]{1,0:T(8,128)(2,1)S(1)} all-gather(bf16[112,256]{1,0:T(8,128)(2,1)S(1)} %fusion.77), channel_id=1, replica_groups=mesh['img'=4,'row'=8] {'row'}, dimensions={0}, use_global_device_ids=true | all-gather | bytes 516096 | tf_op jit(solution)/shard_map/all_gather | solution.py:318
  106.0 7.4 %attend.1 = (f32[448,256]{1,0:T(8,128)S(1)}, f32[8,448,128]{2,1,0:T(8,128)S(1)}) custom-call(bf16[448,256]{1,0:T(8,128)(2,1)S(1)} %fusion.18.q_ref, bf16[896,256]{1,0:T(8,128)(2,1)S(1)} %all_gather.13.k_ref, bf16[896,256]{1,0:T(8,128)(2,1)S(1)} %all_gather.14.v_ref, f32[1,896]{1,0:T(1,128)S(1)} %select_n.45.mask_ref), custom_call_target="tpu_custom_call" | custom-call | tf_op jit(solution)/shard_map/attend/pallas_call | solution.py:107
  118.6 6.8 %multiply_convert_fusion = (bf16[448,1024]{1,0:T(8,128)(2,1)}, f32[448,1024]{1,0:T(8,128)S(1)}, f32[448,1024]{1,0:T(8,128)S(1)}) fusion(f32[1024]{0:T(1024)S(1)} %bitcast.294, bf16[256,1024]{1,0:T(8,128)(2,1)} %reshape.545, f32[448,256]{1,0:T(8,128)} %copy-done.10, f32[256]{0:T(256)S(1)} %bitcast.286, f32[256]{0:T(256)S(1)} %bitcast.270, ...), kind=kOutput, calls=%fused_computation.16 | convolution fusion | flops 265732096 | bytes 5580288 | tf_op jit(solution)/shard_map/dot_general | solution.py:238
  130.3 11.3 %attend_back.1 = (f32[448,256]{1,0:T(8,128)}, f32[512,896]{1,0:T(8,128)}) custom-call(bf16[448,256]{1,0:T(8,128)(2,1)} %copy-done.5, bf16[896,256]{1,0:T(8,128)(2,1)} %copy-done.3, bf16[896,256]{1,0:T(8,128)(2,1)} %copy-done.4, f32[1,896]{1,0:T(1,128)} %copy-done.7, f32[448,256]{1,0:T(8,128)} %copy-done.1, f32[8,448,128]{2,1,0:T(8,128)} %copy-done.6, ...), custom_call_target="tpu_custom_call" | custom-call | tf_op jit(solution)/shard_map/attend_back/pallas_call | solution.py:159
  141.6 2.8 slice_bitcast_fusion.1
  152.4 2.5 copy.32
  159.7 3.8 fusion.45
  169.2 7.2 %fusion.6 = f32[256,1024]{1,0:T(8,128)} fusion(f32[1024,256]{1,0:T(8,128)} %fusion.45, f32[3,1024,1024]{2,1,0:T(8,128)} %param.27), kind=kOutput, calls=%fused_computation.7 | convolution fusion | flops 3221225472 | bytes 6291456 | tf_op jit(solution)/shard_map/dot_general | solution.py:242
  180.5 6.0 %fusion.2 = f32[256,1024]{1,0:T(8,128)S(1)} fusion(f32[1024,256]{1,0:T(8,128)S(1)} %fusion.139, f32[3,1024,1024]{2,1,0:T(8,128)} %param.27), kind=kOutput, calls=%fused_computation.3 | convolution fusion | flops 3221225472 | bytes 6291456 | tf_op jit(solution)/shard_map/dot_general | solution.py:242
  186.5 3.8 fusion.43
  190.3 2.5 reshape.555
  193.8 25.9 %reduce-scatter.7.cloned.1.call-done = f32[112,256]{1,0:T(8,128)} async-done(((f32[896,256]{1,0:T(8,128)}), f32[112,256]{1,0:T(8,128)}) %reduce-scatter.7.cloned.1.call-update) | async-done | bytes 114704
  227.4 5.8 %fusion = f32[256,1024]{1,0:T(8,128)S(1)} fusion(f32[1024,256]{1,0:T(8,128)S(1)} %fusion.140, f32[3,1024,1024]{2,1,0:T(8,128)} %param.27), kind=kOutput, calls=%fused_computation.1 | convolution fusion | flops 3221225472 | bytes 6291456 | tf_op jit(solution)/shard_map/dot_general | solution.py:242
  233.2 3.8 fusion.40
  239.5 144.6 %all-reduce.11.cloned.1.call-done = (f32[32,2048]{1,0:T(8,128)}, f32[32,4096]{1,0:T(8,128)}, f32[32,2048]{1,0:T(8,128)}, f32[32,8192]{1,0:T(8,128)}, f32[32,8192]{1,0:T(8,128)}, /*index=5*/f32[32,8192]{1,0:T(8,128)}) async-done(((f32[32,2048]{1,0:T(8,128)}, f32[32,4096]{1,0:T(8,128)}, f32[32,2048]{1,0:T(8,128)}, f32[32,8192]{1,0:T(8,128)}, f32[32,8192]{1,0:T(8,128)}, /*index=5*/f32[32,8192]{1,0:T(8,128)}), ...) | async-done | bytes 4194320
  394.1 8.4 %fusion.125 = (f32[1,1024,1024]{2,1,0:T(8,128)}, f32[1,1024,1024]{2,1,0:T(8,128)}) fusion(f32[3,1024,1024]{2,1,0:T(8,128)} %param.27), kind=kLoop, calls=%fused_computation.246 | loop fusion | bytes 16777216 | tf_op jit(solution)/shard_map/slice | solution.py:233
  413.3 3.0 collective-permute-start.2
  419.5 40.4 %psum.7 = f32[25,256]{1,0:T(8,128)S(1)} all-reduce(f32[25,256]{1,0:T(8,128)S(1)} %concatenate.43), channel_id=1, replica_groups=mesh['img'=4,'row'=8] {'img','row'}, use_global_device_ids=true, to_apply=%region_42.43 | all-reduce | flops 6400 | bytes 51200 | tf_op jit(solution)/shard_map/psum | solution.py:435
  462.7 4.6 copy.49
  478.8 5.7 %fusion.20 = f32[1,1,8,1024]{3,2,1,0:T(8,128)S(1)} fusion(f32[8,1024]{1,0:T(8,128)S(1)} %fusion.84, f32[3,1024,1024]{2,1,0:T(8,128)} %param.27), kind=kOutput, calls=%fused_computation.41 | convolution fusion | flops 100663296 | bytes 4259840 | tf_op jit(solution)/shard_map/dot_general | solution.py:242
  (273 shorter events, 112.8 us)
Async XLA Ops:
  7.2 217.3 %copy-start = (f32[512,512]{1,0:T(8,128)S(1)}, f32[512,512]{1,0:T(8,128)}, u32[]{:S(2)}) copy-start(f32[512,512]{1,0:T(8,128)} %param.26) | copy-start | bytes 3145732
  7.2 69.0 %all-gather.5.cloned.1.call-start = ((), (), s32[]{:S(2)}) async-start(), calls=%async_computation.2 | async-start | bytes 4325376 | tf_op jit(solution)/shard_map/all_gather | solution.py:272
  9.0 183.8 %reduce-scatter.9.cloned.1.call-start = ((), (), s32[]{:S(2)}) async-start(), calls=%async_computation.5 | async-start | bytes 1032192
  9.8 12.3 %collective-permute-start.1 = (bf16[1,56,256]{2,1,0:T(8,128)(2,1)S(1)}, bf16[1,56,256]{2,1,0:T(8,128)(2,1)S(1)}, u32[]{:S(2)}, u32[]{:S(2)}) collective-permute-start(bf16[1,56,256]{2,1,0:T(8,128)(2,1)S(1)} %get-tuple-element.91), channel_id=1, source_target_pairs={{1,0},{2,1},{3,2},{4,3},{5,4},{6,5},{7,6},{9,8},{10,9},{11,10},{12... | collective-permute-start | bytes 86024 | tf_op jit(solution)/shard_map/ppermute | solution.py:186
  11.1 11.0 %collective-permute-start = (bf16[1,56,256]{2,1,0:T(8,128)(2,1)S(1)}, bf16[1,56,256]{2,1,0:T(8,128)(2,1)S(1)}, u32[]{:S(2)}, u32[]{:S(2)}) collective-permute-start(bf16[1,56,256]{2,1,0:T(8,128)(2,1)S(1)} %get-tuple-element.90), channel_id=1, source_target_pairs={{0,1},{1,2},{2,3},{3,4},{4,5},{5,6},{6,7},{8,9},{9,10},{10,11},{11... | collective-permute-start | bytes 86024 | tf_op jit(solution)/shard_map/ppermute | solution.py:184
  21.5 84.5 %copy-start.7 = (f32[1,896]{1,0:T(1,128)}, f32[1,896]{1,0:T(1,128)S(1)}, u32[]{:S(2)}) copy-start(f32[1,896]{1,0:T(1,128)S(1)} %select_n.45.mask_ref) | copy-start | bytes 10756
  25.7 57.3 %copy-start.21 = (bf16[112,1024]{1,0:T(8,128)(2,1)}, bf16[112,1024]{1,0:T(8,128)(2,1)S(1)}, u32[]{:S(2)}) copy-start(bf16[112,1024]{1,0:T(8,128)(2,1)S(1)} %reshape.541) | copy-start | bytes 688132
  146.9 72.9 %reduce-scatter.7.cloned.1.call-start = ((), (), s32[]{:S(2)}) async-start(), calls=%async_computation.4 | async-start | bytes 1032192
  163.5 220.6 %all-reduce.11.cloned.1.call-start = ((), (), s32[]{:S(2)}) async-start(), calls=%async_computation.6 | async-start | bytes 8388608
  190.3 30.5 %copy-start.15 = (bf16[256,512]{1,0:T(8,128)(2,1)S(1)}, bf16[256,512]{1,0:T(8,128)(2,1)}, u32[]{:S(2)}) copy-start(bf16[256,512]{1,0:T(8,128)(2,1)} %copy-done.14) | copy-start | bytes 786436
  239.4 150.3 %copy-start.30 = (f32[1,32768]{1,0:T(1,128)S(1)}, f32[1,32768]{1,0:T(1,128)}, u32[]{:S(2)}) copy-start(f32[1,32768]{1,0:T(1,128)} %param.18) | copy-start | bytes 393220
  239.4 150.3 %copy-start.31 = (f32[1,32768]{1,0:T(1,128)S(1)}, f32[1,32768]{1,0:T(1,128)}, u32[]{:S(2)}) copy-start(f32[1,32768]{1,0:T(1,128)} %param.19) | copy-start | bytes 393220
  239.4 151.9 %copy-start.19 = (bf16[1,8,56,256]{3,2,1,0:T(8,128)(2,1)S(1)}, bf16[1,8,56,256]{3,2,1,0:T(8,128)(2,1)}, u32[]{:S(2)}) copy-start(bf16[1,8,56,256]{3,2,1,0:T(8,128)(2,1)} %param.15) | copy-start | bytes 688132
  239.5 223.3 %all-gather.7.cloned.1.call-start = ((), (), s32[]{:S(2)}) async-start(), calls=%async_computation.3 | async-start | bytes 4325376 | tf_op jit(solution)/shard_map/all_gather | solution.py:456
  410.6 49.4 %copy-start.34 = (f32[25,256]{1,0:T(8,128)S(1)}, f32[25,256]{1,0:T(8,128)}, u32[]{:S(2)}) copy-start(f32[25,256]{1,0:T(8,128)} %param.21) | copy-start | bytes 76804
  411.9 49.6 %copy-start.36 = (f32[1,256]{1,0:T(1,128)S(1)}, f32[1,256]{1,0:T(1,128)}, u32[]{:S(2)}) copy-start(f32[1,256]{1,0:T(1,128)} %copy-done.35) | copy-start | bytes 3076
  411.9 49.7 %copy-start.38 = (f32[1,256]{1,0:T(1,128)S(1)}, f32[1,256]{1,0:T(1,128)}, u32[]{:S(2)}) copy-start(f32[1,256]{1,0:T(1,128)} %copy-done.37) | copy-start | bytes 3076
  411.9 49.7 %copy-start.40 = (f32[1,256]{1,0:T(1,128)S(1)}, f32[1,256]{1,0:T(1,128)}, u32[]{:S(2)}) copy-start(f32[1,256]{1,0:T(1,128)} %copy-done.39) | copy-start | bytes 3076
  411.9 49.7 %copy-start.42 = (f32[1,256]{1,0:T(1,128)S(1)}, f32[1,256]{1,0:T(1,128)}, u32[]{:S(2)}) copy-start(f32[1,256]{1,0:T(1,128)} %copy-done.41) | copy-start | bytes 3076
  411.9 49.7 %copy-start.44 = (f32[1,256]{1,0:T(1,128)S(1)}, f32[1,256]{1,0:T(1,128)}, u32[]{:S(2)}) copy-start(f32[1,256]{1,0:T(1,128)} %copy-done.43) | copy-start | bytes 3076
  411.9 49.7 %copy-start.46 = (f32[1,256]{1,0:T(1,128)S(1)}, f32[1,256]{1,0:T(1,128)}, u32[]{:S(2)}) copy-start(f32[1,256]{1,0:T(1,128)} %copy-done.45) | copy-start | bytes 3076
  411.9 49.7 %copy-start.48 = (f32[1,256]{1,0:T(1,128)S(1)}, f32[1,256]{1,0:T(1,128)}, u32[]{:S(2)}) copy-start(f32[1,256]{1,0:T(1,128)} %copy-done.47) | copy-start | bytes 3076
  412.0 49.5 %collective-permute-start.3 = (bf16[1,56,256]{2,1,0:T(8,128)(2,1)S(1)}, bf16[1,56,256]{2,1,0:T(8,128)(2,1)S(1)}, u32[]{:S(2)}, u32[]{:S(2)}) collective-permute-start(bf16[1,56,256]{2,1,0:T(8,128)(2,1)S(1)} %get-tuple-element.89), channel_id=1, source_target_pairs={{1,0},{2,1},{3,2},{4,3},{5,4},{6,5},{7,6},{9,8},{10,9},{11,10},{12... | collective-permute-start | bytes 86024 | tf_op jit(solution)/shard_map/ppermute | solution.py:186
  413.3 48.2 %collective-permute-start.2 = (bf16[1,56,256]{2,1,0:T(8,128)(2,1)S(1)}, bf16[1,56,256]{2,1,0:T(8,128)(2,1)S(1)}, u32[]{:S(2)}, u32[]{:S(2)}) collective-permute-start(bf16[1,56,256]{2,1,0:T(8,128)(2,1)S(1)} %get-tuple-element.88), channel_id=1, source_target_pairs={{0,1},{1,2},{2,3},{3,4},{4,5},{5,6},{6,7},{8,9},{9,10},{10,11},{11... | collective-permute-start | bytes 86024 | tf_op jit(solution)/shard_map/ppermute | solution.py:184
  (43 other events, 254.3 us)
Sparse Core Ops, SparseCore 0:
  11.5 64.6 all-gather.4
  147.0 34.0 reduce-scatter.8
  184.3 35.4 reduce-scatter.6
  239.6 144.5 all-reduce.10
  391.4 61.6 all-gather.6

commit v2 on v1

v2 whole, which is shorter than its diff:
```python
import functools
import math

import jax
import jax.numpy as jnp
from jax import lax
from jax.experimental import pallas as pl
from jax.experimental.pallas import tpu as pltpu
from jax.sharding import PartitionSpec as P

HEADS = 8
FF = 1024
STEP = 5

NORM_EPS = 1e-05
ADAM_EPS = 1e-08
BETA = 0.5
WEIGHT_DECAY = 0.05
EMA_KEEP = 0.75
VECTOR_RATE = 0.06
MATRIX_RATES = (0.04, 0.02, 0.25, 0.02, 0.01, 0.01)
CORRECTION = 1.0 - BETA**STEP
LOG2E = math.log2(math.e)
f32 = jnp.float32
bf16 = jnp.bfloat16
LATE = (5, 1, 0, 2)
EARLY = (3, 4)


def matrix_shapes(width, hidden):
    return (
        (width, width),
        (width, 2 * width),
        (width, width),
        (width, hidden),
        (hidden, width),
        (4 * width, width),
    )


def contract(a, b, ca, cb, **kw):
    return lax.dot_general(
        a, b, (((ca,), (cb,)), ((), ())), preferred_element_type=f32, **kw
    )


def swap(x, axis, step):
    count = lax.axis_size(axis)
    return lax.ppermute(x, axis, [(i, i ^ step) for i in range(count)])


def row_groups():
    left = lax.axis_size("row") // 2
    groups, stride = [(1, 2)], 2
    while left > 1:
        size = 4 if left % 4 == 0 else 2
        groups.append((stride, size))
        left //= size
        stride *= size
    return groups


def gather_group(x, axis, stride, size):
    return jnp.stack([x] + [swap(x, axis, j * stride) for j in range(1, size)])


def gather_rows(x):
    groups = row_groups()
    for stride, size in groups[1:] + groups[:1]:
        x = gather_group(x, "row", stride, size)
    return x


def gather_all(x):
    return gather_rows(gather_group(x, "img", 1, lax.axis_size("img")))


def pair_sum(terms):
    while len(terms) > 1:
        terms = [a + b for a, b in zip(terms[::2], terms[1::2])]
    return terms[0]


def total_all(x):
    groups = [("row", stride, size) for stride, size in row_groups()]
    for axis, stride, size in groups + [("img", 1, lax.axis_size("img"))]:
        x = pair_sum([x] + [swap(x, axis, j * stride) for j in range(1, size)])
    return x


def rel_digits():
    groups = row_groups()
    return [groups[0]] + groups[1:][::-1]


def rel_rows():
    rel = jnp.zeros((1,), jnp.int32)
    for stride, size in rel_digits():
        rel = (rel[:, None] + stride * jnp.arange(size, dtype=jnp.int32)[None, :]).reshape(-1)
    return lax.axis_index("row") ^ rel


def source(block):
    sizes = lax.axis_size("img")
    img, rest = block % sizes, block // sizes
    rel = 0
    for stride, size in reversed(rel_digits()):
        rel = rel + (rest % size) * stride
        rest = rest // size
    row = lax.axis_index("row") ^ rel
    return (lax.axis_index("img") ^ img) * lax.axis_size("row") + row


def device_count():
    return lax.axis_size("img") * lax.axis_size("row")


def run(name, body, outs, args, scratch=(), mib=40, scalars=(), flops=0, moved=0):
    specs = [
        pl.BlockSpec(memory_space=pltpu.SMEM) if index in scalars else pl.BlockSpec(memory_space=pltpu.VMEM)
        for index in range(len(args))
    ]
    return pl.pallas_call(
        body,
        out_shape=tuple(jax.ShapeDtypeStruct(shape, dtype) for shape, dtype in outs),
        in_specs=specs,
        out_specs=tuple(pl.BlockSpec(memory_space=pltpu.VMEM) for _ in outs),
        scratch_shapes=[pltpu.VMEM(shape, dtype) for shape, dtype in scratch],
        compiler_params=pltpu.CompilerParams(vmem_limit_bytes=mib * 2**20),
        cost_estimate=pl.CostEstimate(flops=flops, bytes_accessed=moved, transcendentals=0),
        name=name,
    )(*args)


def each_block(count, body):
    if count <= 32:
        for index in range(count):
            body(index)
    else:

        def step(index, carry):
            body(index)
            return carry

        lax.fori_loop(0, count, step, 0)


def put_rows(ref, start, cols, value):
    count = value.shape[0]
    if count % 8 == 0:
        ref[pl.ds(pl.multiple_of(start, 8), count), cols] = value
    else:
        for row in range(count):
            ref[pl.ds(start + row, 1), cols] = value[row : row + 1]


def get_rows(ref, start, count, cols):
    if count % 8 == 0:
        return ref[pl.ds(pl.multiple_of(start, 8), count), cols]
    return jnp.concatenate([ref[pl.ds(start + row, 1), cols] for row in range(count)], axis=0)


def layout(width, group):
    dims = matrix_shapes(width, FF)
    found, start = [], 0
    for j in group:
        rows = dims[j][0] // device_count()
        blocks = dims[j][1] // width
        found.append((j, start, rows, blocks))
        start += rows * blocks
    return found, start


def packed_starts(width):
    dims = matrix_shapes(width, FF)
    starts, start = [], 0
    for m, n in dims:
        starts.append(start)
        start += m * n // device_count()
    return starts


def spread(block, parts, mats, start_of):
    for (j, first, rows, blocks), ref in zip(parts, mats):
        for col in range(blocks):
            piece = block[first + col * rows : first + (col + 1) * rows]
            put_rows(ref, start_of * rows, slice(col * 256, col * 256 + 256), piece)


def collect(out_ref, index, parts, mats, start_of):
    for (j, first, rows, blocks), ref in zip(parts, mats):
        for col in range(blocks):
            piece = get_rows(ref, start_of * rows, rows, slice(col * 256, col * 256 + 256))
            out_ref[index, first + col * rows : first + (col + 1) * rows, :] = piece


def norm_parts(values):
    centred = values - jnp.mean(values, axis=-1, keepdims=True)
    inverse = lax.rsqrt(jnp.mean(centred * centred, axis=-1, keepdims=True) + NORM_EPS)
    return centred * inverse, inverse


def norm_back(grad, unit, inverse, gain):
    grad_unit = grad * gain
    back = grad_unit - jnp.mean(grad_unit, axis=-1, keepdims=True)
    back = back - unit * jnp.mean(grad_unit * unit, axis=-1, keepdims=True)
    gain_sum = jnp.sum(grad * unit, axis=0, keepdims=True)
    return back * inverse, gain_sum, jnp.sum(grad, axis=0, keepdims=True)


def turned(value):
    return value.astype(f32).T.astype(bf16)


def col_sum(value):
    return jnp.sum(value, axis=0, keepdims=True)


def pack_kernel(width, w_ref, late_ref, early_ref, chunk):
    to_chunk(w_ref, chunk, width)
    split = late_ref.shape[0]
    late_ref[...] = chunk[0:split, :].astype(bf16)
    early_ref[...] = chunk[split:, :].astype(bf16)


def to_chunk(flat_ref, out_ref, width):
    dims, starts, base = matrix_shapes(width, FF), packed_starts(width), 0
    for group in (LATE, EARLY):
        parts, count = layout(width, group)
        for j, first, rows, blocks in parts:
            for col in range(blocks):
                for row in range(rows):
                    at = starts[j] + row * dims[j][1] + col * width
                    place = base + first + col * rows + row
                    out_ref[place : place + 1, :] = flat_ref[0:1, at : at + width]
        base += count


def from_chunk(values, base, group, out_ref, width):
    dims, starts = matrix_shapes(width, FF), packed_starts(width)
    parts, _ = layout(width, group)
    for j, first, rows, blocks in parts:
        for col in range(blocks):
            for row in range(rows):
                at = starts[j] + row * dims[j][1] + col * width
                place = base + first + col * rows + row
                out_ref[0:1, at : at + width] = values[place : place + 1, :]


def moments_kernel(width, *refs):
    for index in range(4):
        to_chunk(refs[index], refs[4 + index], width)


def bases_kernel(
    narrow_ref, pair_ref, wide_ref, narrow_out, turned_out, pair_out, wide_out, own_narrow, own_wide, tall
):
    count = device_count()
    rank = lax.axis_index("img") * lax.axis_size("row") + lax.axis_index("row")
    narrow_out[...] = narrow_ref[...].astype(bf16)
    pair_out[...] = pair_ref[...].astype(bf16)
    wide_out[...] = wide_ref[...].astype(bf16)
    for index, j in enumerate((0, 2, 3, 5)):
        turned_out[index] = narrow_ref[j].T.astype(bf16)
    for out_ref, source_ref, picks in ((own_narrow, narrow_ref, (0, 2, 3, 5)), (own_wide, wide_ref, (1, 2))):
        size = source_ref.shape[1]
        rows = size // count
        pad = 8 if rows < 8 else rows
        for index, j in enumerate(picks):
            mine = get_rows(source_ref.at[j], rank * rows, rows, slice(None))
            if rows < pad:
                mine = jnp.concatenate([mine, jnp.zeros((pad - rows, size), f32)], axis=0)
            lanes = 128
            if pad < lanes:
                mine = jnp.concatenate([mine, jnp.zeros((lanes - pad, size), f32)], axis=0)
            tall[0:size, :] = mine.T

            def body(block):
                put_rows(tall, size + block * rows, slice(None), get_rows(tall, source(block) * rows, rows, slice(None)))

            each_block(count, body)
            out_ref[index] = tall[size : 2 * size, :].T[0 : out_ref.shape[1]]


def unpack_kernel(groups, *refs):
    pieces, outs, mats = refs[:groups], refs[groups : groups + 4], refs[groups + 4 :]
    parts, _ = layout(256, LATE)
    done = 0
    for piece in pieces:
        count = piece.shape[0]

        def body(block, piece=piece, done=done):
            spread(piece[block].astype(f32), parts, mats, source(block + done))

        each_block(count, body)
        done += count
    for out_ref, ref in zip(outs, mats):
        out_ref[...] = ref[...].astype(bf16)


def shifted_frame(frame_ref, tile_ref, up_ref, down_ref):
    rows, cols, width = frame_ref.shape[0] - 2, 56, 256
    frame_ref[...] = jnp.zeros_like(frame_ref)
    frame_ref[0, 8 : 8 + cols, :] = up_ref[...].astype(f32)[-cols:]
    frame_ref[1 : 1 + rows, 8 : 8 + cols, :] = tile_ref[...].astype(f32).reshape(rows, cols, width)
    frame_ref[rows + 1, 8 : 8 + cols, :] = down_ref[...].astype(f32)[:cols]
    return [frame_ref[:, 7 + shift : 7 + shift + cols, :] for shift in range(3)]


def front_kernel(tile_ref, up_ref, down_ref, vec_ref, x0_ref, h1_ref, frame):
    rows = frame.shape[0] - 2
    moved = shifted_frame(frame, tile_ref, up_ref, down_ref)
    total = moved[1][1:-1] + vec_ref[9:10, :]
    for tap in range(9):
        total = total + vec_ref[tap : tap + 1, :] * moved[tap % 3][tap // 3 : tap // 3 + rows]
    x0 = total.reshape(x0_ref.shape)
    x0_ref[...] = x0
    unit, _ = norm_parts(x0)
    h1_ref[...] = (unit * vec_ref[10:11, :] + vec_ref[11:12, :]).astype(bf16)


def picked_cells(shape, cell_axis, size_ref, corner, tile_rows, cols):
    half = cols // 2
    key_shape = tuple(1 if axis == cell_axis else n for axis, n in enumerate(shape))
    key = lax.broadcasted_iota(jnp.int32, key_shape, 1 - cell_axis)
    row = jnp.zeros_like(key)
    for step in range(1, tile_rows // 2):
        row = row + (key >= step * half).astype(jnp.int32)
    col = 2 * (key - row * half) + corner % 2
    row = 2 * row + corner // 2
    inside = (row + lax.axis_index("row") * tile_rows < size_ref[0, 0]) & (col < size_ref[0, 1])
    target = jnp.where(inside, row * cols + col, -1)
    cell = lax.broadcasted_iota(jnp.int32, shape, cell_axis)
    return (cell == target).astype(f32).astype(bf16)


def keys_kernel(tile_rows, cols, size_ref, h1_ref, vec_ref, reduce_ref, keyval_ref, blocks_ref, c_ref, kn_ref, kv_ref):
    keys = c_ref.shape[0]
    for corner in range(4):
        pick = picked_cells((keys, h1_ref.shape[0]), 1, size_ref, corner, tile_rows, cols)
        blocks_ref[:, corner * 256 : corner * 256 + 256] = contract(pick, h1_ref[...], 1, 0).astype(bf16)
    c = contract(blocks_ref[...], reduce_ref[...], 1, 0) + vec_ref[13:14, :]
    c_ref[...] = c
    unit, _ = norm_parts(c)
    kn = (unit * vec_ref[14:15, :] + vec_ref[15:16, :]).astype(bf16)
    kn_ref[...] = kn
    kv = contract(kn, keyval_ref[...], 1, 0)
    kv_ref[:, 0:256] = kv[:, 0:256].astype(bf16)
    kv_ref[:, 256:512] = (kv[:, 256:512] + vec_ref[16:17, :]).astype(bf16)


def over_heads(body, heads, unroll):
    if unroll:
        for head in range(heads):
            body(head)
    else:

        def step(head, carry):
            body(head)
            return carry

        lax.fori_loop(0, heads, step, 0)


def over_blocks(block, tokens, step):
    if tokens == step:
        block(0)
    else:

        def go(index, carry):
            block(pl.multiple_of(index * step, step))
            return carry

        lax.fori_loop(0, tokens // step, go, 0)


def head_columns(head):
    group = head // 4
    if isinstance(head, int):
        return slice(group * 128, group * 128 + 128)
    return pl.ds(pl.multiple_of(group * 128, 128), 128)


def head_rows(head, base=0):
    if isinstance(head, int):
        return slice(base + head * 32, base + head * 32 + 32)
    return pl.ds(pl.multiple_of(base + head * 32, 32), 32)


def attend_kernel(
    step, unroll, h1_ref, query_ref, vec_ref, near_ref, far_ref, mask_ref, q_ref, k_ref, v_ref, o_ref, log_ref
):
    tokens = h1_ref.shape[0]
    half = near_ref.shape[0]
    for start, ref in ((0, near_ref), (half, far_ref)):
        k_ref[start : start + half, :] = ref[:, 0:256]
        v_ref[start : start + half, :] = ref[:, 256:512]
    q_ref[...] = (contract(h1_ref[...], query_ref[...], 1, 0) + vec_ref[12:13, :]).astype(bf16)
    scale = 32**-0.5 * LOG2E
    lane = lax.broadcasted_iota(jnp.int32, (1, 128), 1)
    mask = mask_ref[...]

    def one_head(head):
        cols = head_columns(head)
        mine = lane // 32 == head % 4
        keys = jnp.where(mine, k_ref[:, cols], 0)
        values = jnp.where(mine, v_ref[:, cols], 0)

        def block(start):
            rows = pl.ds(start, step)
            scores = contract(q_ref[rows, cols], keys, 1, 1) * scale + mask
            top = jnp.max(scores, axis=1, keepdims=True)
            exponent = jnp.exp2(scores - top)
            total = jnp.sum(exponent, axis=1, keepdims=True)
            probs = (exponent * (1.0 / total)).astype(bf16)
            out = contract(probs, values, 1, 0)
            o_ref[rows, cols] = jnp.where(mine, out, o_ref[rows, cols])
            log_ref[rows, :] = jnp.where(lane == head, top + jnp.log2(total), log_ref[rows, :])

        over_blocks(block, tokens, step)

    over_heads(one_head, HEADS, unroll)


def feed_kernel(
    o_ref, x0_ref, out_ref, early_ref, vec_ref, dy_ref, y_ref, do_ref, dx1_ref, up_grad, down_grad, out_grad, sums_ref,
    up_ref, down_ref, up_wide, down_wide,
):
    parts, _ = layout(256, EARLY)

    def body(block):
        spread(early_ref[block].astype(f32), parts, (up_wide, down_wide), block)

    each_block(early_ref.shape[0], body)
    up_ref[...] = up_wide[...].astype(bf16)
    down_ref[...] = down_wide[...].astype(bf16)
    o = o_ref[...].astype(bf16)
    x1 = x0_ref[...] + (contract(o, out_ref[...], 1, 0) + vec_ref[17:18, :])
    unit, inverse = norm_parts(x1)
    h2 = (unit * vec_ref[18:19, :] + vec_ref[19:20, :]).astype(bf16)
    dy_low = dy_ref[...]
    dy = dy_low.astype(f32)
    dyt = turned(dy_low)
    h2t = turned(h2)
    y = x1 + vec_ref[20:21, :]
    dh2 = jnp.zeros_like(y)
    for col in range(FF // 256):
        cols = slice(col * 256, col * 256 + 256)
        u = contract(h2, up_ref[:, cols], 1, 0) + vec_ref[21 + col : 22 + col, :]
        phi_sum = 0.5 * (1.0 + lax.erf(u * (2.0**-0.5)))
        density = jnp.exp(-0.5 * u * u) * ((2.0 * math.pi) ** -0.5)
        g = (u * phi_sum).astype(bf16)
        y = y + contract(g, down_ref[cols, :], 1, 0)
        down_grad[:, cols] = contract(dyt, g, 1, 0)
        du = (contract(dy_low, down_ref[cols, :], 1, 1) * (phi_sum + u * density)).astype(bf16)
        up_grad[:, cols] = contract(h2t, du, 1, 0)
        sums_ref[21 + col : 22 + col, :] = col_sum(du.astype(f32))
        dh2 = dh2 + contract(du, up_ref[:, cols], 1, 1)
    y_ref[...] = y.astype(bf16)
    back, gain_sum, bias_sum = norm_back(dh2, unit, inverse, vec_ref[18:19, :])
    dx1 = dy + back
    dx1_ref[...] = dx1
    da = dx1.astype(bf16)
    do_ref[...] = contract(da, out_ref[...], 1, 1).astype(bf16)
    out_grad[...] = contract(turned(o), da, 1, 0)
    sums_ref[0:17, :] = jnp.zeros((17, 256), f32)
    sums_ref[17:18, :] = col_sum(da.astype(f32))
    sums_ref[18:19, :] = gain_sum
    sums_ref[19:20, :] = bias_sum
    sums_ref[20:21, :] = col_sum(dy)


def rotate(left_turned, grad, right):
    half = contract(left_turned, grad.astype(bf16), 1, 0).astype(bf16)
    return contract(half, right, 1, 0)


def rotate_turned(grad_turned, left, right):
    half = contract(grad_turned.astype(bf16), left, 1, 0).astype(bf16)
    return contract(turned(half), right, 1, 0)


def share_out(keep_ref, send_ref, parts, mats):
    half = keep_ref.shape[0]
    for ref, base in ((keep_ref, 0), (send_ref, half)):

        def body(block, ref=ref, base=base):
            collect(ref, block, parts, mats, source(block + base))

        each_block(half, body)


def early_turn_kernel(up_grad, down_grad, turned_ref, narrow_ref, wide_ref, keep_ref, send_ref, up, down):
    up[...] = rotate(turned_ref[3], up_grad[...], wide_ref[0])
    down[...] = rotate_turned(down_grad[...], wide_ref[1], narrow_ref[6])
    share_out(keep_ref, send_ref, layout(256, EARLY)[0], (up, down))


def attend_back_kernel(
    step, unroll, q_ref, k_ref, v_ref, mask_ref, o_ref, log_ref, g_ref, h1_ref,
    dq_ref, keep_ref, send_ref, query_grad, bias_ref, dq_wide, dkv, ps, dss, qt, gt,
):
    tokens, width = q_ref.shape
    scale = 32**-0.5
    lane = lax.broadcasted_iota(jnp.int32, (1, 128), 1)
    mask = mask_ref[...]
    qt[...] = turned(q_ref[...])
    gt[...] = turned(g_ref[...])

    def one_head(head):
        cols = head_columns(head)
        mine = lane // 32 == head % 4
        keys = jnp.where(mine, k_ref[:, cols], 0)
        values = jnp.where(mine, v_ref[:, cols], 0)

        def block(start):
            rows = pl.ds(start, step)
            grad = g_ref[rows, cols]
            inner = jnp.sum(jnp.where(mine, grad.astype(f32) * o_ref[rows, cols], 0.0), axis=1, keepdims=True)
            if isinstance(head, int):
                log = log_ref[rows, head : head + 1]
            else:
                log = jnp.sum(jnp.where(lane == head, log_ref[rows, :], 0.0), axis=1, keepdims=True)
            scores = contract(q_ref[rows, cols], keys, 1, 1)
            probs = jnp.exp2(scores * (scale * LOG2E) + mask - log)
            grad_scores = (probs * (contract(grad, values, 1, 1) - inner)).astype(bf16)
            ps[rows, :] = probs.astype(bf16)
            dss[rows, :] = grad_scores
            out = contract(grad_scores, keys, 1, 0) * scale
            dq_wide[rows, cols] = jnp.where(mine, out, dq_wide[rows, cols])

        over_blocks(block, tokens, step)
        dkv[head_rows(head), :] = contract(qt[head_rows(head), :], dss[...], 1, 0) * scale
        dkv[head_rows(head, width), :] = contract(gt[head_rows(head), :], ps[...], 1, 0)

    over_heads(one_head, HEADS, unroll)
    dq = dq_wide[...].astype(bf16)
    dq_ref[...] = dq
    bias_ref[...] = col_sum(dq.astype(f32))
    half = keep_ref.shape[0]
    keep_ref[...] = dkv[:, 0:half].T
    send_ref[...] = dkv[:, half:].T
    query_grad[...] = contract(turned(h1_ref[...]), dq, 1, 0)


def split_kernel(count, terms, *refs):
    total = refs[0][...].astype(f32)
    for ref in refs[1:terms]:
        total = total + ref[...].astype(f32)
    rows = total.shape[0] // count
    refs[terms][...] = total[:rows]
    for index in range(1, count):
        refs[terms + index][...] = total[index * rows : (index + 1) * rows].astype(bf16)


def split_sum(terms, count):
    rows = terms[0].shape[0] // count
    tail = terms[0].shape[1:]
    outs = [((rows,) + tail, f32)] + [((rows,) + tail, bf16)] * (count - 1)
    return run("split_sum", functools.partial(split_kernel, count, len(terms)), outs, terms, mib=30)


def scatter_sum(keep, send, groups):
    terms = [keep, swap(send, "row", 1)]
    for axis, stride, size in groups:
        parts = split_sum(terms, size)
        terms = [parts[0]] + [swap(parts[j], axis, j * stride) for j in range(1, size)]
    return terms


def row_parts():
    return [("row", stride, size) for stride, size in rel_digits()[1:]]


def side_by_side(x, groups):
    for axis, stride, size in groups:
        x = jnp.concatenate([x] + [swap(x, axis, j * stride) for j in range(1, size)], axis=0)
    return x


def middle_turn_kernel(query_grad, out_grad, turned_ref, narrow_ref, query_ref, out_ref):
    query_ref[...] = rotate(turned_ref[0], query_grad[...], narrow_ref[1])
    out_ref[...] = rotate(turned_ref[2], out_grad[...], narrow_ref[4])


def keys_back_kernel(
    terms, *refs
):
    (kn_ref, c_ref, vec_ref, keyval_ref, blocks_ref, turned_ref, narrow_ref, pair_ref, wide_ref, query, out,
     keep_ref, send_ref, dc_ref, sums_ref, reduce, keyval) = refs[terms:]
    dkv = refs[0][...]
    for ref in refs[1:terms]:
        dkv = dkv + ref[...].astype(f32)
    high = dkv.astype(bf16)
    rest = (dkv - high.astype(f32)).astype(bf16)
    dkn = contract(high, keyval_ref[...], 1, 1) + contract(rest, keyval_ref[...], 1, 1)
    unit, inverse = norm_parts(c_ref[...])
    back, gain_sum, bias_sum = norm_back(dkn, unit, inverse, vec_ref[14:15, :])
    dc = back.astype(bf16)
    dc_ref[...] = dc
    knt = turned(kn_ref[...])
    keyval[...] = rotate(turned_ref[1], contract(knt, high, 1, 0) + contract(knt, rest, 1, 0), pair_ref[...])
    reduce[...] = rotate_turned(contract(turned(dc), blocks_ref[...], 1, 0), wide_ref[2], narrow_ref[7])
    share_out(keep_ref, send_ref, layout(256, LATE)[0], (reduce, keyval, query, out))
    sums_ref[0:1, :] = col_sum(dc.astype(f32))
    sums_ref[1:2, :] = gain_sum
    sums_ref[2:3, :] = bias_sum
    sums_ref[3:4, :] = col_sum(dkv[:, 256:512])


def cells_back_kernel(
    tile_rows, cols, size_ref, dq_ref, dc_ref, query_ref, reduce_ref, x0_ref, dx1_ref, vec_ref, tile_ref, up_ref, down_ref,
    feed_sums, key_sums, query_sum, dx0_ref, head_ref, tail_ref, sums_ref, frame,
):
    tokens = x0_ref.shape[0]
    dh1 = contract(dq_ref[...], query_ref[...], 1, 1)
    for corner in range(4):
        pick = picked_cells((tokens, dc_ref.shape[0]), 0, size_ref, corner, tile_rows, cols)
        placed = contract(pick, dc_ref[...], 1, 0).astype(bf16)
        dh1 = dh1 + contract(placed, reduce_ref[corner * 256 : corner * 256 + 256, :], 1, 1)
    unit, inverse = norm_parts(x0_ref[...])
    back, gain_sum, bias_sum = norm_back(dh1, unit, inverse, vec_ref[10:11, :])
    dx0 = dx1_ref[...] + back
    dx0_ref[...] = dx0
    head_ref[...] = dx0[0:64].astype(bf16)
    tail_ref[...] = dx0[tokens - 64 :].astype(bf16)
    sums_ref[...] = feed_sums[...]
    moved = shifted_frame(frame, tile_ref, up_ref, down_ref)
    grid = dx0.reshape(tile_rows, cols, 256)
    for tap in range(9):
        product = moved[tap % 3][tap // 3 : tap // 3 + tile_rows] * grid
        sums_ref[tap : tap + 1, :] = col_sum(product.reshape(tokens, 256))
    sums_ref[9:10, :] = col_sum(dx0)
    sums_ref[10:11, :] = gain_sum
    sums_ref[11:12, :] = bias_sum
    sums_ref[12:13, :] = query_sum[...]
    sums_ref[13:17, :] = key_sums[...]


def input_grad_kernel(tile_rows, dx0_ref, up_ref, down_ref, vec_ref, out_ref, frame):
    moved = shifted_frame(frame, dx0_ref, up_ref, down_ref)
    total = moved[1][1:-1]
    for tap in range(9):
        down, right = 2 - tap // 3, 2 - tap % 3
        total = total + vec_ref[tap : tap + 1, :] * moved[right][down : down + tile_rows]
    out_ref[...] = total.reshape(out_ref.shape)


def adam_kernel(base, terms, *refs):
    first_ref, second_ref, moment_ref, square_ref, step_ref = refs[terms:]
    total = refs[0][...]
    for ref in refs[1:terms]:
        total = total + ref[...].astype(f32)
    rows = total.shape[0]
    moment = BETA * first_ref[base : base + rows, :] + (1.0 - BETA) * total
    square = BETA * second_ref[base : base + rows, :] + (1.0 - BETA) * total * total
    moment_ref[...] = moment
    square_ref[...] = square
    step = moment * (1.0 / CORRECTION) / (jnp.sqrt(square * (1.0 / CORRECTION)) + ADAM_EPS)
    step_ref[...] = step.astype(bf16)


def finish_kernel(
    width, late_near, late_far, early_near, early_far, own_narrow, own_wide, narrow_ref, pair_ref, wide_ref,
    weights_ref, ema_ref, late_first, late_second, early_first, early_second,
    weights_out, ema_out, first_out, second_out, chunk,
):
    rights = {
        0: narrow_ref.at[1], 1: pair_ref, 2: narrow_ref.at[4], 3: wide_ref.at[0], 4: narrow_ref.at[6], 5: narrow_ref.at[7]
    }
    lefts = {0: (own_narrow, 0), 1: (own_narrow, 1), 2: (own_narrow, 2), 3: (own_narrow, 3), 4: (own_wide, 0), 5: (own_wide, 1)}
    base = 0
    for group, near, far in ((LATE, late_near, late_far), (EARLY, early_near, early_far)):
        parts, count = layout(width, group)
        blocks_near = near[...].astype(f32)
        blocks_far = far[...].astype(f32)
        for j, first, rows, blocks in parts:
            left_ref, index = lefts[j]
            left = left_ref[index].astype(bf16)
            half = left.shape[1] // 2
            sides = []
            for col in range(blocks):
                at = slice(first + col * rows, first + (col + 1) * rows)
                near_part = blocks_near[:, at, :].reshape(half, width).astype(bf16)
                far_part = blocks_far[:, at, :].reshape(half, width).astype(bf16)
                sides.append(contract(left[:, 0:half], near_part, 1, 0) + contract(left[:, half:], far_part, 1, 0))
            side = sides[0] if blocks == 1 else jnp.concatenate(sides, axis=1)
            full = contract(side.astype(bf16), rights[j][...], 1, 1)
            for col in range(blocks):
                at = slice(base + first + col * rows, base + first + (col + 1) * rows)
                old = weights_ref[at, :]
                piece = full[0:rows, col * width : (col + 1) * width]
                chunk[at, :] = old - MATRIX_RATES[j] * (piece + WEIGHT_DECAY * old)
        base += count
    from_chunk(chunk, 0, LATE, weights_out, width)
    split = layout(width, LATE)[1]
    from_chunk(chunk, split, EARLY, weights_out, width)
    chunk[...] = EMA_KEEP * ema_ref[...] + (1.0 - EMA_KEEP) * chunk[...]
    from_chunk(chunk, 0, LATE, ema_out, width)
    from_chunk(chunk, split, EARLY, ema_out, width)
    for late, early, out in ((late_first, early_first, first_out), (late_second, early_second, second_out)):
        from_chunk(late, 0, LATE, out, width)
        from_chunk(early, 0, EARLY, out, width)


def vector_kernel(total_ref, vec_ref, first_ref, second_ref, ema_ref, vec_out, first_out, second_out, ema_out):
    total = total_ref[...]
    moment = BETA * first_ref[...] + (1.0 - BETA) * total
    square = BETA * second_ref[...] + (1.0 - BETA) * total * total
    first_out[...] = moment
    second_out[...] = square
    step = moment * (1.0 / CORRECTION) / (jnp.sqrt(square * (1.0 / CORRECTION)) + ADAM_EPS)
    new = vec_ref[...] - VECTOR_RATE * step
    vec_out[...] = new
    ema_out[...] = EMA_KEEP * ema_ref[...] + (1.0 - EMA_KEEP) * new


def on_device(
    patches,
    cotangent,
    image_sizes,
    weights,
    first_moment,
    second_moment,
    weight_ema,
    vectors,
    vec_first,
    vec_second,
    vec_ema,
    basis_narrow,
    basis_pair,
    basis_wide,
):
    _, rows, cols, width = patches.shape
    tokens = rows * cols
    shards = device_count()
    tile = patches.reshape(tokens, width)
    dy = cotangent.reshape(tokens, width)
    per = weights.shape[1]
    late_rows, early_rows = layout(width, LATE)[1], layout(width, EARLY)[1]
    chunk = late_rows + early_rows
    ranks = lax.axis_size("row")
    own_keys = tokens // 4
    keys = own_keys * ranks
    frame = ((rows + 2, cols + 16, width), f32)
    img_part = ("img", 1, lax.axis_size("img"))
    xy_parts = row_parts()

    def border(head, tail):
        up = lax.ppermute(tail, "row", [(i, i + 1) for i in range(ranks - 1)])
        return up, lax.ppermute(head, "row", [(i + 1, i) for i in range(ranks - 1)])

    late, early = run(
        "pack",
        functools.partial(pack_kernel, width),
        [((late_rows, width), bf16), ((early_rows, width), bf16)],
        [weights],
        scratch=[((chunk, width), f32)],
        mib=8,
    )
    up_halo, down_halo = border(tile[:64], tile[tokens - 64 :])
    late_near = side_by_side(late[None], [img_part] + xy_parts[::-1])
    late_far = swap(late_near, "row", 1)
    early_all = lax.all_gather(early, ("img", "row"), axis=0, tiled=False)

    x0, h1 = run(
        "front",
        front_kernel,
        [((tokens, width), f32), ((tokens, width), bf16)],
        [tile, up_halo, down_halo, vectors],
        scratch=[frame],
        mib=16,
    )
    w_reduce, w_keyval, w_query, w_out = run(
        "unpack",
        functools.partial(unpack_kernel, 2),
        [((4 * width, width), bf16), ((width, 2 * width), bf16), ((width, width), bf16), ((width, width), bf16)],
        [late_near, late_far],
        scratch=[((4 * width, width), f32), ((width, 2 * width), f32), ((width, width), f32), ((width, width), f32)],
        mib=16,
    )
    blocks, c, kn, own_kv = run(
        "keys",
        functools.partial(keys_kernel, rows, cols),
        [((own_keys, 4 * width), bf16), ((own_keys, width), f32), ((own_keys, width), bf16), ((own_keys, 2 * width), bf16)],
        [image_sizes, h1, vectors, w_reduce, w_keyval],
        scalars=(0,),
        mib=16,
    )
    kv_near = side_by_side(own_kv, xy_parts[::-1])
    kv_far = swap(kv_near, "row", 1)

    rounded = run(
        "bases",
        bases_kernel,
        [
            ((8, width, width), bf16),
            ((4, width, width), bf16),
            ((2 * width, 2 * width), bf16),
            ((3, FF, FF), bf16),
            ((4, 16, width), f32),
            ((2, max(16, FF // shards), FF), f32),
        ],
        [basis_narrow, basis_pair, basis_wide],
        scratch=[((2 * FF, 128), f32)],
        mib=48,
    )
    narrow, narrow_turned, pair, wide, own_narrow, own_wide = rounded
    old_chunk, ema_chunk, first_chunk, second_chunk = run(
        "moments",
        functools.partial(moments_kernel, width),
        [((chunk, width), f32)] * 4,
        [weights, weight_ema, first_moment, second_moment],
        mib=8,
    )

    height, across = image_sizes[0, 0], image_sizes[0, 1]
    key_row = rel_rows()[:, None, None] * (rows // 2) + jnp.arange(rows // 2)[None, :, None]
    key_col = jnp.arange(cols // 2)[None, None, :]
    allowed = (2 * key_row < height) & (2 * key_col < across)
    mask = jnp.where(allowed, 0.0, -1e30).astype(f32).reshape(1, -1)

    unroll = keys <= 1024
    step = tokens if unroll else 32
    q, k, v, o, log = run(
        "attend",
        functools.partial(attend_kernel, step, unroll),
        [((tokens, width), bf16), ((keys, width), bf16), ((keys, width), bf16), ((tokens, width), f32), ((tokens, 128), f32)],
        [h1, w_query, vectors, kv_near, kv_far, mask],
        mib=44,
        flops=4 * tokens * keys * width * 8,
    )
    y, do, dx1, up_grad, down_grad, out_grad, feed_sums = run(
        "feed",
        feed_kernel,
        [
            ((tokens, width), bf16),
            ((tokens, width), bf16),
            ((tokens, width), f32),
            ((width, FF), f32),
            ((width, FF), f32),
            ((width, width), f32),
            ((25, width), f32),
        ],
        [o, x0, w_out, early_all, vectors, dy],
        scratch=[((width, FF), bf16), ((FF, width), bf16), ((width, FF), f32), ((FF, width), f32)],
        mib=40,
        flops=12 * tokens * FF * width,
    )
    half = (shards // 2, early_rows, width)
    early_keep, early_send = run(
        "early_turn",
        early_turn_kernel,
        [(half, f32), (half, f32)],
        [up_grad, down_grad, narrow_turned, narrow, wide],
        scratch=[((width, FF), f32), ((FF, width), f32)],
        mib=32,
        flops=4 * FF * FF * width,
    )
    early_terms = scatter_sum(early_keep, early_send, xy_parts + [img_part])

    dq, dkv_keep, dkv_send, query_grad, query_sum = run(
        "attend_back",
        functools.partial(attend_back_kernel, step, unroll),
        [
            ((tokens, width), bf16),
            ((keys // 2, 2 * width), f32),
            ((keys // 2, 2 * width), f32),
            ((width, width), f32),
            ((1, width), f32),
        ],
        [q, k, v, mask, o, log, do, h1],
        scratch=[
            ((tokens, width), f32),
            ((2 * width, keys), f32),
            ((tokens, keys), bf16),
            ((tokens, keys), bf16),
            ((width, tokens), bf16),
            ((width, tokens), bf16),
        ],
        mib=44 if unroll else 60,
        flops=10 * tokens * keys * width * 8,
    )
    dkv_terms = scatter_sum(dkv_keep, dkv_send, xy_parts)
    query_turn, out_turn = run(
        "middle_turn",
        middle_turn_kernel,
        [((width, width), f32), ((width, width), f32)],
        [query_grad, out_grad, narrow_turned, narrow],
        mib=12,
        flops=8 * width**3,
    )
    half = (shards // 2, late_rows, width)
    late_keep, late_send, dc, key_sums = run(
        "keys_back",
        functools.partial(keys_back_kernel, len(dkv_terms)),
        [(half, f32), (half, f32), ((own_keys, width), bf16), ((4, width), f32)],
        list(dkv_terms)
        + [kn, c, vectors, w_keyval, blocks, narrow_turned, narrow, pair, wide, query_turn, out_turn],
        scratch=[((4 * width, width), f32), ((width, 2 * width), f32)],
        mib=36,
        flops=2 * FF * FF * width,
    )
    late_terms = scatter_sum(late_keep, late_send, xy_parts + [img_part])
    dx0, head, tail, vec_grads = run(
        "cells_back",
        functools.partial(cells_back_kernel, rows, cols),
        [((tokens, width), f32), ((64, width), bf16), ((64, width), bf16), ((25, width), f32)],
        [image_sizes, dq, dc, w_query, w_reduce, x0, dx1, vectors, tile, up_halo, down_halo, feed_sums, key_sums, query_sum],
        scratch=[frame],
        scalars=(0,),
        mib=24,
        flops=10 * tokens * width * width,
    )
    grad_up, grad_down = border(head, tail)
    (grad_input,) = run(
        "input_grad",
        functools.partial(input_grad_kernel, rows),
        [((tokens, width), f32)],
        [dx0, grad_up, grad_down, vectors],
        scratch=[frame],
        mib=16,
    )

    def adam(terms, base, count):
        return run(
            "adam",
            functools.partial(adam_kernel, base, len(terms)),
            [((count, width), f32), ((count, width), f32), ((count, width), bf16)],
            list(terms) + [first_chunk, second_chunk],
            mib=8,
        )

    flat_terms = [t.reshape(early_rows, width) for t in early_terms]
    early_first, early_second, early_step = adam(flat_terms, late_rows, early_rows)
    flat_terms = [t.reshape(late_rows, width) for t in late_terms]
    late_first, late_second, late_step = adam(flat_terms, 0, late_rows)
    early_near = side_by_side(early_step[None], [img_part] + xy_parts[::-1])
    early_far = swap(early_near, "row", 1)
    step_near = side_by_side(late_step[None], [img_part] + xy_parts[::-1])
    step_far = swap(step_near, "row", 1)

    vec_total = total_all(vec_grads)
    new_vectors, vec_moment, vec_square, new_vec_ema = run(
        "vector_step",
        vector_kernel,
        [(vectors.shape, f32)] * 4,
        [vec_total, vectors, vec_first, vec_second, vec_ema],
        mib=4,
    )
    new_weights, new_ema, new_first, new_second = run(
        "finish",
        functools.partial(finish_kernel, width),
        [((1, per), f32)] * 4,
        [
            step_near, step_far, early_near, early_far, own_narrow, own_wide, narrow, pair, wide,
            old_chunk, ema_chunk, late_first, late_second, early_first, early_second,
        ],
        scratch=[((chunk, width), f32)],
        mib=40,
    )
    return (
        y.reshape(patches.shape),
        grad_input.reshape(patches.shape),
        new_weights,
        new_first,
        new_second,
        new_ema,
        new_vectors,
        vec_moment,
        vec_square,
        new_vec_ema,
    )


def solution(mesh):
    tiles = P("img", "row", None, None)
    packed = P(("img", "row"), None)
    return jax.shard_map(
        on_device,
        mesh=mesh,
        in_specs=(tiles, tiles, P("img", None)) + (packed,) * 4 + (P(),) * 7,
        out_specs=(tiles, tiles) + (packed,) * 4 + (P(),) * 4,
        check_vma=False,
    )
```

time: 508 us -> 205 us (0.40); the launches traced: 501 us -> 203 us
  waiting for transfers between devices: 221 us -> 56.7 us
  matrix products: 84.1 us -> 0 us
  blocking collectives: 59.1 us -> 0 us
  starting transfers between devices: 9.31 us -> 64.7 us
  local copies, waits for them, and re-layouts: 73.6 us -> 20.6 us
  Pallas kernels: 18.7 us -> 45.1 us
  other arithmetic: 20 us -> 1.55 us
    unnamed x8 -> x1, waiting for transfers between devices: 171 us -> 0.02 us
    dot_general x42 -> x0, matrix products: 84.1 us -> none  [the longest x26 62.5 us: high_dot(): jnp.dot(left_side, right_side, precision=HIGH, preferred_element_type=jnp...]
    ppermute x4 -> x54, starting transfers between devices: 8.64 us -> 64.7 us  [the longest x50 58.4 us: swap(): return lax.ppermute(x, axis, [(i, i ^ step) for i in range(count)])]
    ppermute x4 -> x54, waiting for transfers between devices: 0.01 us -> 52.4 us  [the longest x50 52 us: swap(): return lax.ppermute(x, axis, [(i, i ^ step) for i in range(count)])]
    all_gather x2 -> x1, waiting for transfers between devices: 50.4 us -> 4.22 us  [on_device(): early_all = lax.all_gather(early, ('img', 'row'), axis=0, tiled=False)]
    psum x1 -> x0, blocking collectives: 40.4 us -> none  [on_device(): vec_total = lax.psum(vec_grads, ('img', 'row'))]
    pallas_call x2 -> x23, Pallas kernels: 18.7 us -> 45.1 us  [run(): pl.pallas_call(body, out_shape=tuple((jax.ShapeDtypeStruct(shape, dtype)...]
    reshape x24 -> x0, local copies, waits for them, and re-layouts: 22.2 us -> none  [the longest x6 11.6 us: on_device(): high_dot(high_dot(basis_left.T, local_grad), basis_right)]
  transfers between devices with their start and end apart: 9 -> 55, of which waited for: 3 -> 35; matrix products, arithmetic and copies ran while one was open for 17% -> 2% of each run, Pallas kernels for 0% -> 14%
where the time goes in v2:
time: 205 us; the launch traced here: 203 us
  starting transfers between devices  64.7 us (32%)
  waiting for transfers between devices  56.7 us (28%)
  Pallas kernels  45.1 us (22%)
  local copies, waits for them, and re-layouts  20.6 us (10%)
  between operations  14.8 us (7%)
    ppermute x50, starting transfers between devices, swap(): return lax.ppermute(x, axis, [(i, i ^ step) for i in range(count)])  58.4 us
    ppermute x50, waiting for transfers between devices, swap(): return lax.ppermute(x, axis, [(i, i ^ step) for i in range(count)])  52 us
    pallas_call x23, Pallas kernels, run(): pl.pallas_call(body, out_shape=tuple((jax.ShapeDtypeStruct(shape, dtype)...  45.1 us
    unnamed x107, local copies, waits for them, and re-layouts  18.2 us
    all_gather x1, waiting for transfers between devices, on_device(): early_all = lax.all_gather(early, ('img', 'row'), axis=0, tiled=False)  4.22 us
  transfers between devices with their start and end apart: 55, of which 35 were waited for; matrix products, arithmetic and copies ran while one was open for 2% of the time, Pallas kernels for 14%

profile of v2, /device:TPU:0, one launch (start us, length us, event | category | flops | bytes accessed | tf_op | source)
XLA Modules:
  0.0 203.4 jit_solution(2918200525570954919)
XLA Ops:
  8.8 3.0 %collective-permute-start.2 = (bf16[1,64,256]{2,1,0:T(8,128)(2,1)S(1)}, bf16[1,64,256]{2,1,0:T(8,128)(2,1)S(1)}, u32[]{:S(2)}, u32[]{:S(2)}) collective-permute-start(bf16[1,64,256]{2,1,0:T(8,128)(2,1)S(1)} %bitcast.24), channel_id=1, source_target_pairs={{0,8},{8,0},{16,24},{24,16},{1,9},{9,1},{17,25},{25,17},{2,10},{10... | collective-permute-start | bytes 98312 | tf_op jit(solution)/shard_map/ppermute | solution.py:49
  11.8 2.6 %collective-permute-start.3 = (bf16[1,64,256]{2,1,0:T(8,128)(2,1)S(1)}, bf16[1,64,256]{2,1,0:T(8,128)(2,1)S(1)}, u32[]{:S(2)}, u32[]{:S(2)}) collective-permute-start(bf16[1,64,256]{2,1,0:T(8,128)(2,1)S(1)} %bitcast.25), channel_id=1, source_target_pairs={{0,16},{8,24},{16,0},{24,8},{1,17},{9,25},{17,1},{25,9},{2,18},{10... | collective-permute-start | bytes 98312 | tf_op jit(solution)/shard_map/ppermute | solution.py:49
  14.5 2.8 %collective-permute-done.3 = bf16[1,64,256]{2,1,0:T(8,128)(2,1)S(1)} collective-permute-done((bf16[1,64,256]{2,1,0:T(8,128)(2,1)S(1)}, bf16[1,64,256]{2,1,0:T(8,128)(2,1)S(1)}, u32[]{:S(2)}, u32[]{:S(2)}) %collective-permute-start.3) | collective-permute-done | bytes 32800 | tf_op jit(solution)/shard_map/ppermute | solution.py:49
  17.2 2.9 %collective-permute-done.4 = bf16[1,64,256]{2,1,0:T(8,128)(2,1)S(1)} collective-permute-done((bf16[1,64,256]{2,1,0:T(8,128)(2,1)S(1)}, bf16[1,64,256]{2,1,0:T(8,128)(2,1)S(1)}, u32[]{:S(2)}, u32[]{:S(2)}) %collective-permute-start.4) | collective-permute-done | bytes 32800 | tf_op jit(solution)/shard_map/ppermute | solution.py:49
  23.7 2.5 %collective-permute-done.5 = bf16[4,64,256]{2,1,0:T(8,128)(2,1)S(1)} collective-permute-done((bf16[4,64,256]{2,1,0:T(8,128)(2,1)S(1)}, bf16[4,64,256]{2,1,0:T(8,128)(2,1)S(1)}, u32[]{:S(2)}, u32[]{:S(2)}) %collective-permute-start.5) | collective-permute-done | bytes 131104 | tf_op jit(solution)/shard_map/ppermute | solution.py:49
  30.2 2.4 %collective-permute-start = (bf16[64,256]{1,0:T(8,128)(2,1)S(1)}, bf16[64,256]{1,0:T(8,128)(2,1)S(1)}, u32[]{:S(2)}, u32[]{:S(2)}) collective-permute-start(bf16[64,256]{1,0:T(8,128)(2,1)S(1)} %get-tuple-element.181), channel_id=1, source_target_pairs={{0,1},{1,2},{2,3},{3,4},{4,5},{5,6},{6,7},{8,9},{9,10},{10,11},{11... | collective-permute-start | bytes 98312 | tf_op jit(solution)/shard_map/ppermute | solution.py:750
  48.4 3.2 %collective-permute-done.11 = bf16[112,512]{1,0:T(8,128)(2,1)S(1)} collective-permute-done((bf16[112,512]{1,0:T(8,128)(2,1)S(1)}, bf16[112,512]{1,0:T(8,128)(2,1)S(1)}, u32[]{:S(2)}, u32[]{:S(2)}) %collective-permute-start.11) | collective-permute-done | bytes 114720 | tf_op jit(solution)/shard_map/ppermute | solution.py:49
  54.7 7.6 %attend.1 = (bf16[448,256]{1,0:T(8,128)(2,1)S(1)}, bf16[896,256]{1,0:T(8,128)(2,1)S(1)}, bf16[896,256]{1,0:T(8,128)(2,1)S(1)}, f32[448,256]{1,0:T(8,128)S(1)}, f32[448,128]{1,0:T(8,128)S(1)}) custom-call(bf16[448,256]{1,0:T(8,128)(2,1)S(1)} %get-tuple-element.95.h1_ref, bf16[256,256]{1,0:T(8,128)(2,1)S(1)} %get-tuple-element.97.query_ref, ...), custom_call_target="tpu_custom_call" | custom-call | flops 3288334336 | tf_op jit(solution)/shard_map/attend/pallas_call | solution.py:123
  66.0 4.2 %all-gather.3.cloned.1.call-done = bf16[2048,256]{1,0:T(8,128)(2,1)} async-done(((bf16[64,256]{1,0:T(8,128)(2,1)}), bf16[2048,256]{1,0:T(8,128)(2,1)}) %all-gather.3.cloned.1.call-update) | async-done | bytes 1048592 | tf_op jit(solution)/shard_map/all_gather | solution.py:764
  72.4 3.2 %feed.1 = (bf16[448,256]{1,0:T(8,128)(2,1)}, bf16[448,256]{1,0:T(8,128)(2,1)S(1)}, f32[448,256]{1,0:T(8,128)S(1)}, f32[256,1024]{1,0:T(8,128)S(1)}, f32[256,1024...) custom-call(f32[448,256]{1,0:T(8,128)S(1)} %copy-done.34, f32[448,256]{1,0:T(8,128)S(1)} %get-tuple-element.102.x0_ref, ...), custom_call_target="tpu_custom_call" | custom-call | flops 1409286144 | tf_op jit(solution)/shard_map/feed/pallas_call | solution.py:123
  80.2 10.1 %attend_back.1 = (bf16[448,256]{1,0:T(8,128)(2,1)S(1)}, f32[448,512]{1,0:T(8,128)S(1)}, f32[448,512]{1,0:T(8,128)}, f32[256,256]{1,0:T(8,128)S(1)}, f32[1,256]{1,0:T(1,128)S(1)}) custom-call(bf16[448,256]{1,0:T(8,128)(2,1)S(1)} %copy-done.40, bf16[896,256]{1,0:T(8,128)(2,1)S(1)} %copy-done.36, bf16[896,256]{1,0:T(8,128)(2,1)S(1)} %copy-done.38, ...), custom_call_target="tpu_custom_call" | custom-call | flops 8220835840 | tf_op jit(solution)/shard_map/attend_back/pallas_call | solution.py:123
  90.5 9.2 %bases.1 = (bf16[8,256,256]{2,1,0:T(8,128)(2,1)S(1)}, bf16[4,256,256]{2,1,0:T(8,128)(2,1)S(1)}, bf16[512,512]{1,0:T(8,128)(2,1)S(1)}, bf16[3,1024,1024]{2,1,0:T(...) custom-call(f32[8,256,256]{2,1,0:T(8,128)S(1)} %copy-done.2, f32[512,512]{1,0:T(8,128)S(1)} %copy-done.9, ...), custom_call_target="tpu_custom_call" | custom-call | tf_op jit(solution)/shard_map/bases/pallas_call | solution.py:123
  99.7 2.8 %copy-done = bf16[3,1024,1024]{2,1,0:T(8,128)(2,1)S(1)} copy-done((bf16[3,1024,1024]{2,1,0:T(8,128)(2,1)S(1)}, bf16[3,1024,1024]{2,1,0:T(8,128)(2,1)}, u32[]{:S(2)}) %copy-start) | copy-done | bytes 6291480
  119.4 2.8 %collective-permute-done.34.refs_1_ = bf16[4,64,256]{2,1,0:T(8,128)(2,1)S(1)} collective-permute-done((bf16[4,64,256]{2,1,0:T(8,128)(2,1)S(1)}, bf16[4,64,256]{2,1,0:T(8,128)(2,1)S(1)}, u32[]{:S(2)}, u32[]{:S(2)}) %collective-permute-start.34) | collective-permute-done | bytes 131104 | tf_op jit(solution)/shard_map/ppermute | solution.py:49
  122.2 2.9 %collective-permute-done.35.refs_2_ = bf16[4,64,256]{2,1,0:T(8,128)(2,1)S(1)} collective-permute-done((bf16[4,64,256]{2,1,0:T(8,128)(2,1)S(1)}, bf16[4,64,256]{2,1,0:T(8,128)(2,1)S(1)}, u32[]{:S(2)}, u32[]{:S(2)}) %collective-permute-start.35) | collective-permute-done | bytes 131104 | tf_op jit(solution)/shard_map/ppermute | solution.py:49
  136.0 2.3 %collective-permute-start.42 = (bf16[1,64,256]{2,1,0:T(8,128)(2,1)S(1)}, bf16[1,64,256]{2,1,0:T(8,128)(2,1)S(1)}, u32[]{:S(2)}, u32[]{:S(2)}) collective-permute-start(bf16[1,64,256]{2,1,0:T(8,128)(2,1)S(1)} %bitcast.34), channel_id=1, source_target_pairs={{0,24},{8,16},{16,8},{24,0},{1,25},{9,17},{17,9},{25,1},{2,26},{10... | collective-permute-start | bytes 98312 | tf_op jit(solution)/shard_map/ppermute | solution.py:49
  138.8 2.9 %collective-permute-done.42 = bf16[1,64,256]{2,1,0:T(8,128)(2,1)S(1)} collective-permute-done((bf16[1,64,256]{2,1,0:T(8,128)(2,1)S(1)}, bf16[1,64,256]{2,1,0:T(8,128)(2,1)S(1)}, u32[]{:S(2)}, u32[]{:S(2)}) %collective-permute-start.42) | collective-permute-done | bytes 32800 | tf_op jit(solution)/shard_map/ppermute | solution.py:49
  151.8 2.3 %collective-permute-done.22.refs_3_ = bf16[4,64,256]{2,1,0:T(8,128)(2,1)S(1)} collective-permute-done((bf16[4,64,256]{2,1,0:T(8,128)(2,1)S(1)}, bf16[4,64,256]{2,1,0:T(8,128)(2,1)S(1)}, u32[]{:S(2)}, u32[]{:S(2)}) %collective-permute-start.22) | collective-permute-done | bytes 131104 | tf_op jit(solution)/shard_map/ppermute | solution.py:49
  154.2 2.8 %collective-permute-start.24 = (bf16[1,64,256]{2,1,0:T(8,128)(2,1)S(1)}, bf16[1,64,256]{2,1,0:T(8,128)(2,1)S(1)}, u32[]{:S(2)}, u32[]{:S(2)}) collective-permute-start(bf16[1,64,256]{2,1,0:T(8,128)(2,1)S(1)} %get-tuple-element.145), channel_id=1, source_target_pairs={{0,16},{8,24},{16,0},{24,8},{1,17},{9,25},{17,1},{25,9},{2,18},{10... | collective-permute-start | bytes 98312 | tf_op jit(solution)/shard_map/ppermute | solution.py:49
  159.1 4.0 %collective-permute-done.25 = bf16[1,64,256]{2,1,0:T(8,128)(2,1)S(1)} collective-permute-done((bf16[1,64,256]{2,1,0:T(8,128)(2,1)S(1)}, bf16[1,64,256]{2,1,0:T(8,128)(2,1)S(1)}, u32[]{:S(2)}, u32[]{:S(2)}) %collective-permute-start.25) | collective-permute-done | bytes 32800 | tf_op jit(solution)/shard_map/ppermute | solution.py:49
  165.3 2.3 %collective-permute-start.28 = (bf16[1,64,256]{2,1,0:T(8,128)(2,1)S(1)}, bf16[1,64,256]{2,1,0:T(8,128)(2,1)S(1)}, u32[]{:S(2)}, u32[]{:S(2)}) collective-permute-start(bf16[1,64,256]{2,1,0:T(8,128)(2,1)S(1)} %bitcast.30), channel_id=1, source_target_pairs={{0,24},{8,16},{16,8},{24,0},{1,25},{9,17},{17,9},{25,1},{2,26},{10... | collective-permute-start | bytes 98312 | tf_op jit(solution)/shard_map/ppermute | solution.py:49
  168.1 2.9 %collective-permute-done.28 = bf16[1,64,256]{2,1,0:T(8,128)(2,1)S(1)} collective-permute-done((bf16[1,64,256]{2,1,0:T(8,128)(2,1)S(1)}, bf16[1,64,256]{2,1,0:T(8,128)(2,1)S(1)}, u32[]{:S(2)}, u32[]{:S(2)}) %collective-permute-start.28) | collective-permute-done | bytes 32800 | tf_op jit(solution)/shard_map/ppermute | solution.py:49
  186.7 2.4 %collective-permute-start.53 = (f32[25,256]{1,0:T(8,128)S(1)}, f32[25,256]{1,0:T(8,128)S(1)}, u32[]{:S(2)}, u32[]{:S(2)}) collective-permute-start(f32[25,256]{1,0:T(8,128)S(1)} %add_add_fusion.1), channel_id=1, source_target_pairs={{0,24},{8,16},{16,8},{24,0},{1,25},{9,17},{17,9},{25,1},{2,26},{10... | collective-permute-start | bytes 76808 | tf_op jit(solution)/shard_map/ppermute | solution.py:49
  194.1 2.4 %finish.1 = (f32[1,32768]{1,0:T(1,128)}, f32[1,32768]{1,0:T(1,128)}, f32[1,32768]{1,0:T(1,128)}, f32[1,32768]{1,0:T(1,128)}) custom-call(bf16[16,64,256]{2,1,0:T(8,128)(2,1)S(1)} %constant_dynamic-update-slice_fusion.11.late_near, bf16[16,64,256]{2,1,0:T(8,128)(2,1)S(1)} %collective-permute-done.32.late_far, ...), custom_call_target="tpu_custom_call" | custom-call | tf_op jit(solution)/shard_map/finish/pallas_call | solution.py:123
  (236 shorter events, 102.1 us)
Async XLA Ops:
  7.2 63.0 %all-gather.3.cloned.1.call-start = ((), (), s32[]{:S(2)}) async-start(), calls=%async_computation | async-start | bytes 1081344 | tf_op jit(solution)/shard_map/all_gather | solution.py:764
  20.2 6.1 %collective-permute-start.5 = (bf16[4,64,256]{2,1,0:T(8,128)(2,1)S(1)}, bf16[4,64,256]{2,1,0:T(8,128)(2,1)S(1)}, u32[]{:S(2)}, u32[]{:S(2)}) collective-permute-start(bf16[4,64,256]{2,1,0:T(8,128)(2,1)S(1)} %pad_maximum_fusion), channel_id=1, source_target_pairs={{0,2},{1,3},{2,0},{3,1},{4,6},{5,7},{6,4},{7,5},{8,10},{9,11},{10,... | collective-permute-start | bytes 393224 | tf_op jit(solution)/shard_map/ppermute | solution.py:49
  21.7 6.0 %collective-permute-start.6 = (bf16[4,64,256]{2,1,0:T(8,128)(2,1)S(1)}, bf16[4,64,256]{2,1,0:T(8,128)(2,1)S(1)}, u32[]{:S(2)}, u32[]{:S(2)}) collective-permute-start(bf16[4,64,256]{2,1,0:T(8,128)(2,1)S(1)} %pad_maximum_fusion), channel_id=1, source_target_pairs={{0,4},{1,5},{2,6},{3,7},{4,0},{5,1},{6,2},{7,3},{8,12},{9,13},{10,... | collective-permute-start | bytes 393224 | tf_op jit(solution)/shard_map/ppermute | solution.py:49
  23.2 6.1 %collective-permute-start.7 = (bf16[4,64,256]{2,1,0:T(8,128)(2,1)S(1)}, bf16[4,64,256]{2,1,0:T(8,128)(2,1)S(1)}, u32[]{:S(2)}, u32[]{:S(2)}) collective-permute-start(bf16[4,64,256]{2,1,0:T(8,128)(2,1)S(1)} %pad_maximum_fusion), channel_id=1, source_target_pairs={{0,6},{1,7},{2,4},{3,5},{4,2},{5,3},{6,0},{7,1},{8,14},{9,15},{10,... | collective-permute-start | bytes 393224 | tf_op jit(solution)/shard_map/ppermute | solution.py:49
  29.4 8.8 %collective-permute-start.8 = (bf16[16,64,256]{2,1,0:T(8,128)(2,1)S(1)}, bf16[16,64,256]{2,1,0:T(8,128)(2,1)S(1)}, u32[]{:S(2)}, u32[]{:S(2)}) collective-permute-start(bf16[16,64,256]{2,1,0:T(8,128)(2,1)S(1)} %constant_dynamic-update-slice_fusion.refs_0_), channel_id=1, source_target_pairs={{0,1},{1,0},{2,3},{3,2},{4,5},{5,4},{6,7},{7,6},{8,9},{9,8},{10,11... | collective-permute-start | bytes 1572872 | tf_op jit(solution)/shard_map/ppermute | solution.py:49
  44.8 6.8 %collective-permute-start.11 = (bf16[112,512]{1,0:T(8,128)(2,1)S(1)}, bf16[112,512]{1,0:T(8,128)(2,1)S(1)}, u32[]{:S(2)}, u32[]{:S(2)}) collective-permute-start(bf16[112,512]{1,0:T(8,128)(2,1)S(1)} %get-tuple-element.100), channel_id=1, source_target_pairs={{0,6},{1,7},{2,4},{3,5},{4,2},{5,3},{6,0},{7,1},{8,14},{9,15},{10,... | collective-permute-start | bytes 344072 | tf_op jit(solution)/shard_map/ppermute | solution.py:49
  90.3 14.4 %collective-permute-start.13 = (f32[448,512]{1,0:T(8,128)}, f32[448,512]{1,0:T(8,128)S(1)}, u32[]{:S(2)}, u32[]{:S(2)}) collective-permute-start(f32[448,512]{1,0:T(8,128)} %get-tuple-element.113), channel_id=1, source_target_pairs={{0,1},{1,0},{2,3},{3,2},{4,5},{5,4},{6,7},{7,6},{8,9},{9,8},{10,11... | collective-permute-start | bytes 2752520 | tf_op jit(solution)/shard_map/ppermute | solution.py:49
  104.3 11.3 %collective-permute-start.33 = (f32[16,64,256]{2,1,0:T(8,128)S(1)}, f32[16,64,256]{2,1,0:T(8,128)S(1)}, u32[]{:S(2)}, u32[]{:S(2)}) collective-permute-start(f32[16,64,256]{2,1,0:T(8,128)S(1)} %get-tuple-element.153), channel_id=1, source_target_pairs={{0,1},{1,0},{2,3},{3,2},{4,5},{5,4},{6,7},{7,6},{8,9},{9,8},{10,11... | collective-permute-start | bytes 3145736 | tf_op jit(solution)/shard_map/ppermute | solution.py:49
  106.1 6.0 %collective-permute-start.15 = (bf16[112,512]{1,0:T(8,128)(2,1)S(1)}, bf16[112,512]{1,0:T(8,128)(2,1)S(1)}, u32[]{:S(2)}, u32[]{:S(2)}) collective-permute-start(bf16[112,512]{1,0:T(8,128)(2,1)S(1)} %get-tuple-element.116), channel_id=1, source_target_pairs={{0,4},{1,5},{2,6},{3,7},{4,0},{5,1},{6,2},{7,3},{8,12},{9,13},{10,... | collective-permute-start | bytes 344072 | tf_op jit(solution)/shard_map/ppermute | solution.py:49
  107.1 6.6 %collective-permute-start.16 = (bf16[112,512]{1,0:T(8,128)(2,1)S(1)}, bf16[112,512]{1,0:T(8,128)(2,1)S(1)}, u32[]{:S(2)}, u32[]{:S(2)}) collective-permute-start(bf16[112,512]{1,0:T(8,128)(2,1)S(1)} %get-tuple-element.117), channel_id=1, source_target_pairs={{0,6},{1,7},{2,4},{3,5},{4,2},{5,3},{6,0},{7,1},{8,14},{9,15},{10,... | collective-permute-start | bytes 344072 | tf_op jit(solution)/shard_map/ppermute | solution.py:49
  115.6 29.7 %collective-permute-start.19 = (f32[16,64,256]{2,1,0:T(8,128)S(1)}, f32[16,64,256]{2,1,0:T(8,128)S(1)}, u32[]{:S(2)}, u32[]{:S(2)}) collective-permute-start(f32[16,64,256]{2,1,0:T(8,128)S(1)} %get-tuple-element.138), channel_id=1, source_target_pairs={{0,1},{1,0},{2,3},{3,2},{4,5},{5,4},{6,7},{7,6},{8,9},{9,8},{10,11... | collective-permute-start | bytes 3145736 | tf_op jit(solution)/shard_map/ppermute | solution.py:49
  115.8 6.4 %collective-permute-start.34 = (bf16[4,64,256]{2,1,0:T(8,128)(2,1)S(1)}, bf16[4,64,256]{2,1,0:T(8,128)(2,1)S(1)}, u32[]{:S(2)}, u32[]{:S(2)}) collective-permute-start(bf16[4,64,256]{2,1,0:T(8,128)(2,1)S(1)} %get-tuple-element.155), channel_id=1, source_target_pairs={{0,2},{1,3},{2,0},{3,1},{4,6},{5,7},{6,4},{7,5},{8,10},{9,11},{10,... | collective-permute-start | bytes 393224 | tf_op jit(solution)/shard_map/ppermute | solution.py:49
  116.7 8.4 %collective-permute-start.35 = (bf16[4,64,256]{2,1,0:T(8,128)(2,1)S(1)}, bf16[4,64,256]{2,1,0:T(8,128)(2,1)S(1)}, u32[]{:S(2)}, u32[]{:S(2)}) collective-permute-start(bf16[4,64,256]{2,1,0:T(8,128)(2,1)S(1)} %get-tuple-element.156), channel_id=1, source_target_pairs={{0,4},{1,5},{2,6},{3,7},{4,0},{5,1},{6,2},{7,3},{8,12},{9,13},{10,... | collective-permute-start | bytes 393224 | tf_op jit(solution)/shard_map/ppermute | solution.py:49
  118.1 6.9 %collective-permute-start.36 = (bf16[4,64,256]{2,1,0:T(8,128)(2,1)S(1)}, bf16[4,64,256]{2,1,0:T(8,128)(2,1)S(1)}, u32[]{:S(2)}, u32[]{:S(2)}) collective-permute-start(bf16[4,64,256]{2,1,0:T(8,128)(2,1)S(1)} %get-tuple-element.157), channel_id=1, source_target_pairs={{0,6},{1,7},{2,4},{3,5},{4,2},{5,3},{6,0},{7,1},{8,14},{9,15},{10,... | collective-permute-start | bytes 393224 | tf_op jit(solution)/shard_map/ppermute | solution.py:49
  125.1 6.9 %collective-permute-start.37 = (bf16[1,64,256]{2,1,0:T(8,128)(2,1)S(1)}, bf16[1,64,256]{2,1,0:T(8,128)(2,1)S(1)}, u32[]{:S(2)}, u32[]{:S(2)}) collective-permute-start(bf16[1,64,256]{2,1,0:T(8,128)(2,1)S(1)} %get-tuple-element.159), channel_id=1, source_target_pairs={{0,8},{8,0},{16,24},{24,16},{1,9},{9,1},{17,25},{25,17},{2,10},{10... | collective-permute-start | bytes 98312 | tf_op jit(solution)/shard_map/ppermute | solution.py:49
  141.7 6.5 %collective-permute-start.43 = (bf16[4,64,256]{2,1,0:T(8,128)(2,1)S(1)}, bf16[4,64,256]{2,1,0:T(8,128)(2,1)S(1)}, u32[]{:S(2)}, u32[]{:S(2)}) collective-permute-start(bf16[4,64,256]{2,1,0:T(8,128)(2,1)S(1)} %pad_maximum_fusion.2), channel_id=1, source_target_pairs={{0,2},{1,3},{2,0},{3,1},{4,6},{5,7},{6,4},{7,5},{8,10},{9,11},{10,... | collective-permute-start | bytes 393224 | tf_op jit(solution)/shard_map/ppermute | solution.py:49
  143.1 7.2 %collective-permute-start.44 = (bf16[4,64,256]{2,1,0:T(8,128)(2,1)S(1)}, bf16[4,64,256]{2,1,0:T(8,128)(2,1)S(1)}, u32[]{:S(2)}, u32[]{:S(2)}) collective-permute-start(bf16[4,64,256]{2,1,0:T(8,128)(2,1)S(1)} %pad_maximum_fusion.2), channel_id=1, source_target_pairs={{0,4},{1,5},{2,6},{3,7},{4,0},{5,1},{6,2},{7,3},{8,12},{9,13},{10,... | collective-permute-start | bytes 393224 | tf_op jit(solution)/shard_map/ppermute | solution.py:49
  144.0 14.6 %collective-permute-start.45 = (bf16[4,64,256]{2,1,0:T(8,128)(2,1)S(1)}, bf16[4,64,256]{2,1,0:T(8,128)(2,1)S(1)}, u32[]{:S(2)}, u32[]{:S(2)}) collective-permute-start(bf16[4,64,256]{2,1,0:T(8,128)(2,1)S(1)} %pad_maximum_fusion.2), channel_id=1, source_target_pairs={{0,6},{1,7},{2,4},{3,5},{4,2},{5,3},{6,0},{7,1},{8,14},{9,15},{10,... | collective-permute-start | bytes 393224 | tf_op jit(solution)/shard_map/ppermute | solution.py:49
  148.2 5.9 %collective-permute-start.22 = (bf16[4,64,256]{2,1,0:T(8,128)(2,1)S(1)}, bf16[4,64,256]{2,1,0:T(8,128)(2,1)S(1)}, u32[]{:S(2)}, u32[]{:S(2)}) collective-permute-start(bf16[4,64,256]{2,1,0:T(8,128)(2,1)S(1)} %get-tuple-element.142), channel_id=1, source_target_pairs={{0,6},{1,7},{2,4},{3,5},{4,2},{5,3},{6,0},{7,1},{8,14},{9,15},{10,... | collective-permute-start | bytes 393224 | tf_op jit(solution)/shard_map/ppermute | solution.py:49
  150.2 28.9 %collective-permute-start.47 = (f32[25,256]{1,0:T(8,128)S(1)}, f32[25,256]{1,0:T(8,128)S(1)}, u32[]{:S(2)}, u32[]{:S(2)}) collective-permute-start(f32[25,256]{1,0:T(8,128)S(1)} %get-tuple-element.175), channel_id=1, source_target_pairs={{0,1},{1,0},{2,3},{3,2},{4,5},{5,4},{6,7},{7,6},{8,9},{9,8},{10,11... | collective-permute-start | bytes 76808 | tf_op jit(solution)/shard_map/ppermute | solution.py:49
  157.1 6.0 %collective-permute-start.25 = (bf16[1,64,256]{2,1,0:T(8,128)(2,1)S(1)}, bf16[1,64,256]{2,1,0:T(8,128)(2,1)S(1)}, u32[]{:S(2)}, u32[]{:S(2)}) collective-permute-start(bf16[1,64,256]{2,1,0:T(8,128)(2,1)S(1)} %get-tuple-element.146), channel_id=1, source_target_pairs={{0,24},{8,16},{16,8},{24,0},{1,25},{9,17},{17,9},{25,1},{2,26},{10... | collective-permute-start | bytes 98312 | tf_op jit(solution)/shard_map/ppermute | solution.py:49
  158.6 35.5 %collective-permute-start.46 = (bf16[16,64,256]{2,1,0:T(8,128)(2,1)S(1)}, bf16[16,64,256]{2,1,0:T(8,128)(2,1)S(1)}, u32[]{:S(2)}, u32[]{:S(2)}) collective-permute-start(bf16[16,64,256]{2,1,0:T(8,128)(2,1)S(1)} %constant_dynamic-update-slice_fusion.18.early_near), channel_id=1, source_target_pairs={{0,1},{1,0},{2,3},{3,2},{4,5},{5,4},{6,7},{7,6},{8,9},{9,8},{10,11... | collective-permute-start | bytes 1572872 | tf_op jit(solution)/shard_map/ppermute | solution.py:49
  173.2 5.9 %collective-permute-start.31 = (bf16[4,64,256]{2,1,0:T(8,128)(2,1)S(1)}, bf16[4,64,256]{2,1,0:T(8,128)(2,1)S(1)}, u32[]{:S(2)}, u32[]{:S(2)}) collective-permute-start(bf16[4,64,256]{2,1,0:T(8,128)(2,1)S(1)} %pad_maximum_fusion.1), channel_id=1, source_target_pairs={{0,6},{1,7},{2,4},{3,5},{4,2},{5,3},{6,0},{7,1},{8,14},{9,15},{10,... | collective-permute-start | bytes 393224 | tf_op jit(solution)/shard_map/ppermute | solution.py:49
  179.1 15.0 %collective-permute-start.32 = (bf16[16,64,256]{2,1,0:T(8,128)(2,1)S(1)}, bf16[16,64,256]{2,1,0:T(8,128)(2,1)S(1)}, u32[]{:S(2)}, u32[]{:S(2)}) collective-permute-start(bf16[16,64,256]{2,1,0:T(8,128)(2,1)S(1)} %constant_dynamic-update-slice_fusion.11.late_near), channel_id=1, source_target_pairs={{0,1},{1,0},{2,3},{3,2},{4,5},{5,4},{6,7},{7,6},{8,9},{9,8},{10,11... | collective-permute-start | bytes 1572872 | tf_op jit(solution)/shard_map/ppermute | solution.py:49
  (74 other events, 749.8 us)
Sparse Core Ops, SparseCore 0:
  14.6 55.5 all-gather.2

commit v3 on v2

v3 whole, which is shorter than its diff:
```python
import functools
import math

import jax
import jax.numpy as jnp
from jax import lax
from jax.experimental import pallas as pl
from jax.experimental.pallas import tpu as pltpu
from jax.sharding import PartitionSpec as P

HEADS = 8
FF = 1024
STEP = 5

NORM_EPS = 1e-05
ADAM_EPS = 1e-08
BETA = 0.5
WEIGHT_DECAY = 0.05
EMA_KEEP = 0.75
VECTOR_RATE = 0.06
MATRIX_RATES = (0.04, 0.02, 0.25, 0.02, 0.01, 0.01)
CORRECTION = 1.0 - BETA**STEP
LOG2E = math.log2(math.e)
f32 = jnp.float32
bf16 = jnp.bfloat16
LATE = (5, 1, 0, 2)
EARLY = (3, 4)


def matrix_shapes(width, hidden):
    return (
        (width, width),
        (width, 2 * width),
        (width, width),
        (width, hidden),
        (hidden, width),
        (4 * width, width),
    )


def contract(a, b, ca, cb, **kw):
    return lax.dot_general(
        a, b, (((ca,), (cb,)), ((), ())), preferred_element_type=f32, **kw
    )


def swap(x, axis, step):
    count = lax.axis_size(axis)
    return lax.ppermute(x, axis, [(i, i ^ step) for i in range(count)])


def row_groups():
    left = lax.axis_size("row") // 2
    groups, stride = [(1, 2)], 2
    while left > 1:
        size = 4 if left % 4 == 0 else 2
        groups.append((stride, size))
        left //= size
        stride *= size
    return groups


def rel_digits():
    groups = row_groups()
    return [groups[0]] + groups[1:][::-1]


def source(block):
    sizes = lax.axis_size("img")
    img, rest = block % sizes, block // sizes
    rel = 0
    for stride, size in reversed(rel_digits()):
        rel = rel + (rest % size) * stride
        rest = rest // size
    row = lax.axis_index("row") ^ rel
    return (lax.axis_index("img") ^ img) * lax.axis_size("row") + row


def device_count():
    return lax.axis_size("img") * lax.axis_size("row")


def run(name, body, outs, args, scratch=(), mib=6, scalars=(), micros=1.0, after=(), raw=(), sems=0):
    count = len(args)

    def without(*refs):
        body(*refs[:count], *refs[count + len(after) :])

    space = {index: pltpu.SMEM for index in scalars} | {index: pl.ANY for index in raw}
    specs = [pl.BlockSpec(memory_space=space.get(index, pltpu.VMEM)) for index in range(count)]
    return pl.pallas_call(
        without,
        out_shape=tuple(jax.ShapeDtypeStruct(shape, dtype) for shape, dtype in outs),
        in_specs=specs + [pl.BlockSpec(memory_space=pl.ANY)] * len(after),
        out_specs=tuple(pl.BlockSpec(memory_space=pltpu.VMEM) for _ in outs),
        scratch_shapes=[pltpu.VMEM(shape, dtype) for shape, dtype in scratch]
        + ([pltpu.SemaphoreType.DMA((sems,))] if sems else []),
        compiler_params=pltpu.CompilerParams(vmem_limit_bytes=mib * 2**20),
        cost_estimate=pl.CostEstimate(flops=0, bytes_accessed=int(micros * 3.6e6), transcendentals=0),
        name=name,
    )(*args, *after)


def each_block(count, body):
    if count <= 32:
        for index in range(count):
            body(index)
    else:

        def step(index, carry):
            body(index)
            return carry

        lax.fori_loop(0, count, step, 0)


def put_rows(ref, start, cols, value):
    count = value.shape[0]
    if count % 8 == 0:
        ref[pl.ds(pl.multiple_of(start, 8), count), cols] = value
    else:
        for row in range(count):
            ref[pl.ds(start + row, 1), cols] = value[row : row + 1]


def get_rows(ref, start, count, cols):
    if count % 8 == 0:
        return ref[pl.ds(pl.multiple_of(start, 8), count), cols]
    return jnp.concatenate([ref[pl.ds(start + row, 1), cols] for row in range(count)], axis=0)


def layout(width, group):
    dims = matrix_shapes(width, FF)
    found, start = [], 0
    for j in group:
        rows = dims[j][0] // device_count()
        blocks = dims[j][1] // width
        found.append((j, start, rows, blocks))
        start += rows * blocks
    return found, start


def packed_starts(width):
    dims = matrix_shapes(width, FF)
    starts, start = [], 0
    for m, n in dims:
        starts.append(start)
        start += m * n // device_count()
    return starts


def spread(block, parts, mats, start_of):
    for (j, first, rows, blocks), ref in zip(parts, mats):
        for col in range(blocks):
            piece = block[first + col * rows : first + (col + 1) * rows]
            put_rows(ref, start_of * rows, slice(col * 256, col * 256 + 256), piece)


def collect(out_ref, index, parts, mats, start_of):
    for (j, first, rows, blocks), ref in zip(parts, mats):
        for col in range(blocks):
            piece = get_rows(ref, start_of * rows, rows, slice(col * 256, col * 256 + 256))
            out_ref[index, first + col * rows : first + (col + 1) * rows, :] = piece


def norm_parts(values):
    centred = values - jnp.mean(values, axis=-1, keepdims=True)
    inverse = lax.rsqrt(jnp.mean(centred * centred, axis=-1, keepdims=True) + NORM_EPS)
    return centred * inverse, inverse


def norm_back(grad, unit, inverse, gain):
    grad_unit = grad * gain
    back = grad_unit - jnp.mean(grad_unit, axis=-1, keepdims=True)
    back = back - unit * jnp.mean(grad_unit * unit, axis=-1, keepdims=True)
    gain_sum = jnp.sum(grad * unit, axis=0, keepdims=True)
    return back * inverse, gain_sum, jnp.sum(grad, axis=0, keepdims=True)


def turned(value):
    return value.astype(f32).T.astype(bf16)


def col_sum(value):
    return jnp.sum(value, axis=0, keepdims=True)


def pack_kernel(width, w_ref, out_ref, chunk):
    to_chunk(w_ref, chunk, width)
    out_ref[...] = chunk[...].astype(bf16)


def to_chunk(flat_ref, out_ref, width):
    dims, starts, base = matrix_shapes(width, FF), packed_starts(width), 0
    for group in (LATE, EARLY):
        parts, count = layout(width, group)
        for j, first, rows, blocks in parts:
            for col in range(blocks):
                for row in range(rows):
                    at = starts[j] + row * dims[j][1] + col * width
                    place = base + first + col * rows + row
                    out_ref[place : place + 1, :] = flat_ref[0:1, at : at + width]
        base += count


def from_chunk(values, base, group, out_ref, width):
    dims, starts = matrix_shapes(width, FF), packed_starts(width)
    parts, _ = layout(width, group)
    for j, first, rows, blocks in parts:
        for col in range(blocks):
            for row in range(rows):
                at = starts[j] + row * dims[j][1] + col * width
                place = base + first + col * rows + row
                out_ref[0:1, at : at + width] = values[place : place + 1, :]


def moments_kernel(width, *refs):
    for index in range(4):
        to_chunk(refs[index], refs[4 + index], width)


def own_rows(matrix_ref, out_ref, tall):
    count = device_count()
    rank = lax.axis_index("img") * lax.axis_size("row") + lax.axis_index("row")
    size = matrix_ref.shape[0]
    rows = size // count
    place = lax.broadcasted_iota(jnp.int32, (128, 1), 0)
    place = jnp.where(place < rows, place + rank * rows, -1)
    pick = (lax.broadcasted_iota(jnp.int32, (128, size), 1) == place).astype(f32).astype(bf16)
    tall[0:size, :] = contract(pick, matrix_ref[...], 1, 0).T

    def body(block):
        put_rows(tall, size + block * rows, slice(None), get_rows(tall, source(block) * rows, rows, slice(None)))

    each_block(count, body)
    out_ref[...] = tall[size : 2 * size, :].T[0 : out_ref.shape[0]]


def small_bases_kernel(narrow_ref, pair_ref, narrow_out, turned_out, pair_out, own_ref, tall):
    narrow_out[...] = narrow_ref[...].astype(bf16)
    pair_out[...] = pair_ref[...].astype(bf16)
    for index, j in enumerate((0, 2, 3, 5)):
        turned_out[index] = narrow_ref[j].T.astype(bf16)
        own_rows(narrow_out.at[j], own_ref.at[index], tall)


def wide_bases_kernel(wide_ref, wide_out, own_ref, tall, buffer, sems):
    count, size = wide_ref.shape[0], wide_ref.shape[1]
    rows, depth = buffer.shape[1], buffer.shape[0]
    each = size // rows
    total = count * each

    def copy(index):
        at = wide_ref.at[index // each, pl.ds(index % each * rows, rows)]
        return pltpu.make_async_copy(at, buffer.at[index % depth], sems.at[index % depth])

    for index in range(depth):
        copy(index).start()
    for index in range(total):
        copy(index).wait()
        first = index % each * rows
        wide_out[index // each, first : first + rows, :] = buffer[index % depth].astype(bf16)
        if index + depth < total:
            copy(index + depth).start()
    for index in range(2):
        own_rows(wide_out.at[index + 1], own_ref.at[index], tall)


def stack_kernel(split, *refs):
    count = len(refs) - 2
    for index in range(count):
        refs[count][index] = refs[index][0:split, :]
        refs[count + 1][index] = refs[index][split:, :]


def unpack(pieces, group, mats):
    parts, _ = layout(256, group)
    wanted = [(part, ref) for part, ref in zip(parts, mats) if ref is not None]
    done = 0
    for piece in pieces:

        def body(block, piece=piece, done=done):
            spread(piece[block].astype(f32), [p for p, _ in wanted], [r for _, r in wanted], source(block + done))

        each_block(piece.shape[0], body)
        done += piece.shape[0]


def shifted_frame(frame_ref, tile_ref, up_ref, down_ref):
    rows, cols, width = frame_ref.shape[0] - 2, 56, 256
    frame_ref[...] = jnp.zeros_like(frame_ref)
    frame_ref[0, 8 : 8 + cols, :] = up_ref[...].astype(f32)[-cols:]
    frame_ref[1 : 1 + rows, 8 : 8 + cols, :] = tile_ref[...].astype(f32).reshape(rows, cols, width)
    frame_ref[rows + 1, 8 : 8 + cols, :] = down_ref[...].astype(f32)[:cols]
    return [frame_ref[:, 7 + shift : 7 + shift + cols, :] for shift in range(3)]


def front_kernel(tile_rows, cols, size_ref, tile_ref, up_ref, down_ref, vec_ref, x0_ref, h1_ref, mask_ref, vec_out, frame):
    rows = frame.shape[0] - 2
    vec_out[...] = vec_ref[...]
    moved = shifted_frame(frame, tile_ref, up_ref, down_ref)
    total = moved[1][1:-1] + vec_ref[9:10, :]
    for tap in range(9):
        total = total + vec_ref[tap : tap + 1, :] * moved[tap % 3][tap // 3 : tap // 3 + rows]
    x0 = total.reshape(x0_ref.shape)
    x0_ref[...] = x0
    unit, _ = norm_parts(x0)
    h1_ref[...] = (unit * vec_ref[10:11, :] + vec_ref[11:12, :]).astype(bf16)
    half = cols // 2
    own = tile_rows // 2 * half
    key = lax.broadcasted_iota(jnp.int32, mask_ref.shape, 1)
    block = jnp.zeros_like(key)
    for start in range(own, mask_ref.shape[1], own):
        block = block + (key >= start).astype(jnp.int32)
    key = key - block * own
    row = jnp.zeros_like(key)
    for start in range(half, own, half):
        row = row + (key >= start).astype(jnp.int32)
    col = key - row * half
    rel = jnp.zeros_like(key)
    for stride, size in reversed(rel_digits()):
        rel = rel + (block & (size - 1)) * stride
        block = block >> (size.bit_length() - 1)
    row = row + (rel ^ lax.axis_index("row")) * (tile_rows // 2)
    inside = (2 * row < size_ref[0, 0]) & (2 * col < size_ref[0, 1])
    mask_ref[...] = jnp.where(inside, 0.0, -1e30)


def picked_cells(shape, cell_axis, size_ref, corner, tile_rows, cols):
    half = cols // 2
    key_shape = tuple(1 if axis == cell_axis else n for axis, n in enumerate(shape))
    key = lax.broadcasted_iota(jnp.int32, key_shape, 1 - cell_axis)
    row = jnp.zeros_like(key)
    for step in range(1, tile_rows // 2):
        row = row + (key >= step * half).astype(jnp.int32)
    col = 2 * (key - row * half) + corner % 2
    row = 2 * row + corner // 2
    inside = (row + lax.axis_index("row") * tile_rows < size_ref[0, 0]) & (col < size_ref[0, 1])
    target = jnp.where(inside, row * cols + col, -1)
    cell = lax.broadcasted_iota(jnp.int32, shape, cell_axis)
    return (cell == target).astype(f32).astype(bf16)


def keys_kernel(
    tile_rows, cols, size_ref, h1_ref, vec_ref, near_ref, far_ref,
    reduce_ref, keyval_ref, query_ref, out_ref, blocks_ref, c_ref, kn_ref, kv_ref,
    reduce_wide, keyval_wide, query_wide, out_wide,
):
    unpack((near_ref, far_ref), LATE, (reduce_wide, keyval_wide, query_wide, out_wide))
    reduce_ref[...] = reduce_wide[...].astype(bf16)
    keyval_ref[...] = keyval_wide[...].astype(bf16)
    query_ref[...] = query_wide[...].astype(bf16)
    out_ref[...] = out_wide[...].astype(bf16)
    keys = c_ref.shape[0]
    for corner in range(4):
        pick = picked_cells((keys, h1_ref.shape[0]), 1, size_ref, corner, tile_rows, cols)
        blocks_ref[:, corner * 256 : corner * 256 + 256] = contract(pick, h1_ref[...], 1, 0).astype(bf16)
    c = contract(blocks_ref[...], reduce_ref[...], 1, 0) + vec_ref[13:14, :]
    c_ref[...] = c
    unit, _ = norm_parts(c)
    kn = (unit * vec_ref[14:15, :] + vec_ref[15:16, :]).astype(bf16)
    kn_ref[...] = kn
    kv = contract(kn, keyval_ref[...], 1, 0)
    kv_ref[:, 0:256] = kv[:, 0:256].astype(bf16)
    kv_ref[:, 256:512] = (kv[:, 256:512] + vec_ref[16:17, :]).astype(bf16)


def over_heads(body, first, last, unroll):
    if unroll:
        for head in range(first, last):
            body(head)
    else:

        def step(head, carry):
            body(head)
            return carry

        lax.fori_loop(first, last, step, 0)


def over_blocks(block, tokens, step):
    if tokens == step:
        block(0)
    else:

        def go(index, carry):
            block(pl.multiple_of(index * step, step))
            return carry

        lax.fori_loop(0, tokens // step, go, 0)


def head_columns(head):
    group = head // 4
    if isinstance(head, int):
        return slice(group * 128, group * 128 + 128)
    return pl.ds(pl.multiple_of(group * 128, 128), 128)


def head_rows(head, base=0):
    if isinstance(head, int):
        return slice(base + head * 32, base + head * 32 + 32)
    return pl.ds(pl.multiple_of(base + head * 32, 32), 32)


def attend_kernel(
    step, unroll, h1_ref, query_ref, vec_ref, near_ref, far_ref, mask_ref, q_ref, k_ref, v_ref, o_ref, log_ref
):
    tokens = h1_ref.shape[0]
    half = near_ref.shape[0]
    for start, ref in ((0, near_ref), (half, far_ref)):
        k_ref[start : start + half, :] = ref[:, 0:256]
        v_ref[start : start + half, :] = ref[:, 256:512]
    q_ref[...] = (contract(h1_ref[...], query_ref[...], 1, 0) + vec_ref[12:13, :]).astype(bf16)
    scale = 32**-0.5 * LOG2E
    lane = lax.broadcasted_iota(jnp.int32, (1, 128), 1)
    mask = mask_ref[...]

    def one_head(head):
        cols = head_columns(head)
        mine = lane // 32 == head % 4
        keys = jnp.where(mine, k_ref[:, cols], 0)
        values = jnp.where(mine, v_ref[:, cols], 0)

        def block(start):
            rows = pl.ds(start, step)
            scores = contract(q_ref[rows, cols], keys, 1, 1) * scale + mask
            top = jnp.max(scores, axis=1, keepdims=True)
            exponent = jnp.exp2(scores - top)
            total = jnp.sum(exponent, axis=1, keepdims=True)
            probs = (exponent * (1.0 / total)).astype(bf16)
            out = contract(probs, values, 1, 0)
            o_ref[rows, cols] = jnp.where(mine, out, o_ref[rows, cols])
            log_ref[rows, :] = jnp.where(lane == head, top + jnp.log2(total), log_ref[rows, :])

        over_blocks(block, tokens, step)

    over_heads(one_head, 0, HEADS, unroll)


def feed_kernel(
    o_ref, x0_ref, out_ref, near_ref, far_ref, vec_ref, dy_ref,
    y_ref, do_ref, dx1_ref, up_grad, down_grad, out_grad, sums_ref, up_ref, down_ref, up_wide, down_wide,
):
    unpack((near_ref, far_ref), EARLY, (up_wide, down_wide))
    up_ref[...] = up_wide[...].astype(bf16)
    down_ref[...] = down_wide[...].astype(bf16)
    o = o_ref[...].astype(bf16)
    x1 = x0_ref[...] + (contract(o, out_ref[...], 1, 0) + vec_ref[17:18, :])
    unit, inverse = norm_parts(x1)
    h2 = (unit * vec_ref[18:19, :] + vec_ref[19:20, :]).astype(bf16)
    dy_low = dy_ref[...]
    dy = dy_low.astype(f32)
    dyt = turned(dy_low)
    h2t = turned(h2)
    y = x1 + vec_ref[20:21, :]
    dh2 = jnp.zeros_like(y)
    for col in range(FF // 256):
        cols = slice(col * 256, col * 256 + 256)
        u = contract(h2, up_ref[:, cols], 1, 0) + vec_ref[21 + col : 22 + col, :]
        phi_sum = 0.5 * (1.0 + lax.erf(u * (2.0**-0.5)))
        density = jnp.exp(-0.5 * u * u) * ((2.0 * math.pi) ** -0.5)
        g = (u * phi_sum).astype(bf16)
        y = y + contract(g, down_ref[cols, :], 1, 0)
        down_grad[:, cols] = contract(dyt, g, 1, 0)
        du = (contract(dy_low, down_ref[cols, :], 1, 1) * (phi_sum + u * density)).astype(bf16)
        up_grad[:, cols] = contract(h2t, du, 1, 0)
        sums_ref[21 + col : 22 + col, :] = col_sum(du.astype(f32))
        dh2 = dh2 + contract(du, up_ref[:, cols], 1, 1)
    y_ref[...] = y.astype(bf16)
    back, gain_sum, bias_sum = norm_back(dh2, unit, inverse, vec_ref[18:19, :])
    dx1 = dy + back
    dx1_ref[...] = dx1
    da = dx1.astype(bf16)
    do_ref[...] = contract(da, out_ref[...], 1, 1).astype(bf16)
    out_grad[...] = contract(turned(o), da, 1, 0)
    sums_ref[0:17, :] = jnp.zeros((17, 256), f32)
    sums_ref[17:18, :] = col_sum(da.astype(f32))
    sums_ref[18:19, :] = gain_sum
    sums_ref[19:20, :] = bias_sum
    sums_ref[20:21, :] = col_sum(dy)


def rotate(left_turned, grad, right):
    half = contract(left_turned, grad.astype(bf16), 1, 0).astype(bf16)
    return contract(half, right, 1, 0)


def rotate_turned(grad_turned, left, right):
    half = contract(grad_turned.astype(bf16), left, 1, 0).astype(bf16)
    return contract(turned(half), right, 1, 0)


def share_out(keep_ref, send_ref, parts, mats):
    half = keep_ref.shape[0]
    for ref, base in ((keep_ref, 0), (send_ref, half)):

        def body(block, ref=ref, base=base):
            collect(ref, block, parts, mats, source(block + base))

        each_block(half, body)


def early_turn_kernel(up_grad, down_grad, turned_ref, narrow_ref, wide_ref, keep_ref, send_ref, up, down):
    up[...] = rotate(turned_ref[3], up_grad[...], wide_ref[0])
    down[...] = rotate_turned(down_grad[...], wide_ref[1], narrow_ref[6])
    share_out(keep_ref, send_ref, layout(256, EARLY)[0], (up, down))


def middle_turn_kernel(query_left, query_right, out_grad, turned_ref, narrow_ref, query_ref, out_ref):
    query_grad = jnp.concatenate([query_left[...], query_right[...]], axis=1)
    query_ref[...] = rotate(turned_ref[0], query_grad, narrow_ref[1])
    out_ref[...] = rotate(turned_ref[2], out_grad[...], narrow_ref[4])


def attend_back_kernel(
    step, unroll, group, q_ref, k_ref, v_ref, mask_ref, o_ref, log_ref, g_ref, h1_ref,
    dq_ref, keep_ref, send_ref, query_grad, bias_ref, dq_wide, dkv, ps, dss, qt, gt,
):
    tokens = q_ref.shape[0]
    scale = 32**-0.5
    lane = lax.broadcasted_iota(jnp.int32, (1, 128), 1)
    mask = mask_ref[...]
    cols = slice(group * 128, group * 128 + 128)
    qt[...] = turned(q_ref[:, cols])
    gt[...] = turned(g_ref[:, cols])

    def one_head(head):
        mine = lane // 32 == head
        keys = jnp.where(mine, k_ref[:, cols], 0)
        values = jnp.where(mine, v_ref[:, cols], 0)

        def block(start):
            rows = pl.ds(start, step)
            grad = g_ref[rows, cols]
            inner = jnp.sum(jnp.where(mine, grad.astype(f32) * o_ref[rows, cols], 0.0), axis=1, keepdims=True)
            if isinstance(head, int):
                log = log_ref[rows, group * 4 + head : group * 4 + head + 1]
            else:
                log = jnp.sum(jnp.where(lane == head + group * 4, log_ref[rows, :], 0.0), axis=1, keepdims=True)
            scores = contract(q_ref[rows, cols], keys, 1, 1)
            probs = jnp.exp2(scores * (scale * LOG2E) + mask - log)
            grad_scores = (probs * (contract(grad, values, 1, 1) - inner)).astype(bf16)
            ps[rows, :] = probs.astype(bf16)
            dss[rows, :] = grad_scores
            out = contract(grad_scores, keys, 1, 0) * scale
            dq_wide[rows, :] = jnp.where(mine, out, dq_wide[rows, :])

        over_blocks(block, tokens, step)
        dkv[head_rows(head), :] = contract(qt[head_rows(head), :], dss[...], 1, 0) * scale
        dkv[head_rows(head, 128), :] = contract(gt[head_rows(head), :], ps[...], 1, 0)

    over_heads(one_head, 0, 4, unroll)
    dq = dq_wide[...].astype(bf16)
    dq_ref[...] = dq
    bias_ref[...] = col_sum(dq.astype(f32))
    half = keep_ref.shape[0]
    keep_ref[...] = dkv[:, 0:half].T
    send_ref[...] = dkv[:, half:].T
    query_grad[...] = contract(turned(h1_ref[...]), dq, 1, 0)


def total_of(refs):
    total = refs[0][...]
    for ref in refs[1:]:
        total = total + ref[...].astype(f32)
    return total


def split_kernel(count, terms, *refs):
    total = total_of(refs[:terms])
    rows = total.shape[0] // count
    refs[terms][...] = total[:rows]
    for index in range(1, count):
        refs[terms + index][...] = total[index * rows : (index + 1) * rows].astype(bf16)


def split_sum(terms, count, after=()):
    rows = terms[0].shape[0] // count
    tail = terms[0].shape[1:]
    outs = [((rows,) + tail, f32)] + [((rows,) + tail, bf16)] * (count - 1)
    return run("split_sum", functools.partial(split_kernel, count, len(terms)), outs, terms, micros=0.6, after=after)


def split_heads_kernel(count, left_keep, left_got, right_keep, right_got, *outs):
    rows = outs[0].shape[0]
    for index in range(count):
        at = slice(index * rows, (index + 1) * rows)
        left = left_keep[at, :] + left_got[at, :]
        right = right_keep[at, :] + right_got[at, :]
        parts = (left[:, 0:128], right[:, 0:128], left[:, 128:256], right[:, 128:256])
        for place, part in enumerate(parts):
            cols = slice(place * 128, place * 128 + 128)
            outs[index][:, cols] = part if index == 0 else part.astype(bf16)


def pair_total(values):
    while len(values) > 1:
        values = [a + b for a, b in zip(values[::2], values[1::2])]
    return values[0]


def two_parts(value):
    high = value.astype(bf16)
    return high, (value - high.astype(f32)).astype(bf16)


def split_with_vectors_kernel(count, terms, first, *refs):
    vec_terms = 2 if first else 1
    keep_ref, vec_ref = refs[terms + vec_terms], refs[terms + vec_terms + 1]
    sends = refs[terms + vec_terms + 2 :]
    if first:
        total = total_of(refs[:terms])
        vec = refs[terms][...] + refs[terms + 1][...]
    else:
        rows = refs[0].shape[0]
        total = refs[0][...]
        for ref in refs[1:terms]:
            total = total + ref[0:rows, :].astype(f32)
        vec = pair_total([refs[terms][...]] + [vector_part(ref, rows) for ref in refs[1:terms]])
    rows = total.shape[0] // count
    keep_ref[...] = total[:rows]
    high, rest = two_parts(vec)
    vec_ref[...] = high.astype(f32) + rest.astype(f32)
    for index, ref in enumerate(sends, 1):
        ref[0:rows, :] = total[index * rows : (index + 1) * rows].astype(bf16)
        ref[rows : rows + 32, :] = high
        ref[rows + 32 : rows + 64, :] = rest


def vector_part(ref, rows):
    return ref[rows : rows + 32, :].astype(f32) + ref[rows + 32 : rows + 64, :].astype(f32)


def split_with_vectors(terms, vec_terms, count, first, after=()):
    rows = terms[0].shape[0] // count
    width = terms[0].shape[1]
    outs = [((rows, width), f32), ((32, width), f32)] + [((rows + 64, width), bf16)] * (count - 1)
    body = functools.partial(split_with_vectors_kernel, count, len(terms), first)
    return run("split_with_vectors", body, outs, list(terms) + list(vec_terms), micros=0.6, after=after)


def row_parts():
    return [("row", stride, size) for stride, size in rel_digits()[1:]]


def one_by_one(groups):
    return [(axis, stride << bit, 2) for axis, stride, size in groups for bit in reversed(range(size.bit_length() - 1))]


def side_by_side(x, groups):
    for axis, stride, size in groups:
        x = jnp.concatenate([x] + [swap(x, axis, j * stride) for j in range(1, size)], axis=0)
    return x


def keys_back_kernel(
    terms, *refs
):
    (kn_ref, c_ref, vec_ref, keyval_ref, blocks_ref, turned_ref, narrow_ref, pair_ref, wide_ref, query, out,
     keep_ref, send_ref, dc_ref, sums_ref, reduce, keyval) = refs[terms:]
    dkv = total_of(refs[:terms])
    high, rest = two_parts(dkv)
    dkn = contract(high, keyval_ref[...], 1, 1) + contract(rest, keyval_ref[...], 1, 1)
    unit, inverse = norm_parts(c_ref[...])
    back, gain_sum, bias_sum = norm_back(dkn, unit, inverse, vec_ref[14:15, :])
    dc = back.astype(bf16)
    dc_ref[...] = dc
    knt = turned(kn_ref[...])
    keyval[...] = rotate(turned_ref[1], contract(knt, high, 1, 0) + contract(knt, rest, 1, 0), pair_ref[...])
    reduce[...] = rotate_turned(contract(turned(dc), blocks_ref[...], 1, 0), wide_ref[2], narrow_ref[7])
    share_out(keep_ref, send_ref, layout(256, LATE)[0], (reduce, keyval, query, out))
    sums_ref[0:1, :] = col_sum(dc.astype(f32))
    sums_ref[1:2, :] = gain_sum
    sums_ref[2:3, :] = bias_sum
    sums_ref[3:4, :] = col_sum(dkv[:, 256:512])


def cells_back_kernel(
    tile_rows, cols, size_ref, dq_left, dq_right, dc_ref, query_ref, reduce_ref, x0_ref, dx1_ref, vec_ref, tile_ref, up_ref, down_ref,
    feed_sums, key_sums, left_sum, right_sum, dx0_ref, head_ref, tail_ref, sums_ref, frame,
):
    tokens = x0_ref.shape[0]
    dh1 = contract(dq_left[...], query_ref[:, 0:128], 1, 1) + contract(dq_right[...], query_ref[:, 128:256], 1, 1)
    for corner in range(4):
        pick = picked_cells((tokens, dc_ref.shape[0]), 0, size_ref, corner, tile_rows, cols)
        placed = contract(pick, dc_ref[...], 1, 0).astype(bf16)
        dh1 = dh1 + contract(placed, reduce_ref[corner * 256 : corner * 256 + 256, :], 1, 1)
    unit, inverse = norm_parts(x0_ref[...])
    back, gain_sum, bias_sum = norm_back(dh1, unit, inverse, vec_ref[10:11, :])
    dx0 = dx1_ref[...] + back
    dx0_ref[...] = dx0
    head_ref[...] = dx0[0:64].astype(bf16)
    tail_ref[...] = dx0[tokens - 64 :].astype(bf16)
    sums_ref[0:25, :] = feed_sums[...]
    sums_ref[25:32, :] = jnp.zeros((7, 256), f32)
    moved = shifted_frame(frame, tile_ref, up_ref, down_ref)
    grid = dx0.reshape(tile_rows, cols, 256)
    for tap in range(9):
        product = moved[tap % 3][tap // 3 : tap // 3 + tile_rows] * grid
        sums_ref[tap : tap + 1, :] = col_sum(product.reshape(tokens, 256))
    sums_ref[9:10, :] = col_sum(dx0)
    sums_ref[10:11, :] = gain_sum
    sums_ref[11:12, :] = bias_sum
    sums_ref[12:13, 0:128] = left_sum[...]
    sums_ref[12:13, 128:256] = right_sum[...]
    sums_ref[13:17, :] = key_sums[...]


def input_grad_kernel(tile_rows, dx0_ref, up_ref, down_ref, vec_ref, out_ref, frame):
    moved = shifted_frame(frame, dx0_ref, up_ref, down_ref)
    total = moved[1][1:-1]
    for tap in range(9):
        down, right = 2 - tap // 3, 2 - tap % 3
        total = total + vec_ref[tap : tap + 1, :] * moved[right][down : down + tile_rows]
    out_ref[...] = total.reshape(out_ref.shape)


def moments_of(total, first, second, moment_ref, square_ref):
    moment = BETA * first + (1.0 - BETA) * total
    square = BETA * second + (1.0 - BETA) * total * total
    moment_ref[...] = moment
    square_ref[...] = square
    return moment * (1.0 / CORRECTION) / (jnp.sqrt(square * (1.0 / CORRECTION)) + ADAM_EPS)


def adam_kernel(base, terms, *refs):
    first_ref, second_ref, moment_ref, square_ref, step_ref = refs[terms:]
    total = total_of(refs[:terms])
    at = slice(base, base + total.shape[0])
    step_ref[...] = moments_of(total, first_ref[at, :], second_ref[at, :], moment_ref, square_ref).astype(bf16)


def late_adam_kernel(terms, *refs):
    (own_vec, first_ref, second_ref, vec_ref, vec_first, vec_second, vec_ema,
     moment_ref, square_ref, step_ref, vec_out, vec_first_out, vec_second_out, vec_ema_out) = refs[terms:]
    rows = refs[0].shape[0]
    total = refs[0][...]
    for ref in refs[1:terms]:
        total = total + ref[0:rows, :].astype(f32)
    step_ref[...] = moments_of(total, first_ref[0:rows, :], second_ref[0:rows, :], moment_ref, square_ref).astype(bf16)
    vec = pair_total([own_vec[...]] + [vector_part(ref, rows) for ref in refs[1:terms]])
    vec = vec[0 : vec_ref.shape[0]]
    new = vec_ref[...] - VECTOR_RATE * moments_of(vec, vec_first[...], vec_second[...], vec_first_out, vec_second_out)
    vec_out[...] = new
    vec_ema_out[...] = EMA_KEEP * vec_ema[...] + (1.0 - EMA_KEEP) * new


def step_sides(group, width, refs, own_narrow, own_wide, second):
    lefts = {0: (own_narrow, 0), 1: (own_narrow, 1), 2: (own_narrow, 2), 3: (own_narrow, 3), 4: (own_wide, 0), 5: (own_wide, 1)}
    found = []
    values = refs[...].astype(f32)
    for j, first, rows, blocks in layout(width, group)[0]:
        left_ref, index = lefts[j]
        half = left_ref.shape[2] // 2
        left = left_ref[index][:, half * second : half * (second + 1)].astype(bf16)
        sides = []
        for col in range(blocks):
            part = values[:, first + col * rows : first + (col + 1) * rows, :]
            sides.append(contract(left, part.reshape(half, width).astype(bf16), 1, 0))
        found.append(sides[0] if blocks == 1 else jnp.concatenate(sides, axis=1))
    return found


def right_of(j, narrow_ref, pair_ref, wide_ref):
    return {0: narrow_ref.at[1], 1: pair_ref, 2: narrow_ref.at[4], 3: wide_ref.at[0], 4: narrow_ref.at[6], 5: narrow_ref.at[7]}[j][...]


def update_rows(group, width, base, sides, rights, weights_ref, chunk):
    for (j, first, rows, blocks), side in zip(layout(width, group)[0], sides):
        full = contract(side.astype(bf16), right_of(j, *rights), 1, 1)
        for col in range(blocks):
            start = first + col * rows
            old = weights_ref[base + start : base + start + rows, :]
            piece = full[0:rows, col * width : (col + 1) * width]
            chunk[start : start + rows, :] = old - MATRIX_RATES[j] * (piece + WEIGHT_DECAY * old)


def early_finish_kernel(
    width, late_near, early_near, early_far, own_narrow, own_wide, narrow_ref, pair_ref, wide_ref,
    weights_ref, late_first, late_second, early_first, early_second,
    new_ref, first_out, second_out, *late_sides,
):
    near = step_sides(EARLY, width, early_near, own_narrow, own_wide, 0)
    far = step_sides(EARLY, width, early_far, own_narrow, own_wide, 1)
    sides = [a + b for a, b in zip(near, far)]
    base = layout(width, LATE)[1]
    update_rows(EARLY, width, base, sides, (narrow_ref, pair_ref, wide_ref), weights_ref, new_ref)
    for late, early, out in ((late_first, early_first, first_out), (late_second, early_second, second_out)):
        from_chunk(late, 0, LATE, out, width)
        from_chunk(early, 0, EARLY, out, width)
    for ref, side in zip(late_sides, step_sides(LATE, width, late_near, own_narrow, own_wide, 0)):
        ref[...] = side


def finish_kernel(
    width, late_far, reduce_side, keyval_side, query_side, out_side, early_new, own_narrow, own_wide, narrow_ref, pair_ref, wide_ref,
    weights_ref, ema_ref, weights_out, ema_out, chunk,
):
    far = step_sides(LATE, width, late_far, own_narrow, own_wide, 1)
    near = (reduce_side, keyval_side, query_side, out_side)
    sides = [a[...] + b for a, b in zip(near, far)]
    split = layout(width, LATE)[1]
    update_rows(LATE, width, 0, sides, (narrow_ref, pair_ref, wide_ref), weights_ref, chunk)
    chunk[split:, :] = early_new[...]
    from_chunk(chunk, 0, LATE, weights_out, width)
    from_chunk(chunk, split, EARLY, weights_out, width)
    chunk[...] = EMA_KEEP * ema_ref[...] + (1.0 - EMA_KEEP) * chunk[...]
    from_chunk(chunk, 0, LATE, ema_out, width)
    from_chunk(chunk, split, EARLY, ema_out, width)


def on_device(
    patches,
    cotangent,
    image_sizes,
    weights,
    first_moment,
    second_moment,
    weight_ema,
    vectors,
    vec_first,
    vec_second,
    vec_ema,
    basis_narrow,
    basis_pair,
    basis_wide,
):
    _, rows, cols, width = patches.shape
    tokens = rows * cols
    shards = device_count()
    tile = patches.reshape(tokens, width)
    dy = cotangent.reshape(tokens, width)
    per = weights.shape[1]
    late_rows, early_rows = layout(width, LATE)[1], layout(width, EARLY)[1]
    chunk = late_rows + early_rows
    ranks = lax.axis_size("row")
    own_keys = tokens // 4
    keys = own_keys * ranks
    frame = ((rows + 2, cols + 16, width), f32)
    img_part = ("img", 1, lax.axis_size("img"))
    xy_parts = row_parts()

    def border(head, tail):
        up = lax.ppermute(tail, "row", [(i, i + 1) for i in range(ranks - 1)])
        return up, lax.ppermute(head, "row", [(i + 1, i) for i in range(ranks - 1)])

    gather_groups = xy_parts[::-1]
    lines = lax.axis_size("img")

    (packed,) = run(
        "pack",
        functools.partial(pack_kernel, width),
        [((chunk, width), bf16)],
        [weights],
        scratch=[((chunk, width), f32)],
    )
    up_halo, down_halo = border(tile[:64], tile[tokens - 64 :])
    slices = [packed] + [swap(packed, "img", j) for j in range(1, lines)]
    old_chunk, ema_chunk, first_chunk, second_chunk = run(
        "moments",
        functools.partial(moments_kernel, width),
        [((chunk, width), f32)] * 4,
        [weights, weight_ema, first_moment, second_moment],
        after=[packed],
    )
    narrow, narrow_turned, pair, own_narrow = run(
        "small_bases",
        small_bases_kernel,
        [((8, width, width), bf16), ((4, width, width), bf16), ((2 * width, 2 * width), bf16), ((4, 16, width), f32)],
        [basis_narrow, basis_pair],
        scratch=[((2 * width, 128), f32)],
        micros=1.5,
        after=[packed],
    )
    x0, h1, mask, vec = run(
        "front",
        functools.partial(front_kernel, rows, cols),
        [((tokens, width), f32), ((tokens, width), bf16), ((1, keys), f32), (vectors.shape, f32)],
        [image_sizes, tile, up_halo, down_halo, vectors],
        scratch=[frame],
        scalars=(0,),
        micros=1.3,
    )
    late_line, early_line = run(
        "stack",
        functools.partial(stack_kernel, late_rows),
        [((lines, late_rows, width), bf16), ((lines, early_rows, width), bf16)],
        slices,
        micros=0.4,
        after=[own_narrow, ema_chunk, vec],
    )
    late_near = side_by_side(late_line, gather_groups)
    late_far = swap(late_near, "row", 1)
    early_near = side_by_side(early_line, one_by_one(xy_parts)[::-1])
    early_far = swap(early_near, "row", 1)
    wide, own_wide = run(
        "wide_bases",
        wide_bases_kernel,
        [((3, FF, FF), bf16), ((2, max(16, FF // shards), FF), f32)],
        [basis_wide],
        scratch=[((2 * FF, 128), f32), ((4, width, FF), f32)],
        micros=5.0,
        mib=8,
        raw=(0,),
        sems=4,
        after=[late_line],
    )
    w_reduce, w_keyval, w_query, w_out, blocks, c, kn, own_kv = run(
        "keys",
        functools.partial(keys_kernel, rows, cols),
        [
            ((4 * width, width), bf16),
            ((width, 2 * width), bf16),
            ((width, width), bf16),
            ((width, width), bf16),
            ((own_keys, 4 * width), bf16),
            ((own_keys, width), f32),
            ((own_keys, width), bf16),
            ((own_keys, 2 * width), bf16),
        ],
        [image_sizes, h1, vec, late_near, late_far],
        scratch=[((4 * width, width), f32), ((width, 2 * width), f32), ((width, width), f32), ((width, width), f32)],
        scalars=(0,),
        micros=1.5,
        after=[own_wide],
    )
    kv_near = side_by_side(own_kv, gather_groups)
    kv_far = swap(kv_near, "row", 1)

    unroll = keys <= 1024
    step = tokens if unroll else 32
    q, k, v, o, log = run(
        "attend",
        functools.partial(attend_kernel, step, unroll),
        [((tokens, width), bf16), ((keys, width), bf16), ((keys, width), bf16), ((tokens, width), f32), ((tokens, 128), f32)],
        [h1, w_query, vec, kv_near, kv_far, mask],
        mib=8 if unroll else 44,
        micros=8.0,
    )
    y, do, dx1, up_grad, down_grad, out_grad, feed_sums = run(
        "feed",
        feed_kernel,
        [
            ((tokens, width), bf16),
            ((tokens, width), bf16),
            ((tokens, width), f32),
            ((width, FF), f32),
            ((width, FF), f32),
            ((width, width), f32),
            (vectors.shape, f32),
        ],
        [o, x0, w_out, early_near, early_far, vec, dy],
        scratch=[((width, FF), bf16), ((FF, width), bf16), ((width, FF), f32), ((FF, width), f32)],
        mib=12,
        micros=3.5,
    )
    half = (shards // 2, early_rows, width)
    early_keep, early_send = run(
        "early_turn",
        early_turn_kernel,
        [(half, f32), (half, f32)],
        [up_grad, down_grad, narrow_turned, narrow, wide],
        scratch=[((width, FF), f32), ((FF, width), f32)],
        mib=10,
        micros=2.0,
    )

    def back(group, after):
        return run(
            "attend_back",
            functools.partial(attend_back_kernel, step, unroll, group),
            [
                ((tokens, 128), bf16),
                ((keys // 2, width), f32),
                ((keys // 2, width), f32),
                ((width, 128), f32),
                ((1, 128), f32),
            ],
            [q, k, v, mask, o, log, do, h1],
            scratch=[
                ((tokens, 128), f32),
                ((width, keys), f32),
                ((tokens, keys), bf16),
                ((tokens, keys), bf16),
                ((128, tokens), bf16),
                ((128, tokens), bf16),
            ],
            mib=14 if unroll else 60,
            micros=5.0,
            after=after,
        )

    pairs = one_by_one(xy_parts + [img_part])
    dq_left, left_keep, left_send, query_left, left_sum = back(0, [early_keep])
    early_terms = [early_keep, swap(early_send, "row", 1)]
    early_keep, early_send = split_sum(early_terms, 2, after=[query_left])
    early_terms = [early_keep, swap(early_send, *pairs[0][:2])]
    left_got = swap(left_send, "row", 1)
    dq_right, right_keep, right_send, query_right, right_sum = back(1, [early_keep])
    right_got = swap(right_send, "row", 1)
    dkv_keep, *dkv_sends = run(
        "split_heads",
        functools.partial(split_heads_kernel, xy_parts[0][2]),
        [((keys // 2 // xy_parts[0][2], 2 * width), f32)]
        + [((keys // 2 // xy_parts[0][2], 2 * width), bf16)] * (xy_parts[0][2] - 1),
        [left_keep, left_got, right_keep, right_got],
        micros=0.8,
    )
    axis, stride, size = xy_parts[0]
    dkv_terms = [dkv_keep] + [swap(x, axis, j * stride) for j, x in enumerate(dkv_sends, 1)]
    for axis, stride, size in xy_parts[1:]:
        keep, *sends = split_sum(dkv_terms, size)
        dkv_terms = [keep] + [swap(x, axis, j * stride) for j, x in enumerate(sends, 1)]
    query_turn, out_turn = run(
        "middle_turn",
        middle_turn_kernel,
        [((width, width), f32), ((width, width), f32)],
        [query_left, query_right, out_grad, narrow_turned, narrow],
        micros=0.7,
    )
    early_keep, early_send = split_sum(early_terms, 2, after=[query_turn])
    early_terms = [early_keep, swap(early_send, *pairs[1][:2])]
    half = (shards // 2, late_rows, width)
    late_keep, late_send, dc, key_sums = run(
        "keys_back",
        functools.partial(keys_back_kernel, len(dkv_terms)),
        [(half, f32), (half, f32), ((own_keys, width), bf16), ((4, width), f32)],
        list(dkv_terms) + [kn, c, vec, w_keyval, blocks, narrow_turned, narrow, pair, wide, query_turn, out_turn],
        scratch=[((4 * width, width), f32), ((width, 2 * width), f32)],
        micros=2.0,
        after=[early_keep],
    )
    late_got = swap(late_send, "row", 1)
    dx0, head, tail, vec_grads = run(
        "cells_back",
        functools.partial(cells_back_kernel, rows, cols),
        [((tokens, width), f32), ((64, width), bf16), ((64, width), bf16), ((32, width), f32)],
        [
            image_sizes, dq_left, dq_right, dc, w_query, w_reduce, x0, dx1, vec, tile, up_halo, down_halo,
            feed_sums, key_sums, left_sum, right_sum,
        ],
        scratch=[frame],
        scalars=(0,),
        micros=2.0,
    )
    vec_terms = [vec_grads, swap(vec_grads, "row", 1)]
    grad_up, grad_down = border(head, tail)
    late_terms = [late_keep.reshape(-1, width), late_got.reshape(-1, width)]
    waits = [[early_keep], [grad_up, grad_down]]
    for index, (axis, stride, size) in enumerate(xy_parts + [img_part]):
        if index + 2 < len(pairs):
            early_keep, early_send = split_sum(early_terms, 2, after=[dc] if index == 0 else [late_keep])
            early_terms = [early_keep, swap(early_send, *pairs[index + 2][:2])]
            waits[0] = [early_keep]
        late_keep, own_vec, *sends = split_with_vectors(
            late_terms, vec_terms, size, index == 0, waits[0] if index == 0 else waits[0] + waits[1]
        )
        late_terms = [late_keep] + [swap(x, axis, j * stride) for j, x in enumerate(sends, 1)]
        vec_terms = [own_vec]
    for axis, stride, _ in pairs[2 + len(xy_parts) + 1 :]:
        early_keep, early_send = split_sum(early_terms, 2)
        early_terms = [early_keep, swap(early_send, axis, stride)]
    early_first, early_second, early_step = run(
        "adam",
        functools.partial(adam_kernel, late_rows, 2),
        [((early_rows, width), f32), ((early_rows, width), f32), ((early_rows, width), bf16)],
        [t.reshape(early_rows, width) for t in early_terms] + [first_chunk, second_chunk],
        micros=0.6,
    )
    steps_line = side_by_side(early_step[None], one_by_one([img_part])[::-1])
    (grad_input,) = run(
        "input_grad",
        functools.partial(input_grad_kernel, rows),
        [((tokens, width), f32)],
        [dx0, grad_up, grad_down, vec],
        scratch=[frame],
        micros=1.5,
        after=[late_keep],
    )
    late_first, late_second, late_step, new_vectors, vec_moment, vec_square, new_vec_ema = run(
        "late_adam",
        functools.partial(late_adam_kernel, len(late_terms)),
        [((late_rows, width), f32), ((late_rows, width), f32), ((late_rows, width), bf16)] + [(vectors.shape, f32)] * 4,
        late_terms + [own_vec, first_chunk, second_chunk, vec, vec_first, vec_second, vec_ema],
        micros=0.8,
        after=[early_step, grad_input],
    )
    step_near = side_by_side(late_step[None], [img_part] + gather_groups)
    step_far = swap(step_near, "row", 1)
    steps_near = side_by_side(steps_line, one_by_one(xy_parts)[::-1])
    steps_far = swap(steps_near, "row", 1)

    early_new, new_first, new_second, *late_sides = run(
        "early_finish",
        functools.partial(early_finish_kernel, width),
        [((early_rows, width), f32), ((1, per), f32), ((1, per), f32)]
        + [((own_wide.shape[1], width), f32)]
        + [((own_narrow.shape[1], cols_of * width), f32) for cols_of in (2, 1, 1)],
        [
            step_near, steps_near, steps_far, own_narrow, own_wide, narrow, pair, wide,
            old_chunk, late_first, late_second, early_first, early_second,
        ],
        micros=2.0,
    )
    new_weights, new_ema = run(
        "finish",
        functools.partial(finish_kernel, width),
        [((1, per), f32)] * 2,
        [step_far, *late_sides, early_new, own_narrow, own_wide, narrow, pair, wide, old_chunk, ema_chunk],
        scratch=[((chunk, width), f32)],
        micros=1.5,
        after=[new_first],
    )
    return (
        y.reshape(patches.shape),
        grad_input.reshape(patches.shape),
        new_weights,
        new_first,
        new_second,
        new_ema,
        new_vectors,
        vec_moment,
        vec_square,
        new_vec_ema,
    )


def solution(mesh):
    tiles = P("img", "row", None, None)
    packed = P(("img", "row"), None)
    return jax.shard_map(
        on_device,
        mesh=mesh,
        in_specs=(tiles, tiles, P("img", None)) + (packed,) * 4 + (P(),) * 7,
        out_specs=(tiles, tiles) + (packed,) * 4 + (P(),) * 4,
        check_vma=False,
    )
```

time: 205 us -> 167 us (0.81)
  between operations: 14.8 us -> 1.21 us
  starting transfers between devices: 64.7 us -> 56.2 us
  Pallas kernels: 45.1 us -> 39 us
  waiting for transfers between devices: 56.7 us -> 52.3 us
  local copies, waits for them, and re-layouts: 20.6 us -> 17.2 us
    ppermute x50 -> x44, starting transfers between devices: 58.4 us -> 48.8 us  [swap(): return lax.ppermute(x, axis, [(i, i ^ step) for i in range(count)])]
    pallas_call x23 -> x27, Pallas kernels: 45.1 us -> 39 us  [run(): pl.pallas_call(without, out_shape=tuple((jax.ShapeDtypeStruct(shape, dtyp...]
    all_gather x1 -> x0, waiting for transfers between devices: 4.22 us -> none  [on_device(): early_all = lax.all_gather(early, ('img', 'row'), axis=0, tiled=False)]
    unnamed x107 -> x56, local copies, waits for them, and re-layouts: 18.2 us -> 16.3 us
    ppermute x50 -> x44, waiting for transfers between devices: 52 us -> 52.3 us  [swap(): return lax.ppermute(x, axis, [(i, i ^ step) for i in range(count)])]
  transfers between devices with their start and end apart: 55 -> 48, of which waited for: 35 -> 21; matrix products, arithmetic and copies ran while one was open for 2% -> 1% of each run, Pallas kernels for 14% -> 18%
where the time goes in v3:
time: 167 us; the launch traced here: 166 us
  starting transfers between devices  56.2 us (34%)
  waiting for transfers between devices  52.3 us (31%)
  Pallas kernels  39 us (23%)
  local copies, waits for them, and re-layouts  17.2 us (10%)
    ppermute x44, waiting for transfers between devices, swap(): return lax.ppermute(x, axis, [(i, i ^ step) for i in range(count)])  52.3 us
    ppermute x44, starting transfers between devices, swap(): return lax.ppermute(x, axis, [(i, i ^ step) for i in range(count)])  48.8 us
    pallas_call x27, Pallas kernels, run(): pl.pallas_call(without, out_shape=tuple((jax.ShapeDtypeStruct(shape, dtyp...  39 us
    unnamed x56, local copies, waits for them, and re-layouts  16.3 us
    ppermute x2, starting transfers between devices, border(): up = lax.ppermute(tail, 'row', [(i, i + 1) for i in range(ranks - 1)])  4.81 us
  transfers between devices with their start and end apart: 48, of which 21 were waited for; matrix products, arithmetic and copies ran while one was open for 1% of the time, Pallas kernels for 18%

profile of v3, /device:TPU:0, one launch (start us, length us, event | category | flops | bytes accessed | tf_op | source)
XLA Modules:
  0.0 166.0 jit_solution(635372407786335197)
XLA Ops:
  1.6 5.1 %collective-permute-start.4 = (bf16[128,256]{1,0:T(8,128)(2,1)S(1)}, bf16[128,256]{1,0:T(8,128)(2,1)S(1)}, u32[]{:S(2)}, u32[]{:S(2)}) collective-permute-start(bf16[128,256]{1,0:T(8,128)(2,1)S(1)} %pack.1.refs_2_.refs_4_.refs_0_), channel_id=1, source_target_pairs={{0,24},{8,16},{16,8},{24,0},{1,25},{9,17},{17,9},{25,1},{2,26},{10... | collective-permute-start | bytes 196616 | tf_op jit(solution)/shard_map/ppermute | solution.py:49
  9.4 3.0 %collective-permute-start = (bf16[64,256]{1,0:T(8,128)(2,1)S(1)}, bf16[64,256]{1,0:T(8,128)(2,1)S(1)}, u32[]{:S(2)}, u32[]{:S(2)}) collective-permute-start(bf16[64,256]{1,0:T(8,128)(2,1)S(1)} %get-tuple-element.209), channel_id=1, source_target_pairs={{0,1},{1,2},{2,3},{3,4},{4,5},{5,6},{6,7},{8,9},{9,10},{10,11},{11... | collective-permute-start | bytes 98312 | tf_op jit(solution)/shard_map/ppermute | solution.py:845
  30.0 5.8 %collective-permute-done.6 = bf16[4,64,256]{2,1,0:T(8,128)(2,1)S(1)} collective-permute-done((bf16[4,64,256]{2,1,0:T(8,128)(2,1)S(1)}, bf16[4,64,256]{2,1,0:T(8,128)(2,1)S(1)}, u32[]{:S(2)}, u32[]{:S(2)}) %collective-permute-start.6) | collective-permute-done | bytes 131104 | tf_op jit(solution)/shard_map/ppermute | solution.py:49
  37.6 4.6 %copy-done = f32[3,1024,1024]{2,1,0:T(8,128)S(1)} copy-done((f32[3,1024,1024]{2,1,0:T(8,128)S(1)}, f32[3,1024,1024]{2,1,0:T(8,128)}, u32[]{:S(2)}) %copy-start) | copy-done | bytes 12582936
  42.1 2.8 %wide_bases.1 = (bf16[3,1024,1024]{2,1,0:T(8,128)(2,1)S(1)}, f32[2,32,1024]{2,1,0:T(8,128)S(1)}) custom-call(f32[3,1024,1024]{2,1,0:T(8,128)S(1)} %copy-done, bf16[4,64,256]{2,1,0:T(8,128)(2,1)S(1)} %get-tuple-element.113.refs_1_), custom_call_target="tpu_custom_call" | custom-call | bytes 18000000 | tf_op jit(solution)/shard_map/wide_bases/pallas_call | solution.py:91
  50.1 4.8 %collective-permute-done.9 = bf16[112,512]{1,0:T(8,128)(2,1)S(1)} collective-permute-done((bf16[112,512]{1,0:T(8,128)(2,1)S(1)}, bf16[112,512]{1,0:T(8,128)(2,1)S(1)}, u32[]{:S(2)}, u32[]{:S(2)}) %collective-permute-start.9) | collective-permute-done | bytes 114720 | tf_op jit(solution)/shard_map/ppermute | solution.py:49
  57.4 7.4 %attend.1 = (bf16[448,256]{1,0:T(8,128)(2,1)S(1)}, bf16[896,256]{1,0:T(8,128)(2,1)S(1)}, bf16[896,256]{1,0:T(8,128)(2,1)S(1)}, f32[448,256]{1,0:T(8,128)S(1)}, f32[448,128]{1,0:T(8,128)S(1)}) custom-call(bf16[448,256]{1,0:T(8,128)(2,1)S(1)} %get-tuple-element.109.refs_1_.refs_0_.refs_7_, bf16[256,256]{1,0:T(8,128)(2,1)S(1)} %get-tuple-element.115.refs_1_.refs_4_, ...), custom_call_target="tpu_custom_call" | custom-call | bytes 28800000 | tf_op jit(solution)/shard_map/attend/pallas_call | solution.py:91
  64.9 3.3 %feed.1 = (bf16[448,256]{1,0:T(8,128)(2,1)}, bf16[448,256]{1,0:T(8,128)(2,1)S(1)}, f32[448,256]{1,0:T(8,128)S(1)}, f32[256,1024]{1,0:T(8,128)S(1)}, f32[256,1024...) custom-call(f32[448,256]{1,0:T(8,128)S(1)} %get-tuple-element.118.refs_0_.refs_4_, ...), custom_call_target="tpu_custom_call" | custom-call | bytes 12600000 | tf_op jit(solution)/shard_map/feed/pallas_call | solution.py:91
  70.3 4.5 %attend_back.2 = (bf16[448,128]{1,0:T(8,128)(2,1)S(1)}, f32[448,256]{1,0:T(8,128)S(1)}, f32[448,256]{1,0:T(8,128)S(1)}, f32[256,128]{1,0:T(8,128)S(1)}, f32[1,128]{1,0:T(1,128)S(1)}) custom-call(bf16[448,256]{1,0:T(8,128)(2,1)S(1)} %get-tuple-element.123.refs_0_, bf16[896,256]{1,0:T(8,128)(2,1)S(1)} %get-tuple-element.124.refs_1_, ...), custom_call_target="tpu_custom_call" | custom-call | bytes 18000000 | tf_op jit(solution)/shard_map/attend_back/pallas_call | solution.py:91
  75.4 4.5 %attend_back.3 = (bf16[448,128]{1,0:T(8,128)(2,1)S(1)}, f32[448,256]{1,0:T(8,128)S(1)}, f32[448,256]{1,0:T(8,128)S(1)}, f32[256,128]{1,0:T(8,128)S(1)}, f32[1,128]{1,0:T(1,128)S(1)}) custom-call(bf16[448,256]{1,0:T(8,128)(2,1)S(1)} %get-tuple-element.123.refs_0_, bf16[896,256]{1,0:T(8,128)(2,1)S(1)} %get-tuple-element.124.refs_1_, ...), custom_call_target="tpu_custom_call" | custom-call | bytes 18000000 | tf_op jit(solution)/shard_map/attend_back/pallas_call | solution.py:91
  86.0 5.8 %collective-permute-done.22.refs_1_ = bf16[8,64,256]{2,1,0:T(8,128)(2,1)S(1)} collective-permute-done((bf16[8,64,256]{2,1,0:T(8,128)(2,1)S(1)}, bf16[8,64,256]{2,1,0:T(8,128)(2,1)S(1)}, u32[]{:S(2)}, u32[]{:S(2)}) %collective-permute-start.22) | collective-permute-done | bytes 262176 | tf_op jit(solution)/shard_map/ppermute | solution.py:49
  93.7 2.1 %keys_back.1 = (f32[16,64,256]{2,1,0:T(8,128)S(1)}, f32[16,64,256]{2,1,0:T(8,128)S(1)}, bf16[112,256]{1,0:T(8,128)(2,1)S(1)}, f32[4,256]{1,0:T(4,128)S(1)}) custom-call(f32[112,512]{1,0:T(8,128)S(1)} %get-tuple-element.143.refs_0_, bf16[112,512]{1,0:T(8,128)(2,1)S(1)} %collective-permute-done.19.refs_1_, ...), custom_call_target="tpu_custom_call" | custom-call | bytes 7200000 | tf_op jit(solution)/shard_map/keys_back/pallas_call | solution.py:91
  96.7 5.2 %collective-permute-done.27.refs_1_ = bf16[4,64,256]{2,1,0:T(8,128)(2,1)S(1)} collective-permute-done((bf16[4,64,256]{2,1,0:T(8,128)(2,1)S(1)}, bf16[4,64,256]{2,1,0:T(8,128)(2,1)S(1)}, u32[]{:S(2)}, u32[]{:S(2)}) %collective-permute-start.27) | collective-permute-done | bytes 131104 | tf_op jit(solution)/shard_map/ppermute | solution.py:49
  101.9 2.2 %collective-permute-start.31 = (bf16[2,64,256]{2,1,0:T(8,128)(2,1)S(1)}, bf16[2,64,256]{2,1,0:T(8,128)(2,1)S(1)}, u32[]{:S(2)}, u32[]{:S(2)}) collective-permute-start(bf16[2,64,256]{2,1,0:T(8,128)(2,1)S(1)} %get-tuple-element.178), channel_id=1, source_target_pairs={{0,16},{8,24},{16,0},{24,8},{1,17},{9,25},{17,1},{25,9},{2,18},{10... | collective-permute-start | bytes 196616 | tf_op jit(solution)/shard_map/ppermute | solution.py:49
  104.1 2.2 %cells_back.1 = (f32[448,256]{1,0:T(8,128)S(1)}, bf16[64,256]{1,0:T(8,128)(2,1)S(1)}, bf16[64,256]{1,0:T(8,128)(2,1)S(1)}, f32[32,256]{1,0:T(8,128)S(1)}) custom-call(s32[1,2]{1,0:T(1,128)S(1)} %copy-done.18, bf16[448,128]{1,0:T(8,128)(2,1)S(1)} %get-tuple-element.134.refs_1_, bf16[448,128]{1,0:T(8,128)(2,1)S(1)} %get-tuple-element.138.refs_2_, ...), custom_call_target="tpu_custom_call" | custom-call | bytes 7200000 | tf_op jit(solution)/shard_map/cells_back/pallas_call | solution.py:91
  115.7 3.6 %collective-permute-done.43 = bf16[1,64,256]{2,1,0:T(8,128)(2,1)S(1)} collective-permute-done((bf16[1,64,256]{2,1,0:T(8,128)(2,1)S(1)}, bf16[1,64,256]{2,1,0:T(8,128)(2,1)S(1)}, u32[]{:S(2)}, u32[]{:S(2)}) %collective-permute-start.43) | collective-permute-done | bytes 32800 | tf_op jit(solution)/shard_map/ppermute | solution.py:49
  120.6 4.4 %collective-permute-done.44 = bf16[2,64,256]{2,1,0:T(8,128)(2,1)S(1)} collective-permute-done((bf16[2,64,256]{2,1,0:T(8,128)(2,1)S(1)}, bf16[2,64,256]{2,1,0:T(8,128)(2,1)S(1)}, u32[]{:S(2)}, u32[]{:S(2)}) %collective-permute-start.44) | collective-permute-done | bytes 65568 | tf_op jit(solution)/shard_map/ppermute | solution.py:49
  126.3 2.2 %collective-permute-start.45 = (bf16[4,64,256]{2,1,0:T(8,128)(2,1)S(1)}, bf16[4,64,256]{2,1,0:T(8,128)(2,1)S(1)}, u32[]{:S(2)}, u32[]{:S(2)}) collective-permute-start(bf16[4,64,256]{2,1,0:T(8,128)(2,1)S(1)} %pad_maximum_fusion.3), channel_id=1, source_target_pairs={{0,2},{1,3},{2,0},{3,1},{4,6},{5,7},{6,4},{7,5},{8,10},{9,11},{10,... | collective-permute-start | bytes 393224 | tf_op jit(solution)/shard_map/ppermute | solution.py:49
  128.7 2.0 %collective-permute-start.33 = (bf16[128,256]{1,0:T(8,128)(2,1)S(1)}, bf16[128,256]{1,0:T(8,128)(2,1)S(1)}, u32[]{:S(2)}, u32[]{:S(2)}) collective-permute-start(bf16[128,256]{1,0:T(8,128)(2,1)S(1)} %get-tuple-element.182), channel_id=1, source_target_pairs={{0,16},{8,24},{16,0},{24,8},{1,17},{9,25},{17,1},{25,9},{2,18},{10... | collective-permute-start | bytes 196616 | tf_op jit(solution)/shard_map/ppermute | solution.py:49
  130.7 2.4 %collective-permute-start.34 = (bf16[128,256]{1,0:T(8,128)(2,1)S(1)}, bf16[128,256]{1,0:T(8,128)(2,1)S(1)}, u32[]{:S(2)}, u32[]{:S(2)}) collective-permute-start(bf16[128,256]{1,0:T(8,128)(2,1)S(1)} %get-tuple-element.183), channel_id=1, source_target_pairs={{0,24},{8,16},{16,8},{24,0},{1,25},{9,17},{17,9},{25,1},{2,26},{10... | collective-permute-start | bytes 196616 | tf_op jit(solution)/shard_map/ppermute | solution.py:49
  134.7 2.8 %collective-permute-done.34.refs_3_ = bf16[128,256]{1,0:T(8,128)(2,1)S(1)} collective-permute-done((bf16[128,256]{1,0:T(8,128)(2,1)S(1)}, bf16[128,256]{1,0:T(8,128)(2,1)S(1)}, u32[]{:S(2)}, u32[]{:S(2)}) %collective-permute-start.34) | collective-permute-done | bytes 65568 | tf_op jit(solution)/shard_map/ppermute | solution.py:49
  139.2 2.2 %collective-permute-start.38 = (bf16[1,64,256]{2,1,0:T(8,128)(2,1)S(1)}, bf16[1,64,256]{2,1,0:T(8,128)(2,1)S(1)}, u32[]{:S(2)}, u32[]{:S(2)}) collective-permute-start(bf16[1,64,256]{2,1,0:T(8,128)(2,1)S(1)} %bitcast.24), channel_id=1, source_target_pairs={{0,24},{8,16},{16,8},{24,0},{1,25},{9,17},{17,9},{25,1},{2,26},{10... | collective-permute-start | bytes 98312 | tf_op jit(solution)/shard_map/ppermute | solution.py:49
  152.2 3.3 %collective-permute-done.39 = bf16[4,64,256]{2,1,0:T(8,128)(2,1)S(1)} collective-permute-done((bf16[4,64,256]{2,1,0:T(8,128)(2,1)S(1)}, bf16[4,64,256]{2,1,0:T(8,128)(2,1)S(1)}, u32[]{:S(2)}, u32[]{:S(2)}) %collective-permute-start.39) | collective-permute-done | bytes 131104 | tf_op jit(solution)/shard_map/ppermute | solution.py:49
  155.7 4.5 %collective-permute-done.46 = bf16[8,64,256]{2,1,0:T(8,128)(2,1)S(1)} collective-permute-done((bf16[8,64,256]{2,1,0:T(8,128)(2,1)S(1)}, bf16[8,64,256]{2,1,0:T(8,128)(2,1)S(1)}, u32[]{:S(2)}, u32[]{:S(2)}) %collective-permute-start.46) | collective-permute-done | bytes 262176 | tf_op jit(solution)/shard_map/ppermute | solution.py:49
  (166 shorter events, 73.8 us)
Async XLA Ops:
  1.6 22.2 %collective-permute-start.4 = (bf16[128,256]{1,0:T(8,128)(2,1)S(1)}, bf16[128,256]{1,0:T(8,128)(2,1)S(1)}, u32[]{:S(2)}, u32[]{:S(2)}) collective-permute-start(bf16[128,256]{1,0:T(8,128)(2,1)S(1)} %pack.1.refs_2_.refs_4_.refs_0_), channel_id=1, source_target_pairs={{0,24},{8,16},{16,8},{24,0},{1,25},{9,17},{17,9},{25,1},{2,26},{10... | collective-permute-start | bytes 196616 | tf_op jit(solution)/shard_map/ppermute | solution.py:49
  6.7 17.0 %collective-permute-start.3 = (bf16[128,256]{1,0:T(8,128)(2,1)S(1)}, bf16[128,256]{1,0:T(8,128)(2,1)S(1)}, u32[]{:S(2)}, u32[]{:S(2)}) collective-permute-start(bf16[128,256]{1,0:T(8,128)(2,1)S(1)} %pack.1.refs_2_.refs_4_.refs_0_), channel_id=1, source_target_pairs={{0,16},{8,24},{16,0},{24,8},{1,17},{9,25},{17,1},{25,9},{2,18},{10... | collective-permute-start | bytes 196616 | tf_op jit(solution)/shard_map/ppermute | solution.py:49
  6.7 17.1 %collective-permute-start.2 = (bf16[128,256]{1,0:T(8,128)(2,1)S(1)}, bf16[128,256]{1,0:T(8,128)(2,1)S(1)}, u32[]{:S(2)}, u32[]{:S(2)}) collective-permute-start(bf16[128,256]{1,0:T(8,128)(2,1)S(1)} %pack.1.refs_2_.refs_4_.refs_0_), channel_id=1, source_target_pairs={{0,8},{8,0},{16,24},{24,16},{1,9},{9,1},{17,25},{25,17},{2,10},{10... | collective-permute-start | bytes 196616 | tf_op jit(solution)/shard_map/ppermute | solution.py:49
  8.2 11.9 %collective-permute-start.1 = (bf16[64,256]{1,0:T(8,128)(2,1)S(1)}, bf16[64,256]{1,0:T(8,128)(2,1)S(1)}, u32[]{:S(2)}, u32[]{:S(2)}) collective-permute-start(bf16[64,256]{1,0:T(8,128)(2,1)S(1)} %get-tuple-element.208), channel_id=1, source_target_pairs={{1,0},{2,1},{3,2},{4,3},{5,4},{6,5},{7,6},{9,8},{10,9},{11,10},{12... | collective-permute-start | bytes 98312 | tf_op jit(solution)/shard_map/ppermute | solution.py:846
  9.4 10.6 %collective-permute-start = (bf16[64,256]{1,0:T(8,128)(2,1)S(1)}, bf16[64,256]{1,0:T(8,128)(2,1)S(1)}, u32[]{:S(2)}, u32[]{:S(2)}) collective-permute-start(bf16[64,256]{1,0:T(8,128)(2,1)S(1)} %get-tuple-element.209), channel_id=1, source_target_pairs={{0,1},{1,2},{2,3},{3,4},{4,5},{5,6},{6,7},{8,9},{9,10},{10,11},{11... | collective-permute-start | bytes 98312 | tf_op jit(solution)/shard_map/ppermute | solution.py:845
  25.5 10.3 %collective-permute-start.7 = (bf16[4,64,256]{2,1,0:T(8,128)(2,1)S(1)}, bf16[4,64,256]{2,1,0:T(8,128)(2,1)S(1)}, u32[]{:S(2)}, u32[]{:S(2)}) collective-permute-start(bf16[4,64,256]{2,1,0:T(8,128)(2,1)S(1)} %get-tuple-element.113.refs_1_), channel_id=1, source_target_pairs={{0,6},{1,7},{2,4},{3,5},{4,2},{5,3},{6,0},{7,1},{8,14},{9,15},{10,... | collective-permute-start | bytes 393224 | tf_op jit(solution)/shard_map/ppermute | solution.py:49
  27.0 8.8 %collective-permute-start.6 = (bf16[4,64,256]{2,1,0:T(8,128)(2,1)S(1)}, bf16[4,64,256]{2,1,0:T(8,128)(2,1)S(1)}, u32[]{:S(2)}, u32[]{:S(2)}) collective-permute-start(bf16[4,64,256]{2,1,0:T(8,128)(2,1)S(1)} %get-tuple-element.113.refs_1_), channel_id=1, source_target_pairs={{0,4},{1,5},{2,6},{3,7},{4,0},{5,1},{6,2},{7,3},{8,12},{9,13},{10,... | collective-permute-start | bytes 393224 | tf_op jit(solution)/shard_map/ppermute | solution.py:49
  27.4 8.5 %collective-permute-start.13 = (bf16[4,64,256]{2,1,0:T(8,128)(2,1)S(1)}, bf16[4,64,256]{2,1,0:T(8,128)(2,1)S(1)}, u32[]{:S(2)}, u32[]{:S(2)}) collective-permute-start(bf16[4,64,256]{2,1,0:T(8,128)(2,1)S(1)} %get-tuple-element.121), channel_id=1, source_target_pairs={{0,2},{1,3},{2,0},{3,1},{4,6},{5,7},{6,4},{7,5},{8,10},{9,11},{10,... | collective-permute-start | bytes 393224 | tf_op jit(solution)/shard_map/ppermute | solution.py:49
  35.8 9.3 %collective-permute-start.8 = (bf16[16,64,256]{2,1,0:T(8,128)(2,1)S(1)}, bf16[16,64,256]{2,1,0:T(8,128)(2,1)S(1)}, u32[]{:S(2)}, u32[]{:S(2)}) collective-permute-start(bf16[16,64,256]{2,1,0:T(8,128)(2,1)S(1)} %constant_dynamic-update-slice_fusion.refs_3_), channel_id=1, source_target_pairs={{0,1},{1,0},{2,3},{3,2},{4,5},{5,4},{6,7},{7,6},{8,9},{9,8},{10,11... | collective-permute-start | bytes 1572872 | tf_op jit(solution)/shard_map/ppermute | solution.py:49
  35.9 9.1 %collective-permute-start.14 = (bf16[8,64,256]{2,1,0:T(8,128)(2,1)S(1)}, bf16[8,64,256]{2,1,0:T(8,128)(2,1)S(1)}, u32[]{:S(2)}, u32[]{:S(2)}) collective-permute-start(bf16[8,64,256]{2,1,0:T(8,128)(2,1)S(1)} %pad_maximum_fusion), channel_id=1, source_target_pairs={{0,4},{1,5},{2,6},{3,7},{4,0},{5,1},{6,2},{7,3},{8,12},{9,13},{10,... | collective-permute-start | bytes 786440 | tf_op jit(solution)/shard_map/ppermute | solution.py:49
  45.0 19.9 %collective-permute-start.15 = (bf16[16,64,256]{2,1,0:T(8,128)(2,1)S(1)}, bf16[16,64,256]{2,1,0:T(8,128)(2,1)S(1)}, u32[]{:S(2)}, u32[]{:S(2)}) collective-permute-start(bf16[16,64,256]{2,1,0:T(8,128)(2,1)S(1)} %constant_dynamic-update-slice_fusion.8.refs_3_), channel_id=1, source_target_pairs={{0,1},{1,0},{2,3},{3,2},{4,5},{5,4},{6,7},{7,6},{8,9},{9,8},{10,11... | collective-permute-start | bytes 1572872 | tf_op jit(solution)/shard_map/ppermute | solution.py:49
  46.6 9.0 %collective-permute-start.11 = (bf16[112,512]{1,0:T(8,128)(2,1)S(1)}, bf16[112,512]{1,0:T(8,128)(2,1)S(1)}, u32[]{:S(2)}, u32[]{:S(2)}) collective-permute-start(bf16[112,512]{1,0:T(8,128)(2,1)S(1)} %get-tuple-element.116), channel_id=1, source_target_pairs={{0,6},{1,7},{2,4},{3,5},{4,2},{5,3},{6,0},{7,1},{8,14},{9,15},{10,... | collective-permute-start | bytes 344072 | tf_op jit(solution)/shard_map/ppermute | solution.py:49
  80.2 11.6 %collective-permute-start.22 = (bf16[8,64,256]{2,1,0:T(8,128)(2,1)S(1)}, bf16[8,64,256]{2,1,0:T(8,128)(2,1)S(1)}, u32[]{:S(2)}, u32[]{:S(2)}) collective-permute-start(bf16[8,64,256]{2,1,0:T(8,128)(2,1)S(1)} %get-tuple-element.156), channel_id=1, source_target_pairs={{0,4},{1,5},{2,6},{3,7},{4,0},{5,1},{6,2},{7,3},{8,12},{9,13},{10,... | collective-permute-start | bytes 786440 | tf_op jit(solution)/shard_map/ppermute | solution.py:49
  82.0 9.8 %collective-permute-start.19 = (bf16[112,512]{1,0:T(8,128)(2,1)S(1)}, bf16[112,512]{1,0:T(8,128)(2,1)S(1)}, u32[]{:S(2)}, u32[]{:S(2)}) collective-permute-start(bf16[112,512]{1,0:T(8,128)(2,1)S(1)} %get-tuple-element.144), channel_id=1, source_target_pairs={{0,2},{1,3},{2,0},{3,1},{4,6},{5,7},{6,4},{7,5},{8,10},{9,11},{10,... | collective-permute-start | bytes 344072 | tf_op jit(solution)/shard_map/ppermute | solution.py:49
  82.7 11.0 %collective-permute-start.20 = (bf16[112,512]{1,0:T(8,128)(2,1)S(1)}, bf16[112,512]{1,0:T(8,128)(2,1)S(1)}, u32[]{:S(2)}, u32[]{:S(2)}) collective-permute-start(bf16[112,512]{1,0:T(8,128)(2,1)S(1)} %get-tuple-element.145), channel_id=1, source_target_pairs={{0,4},{1,5},{2,6},{3,7},{4,0},{5,1},{6,2},{7,3},{8,12},{9,13},{10,... | collective-permute-start | bytes 344072 | tf_op jit(solution)/shard_map/ppermute | solution.py:49
  83.9 9.8 %collective-permute-start.21 = (bf16[112,512]{1,0:T(8,128)(2,1)S(1)}, bf16[112,512]{1,0:T(8,128)(2,1)S(1)}, u32[]{:S(2)}, u32[]{:S(2)}) collective-permute-start(bf16[112,512]{1,0:T(8,128)(2,1)S(1)} %get-tuple-element.146), channel_id=1, source_target_pairs={{0,6},{1,7},{2,4},{3,5},{4,2},{5,3},{6,0},{7,1},{8,14},{9,15},{10,... | collective-permute-start | bytes 344072 | tf_op jit(solution)/shard_map/ppermute | solution.py:49
  95.9 11.8 %collective-permute-start.25 = (f32[16,64,256]{2,1,0:T(8,128)S(1)}, f32[16,64,256]{2,1,0:T(8,128)S(1)}, u32[]{:S(2)}, u32[]{:S(2)}) collective-permute-start(f32[16,64,256]{2,1,0:T(8,128)S(1)} %get-tuple-element.169), channel_id=1, source_target_pairs={{0,1},{1,0},{2,3},{3,2},{4,5},{5,4},{6,7},{7,6},{8,9},{9,8},{10,11... | collective-permute-start | bytes 3145736 | tf_op jit(solution)/shard_map/ppermute | solution.py:49
  109.9 16.4 %collective-permute-start.23 = (bf16[64,256]{1,0:T(8,128)(2,1)S(1)}, bf16[64,256]{1,0:T(8,128)(2,1)S(1)}, u32[]{:S(2)}, u32[]{:S(2)}) collective-permute-start(bf16[64,256]{1,0:T(8,128)(2,1)S(1)} %get-tuple-element.166), channel_id=1, source_target_pairs={{0,1},{1,2},{2,3},{3,4},{4,5},{5,6},{6,7},{8,9},{9,10},{10,11},{11... | collective-permute-start | bytes 98312 | tf_op jit(solution)/shard_map/ppermute | solution.py:845
  111.7 16.8 %collective-permute-start.28 = (bf16[320,256]{1,0:T(8,128)(2,1)S(1)}, bf16[320,256]{1,0:T(8,128)(2,1)S(1)}, u32[]{:S(2)}, u32[]{:S(2)}) collective-permute-start(bf16[320,256]{1,0:T(8,128)(2,1)S(1)} %get-tuple-element.174), channel_id=1, source_target_pairs={{0,2},{1,3},{2,0},{3,1},{4,6},{5,7},{6,4},{7,5},{8,10},{9,11},{10,... | collective-permute-start | bytes 491528 | tf_op jit(solution)/shard_map/ppermute | solution.py:49
  112.7 15.8 %collective-permute-start.29 = (bf16[320,256]{1,0:T(8,128)(2,1)S(1)}, bf16[320,256]{1,0:T(8,128)(2,1)S(1)}, u32[]{:S(2)}, u32[]{:S(2)}) collective-permute-start(bf16[320,256]{1,0:T(8,128)(2,1)S(1)} %get-tuple-element.175), channel_id=1, source_target_pairs={{0,4},{1,5},{2,6},{3,7},{4,0},{5,1},{6,2},{7,3},{8,12},{9,13},{10,... | collective-permute-start | bytes 491528 | tf_op jit(solution)/shard_map/ppermute | solution.py:49
  113.9 14.6 %collective-permute-start.30 = (bf16[320,256]{1,0:T(8,128)(2,1)S(1)}, bf16[320,256]{1,0:T(8,128)(2,1)S(1)}, u32[]{:S(2)}, u32[]{:S(2)}) collective-permute-start(bf16[320,256]{1,0:T(8,128)(2,1)S(1)} %get-tuple-element.176), channel_id=1, source_target_pairs={{0,6},{1,7},{2,4},{3,5},{4,2},{5,3},{6,0},{7,1},{8,14},{9,15},{10,... | collective-permute-start | bytes 491528 | tf_op jit(solution)/shard_map/ppermute | solution.py:49
  126.3 24.0 %collective-permute-start.45 = (bf16[4,64,256]{2,1,0:T(8,128)(2,1)S(1)}, bf16[4,64,256]{2,1,0:T(8,128)(2,1)S(1)}, u32[]{:S(2)}, u32[]{:S(2)}) collective-permute-start(bf16[4,64,256]{2,1,0:T(8,128)(2,1)S(1)} %pad_maximum_fusion.3), channel_id=1, source_target_pairs={{0,2},{1,3},{2,0},{3,1},{4,6},{5,7},{6,4},{7,5},{8,10},{9,11},{10,... | collective-permute-start | bytes 393224 | tf_op jit(solution)/shard_map/ppermute | solution.py:49
  146.7 13.7 %collective-permute-start.41 = (bf16[4,64,256]{2,1,0:T(8,128)(2,1)S(1)}, bf16[4,64,256]{2,1,0:T(8,128)(2,1)S(1)}, u32[]{:S(2)}, u32[]{:S(2)}) collective-permute-start(bf16[4,64,256]{2,1,0:T(8,128)(2,1)S(1)} %pad_maximum_fusion.2), channel_id=1, source_target_pairs={{0,6},{1,7},{2,4},{3,5},{4,2},{5,3},{6,0},{7,1},{8,14},{9,15},{10,... | collective-permute-start | bytes 393224 | tf_op jit(solution)/shard_map/ppermute | solution.py:49
  150.3 10.0 %collective-permute-start.46 = (bf16[8,64,256]{2,1,0:T(8,128)(2,1)S(1)}, bf16[8,64,256]{2,1,0:T(8,128)(2,1)S(1)}, u32[]{:S(2)}, u32[]{:S(2)}) collective-permute-start(bf16[8,64,256]{2,1,0:T(8,128)(2,1)S(1)} %pad_maximum_fusion.1), channel_id=1, source_target_pairs={{0,4},{1,5},{2,6},{3,7},{4,0},{5,1},{6,2},{7,3},{8,12},{9,13},{10,... | collective-permute-start | bytes 786440 | tf_op jit(solution)/shard_map/ppermute | solution.py:49
  (43 other events, 307.0 us)

commit v4 on v3

--- a/solution.py
+++ b/solution.py
@@ -86,7 +86,7 @@
     def without(*refs):
         body(*refs[:count], *refs[count + len(after) :])
 
-    space = {index: pltpu.SMEM for index in scalars} | {index: pl.ANY for index in raw}
+    space = {index: pltpu.SMEM for index in scalars} | {index: pltpu.HBM for index in raw}
     specs = [pl.BlockSpec(memory_space=space.get(index, pltpu.VMEM)) for index in range(count)]
     return pl.pallas_call(
         without,
@@ -190,7 +190,7 @@
     out_ref[...] = chunk[...].astype(bf16)
 
 
-def to_chunk(flat_ref, out_ref, width):
+def to_chunk(flat_ref, out_ref, width, index=0):
     dims, starts, base = matrix_shapes(width, FF), packed_starts(width), 0
     for group in (LATE, EARLY):
         parts, count = layout(width, group)
@@ -199,7 +199,7 @@
                 for row in range(rows):
                     at = starts[j] + row * dims[j][1] + col * width
                     place = base + first + col * rows + row
-                    out_ref[place : place + 1, :] = flat_ref[0:1, at : at + width]
+                    out_ref[place : place + 1, :] = flat_ref[index : index + 1, at : at + width]
         base += count
 
 
@@ -214,9 +214,9 @@
                 out_ref[0:1, at : at + width] = values[place : place + 1, :]
 
 
-def moments_kernel(width, *refs):
-    for index in range(4):
-        to_chunk(refs[index], refs[4 + index], width)
+def moments_kernel(width, rows_ref, *outs):
+    for index, ref in enumerate(outs):
+        to_chunk(rows_ref, ref, width, index)
 
 
 def own_rows(matrix_ref, out_ref, tall):
@@ -236,7 +236,7 @@
     out_ref[...] = tall[size : 2 * size, :].T[0 : out_ref.shape[0]]
 
 
-def small_bases_kernel(narrow_ref, pair_ref, narrow_out, turned_out, pair_out, own_ref, tall):
+def narrow_bases_kernel(narrow_ref, pair_ref, narrow_out, turned_out, pair_out, own_ref, tall):
     narrow_out[...] = narrow_ref[...].astype(bf16)
     pair_out[...] = pair_ref[...].astype(bf16)
     for index, j in enumerate((0, 2, 3, 5)):
@@ -266,21 +266,25 @@
         own_rows(wide_out.at[index + 1], own_ref.at[index], tall)
 
 
-def stack_kernel(split, *refs):
-    count = len(refs) - 2
-    for index in range(count):
-        refs[count][index] = refs[index][0:split, :]
-        refs[count + 1][index] = refs[index][split:, :]
-
-
-def unpack(pieces, group, mats):
-    parts, _ = layout(256, group)
-    wanted = [(part, ref) for part, ref in zip(parts, mats) if ref is not None]
+def join_kernel(*refs):
+    start = 0
+    for ref in refs[:-1]:
+        refs[-1][start : start + ref.shape[0]] = ref[...]
+        start += ref.shape[0]
+
+
+def join(pieces, after=()):
+    shape = (sum(x.shape[0] for x in pieces),) + pieces[0].shape[1:]
+    return run("join", join_kernel, [(shape, pieces[0].dtype)], list(pieces), micros=0.4, after=after)[0]
+
+
+def unpack(pieces, group, mats, base=0):
+    parts = [(j, first + base, rows, blocks) for j, first, rows, blocks in layout(256, group)[0]]
     done = 0
     for piece in pieces:
 
         def body(block, piece=piece, done=done):
-            spread(piece[block].astype(f32), [p for p, _ in wanted], [r for _, r in wanted], source(block + done))
+            spread(piece[block].astype(f32), parts, mats, source(block + done))
 
         each_block(piece.shape[0], body)
         done += piece.shape[0]
@@ -295,9 +299,10 @@
     return [frame_ref[:, 7 + shift : 7 + shift + cols, :] for shift in range(3)]
 
 
-def front_kernel(tile_rows, cols, size_ref, tile_ref, up_ref, down_ref, vec_ref, x0_ref, h1_ref, mask_ref, vec_out, frame):
+def front_kernel(tile_rows, cols, size_ref, tile_ref, up_ref, down_ref, vec_ref, x0_ref, h1_ref, mask_ref, vec_out, size_out, frame):
     rows = frame.shape[0] - 2
     vec_out[...] = vec_ref[...]
+    size_out[...] = jnp.where(lax.broadcasted_iota(jnp.int32, size_out.shape, 0) == 0, size_ref[0, 0], size_ref[0, 1])
     moved = shifted_frame(frame, tile_ref, up_ref, down_ref)
     total = moved[1][1:-1] + vec_ref[9:10, :]
     for tap in range(9):
@@ -335,7 +340,7 @@
         row = row + (key >= step * half).astype(jnp.int32)
     col = 2 * (key - row * half) + corner % 2
     row = 2 * row + corner // 2
-    inside = (row + lax.axis_index("row") * tile_rows < size_ref[0, 0]) & (col < size_ref[0, 1])
+    inside = (row + lax.axis_index("row") * tile_rows < size_ref[0:1, 0:1]) & (col < size_ref[1:2, 0:1])
     target = jnp.where(inside, row * cols + col, -1)
     cell = lax.broadcasted_iota(jnp.int32, shape, cell_axis)
     return (cell == target).astype(f32).astype(bf16)
@@ -442,7 +447,7 @@
     o_ref, x0_ref, out_ref, near_ref, far_ref, vec_ref, dy_ref,
     y_ref, do_ref, dx1_ref, up_grad, down_grad, out_grad, sums_ref, up_ref, down_ref, up_wide, down_wide,
 ):
-    unpack((near_ref, far_ref), EARLY, (up_wide, down_wide))
+    unpack((near_ref, far_ref), EARLY, (up_wide, down_wide), layout(256, LATE)[1])
     up_ref[...] = up_wide[...].astype(bf16)
     down_ref[...] = down_wide[...].astype(bf16)
     o = o_ref[...].astype(bf16)
@@ -855,57 +860,35 @@
         [weights],
         scratch=[((chunk, width), f32)],
     )
+    line = join([packed[None]] + [swap(packed, "img", j)[None] for j in range(1, lines)])
     up_halo, down_halo = border(tile[:64], tile[tokens - 64 :])
-    slices = [packed] + [swap(packed, "img", j) for j in range(1, lines)]
-    old_chunk, ema_chunk, first_chunk, second_chunk = run(
-        "moments",
-        functools.partial(moments_kernel, width),
-        [((chunk, width), f32)] * 4,
-        [weights, weight_ema, first_moment, second_moment],
-        after=[packed],
-    )
-    narrow, narrow_turned, pair, own_narrow = run(
-        "small_bases",
-        small_bases_kernel,
-        [((8, width, width), bf16), ((4, width, width), bf16), ((2 * width, 2 * width), bf16), ((4, 16, width), f32)],
-        [basis_narrow, basis_pair],
-        scratch=[((2 * width, 128), f32)],
-        micros=1.5,
-        after=[packed],
-    )
-    x0, h1, mask, vec = run(
+    x0, h1, mask, vec, sizes = run(
         "front",
         functools.partial(front_kernel, rows, cols),
-        [((tokens, width), f32), ((tokens, width), bf16), ((1, keys), f32), (vectors.shape, f32)],
+        [((tokens, width), f32), ((tokens, width), bf16), ((1, keys), f32), (vectors.shape, f32), ((8, 128), jnp.int32)],
         [image_sizes, tile, up_halo, down_halo, vectors],
         scratch=[frame],
         scalars=(0,),
         micros=1.3,
-    )
-    late_line, early_line = run(
-        "stack",
-        functools.partial(stack_kernel, late_rows),
-        [((lines, late_rows, width), bf16), ((lines, early_rows, width), bf16)],
-        slices,
-        micros=0.4,
-        after=[own_narrow, ema_chunk, vec],
-    )
-    late_near = side_by_side(late_line, gather_groups)
-    late_far = swap(late_near, "row", 1)
-    early_near = side_by_side(early_line, one_by_one(xy_parts)[::-1])
-    early_far = swap(early_near, "row", 1)
+        after=[line],
+    )
     wide, own_wide = run(
         "wide_bases",
         wide_bases_kernel,
         [((3, FF, FF), bf16), ((2, max(16, FF // shards), FF), f32)],
         [basis_wide],
-        scratch=[((2 * FF, 128), f32), ((4, width, FF), f32)],
-        micros=5.0,
-        mib=8,
+        scratch=[((2 * FF, 128), f32), ((12, width, FF), f32)],
+        micros=6.0,
+        mib=48,
         raw=(0,),
-        sems=4,
-        after=[late_line],
-    )
+        sems=12,
+        after=[line],
+    )
+    all_near = line
+    for axis, stride, size in gather_groups:
+        pieces = [all_near] + [swap(all_near, axis, j * stride) for j in range(1, size)]
+        all_near = join(pieces, after=[own_wide, vec])
+    all_far = swap(all_near, "row", 1)
     w_reduce, w_keyval, w_query, w_out, blocks, c, kn, own_kv = run(
         "keys",
         functools.partial(keys_kernel, rows, cols),
@@ -919,11 +902,18 @@
             ((own_keys, width), bf16),
             ((own_keys, 2 * width), bf16),
         ],
-        [image_sizes, h1, vec, late_near, late_far],
+        [sizes, h1, vec, all_near, all_far],
         scratch=[((4 * width, width), f32), ((width, 2 * width), f32), ((width, width), f32), ((width, width), f32)],
-        scalars=(0,),
         micros=1.5,
-        after=[own_wide],
+    )
+    narrow, narrow_turned, pair, own_narrow = run(
+        "narrow_bases",
+        narrow_bases_kernel,
+        [((8, width, width), bf16), ((4, width, width), bf16), ((2 * width, 2 * width), bf16), ((4, 16, width), f32)],
+        [basis_narrow, basis_pair],
+        scratch=[((2 * width, 128), f32)],
+        micros=1.5,
+        after=[own_kv],
     )
     kv_near = side_by_side(own_kv, gather_groups)
     kv_far = swap(kv_near, "row", 1)
@@ -937,6 +927,7 @@
         [h1, w_query, vec, kv_near, kv_far, mask],
         mib=8 if unroll else 44,
         micros=8.0,
+        after=[own_narrow],
     )
     y, do, dx1, up_grad, down_grad, out_grad, feed_sums = run(
         "feed",
@@ -950,7 +941,7 @@
             ((width, width), f32),
             (vectors.shape, f32),
         ],
-        [o, x0, w_out, early_near, early_far, vec, dy],
+        [o, x0, w_out, all_near, all_far, vec, dy],
         scratch=[((width, FF), bf16), ((FF, width), bf16), ((width, FF), f32), ((FF, width), f32)],
         mib=12,
         micros=3.5,
@@ -992,22 +983,37 @@
         )
 
     pairs = one_by_one(xy_parts + [img_part])
+    place = 0
+
+    def early_pair(after=()):
+        nonlocal early_terms, place
+        keep, send = split_sum(early_terms, 2, after=after)
+        early_terms = [keep, swap(send, *pairs[place][:2])]
+        place += 1
+        return keep
+
+    early_terms = [early_keep, swap(early_send, "row", 1)]
     dq_left, left_keep, left_send, query_left, left_sum = back(0, [early_keep])
-    early_terms = [early_keep, swap(early_send, "row", 1)]
-    early_keep, early_send = split_sum(early_terms, 2, after=[query_left])
-    early_terms = [early_keep, swap(early_send, *pairs[0][:2])]
+    token = early_pair([query_left])
     left_got = swap(left_send, "row", 1)
-    dq_right, right_keep, right_send, query_right, right_sum = back(1, [early_keep])
+    dq_right, right_keep, right_send, query_right, right_sum = back(1, [token])
     right_got = swap(right_send, "row", 1)
+    axis, stride, size = xy_parts[0]
     dkv_keep, *dkv_sends = run(
         "split_heads",
-        functools.partial(split_heads_kernel, xy_parts[0][2]),
-        [((keys // 2 // xy_parts[0][2], 2 * width), f32)]
-        + [((keys // 2 // xy_parts[0][2], 2 * width), bf16)] * (xy_parts[0][2] - 1),
+        functools.partial(split_heads_kernel, size),
+        [((keys // 2 // size, 2 * width), f32)] + [((keys // 2 // size, 2 * width), bf16)] * (size - 1),
         [left_keep, left_got, right_keep, right_got],
         micros=0.8,
     )
-    axis, stride, size = xy_parts[0]
+    token = early_pair([dkv_keep])
+    old_chunk, ema_chunk, first_chunk, second_chunk = run(
+        "moments",
+        functools.partial(moments_kernel, width),
+        [((chunk, width), f32)] * 4,
+        [jnp.concatenate([weights, weight_ema, first_moment, second_moment], axis=0)],
+        after=[dkv_keep],
+    )
     dkv_terms = [dkv_keep] + [swap(x, axis, j * stride) for j, x in enumerate(dkv_sends, 1)]
     for axis, stride, size in xy_parts[1:]:
         keep, *sends = split_sum(dkv_terms, size)
@@ -1018,9 +1024,8 @@
         [((width, width), f32), ((width, width), f32)],
         [query_left, query_right, out_grad, narrow_turned, narrow],
         micros=0.7,
-    )
-    early_keep, early_send = split_sum(early_terms, 2, after=[query_turn])
-    early_terms = [early_keep, swap(early_send, *pairs[1][:2])]
+        after=[dkv_keep],
+    )
     half = (shards // 2, late_rows, width)
     late_keep, late_send, dc, key_sums = run(
         "keys_back",
@@ -1029,46 +1034,57 @@
         list(dkv_terms) + [kn, c, vec, w_keyval, blocks, narrow_turned, narrow, pair, wide, query_turn, out_turn],
         scratch=[((4 * width, width), f32), ((width, 2 * width), f32)],
         micros=2.0,
-        after=[early_keep],
+        after=[token, old_chunk],
     )
     late_got = swap(late_send, "row", 1)
+    token = early_pair([dc])
     dx0, head, tail, vec_grads = run(
         "cells_back",
         functools.partial(cells_back_kernel, rows, cols),
         [((tokens, width), f32), ((64, width), bf16), ((64, width), bf16), ((32, width), f32)],
         [
-            image_sizes, dq_left, dq_right, dc, w_query, w_reduce, x0, dx1, vec, tile, up_halo, down_halo,
+            sizes, dq_left, dq_right, dc, w_query, w_reduce, x0, dx1, vec, tile, up_halo, down_halo,
             feed_sums, key_sums, left_sum, right_sum,
         ],
         scratch=[frame],
-        scalars=(0,),
         micros=2.0,
+        after=[token],
     )
     vec_terms = [vec_grads, swap(vec_grads, "row", 1)]
     grad_up, grad_down = border(head, tail)
+    while place < len(pairs):
+        token = early_pair()
     late_terms = [late_keep.reshape(-1, width), late_got.reshape(-1, width)]
-    waits = [[early_keep], [grad_up, grad_down]]
-    for index, (axis, stride, size) in enumerate(xy_parts + [img_part]):
-        if index + 2 < len(pairs):
-            early_keep, early_send = split_sum(early_terms, 2, after=[dc] if index == 0 else [late_keep])
-            early_terms = [early_keep, swap(early_send, *pairs[index + 2][:2])]
-            waits[0] = [early_keep]
-        late_keep, own_vec, *sends = split_with_vectors(
-            late_terms, vec_terms, size, index == 0, waits[0] if index == 0 else waits[0] + waits[1]
-        )
-        late_terms = [late_keep] + [swap(x, axis, j * stride) for j, x in enumerate(sends, 1)]
+
+    def late_stage(part, first, after):
+        nonlocal late_terms, vec_terms
+        axis, stride, size = part
+        keep, own_vec, *sends = split_with_vectors(late_terms, vec_terms, size, first, after)
+        late_terms = [keep] + [swap(x, axis, j * stride) for j, x in enumerate(sends, 1)]
         vec_terms = [own_vec]
-    for axis, stride, _ in pairs[2 + len(xy_parts) + 1 :]:
-        early_keep, early_send = split_sum(early_terms, 2)
-        early_terms = [early_keep, swap(early_send, axis, stride)]
+        return keep
+
+    token = late_stage(xy_parts[0], True, [token])
     early_first, early_second, early_step = run(
         "adam",
         functools.partial(adam_kernel, late_rows, 2),
         [((early_rows, width), f32), ((early_rows, width), f32), ((early_rows, width), bf16)],
         [t.reshape(early_rows, width) for t in early_terms] + [first_chunk, second_chunk],
         micros=0.6,
-    )
-    steps_line = side_by_side(early_step[None], one_by_one([img_part])[::-1])
+        after=[token],
+    )
+    for part in xy_parts[1:]:
+        late_stage(part, False, [])
+    steps_pairs = one_by_one(xy_parts + [img_part])[::-1]
+    steps = early_step[None]
+
+    def steps_pair(after=()):
+        nonlocal steps
+        axis, stride, _ = steps_pairs.pop(0)
+        steps = join([steps, swap(steps, axis, stride)], after)
+        return steps
+
+    token = late_stage(img_part, False, [steps_pair()])
     (grad_input,) = run(
         "input_grad",
         functools.partial(input_grad_kernel, rows),
@@ -1076,20 +1092,26 @@
         [dx0, grad_up, grad_down, vec],
         scratch=[frame],
         micros=1.5,
-        after=[late_keep],
+        after=[token],
     )
     late_first, late_second, late_step, new_vectors, vec_moment, vec_square, new_vec_ema = run(
         "late_adam",
         functools.partial(late_adam_kernel, len(late_terms)),
         [((late_rows, width), f32), ((late_rows, width), f32), ((late_rows, width), bf16)] + [(vectors.shape, f32)] * 4,
-        late_terms + [own_vec, first_chunk, second_chunk, vec, vec_first, vec_second, vec_ema],
+        late_terms + vec_terms + [first_chunk, second_chunk, vec, vec_first, vec_second, vec_ema],
         micros=0.8,
-        after=[early_step, grad_input],
-    )
-    step_near = side_by_side(late_step[None], [img_part] + gather_groups)
+        after=[steps_pair(), grad_input],
+    )
+    step_near = late_step[None]
+    after = [late_step]
+    for axis, stride, size in [img_part] + gather_groups:
+        pieces = [step_near] + [swap(step_near, axis, j * stride) for j in range(1, size)]
+        step_near = join(pieces, [steps_pair(after)] if steps_pairs else [])
+        after = [step_near]
+    while steps_pairs:
+        steps_pair()
     step_far = swap(step_near, "row", 1)
-    steps_near = side_by_side(steps_line, one_by_one(xy_parts)[::-1])
-    steps_far = swap(steps_near, "row", 1)
+    steps_near, steps_far = steps, swap(steps, "row", 1)
 
     early_new, new_first, new_second, *late_sides = run(
         "early_finish",
@@ -1110,7 +1132,6 @@
         [step_far, *late_sides, early_new, own_narrow, own_wide, narrow, pair, wide, old_chunk, ema_chunk],
         scratch=[((chunk, width), f32)],
         micros=1.5,
-        after=[new_first],
     )
     return (
         y.reshape(patches.shape),

time: 167 us -> 150 us (0.90)
  local copies, waits for them, and re-layouts: 17.2 us -> 2.82 us
  waiting for transfers between devices: 52.3 us -> 46.5 us
  Pallas kernels: 39 us -> 43.7 us
    unnamed x56 -> x37, local copies, waits for them, and re-layouts: 16.3 us -> 2.03 us
    ppermute x44 -> x41, waiting for transfers between devices: 52.3 us -> 43.5 us  [swap(): return lax.ppermute(x, axis, [(i, i ^ step) for i in range(count)])]
    pallas_call x27 -> x34, Pallas kernels: 39 us -> 43.7 us  [run(): pl.pallas_call(without, out_shape=tuple((jax.ShapeDtypeStruct(shape, dtyp...]
    ppermute x2, waiting for transfers between devices: 0.01 us -> 2.98 us  [border(): lax.ppermute(head, 'row', [(i + 1, i) for i in range(ranks - 1)])]
    ppermute x2, starting transfers between devices: 4.81 us -> 2.56 us  [border(): up = lax.ppermute(tail, 'row', [(i, i + 1) for i in range(ranks - 1)])]
    ppermute x44 -> x41, starting transfers between devices: 48.8 us -> 49.5 us  [swap(): return lax.ppermute(x, axis, [(i, i ^ step) for i in range(count)])]
  transfers between devices with their start and end apart: 48 -> 45, of which waited for: 21 -> 21; matrix products, arithmetic and copies ran while one was open for 1% -> 1% of each run, Pallas kernels for 18% -> 18%
where the time goes in v4:
time: 150 us; the launch traced here: 149 us
  starting transfers between devices  54.7 us (36%)
  waiting for transfers between devices  46.5 us (31%)
  Pallas kernels  43.7 us (29%)
  local copies, waits for them, and re-layouts  2.82 us (2%)
    ppermute x41, starting transfers between devices, swap(): return lax.ppermute(x, axis, [(i, i ^ step) for i in range(count)])  49.5 us
    pallas_call x34, Pallas kernels, run(): pl.pallas_call(without, out_shape=tuple((jax.ShapeDtypeStruct(shape, dtyp...  43.7 us
    ppermute x41, waiting for transfers between devices, swap(): return lax.ppermute(x, axis, [(i, i ^ step) for i in range(count)])  43.5 us
  transfers between devices with their start and end apart: 45, of which 21 were waited for; matrix products, arithmetic and copies ran while one was open for 1% of the time, Pallas kernels for 18%

profile of v4, /device:TPU:0, one launch (start us, length us, event | category | flops | bytes accessed | tf_op | source)
XLA Modules:
  0.0 149.5 jit_solution(7083438718566019565)
XLA Ops:
  1.6 3.1 %collective-permute-start.2 = (bf16[128,256]{1,0:T(8,128)(2,1)S(1)}, bf16[128,256]{1,0:T(8,128)(2,1)S(1)}, u32[]{:S(2)}, u32[]{:S(2)}) collective-permute-start(bf16[128,256]{1,0:T(8,128)(2,1)S(1)} %pack.1), channel_id=1, source_target_pairs={{0,8},{8,0},{16,24},{24,16},{1,9},{9,1},{17,25},{25,17},{2,10},{10... | collective-permute-start | bytes 196616 | tf_op jit(solution)/shard_map/ppermute | solution.py:49
  4.7 2.6 %collective-permute-start.3 = (bf16[128,256]{1,0:T(8,128)(2,1)S(1)}, bf16[128,256]{1,0:T(8,128)(2,1)S(1)}, u32[]{:S(2)}, u32[]{:S(2)}) collective-permute-start(bf16[128,256]{1,0:T(8,128)(2,1)S(1)} %pack.1), channel_id=1, source_target_pairs={{0,16},{8,24},{16,0},{24,8},{1,17},{9,25},{17,1},{25,9},{2,18},{10... | collective-permute-start | bytes 196616 | tf_op jit(solution)/shard_map/ppermute | solution.py:49
  7.3 4.7 %collective-permute-done.3 = bf16[128,256]{1,0:T(8,128)(2,1)S(1)} collective-permute-done((bf16[128,256]{1,0:T(8,128)(2,1)S(1)}, bf16[128,256]{1,0:T(8,128)(2,1)S(1)}, u32[]{:S(2)}, u32[]{:S(2)}) %collective-permute-start.3) | collective-permute-done | bytes 65568 | tf_op jit(solution)/shard_map/ppermute | solution.py:49
  20.5 8.4 %wide_bases.1 = (bf16[3,1024,1024]{2,1,0:T(8,128)(2,1)}, f32[2,32,1024]{2,1,0:T(8,128)S(1)}) custom-call(f32[3,1024,1024]{2,1,0:T(8,128)} %refs_0_.6, bf16[4,128,256]{2,1,0:T(8,128)(2,1)S(1)} %join.8.refs_5_.refs_1_.refs_0_), custom_call_target="tpu_custom_call" | custom-call | bytes 21600000 | tf_op jit(solution)/shard_map/wide_bases/pallas_call | solution.py:91
  30.5 2.9 %collective-permute-start.8 = (bf16[16,128,256]{2,1,0:T(8,128)(2,1)S(1)}, bf16[16,128,256]{2,1,0:T(8,128)(2,1)S(1)}, u32[]{:S(2)}, u32[]{:S(2)}) collective-permute-start(bf16[16,128,256]{2,1,0:T(8,128)(2,1)S(1)} %join.9.refs_3_), channel_id=1, source_target_pairs={{0,1},{1,0},{2,3},{3,2},{4,5},{5,4},{6,7},{7,6},{8,9},{9,8},{10,11... | collective-permute-start | bytes 3145736 | tf_op jit(solution)/shard_map/ppermute | solution.py:49
  33.4 2.3 %collective-permute-done.8.refs_4_ = bf16[16,128,256]{2,1,0:T(8,128)(2,1)S(1)} collective-permute-done((bf16[16,128,256]{2,1,0:T(8,128)(2,1)S(1)}, bf16[16,128,256]{2,1,0:T(8,128)(2,1)S(1)}, u32[]{:S(2)}, u32[]{:S(2)}) %collective-permute-start.8) | collective-permute-done | bytes 1048608 | tf_op jit(solution)/shard_map/ppermute | solution.py:49
  36.6 2.1 %collective-permute-start.9 = (bf16[112,512]{1,0:T(8,128)(2,1)S(1)}, bf16[112,512]{1,0:T(8,128)(2,1)S(1)}, u32[]{:S(2)}, u32[]{:S(2)}) collective-permute-start(bf16[112,512]{1,0:T(8,128)(2,1)S(1)} %get-tuple-element.113.refs_2_), channel_id=1, source_target_pairs={{0,2},{1,3},{2,0},{3,1},{4,6},{5,7},{6,4},{7,5},{8,10},{9,11},{10,... | collective-permute-start | bytes 344072 | tf_op jit(solution)/shard_map/ppermute | solution.py:49
  42.1 2.9 %collective-permute-done.10 = bf16[112,512]{1,0:T(8,128)(2,1)S(1)} collective-permute-done((bf16[112,512]{1,0:T(8,128)(2,1)S(1)}, bf16[112,512]{1,0:T(8,128)(2,1)S(1)}, u32[]{:S(2)}, u32[]{:S(2)}) %collective-permute-start.10) | collective-permute-done | bytes 114720 | tf_op jit(solution)/shard_map/ppermute | solution.py:49
  48.5 7.5 %attend.1 = (bf16[448,256]{1,0:T(8,128)(2,1)S(1)}, bf16[896,256]{1,0:T(8,128)(2,1)S(1)}, bf16[896,256]{1,0:T(8,128)(2,1)S(1)}, f32[448,256]{1,0:T(8,128)S(1)}, f32[448,128]{1,0:T(8,128)S(1)}) custom-call(bf16[448,256]{1,0:T(8,128)(2,1)S(1)} %get-tuple-element.108.refs_1_.refs_0_.refs_7_, bf16[256,256]{1,0:T(8,128)(2,1)S(1)} %get-tuple-element.112.refs_1_.refs_4_, ...), custom_call_target="tpu_custom_call" | custom-call | bytes 28800000 | tf_op jit(solution)/shard_map/attend/pallas_call | solution.py:91
  56.0 3.3 %feed.1 = (bf16[448,256]{1,0:T(8,128)(2,1)}, bf16[448,256]{1,0:T(8,128)(2,1)S(1)}, f32[448,256]{1,0:T(8,128)S(1)}, f32[256,1024]{1,0:T(8,128)S(1)}, f32[256,1024...) custom-call(f32[448,256]{1,0:T(8,128)S(1)} %get-tuple-element.116.refs_0_.refs_4_, ...), custom_call_target="tpu_custom_call" | custom-call | bytes 12600000 | tf_op jit(solution)/shard_map/feed/pallas_call | solution.py:91
  61.4 4.6 %attend_back.2 = (bf16[448,128]{1,0:T(8,128)(2,1)S(1)}, f32[448,256]{1,0:T(8,128)S(1)}, f32[448,256]{1,0:T(8,128)S(1)}, f32[256,128]{1,0:T(8,128)S(1)}, f32[1,128]{1,0:T(1,128)S(1)}) custom-call(bf16[448,256]{1,0:T(8,128)(2,1)S(1)} %get-tuple-element.120.refs_0_, bf16[896,256]{1,0:T(8,128)(2,1)S(1)} %get-tuple-element.121.refs_1_, ...), custom_call_target="tpu_custom_call" | custom-call | bytes 18000000 | tf_op jit(solution)/shard_map/attend_back/pallas_call | solution.py:91
  66.6 4.8 %attend_back.3 = (bf16[448,128]{1,0:T(8,128)(2,1)S(1)}, f32[448,256]{1,0:T(8,128)S(1)}, f32[448,256]{1,0:T(8,128)S(1)}, f32[256,128]{1,0:T(8,128)S(1)}, f32[1,128]{1,0:T(1,128)S(1)}) custom-call(bf16[448,256]{1,0:T(8,128)(2,1)S(1)} %get-tuple-element.120.refs_0_, bf16[896,256]{1,0:T(8,128)(2,1)S(1)} %get-tuple-element.121.refs_1_, ...), custom_call_target="tpu_custom_call" | custom-call | bytes 18000000 | tf_op jit(solution)/shard_map/attend_back/pallas_call | solution.py:91
  78.1 5.0 %collective-permute-done.19.refs_1_ = bf16[8,64,256]{2,1,0:T(8,128)(2,1)S(1)} collective-permute-done((bf16[8,64,256]{2,1,0:T(8,128)(2,1)S(1)}, bf16[8,64,256]{2,1,0:T(8,128)(2,1)S(1)}, u32[]{:S(2)}, u32[]{:S(2)}) %collective-permute-start.19) | collective-permute-done | bytes 262176 | tf_op jit(solution)/shard_map/ppermute | solution.py:49
  87.7 5.2 %collective-permute-done.20.refs_1_ = bf16[4,64,256]{2,1,0:T(8,128)(2,1)S(1)} collective-permute-done((bf16[4,64,256]{2,1,0:T(8,128)(2,1)S(1)}, bf16[4,64,256]{2,1,0:T(8,128)(2,1)S(1)}, u32[]{:S(2)}, u32[]{:S(2)}) %collective-permute-start.20) | collective-permute-done | bytes 131104 | tf_op jit(solution)/shard_map/ppermute | solution.py:49
  96.4 1.9 %collective-permute-done.25.refs_1_ = bf16[2,64,256]{2,1,0:T(8,128)(2,1)S(1)} collective-permute-done((bf16[2,64,256]{2,1,0:T(8,128)(2,1)S(1)}, bf16[2,64,256]{2,1,0:T(8,128)(2,1)S(1)}, u32[]{:S(2)}, u32[]{:S(2)}) %collective-permute-start.25) | collective-permute-done | bytes 65568 | tf_op jit(solution)/shard_map/ppermute | solution.py:49
  104.3 2.1 %collective-permute-done.30.refs_1_ = bf16[1,64,256]{2,1,0:T(8,128)(2,1)S(1)} collective-permute-done((bf16[1,64,256]{2,1,0:T(8,128)(2,1)S(1)}, bf16[1,64,256]{2,1,0:T(8,128)(2,1)S(1)}, u32[]{:S(2)}, u32[]{:S(2)}) %collective-permute-start.30) | collective-permute-done | bytes 32800 | tf_op jit(solution)/shard_map/ppermute | solution.py:49
  106.3 2.4 %collective-permute-start.34 = (bf16[2,64,256]{2,1,0:T(8,128)(2,1)S(1)}, bf16[2,64,256]{2,1,0:T(8,128)(2,1)S(1)}, u32[]{:S(2)}, u32[]{:S(2)}) collective-permute-start(bf16[2,64,256]{2,1,0:T(8,128)(2,1)S(1)} %join.10.refs_5_.refs_0_), channel_id=1, source_target_pairs={{0,16},{8,24},{16,0},{24,8},{1,17},{9,25},{17,1},{25,9},{2,18},{10... | collective-permute-start | bytes 196616 | tf_op jit(solution)/shard_map/ppermute | solution.py:49
  108.7 2.8 %collective-permute-done.34.refs_1_ = bf16[2,64,256]{2,1,0:T(8,128)(2,1)S(1)} collective-permute-done((bf16[2,64,256]{2,1,0:T(8,128)(2,1)S(1)}, bf16[2,64,256]{2,1,0:T(8,128)(2,1)S(1)}, u32[]{:S(2)}, u32[]{:S(2)}) %collective-permute-start.34) | collective-permute-done | bytes 65568 | tf_op jit(solution)/shard_map/ppermute | solution.py:49
  113.7 2.1 %collective-permute-start.31 = (bf16[128,256]{1,0:T(8,128)(2,1)S(1)}, bf16[128,256]{1,0:T(8,128)(2,1)S(1)}, u32[]{:S(2)}, u32[]{:S(2)}) collective-permute-start(bf16[128,256]{1,0:T(8,128)(2,1)S(1)} %get-tuple-element.183), channel_id=1, source_target_pairs={{0,8},{8,0},{16,24},{24,16},{1,9},{9,1},{17,25},{25,17},{2,10},{10... | collective-permute-start | bytes 196616 | tf_op jit(solution)/shard_map/ppermute | solution.py:49
  119.5 3.0 %collective-permute-done.22.refs_2_ = bf16[64,256]{1,0:T(8,128)(2,1)S(1)} collective-permute-done((bf16[64,256]{1,0:T(8,128)(2,1)S(1)}, bf16[64,256]{1,0:T(8,128)(2,1)S(1)}, u32[]{:S(2)}, u32[]{:S(2)}) %collective-permute-start.22) | collective-permute-done | bytes 32800 | tf_op jit(solution)/shard_map/ppermute | solution.py:851
  125.9 3.7 %collective-permute-start.42 = (bf16[8,64,256]{2,1,0:T(8,128)(2,1)S(1)}, bf16[8,64,256]{2,1,0:T(8,128)(2,1)S(1)}, u32[]{:S(2)}, u32[]{:S(2)}) collective-permute-start(bf16[8,64,256]{2,1,0:T(8,128)(2,1)S(1)} %join.12.refs_4_.refs_0_), channel_id=1, source_target_pairs={{0,4},{1,5},{2,6},{3,7},{4,0},{5,1},{6,2},{7,3},{8,12},{9,13},{10,... | collective-permute-start | bytes 786440 | tf_op jit(solution)/shard_map/ppermute | solution.py:49
  130.3 2.2 %collective-permute-start.36 = (bf16[1,64,256]{2,1,0:T(8,128)(2,1)S(1)}, bf16[1,64,256]{2,1,0:T(8,128)(2,1)S(1)}, u32[]{:S(2)}, u32[]{:S(2)}) collective-permute-start(bf16[1,64,256]{2,1,0:T(8,128)(2,1)S(1)} %bitcast.26), channel_id=1, source_target_pairs={{0,16},{8,24},{16,0},{24,8},{1,17},{9,25},{17,1},{25,9},{2,18},{10... | collective-permute-start | bytes 98312 | tf_op jit(solution)/shard_map/ppermute | solution.py:49
  135.1 3.1 %collective-permute-done.37.refs_3_ = bf16[1,64,256]{2,1,0:T(8,128)(2,1)S(1)} collective-permute-done((bf16[1,64,256]{2,1,0:T(8,128)(2,1)S(1)}, bf16[1,64,256]{2,1,0:T(8,128)(2,1)S(1)}, u32[]{:S(2)}, u32[]{:S(2)}) %collective-permute-start.37) | collective-permute-done | bytes 32800 | tf_op jit(solution)/shard_map/ppermute | solution.py:49
  142.0 2.7 %collective-permute-done.39.refs_1_ = bf16[4,64,256]{2,1,0:T(8,128)(2,1)S(1)} collective-permute-done((bf16[4,64,256]{2,1,0:T(8,128)(2,1)S(1)}, bf16[4,64,256]{2,1,0:T(8,128)(2,1)S(1)}, u32[]{:S(2)}, u32[]{:S(2)}) %collective-permute-start.39) | collective-permute-done | bytes 131104 | tf_op jit(solution)/shard_map/ppermute | solution.py:49
  (141 shorter events, 63.0 us)
Async XLA Ops:
  4.7 7.3 %collective-permute-start.3 = (bf16[128,256]{1,0:T(8,128)(2,1)S(1)}, bf16[128,256]{1,0:T(8,128)(2,1)S(1)}, u32[]{:S(2)}, u32[]{:S(2)}) collective-permute-start(bf16[128,256]{1,0:T(8,128)(2,1)S(1)} %pack.1), channel_id=1, source_target_pairs={{0,16},{8,24},{16,0},{24,8},{1,17},{9,25},{17,1},{25,9},{2,18},{10... | collective-permute-start | bytes 196616 | tf_op jit(solution)/shard_map/ppermute | solution.py:49
  13.4 17.0 %collective-permute-start.5 = (bf16[4,128,256]{2,1,0:T(8,128)(2,1)S(1)}, bf16[4,128,256]{2,1,0:T(8,128)(2,1)S(1)}, u32[]{:S(2)}, u32[]{:S(2)}) collective-permute-start(bf16[4,128,256]{2,1,0:T(8,128)(2,1)S(1)} %join.8.refs_5_.refs_1_.refs_0_), channel_id=1, source_target_pairs={{0,2},{1,3},{2,0},{3,1},{4,6},{5,7},{6,4},{7,5},{8,10},{9,11},{10,... | collective-permute-start | bytes 786440 | tf_op jit(solution)/shard_map/ppermute | solution.py:49
  15.0 15.4 %collective-permute-start.6 = (bf16[4,128,256]{2,1,0:T(8,128)(2,1)S(1)}, bf16[4,128,256]{2,1,0:T(8,128)(2,1)S(1)}, u32[]{:S(2)}, u32[]{:S(2)}) collective-permute-start(bf16[4,128,256]{2,1,0:T(8,128)(2,1)S(1)} %join.8.refs_5_.refs_1_.refs_0_), channel_id=1, source_target_pairs={{0,4},{1,5},{2,6},{3,7},{4,0},{5,1},{6,2},{7,3},{8,12},{9,13},{10,... | collective-permute-start | bytes 786440 | tf_op jit(solution)/shard_map/ppermute | solution.py:49
  16.5 13.9 %collective-permute-start.7 = (bf16[4,128,256]{2,1,0:T(8,128)(2,1)S(1)}, bf16[4,128,256]{2,1,0:T(8,128)(2,1)S(1)}, u32[]{:S(2)}, u32[]{:S(2)}) collective-permute-start(bf16[4,128,256]{2,1,0:T(8,128)(2,1)S(1)} %join.8.refs_5_.refs_1_.refs_0_), channel_id=1, source_target_pairs={{0,6},{1,7},{2,4},{3,5},{4,2},{5,3},{6,0},{7,1},{8,14},{9,15},{10,... | collective-permute-start | bytes 786440 | tf_op jit(solution)/shard_map/ppermute | solution.py:49
  17.7 11.2 %collective-permute-start = (bf16[64,256]{1,0:T(8,128)(2,1)S(1)}, bf16[64,256]{1,0:T(8,128)(2,1)S(1)}, u32[]{:S(2)}, u32[]{:S(2)}) collective-permute-start(bf16[64,256]{1,0:T(8,128)(2,1)S(1)} %get-tuple-element.207), channel_id=1, source_target_pairs={{0,1},{1,2},{2,3},{3,4},{4,5},{5,6},{6,7},{8,9},{9,10},{10,11},{11... | collective-permute-start | bytes 98312 | tf_op jit(solution)/shard_map/ppermute | solution.py:850
  19.1 9.9 %collective-permute-start.1 = (bf16[64,256]{1,0:T(8,128)(2,1)S(1)}, bf16[64,256]{1,0:T(8,128)(2,1)S(1)}, u32[]{:S(2)}, u32[]{:S(2)}) collective-permute-start(bf16[64,256]{1,0:T(8,128)(2,1)S(1)} %get-tuple-element.206), channel_id=1, source_target_pairs={{1,0},{2,1},{3,2},{4,3},{5,4},{6,5},{7,6},{9,8},{10,9},{11,10},{12... | collective-permute-start | bytes 98312 | tf_op jit(solution)/shard_map/ppermute | solution.py:851
  38.6 6.4 %collective-permute-start.10 = (bf16[112,512]{1,0:T(8,128)(2,1)S(1)}, bf16[112,512]{1,0:T(8,128)(2,1)S(1)}, u32[]{:S(2)}, u32[]{:S(2)}) collective-permute-start(bf16[112,512]{1,0:T(8,128)(2,1)S(1)} %get-tuple-element.113.refs_2_), channel_id=1, source_target_pairs={{0,4},{1,5},{2,6},{3,7},{4,0},{5,1},{6,2},{7,3},{8,12},{9,13},{10,... | collective-permute-start | bytes 344072 | tf_op jit(solution)/shard_map/ppermute | solution.py:49
  40.1 6.5 %collective-permute-start.11 = (bf16[112,512]{1,0:T(8,128)(2,1)S(1)}, bf16[112,512]{1,0:T(8,128)(2,1)S(1)}, u32[]{:S(2)}, u32[]{:S(2)}) collective-permute-start(bf16[112,512]{1,0:T(8,128)(2,1)S(1)} %get-tuple-element.113.refs_2_), channel_id=1, source_target_pairs={{0,6},{1,7},{2,4},{3,5},{4,2},{5,3},{6,0},{7,1},{8,14},{9,15},{10,... | collective-permute-start | bytes 344072 | tf_op jit(solution)/shard_map/ppermute | solution.py:49
  66.0 6.5 %collective-permute-start.14 = (f32[448,256]{1,0:T(8,128)S(1)}, f32[448,256]{1,0:T(8,128)S(1)}, u32[]{:S(2)}, u32[]{:S(2)}) collective-permute-start(f32[448,256]{1,0:T(8,128)S(1)} %get-tuple-element.137), channel_id=1, source_target_pairs={{0,1},{1,0},{2,3},{3,2},{4,5},{5,4},{6,7},{7,6},{8,9},{9,8},{10,11... | collective-permute-start | bytes 1376264 | tf_op jit(solution)/shard_map/ppermute | solution.py:49
  71.6 11.6 %collective-permute-start.19 = (bf16[8,64,256]{2,1,0:T(8,128)(2,1)S(1)}, bf16[8,64,256]{2,1,0:T(8,128)(2,1)S(1)}, u32[]{:S(2)}, u32[]{:S(2)}) collective-permute-start(bf16[8,64,256]{2,1,0:T(8,128)(2,1)S(1)} %get-tuple-element.153), channel_id=1, source_target_pairs={{0,4},{1,5},{2,6},{3,7},{4,0},{5,1},{6,2},{7,3},{8,12},{9,13},{10,... | collective-permute-start | bytes 786440 | tf_op jit(solution)/shard_map/ppermute | solution.py:49
  73.4 9.8 %collective-permute-start.16 = (bf16[112,512]{1,0:T(8,128)(2,1)S(1)}, bf16[112,512]{1,0:T(8,128)(2,1)S(1)}, u32[]{:S(2)}, u32[]{:S(2)}) collective-permute-start(bf16[112,512]{1,0:T(8,128)(2,1)S(1)} %get-tuple-element.141), channel_id=1, source_target_pairs={{0,2},{1,3},{2,0},{3,1},{4,6},{5,7},{6,4},{7,5},{8,10},{9,11},{10,... | collective-permute-start | bytes 344072 | tf_op jit(solution)/shard_map/ppermute | solution.py:49
  74.1 11.0 %collective-permute-start.17 = (bf16[112,512]{1,0:T(8,128)(2,1)S(1)}, bf16[112,512]{1,0:T(8,128)(2,1)S(1)}, u32[]{:S(2)}, u32[]{:S(2)}) collective-permute-start(bf16[112,512]{1,0:T(8,128)(2,1)S(1)} %get-tuple-element.142), channel_id=1, source_target_pairs={{0,4},{1,5},{2,6},{3,7},{4,0},{5,1},{6,2},{7,3},{8,12},{9,13},{10,... | collective-permute-start | bytes 344072 | tf_op jit(solution)/shard_map/ppermute | solution.py:49
  75.8 9.3 %collective-permute-start.18 = (bf16[112,512]{1,0:T(8,128)(2,1)S(1)}, bf16[112,512]{1,0:T(8,128)(2,1)S(1)}, u32[]{:S(2)}, u32[]{:S(2)}) collective-permute-start(bf16[112,512]{1,0:T(8,128)(2,1)S(1)} %get-tuple-element.143), channel_id=1, source_target_pairs={{0,6},{1,7},{2,4},{3,5},{4,2},{5,3},{6,0},{7,1},{8,14},{9,15},{10,... | collective-permute-start | bytes 344072 | tf_op jit(solution)/shard_map/ppermute | solution.py:49
  86.9 11.5 %collective-permute-start.23 = (f32[16,64,256]{2,1,0:T(8,128)S(1)}, f32[16,64,256]{2,1,0:T(8,128)S(1)}, u32[]{:S(2)}, u32[]{:S(2)}) collective-permute-start(f32[16,64,256]{2,1,0:T(8,128)S(1)} %get-tuple-element.169), channel_id=1, source_target_pairs={{0,1},{1,0},{2,3},{3,2},{4,5},{5,4},{6,7},{7,6},{8,9},{9,8},{10,11... | collective-permute-start | bytes 3145736 | tf_op jit(solution)/shard_map/ppermute | solution.py:49
  98.6 15.0 %collective-permute-start.26 = (bf16[320,256]{1,0:T(8,128)(2,1)S(1)}, bf16[320,256]{1,0:T(8,128)(2,1)S(1)}, u32[]{:S(2)}, u32[]{:S(2)}) collective-permute-start(bf16[320,256]{1,0:T(8,128)(2,1)S(1)} %get-tuple-element.174), channel_id=1, source_target_pairs={{0,2},{1,3},{2,0},{3,1},{4,6},{5,7},{6,4},{7,5},{8,10},{9,11},{10,... | collective-permute-start | bytes 491528 | tf_op jit(solution)/shard_map/ppermute | solution.py:49
  99.3 14.3 %collective-permute-start.27 = (bf16[320,256]{1,0:T(8,128)(2,1)S(1)}, bf16[320,256]{1,0:T(8,128)(2,1)S(1)}, u32[]{:S(2)}, u32[]{:S(2)}) collective-permute-start(bf16[320,256]{1,0:T(8,128)(2,1)S(1)} %get-tuple-element.175), channel_id=1, source_target_pairs={{0,4},{1,5},{2,6},{3,7},{4,0},{5,1},{6,2},{7,3},{8,12},{9,13},{10,... | collective-permute-start | bytes 491528 | tf_op jit(solution)/shard_map/ppermute | solution.py:49
  101.0 12.6 %collective-permute-start.28 = (bf16[320,256]{1,0:T(8,128)(2,1)S(1)}, bf16[320,256]{1,0:T(8,128)(2,1)S(1)}, u32[]{:S(2)}, u32[]{:S(2)}) collective-permute-start(bf16[320,256]{1,0:T(8,128)(2,1)S(1)} %get-tuple-element.176), channel_id=1, source_target_pairs={{0,6},{1,7},{2,4},{3,5},{4,2},{5,3},{6,0},{7,1},{8,14},{9,15},{10,... | collective-permute-start | bytes 491528 | tf_op jit(solution)/shard_map/ppermute | solution.py:49
  111.5 14.3 %collective-permute-start.38 = (bf16[4,64,256]{2,1,0:T(8,128)(2,1)S(1)}, bf16[4,64,256]{2,1,0:T(8,128)(2,1)S(1)}, u32[]{:S(2)}, u32[]{:S(2)}) collective-permute-start(bf16[4,64,256]{2,1,0:T(8,128)(2,1)S(1)} %join.11.refs_11_.refs_0_), channel_id=1, source_target_pairs={{0,2},{1,3},{2,0},{3,1},{4,6},{5,7},{6,4},{7,5},{8,10},{9,11},{10,... | collective-permute-start | bytes 393224 | tf_op jit(solution)/shard_map/ppermute | solution.py:49
  113.7 10.4 %collective-permute-start.31 = (bf16[128,256]{1,0:T(8,128)(2,1)S(1)}, bf16[128,256]{1,0:T(8,128)(2,1)S(1)}, u32[]{:S(2)}, u32[]{:S(2)}) collective-permute-start(bf16[128,256]{1,0:T(8,128)(2,1)S(1)} %get-tuple-element.183), channel_id=1, source_target_pairs={{0,8},{8,0},{16,24},{24,16},{1,9},{9,1},{17,25},{25,17},{2,10},{10... | collective-permute-start | bytes 196616 | tf_op jit(solution)/shard_map/ppermute | solution.py:49
  115.8 8.3 %collective-permute-start.32 = (bf16[128,256]{1,0:T(8,128)(2,1)S(1)}, bf16[128,256]{1,0:T(8,128)(2,1)S(1)}, u32[]{:S(2)}, u32[]{:S(2)}) collective-permute-start(bf16[128,256]{1,0:T(8,128)(2,1)S(1)} %get-tuple-element.184), channel_id=1, source_target_pairs={{0,16},{8,24},{16,0},{24,8},{1,17},{9,25},{17,1},{25,9},{2,18},{10... | collective-permute-start | bytes 196616 | tf_op jit(solution)/shard_map/ppermute | solution.py:49
  117.2 6.9 %collective-permute-start.33 = (bf16[128,256]{1,0:T(8,128)(2,1)S(1)}, bf16[128,256]{1,0:T(8,128)(2,1)S(1)}, u32[]{:S(2)}, u32[]{:S(2)}) collective-permute-start(bf16[128,256]{1,0:T(8,128)(2,1)S(1)} %get-tuple-element.185), channel_id=1, source_target_pairs={{0,24},{8,16},{16,8},{24,0},{1,25},{9,17},{17,9},{25,1},{2,26},{10... | collective-permute-start | bytes 196616 | tf_op jit(solution)/shard_map/ppermute | solution.py:49
  125.9 16.0 %collective-permute-start.42 = (bf16[8,64,256]{2,1,0:T(8,128)(2,1)S(1)}, bf16[8,64,256]{2,1,0:T(8,128)(2,1)S(1)}, u32[]{:S(2)}, u32[]{:S(2)}) collective-permute-start(bf16[8,64,256]{2,1,0:T(8,128)(2,1)S(1)} %join.12.refs_4_.refs_0_), channel_id=1, source_target_pairs={{0,4},{1,5},{2,6},{3,7},{4,0},{5,1},{6,2},{7,3},{8,12},{9,13},{10,... | collective-permute-start | bytes 786440 | tf_op jit(solution)/shard_map/ppermute | solution.py:49
  138.3 6.3 %collective-permute-start.39 = (bf16[4,64,256]{2,1,0:T(8,128)(2,1)S(1)}, bf16[4,64,256]{2,1,0:T(8,128)(2,1)S(1)}, u32[]{:S(2)}, u32[]{:S(2)}) collective-permute-start(bf16[4,64,256]{2,1,0:T(8,128)(2,1)S(1)} %join.13.refs_2_.refs_0_), channel_id=1, source_target_pairs={{0,2},{1,3},{2,0},{3,1},{4,6},{5,7},{6,4},{7,5},{8,10},{9,11},{10,... | collective-permute-start | bytes 393224 | tf_op jit(solution)/shard_map/ppermute | solution.py:49
  138.4 7.9 %collective-permute-start.40 = (bf16[4,64,256]{2,1,0:T(8,128)(2,1)S(1)}, bf16[4,64,256]{2,1,0:T(8,128)(2,1)S(1)}, u32[]{:S(2)}, u32[]{:S(2)}) collective-permute-start(bf16[4,64,256]{2,1,0:T(8,128)(2,1)S(1)} %join.13.refs_2_.refs_0_), channel_id=1, source_target_pairs={{0,4},{1,5},{2,6},{3,7},{4,0},{5,1},{6,2},{7,3},{8,12},{9,13},{10,... | collective-permute-start | bytes 393224 | tf_op jit(solution)/shard_map/ppermute | solution.py:49
  (38 other events, 406.5 us)

commit v5 on v4

--- a/solution.py
+++ b/solution.py
@@ -203,14 +203,13 @@
         base += count
 
 
-def from_chunk(values, base, group, out_ref, width):
+def from_chunk(values, out_ref, width):
     dims, starts = matrix_shapes(width, FF), packed_starts(width)
-    parts, _ = layout(width, group)
-    for j, first, rows, blocks in parts:
+    for j, first, rows, blocks in both_groups(width):
         for col in range(blocks):
             for row in range(rows):
                 at = starts[j] + row * dims[j][1] + col * width
-                place = base + first + col * rows + row
+                place = first + col * rows + row
                 out_ref[0:1, at : at + width] = values[place : place + 1, :]
 
 
@@ -223,10 +222,12 @@
     count = device_count()
     rank = lax.axis_index("img") * lax.axis_size("row") + lax.axis_index("row")
     size = matrix_ref.shape[0]
-    rows = size // count
+    rows, pad = size // count, out_ref.shape[0] // 2
     place = lax.broadcasted_iota(jnp.int32, (128, 1), 0)
-    place = jnp.where(place < rows, place + rank * rows, -1)
-    pick = (lax.broadcasted_iota(jnp.int32, (128, size), 1) == place).astype(f32).astype(bf16)
+    mine = jnp.where(place < rows, place + rank * rows, -1)
+    other = place - pad
+    other = jnp.where((other >= 0) & (other < rows), other + (rank ^ 1) * rows, mine)
+    pick = (lax.broadcasted_iota(jnp.int32, (128, size), 1) == other).astype(f32).astype(bf16)
     tall[0:size, :] = contract(pick, matrix_ref[...], 1, 0).T
 
     def body(block):
@@ -244,7 +245,12 @@
         own_rows(narrow_out.at[j], own_ref.at[index], tall)
 
 
-def wide_bases_kernel(wide_ref, wide_out, own_ref, tall, buffer, sems):
+def own_wide_kernel(wide_ref, own_ref, tall):
+    for index in range(2):
+        own_rows(wide_ref.at[index + 1], own_ref.at[index], tall)
+
+
+def wide_bases_kernel(wide_ref, wide_out, token, buffer, sems):
     count, size = wide_ref.shape[0], wide_ref.shape[1]
     rows, depth = buffer.shape[1], buffer.shape[0]
     each = size // rows
@@ -262,8 +268,7 @@
         wide_out[index // each, first : first + rows, :] = buffer[index % depth].astype(bf16)
         if index + depth < total:
             copy(index + depth).start()
-    for index in range(2):
-        own_rows(wide_out.at[index + 1], own_ref.at[index], tall)
+    token[...] = jnp.zeros_like(token)
 
 
 def join_kernel(*refs):
@@ -610,39 +615,52 @@
     return high, (value - high.astype(f32)).astype(bf16)
 
 
-def split_with_vectors_kernel(count, terms, first, *refs):
+def split_with_vectors_kernel(count, terms, first, early, *refs):
     vec_terms = 2 if first else 1
-    keep_ref, vec_ref = refs[terms + vec_terms], refs[terms + vec_terms + 1]
-    sends = refs[terms + vec_terms + 2 :]
+    early_refs = refs[terms + vec_terms : terms + vec_terms + early]
+    outs = refs[terms + vec_terms + early :]
+    rows = refs[0].shape[0]
     if first:
         total = total_of(refs[:terms])
         vec = refs[terms][...] + refs[terms + 1][...]
     else:
-        rows = refs[0].shape[0]
         total = refs[0][...]
         for ref in refs[1:terms]:
             total = total + ref[0:rows, :].astype(f32)
         vec = pair_total([refs[terms][...]] + [vector_part(ref, rows) for ref in refs[1:terms]])
     rows = total.shape[0] // count
-    keep_ref[...] = total[:rows]
+    outs[0][...] = total[:rows]
     high, rest = two_parts(vec)
-    vec_ref[...] = high.astype(f32) + rest.astype(f32)
+    outs[1][...] = high.astype(f32) + rest.astype(f32)
+    sends = outs[2:]
+    if early:
+        early_total = total_of(early_refs)
+        more = early_total.shape[0] // count
+        outs[2][...] = early_total[:more]
+        sends = outs[3:]
     for index, ref in enumerate(sends, 1):
         ref[0:rows, :] = total[index * rows : (index + 1) * rows].astype(bf16)
         ref[rows : rows + 32, :] = high
         ref[rows + 32 : rows + 64, :] = rest
+        if early:
+            ref[rows + 64 :, :] = early_total[index * more : (index + 1) * more].astype(bf16)
 
 
 def vector_part(ref, rows):
     return ref[rows : rows + 32, :].astype(f32) + ref[rows + 32 : rows + 64, :].astype(f32)
 
 
-def split_with_vectors(terms, vec_terms, count, first, after=()):
+def split_with_vectors(terms, vec_terms, early_terms, count, first, after=()):
     rows = terms[0].shape[0] // count
     width = terms[0].shape[1]
-    outs = [((rows, width), f32), ((32, width), f32)] + [((rows + 64, width), bf16)] * (count - 1)
-    body = functools.partial(split_with_vectors_kernel, count, len(terms), first)
-    return run("split_with_vectors", body, outs, list(terms) + list(vec_terms), micros=0.6, after=after)
+    more = early_terms[0].shape[0] // count if early_terms else 0
+    outs = [((rows, width), f32), ((32, width), f32)]
+    outs += [((more, width), f32)] if early_terms else []
+    outs += [((rows + 64 + more, width), bf16)] * (count - 1)
+    body = functools.partial(split_with_vectors_kernel, count, len(terms), first, len(early_terms))
+    args = list(terms) + list(vec_terms) + list(early_terms)
+    found = run("split_with_vectors", body, outs, args, micros=0.6, after=after)
+    return found[: len(outs) - count + 1], found[len(outs) - count + 1 :]
 
 
 def row_parts():
@@ -712,7 +730,8 @@
     sums_ref[13:17, :] = key_sums[...]
 
 
-def input_grad_kernel(tile_rows, dx0_ref, up_ref, down_ref, vec_ref, out_ref, frame):
+def input_grad_kernel(tile_rows, dx0_ref, up_ref, down_ref, vec_ref, out_ref, token, frame):
+    token[...] = jnp.zeros_like(token)
     moved = shifted_frame(frame, dx0_ref, up_ref, down_ref)
     total = moved[1][1:-1]
     for tap in range(9):
@@ -729,21 +748,17 @@
     return moment * (1.0 / CORRECTION) / (jnp.sqrt(square * (1.0 / CORRECTION)) + ADAM_EPS)
 
 
-def adam_kernel(base, terms, *refs):
-    first_ref, second_ref, moment_ref, square_ref, step_ref = refs[terms:]
-    total = total_of(refs[:terms])
-    at = slice(base, base + total.shape[0])
-    step_ref[...] = moments_of(total, first_ref[at, :], second_ref[at, :], moment_ref, square_ref).astype(bf16)
-
-
-def late_adam_kernel(terms, *refs):
-    (own_vec, first_ref, second_ref, vec_ref, vec_first, vec_second, vec_ema,
+def adam_kernel(terms, *refs):
+    (own_vec, own_early, first_ref, second_ref, vec_ref, vec_first, vec_second, vec_ema,
      moment_ref, square_ref, step_ref, vec_out, vec_first_out, vec_second_out, vec_ema_out) = refs[terms:]
     rows = refs[0].shape[0]
-    total = refs[0][...]
+    late, early = refs[0][...], own_early[...]
     for ref in refs[1:terms]:
-        total = total + ref[0:rows, :].astype(f32)
-    step_ref[...] = moments_of(total, first_ref[0:rows, :], second_ref[0:rows, :], moment_ref, square_ref).astype(bf16)
+        late = late + ref[0:rows, :].astype(f32)
+        early = early + ref[rows + 64 :, :].astype(f32)
+    for total, at in ((late, slice(0, rows)), (early, slice(rows, rows + early.shape[0]))):
+        step = moments_of(total, first_ref[at, :], second_ref[at, :], moment_ref.at[at, :], square_ref.at[at, :])
+        step_ref[at, :] = step.astype(bf16)
     vec = pair_total([own_vec[...]] + [vector_part(ref, rows) for ref in refs[1:terms]])
     vec = vec[0 : vec_ref.shape[0]]
     new = vec_ref[...] - VECTOR_RATE * moments_of(vec, vec_first[...], vec_second[...], vec_first_out, vec_second_out)
@@ -751,68 +766,60 @@
     vec_ema_out[...] = EMA_KEEP * vec_ema[...] + (1.0 - EMA_KEEP) * new
 
 
-def step_sides(group, width, refs, own_narrow, own_wide, second):
+def step_sides(width, chunks, own_narrow, own_wide):
     lefts = {0: (own_narrow, 0), 1: (own_narrow, 1), 2: (own_narrow, 2), 3: (own_narrow, 3), 4: (own_wide, 0), 5: (own_wide, 1)}
     found = []
-    values = refs[...].astype(f32)
-    for j, first, rows, blocks in layout(width, group)[0]:
+    values = chunks[...].astype(f32)
+    for j, first, rows, blocks in both_groups(width):
         left_ref, index = lefts[j]
         half = left_ref.shape[2] // 2
-        left = left_ref[index][:, half * second : half * (second + 1)].astype(bf16)
+        left = left_ref[index][:, 0:half].astype(bf16)
         sides = []
         for col in range(blocks):
             part = values[:, first + col * rows : first + (col + 1) * rows, :]
             sides.append(contract(left, part.reshape(half, width).astype(bf16), 1, 0))
-        found.append(sides[0] if blocks == 1 else jnp.concatenate(sides, axis=1))
+        found.append(sides)
     return found
 
 
-def right_of(j, narrow_ref, pair_ref, wide_ref):
-    return {0: narrow_ref.at[1], 1: pair_ref, 2: narrow_ref.at[4], 3: wide_ref.at[0], 4: narrow_ref.at[6], 5: narrow_ref.at[7]}[j][...]
-
-
-def update_rows(group, width, base, sides, rights, weights_ref, chunk):
-    for (j, first, rows, blocks), side in zip(layout(width, group)[0], sides):
-        full = contract(side.astype(bf16), right_of(j, *rights), 1, 1)
+def both_groups(width):
+    late, count = layout(width, LATE)
+    return late + [(j, first + count, rows, blocks) for j, first, rows, blocks in layout(width, EARLY)[0]]
+
+
+def near_kernel(width, chunks, own_narrow, own_wide, keep_ref, send_ref):
+    for (j, first, rows, blocks), sides in zip(both_groups(width), step_sides(width, chunks, own_narrow, own_wide)):
+        pad = sides[0].shape[0] // 2
+        for col, side in enumerate(sides):
+            at = slice(first + col * rows, first + (col + 1) * rows)
+            keep_ref[at, :] = side[0:rows]
+            send_ref[at, :] = side[pad : pad + rows]
+
+
+def finish_kernel(
+    width, keep_ref, got_ref, narrow_ref, pair_ref, wide_ref, weights_ref, ema_ref, weights_out, ema_out, chunk
+):
+    rights = {0: narrow_ref.at[1], 1: pair_ref, 2: narrow_ref.at[4], 3: wide_ref.at[0], 4: narrow_ref.at[6], 5: narrow_ref.at[7]}
+    sides = keep_ref[...] + got_ref[...]
+    for j, first, rows, blocks in both_groups(width):
+        parts = [sides[first + col * rows : first + (col + 1) * rows] for col in range(blocks)]
+        side = parts[0] if blocks == 1 else jnp.concatenate(parts, axis=1)
+        if rows < 8:
+            side = jnp.concatenate([side, jnp.zeros((8 - rows, side.shape[1]), f32)], axis=0)
+        full = contract(side.astype(bf16), rights[j][...], 1, 1)
         for col in range(blocks):
-            start = first + col * rows
-            old = weights_ref[base + start : base + start + rows, :]
+            at = slice(first + col * rows, first + (col + 1) * rows)
+            old = weights_ref[at, :]
             piece = full[0:rows, col * width : (col + 1) * width]
-            chunk[start : start + rows, :] = old - MATRIX_RATES[j] * (piece + WEIGHT_DECAY * old)
-
-
-def early_finish_kernel(
-    width, late_near, early_near, early_far, own_narrow, own_wide, narrow_ref, pair_ref, wide_ref,
-    weights_ref, late_first, late_second, early_first, early_second,
-    new_ref, first_out, second_out, *late_sides,
-):
-    near = step_sides(EARLY, width, early_near, own_narrow, own_wide, 0)
-    far = step_sides(EARLY, width, early_far, own_narrow, own_wide, 1)
-    sides = [a + b for a, b in zip(near, far)]
-    base = layout(width, LATE)[1]
-    update_rows(EARLY, width, base, sides, (narrow_ref, pair_ref, wide_ref), weights_ref, new_ref)
-    for late, early, out in ((late_first, early_first, first_out), (late_second, early_second, second_out)):
-        from_chunk(late, 0, LATE, out, width)
-        from_chunk(early, 0, EARLY, out, width)
-    for ref, side in zip(late_sides, step_sides(LATE, width, late_near, own_narrow, own_wide, 0)):
-        ref[...] = side
-
-
-def finish_kernel(
-    width, late_far, reduce_side, keyval_side, query_side, out_side, early_new, own_narrow, own_wide, narrow_ref, pair_ref, wide_ref,
-    weights_ref, ema_ref, weights_out, ema_out, chunk,
-):
-    far = step_sides(LATE, width, late_far, own_narrow, own_wide, 1)
-    near = (reduce_side, keyval_side, query_side, out_side)
-    sides = [a[...] + b for a, b in zip(near, far)]
-    split = layout(width, LATE)[1]
-    update_rows(LATE, width, 0, sides, (narrow_ref, pair_ref, wide_ref), weights_ref, chunk)
-    chunk[split:, :] = early_new[...]
-    from_chunk(chunk, 0, LATE, weights_out, width)
-    from_chunk(chunk, split, EARLY, weights_out, width)
+            chunk[at, :] = old - MATRIX_RATES[j] * (piece + WEIGHT_DECAY * old)
+    from_chunk(chunk, weights_out, width)
     chunk[...] = EMA_KEEP * ema_ref[...] + (1.0 - EMA_KEEP) * chunk[...]
-    from_chunk(chunk, 0, LATE, ema_out, width)
-    from_chunk(chunk, split, EARLY, ema_out, width)
+    from_chunk(chunk, ema_out, width)
+
+
+def packed_moments_kernel(width, moment_ref, square_ref, first_out, second_out):
+    from_chunk(moment_ref, first_out, width)
+    from_chunk(square_ref, second_out, width)
 
 
 def on_device(
@@ -872,12 +879,12 @@
         micros=1.3,
         after=[line],
     )
-    wide, own_wide = run(
+    wide, wide_done = run(
         "wide_bases",
         wide_bases_kernel,
-        [((3, FF, FF), bf16), ((2, max(16, FF // shards), FF), f32)],
+        [((3, FF, FF), bf16), ((8, 128), f32)],
         [basis_wide],
-        scratch=[((2 * FF, 128), f32), ((12, width, FF), f32)],
+        scratch=[((12, width, FF), f32)],
         micros=6.0,
         mib=48,
         raw=(0,),
@@ -887,7 +894,7 @@
     all_near = line
     for axis, stride, size in gather_groups:
         pieces = [all_near] + [swap(all_near, axis, j * stride) for j in range(1, size)]
-        all_near = join(pieces, after=[own_wide, vec])
+        all_near = join(pieces, after=[wide_done, vec])
     all_far = swap(all_near, "row", 1)
     w_reduce, w_keyval, w_query, w_out, blocks, c, kn, own_kv = run(
         "keys",
@@ -909,7 +916,7 @@
     narrow, narrow_turned, pair, own_narrow = run(
         "narrow_bases",
         narrow_bases_kernel,
-        [((8, width, width), bf16), ((4, width, width), bf16), ((2 * width, 2 * width), bf16), ((4, 16, width), f32)],
+        [((8, width, width), bf16), ((4, width, width), bf16), ((2 * width, 2 * width), bf16), ((4, 32, width), f32)],
         [basis_narrow, basis_pair],
         scratch=[((2 * width, 128), f32)],
         micros=1.5,
@@ -1037,7 +1044,6 @@
         after=[token, old_chunk],
     )
     late_got = swap(late_send, "row", 1)
-    token = early_pair([dc])
     dx0, head, tail, vec_grads = run(
         "cells_back",
         functools.partial(cells_back_kernel, rows, cols),
@@ -1048,88 +1054,68 @@
         ],
         scratch=[frame],
         micros=2.0,
-        after=[token],
     )
     vec_terms = [vec_grads, swap(vec_grads, "row", 1)]
     grad_up, grad_down = border(head, tail)
-    while place < len(pairs):
-        token = early_pair()
+    while place < len(pairs) - (lines.bit_length() - 1):
+        early_pair([dc])
     late_terms = [late_keep.reshape(-1, width), late_got.reshape(-1, width)]
-
-    def late_stage(part, first, after):
-        nonlocal late_terms, vec_terms
-        axis, stride, size = part
-        keep, own_vec, *sends = split_with_vectors(late_terms, vec_terms, size, first, after)
-        late_terms = [keep] + [swap(x, axis, j * stride) for j, x in enumerate(sends, 1)]
-        vec_terms = [own_vec]
-        return keep
-
-    token = late_stage(xy_parts[0], True, [token])
-    early_first, early_second, early_step = run(
+    early_keep, early_got = [t.reshape(-1, width) for t in early_terms]
+    parts = xy_parts + [img_part]
+    for index, (axis, stride, size) in enumerate(parts):
+        riders = [early_keep, early_got] if index == len(parts) - 1 else []
+        keeps, sends = split_with_vectors(late_terms, vec_terms, riders, size, index == 0, [dx0])
+        late_terms = [keeps[0]] + [swap(x, axis, j * stride) for j, x in enumerate(sends, 1)]
+        vec_terms = [keeps[1]]
+    moments, squares, step, new_vectors, vec_moment, vec_square, new_vec_ema = run(
         "adam",
-        functools.partial(adam_kernel, late_rows, 2),
-        [((early_rows, width), f32), ((early_rows, width), f32), ((early_rows, width), bf16)],
-        [t.reshape(early_rows, width) for t in early_terms] + [first_chunk, second_chunk],
-        micros=0.6,
-        after=[token],
-    )
-    for part in xy_parts[1:]:
-        late_stage(part, False, [])
-    steps_pairs = one_by_one(xy_parts + [img_part])[::-1]
-    steps = early_step[None]
-
-    def steps_pair(after=()):
-        nonlocal steps
-        axis, stride, _ = steps_pairs.pop(0)
-        steps = join([steps, swap(steps, axis, stride)], after)
-        return steps
-
-    token = late_stage(img_part, False, [steps_pair()])
-    (grad_input,) = run(
+        functools.partial(adam_kernel, len(late_terms)),
+        [((chunk, width), f32), ((chunk, width), f32), ((chunk, width), bf16)] + [(vectors.shape, f32)] * 4,
+        late_terms + vec_terms + [keeps[2], first_chunk, second_chunk, vec, vec_first, vec_second, vec_ema],
+        micros=0.8,
+    )
+    step_near = join([step[None]] + [swap(step, "img", j)[None] for j in range(1, lines)])
+    (own_wide,) = run(
+        "own_wide",
+        own_wide_kernel,
+        [((2, 2 * max(16, FF // shards), FF), f32)],
+        [wide],
+        scratch=[((2 * FF, 128), f32)],
+        micros=1.5,
+        after=[step_near],
+    )
+    grad_input, input_done = run(
         "input_grad",
         functools.partial(input_grad_kernel, rows),
-        [((tokens, width), f32)],
+        [((tokens, width), f32), ((8, 128), f32)],
         [dx0, grad_up, grad_down, vec],
         scratch=[frame],
         micros=1.5,
-        after=[token],
-    )
-    late_first, late_second, late_step, new_vectors, vec_moment, vec_square, new_vec_ema = run(
-        "late_adam",
-        functools.partial(late_adam_kernel, len(late_terms)),
-        [((late_rows, width), f32), ((late_rows, width), f32), ((late_rows, width), bf16)] + [(vectors.shape, f32)] * 4,
-        late_terms + vec_terms + [first_chunk, second_chunk, vec, vec_first, vec_second, vec_ema],
-        micros=0.8,
-        after=[steps_pair(), grad_input],
-    )
-    step_near = late_step[None]
-    after = [late_step]
-    for axis, stride, size in [img_part] + gather_groups:
+        after=[own_wide],
+    )
+    for axis, stride, size in gather_groups:
         pieces = [step_near] + [swap(step_near, axis, j * stride) for j in range(1, size)]
-        step_near = join(pieces, [steps_pair(after)] if steps_pairs else [])
-        after = [step_near]
-    while steps_pairs:
-        steps_pair()
-    step_far = swap(step_near, "row", 1)
-    steps_near, steps_far = steps, swap(steps, "row", 1)
-
-    early_new, new_first, new_second, *late_sides = run(
-        "early_finish",
-        functools.partial(early_finish_kernel, width),
-        [((early_rows, width), f32), ((1, per), f32), ((1, per), f32)]
-        + [((own_wide.shape[1], width), f32)]
-        + [((own_narrow.shape[1], cols_of * width), f32) for cols_of in (2, 1, 1)],
-        [
-            step_near, steps_near, steps_far, own_narrow, own_wide, narrow, pair, wide,
-            old_chunk, late_first, late_second, early_first, early_second,
-        ],
+        step_near = join(pieces, [input_done])
+    side_keep, side_send = run(
+        "near",
+        functools.partial(near_kernel, width),
+        [((chunk, width), f32), ((chunk, width), f32)],
+        [step_near, own_narrow, own_wide],
         micros=2.0,
+    )
+    side_got = swap(side_send, "row", 1)
+    new_first, new_second = run(
+        "packed_moments",
+        functools.partial(packed_moments_kernel, width),
+        [((1, per), f32), ((1, per), f32)],
+        [moments, squares],
+        after=[side_keep],
     )
     new_weights, new_ema = run(
         "finish",
         functools.partial(finish_kernel, width),
         [((1, per), f32)] * 2,
-        [step_far, *late_sides, early_new, own_narrow, own_wide, narrow, pair, wide, old_chunk, ema_chunk],
+        [side_keep, side_got, narrow, pair, wide, old_chunk, ema_chunk],
         scratch=[((chunk, width), f32)],
         micros=1.5,
     )

time: 150 us -> 140 us (0.933)
  starting transfers between devices: 54.7 us -> 46.4 us
    ppermute x41 -> x34, starting transfers between devices: 49.5 us -> 41 us  [swap(): return lax.ppermute(x, axis, [(i, i ^ step) for i in range(count)])]
    ppermute x41 -> x34, waiting for transfers between devices: 43.5 us -> 45.1 us  [swap(): return lax.ppermute(x, axis, [(i, i ^ step) for i in range(count)])]
    pallas_call x34 -> x29, Pallas kernels: 43.7 us -> 43.6 us  [run(): pl.pallas_call(without, out_shape=tuple((jax.ShapeDtypeStruct(shape, dtyp...]
  transfers between devices with their start and end apart: 45 -> 38, of which waited for: 21 -> 19; matrix products, arithmetic and copies ran while one was open for 1% -> 1% of each run, Pallas kernels for 18% -> 18%
where the time goes in v5:
time: 140 us
  waiting for transfers between devices  46.6 us (33%)
  starting transfers between devices  46.4 us (33%)
  Pallas kernels  43.6 us (31%)
  local copies, waits for them, and re-layouts  1.8 us (1%)
    ppermute x34, waiting for transfers between devices, swap(): return lax.ppermute(x, axis, [(i, i ^ step) for i in range(count)])  45.1 us
    pallas_call x29, Pallas kernels, run(): pl.pallas_call(without, out_shape=tuple((jax.ShapeDtypeStruct(shape, dtyp...  43.6 us
    ppermute x34, starting transfers between devices, swap(): return lax.ppermute(x, axis, [(i, i ^ step) for i in range(count)])  41 us
    ppermute x2, starting transfers between devices, border(): lax.ppermute(head, 'row', [(i + 1, i) for i in range(ranks - 1)])  2.85 us
  transfers between devices with their start and end apart: 38, of which 19 were waited for; matrix products, arithmetic and copies ran while one was open for 1% of the time, Pallas kernels for 18%

profile of v5, /device:TPU:0, one launch (start us, length us, event | category | flops | bytes accessed | tf_op | source)
XLA Modules:
  0.0 140.2 jit_solution(660416487920880806)
XLA Ops:
  1.6 3.1 %collective-permute-start.2 = (bf16[128,256]{1,0:T(8,128)(2,1)S(1)}, bf16[128,256]{1,0:T(8,128)(2,1)S(1)}, u32[]{:S(2)}, u32[]{:S(2)}) collective-permute-start(bf16[128,256]{1,0:T(8,128)(2,1)S(1)} %pack.1), channel_id=1, source_target_pairs={{0,8},{8,0},{16,24},{24,16},{1,9},{9,1},{17,25},{25,17},{2,10},{10... | collective-permute-start | bytes 196616 | tf_op jit(solution)/shard_map/ppermute | solution.py:49
  4.7 2.6 %collective-permute-start.3 = (bf16[128,256]{1,0:T(8,128)(2,1)S(1)}, bf16[128,256]{1,0:T(8,128)(2,1)S(1)}, u32[]{:S(2)}, u32[]{:S(2)}) collective-permute-start(bf16[128,256]{1,0:T(8,128)(2,1)S(1)} %pack.1), channel_id=1, source_target_pairs={{0,16},{8,24},{16,0},{24,8},{1,17},{9,25},{17,1},{25,9},{2,18},{10... | collective-permute-start | bytes 196616 | tf_op jit(solution)/shard_map/ppermute | solution.py:49
  7.3 4.7 %collective-permute-done.3 = bf16[128,256]{1,0:T(8,128)(2,1)S(1)} collective-permute-done((bf16[128,256]{1,0:T(8,128)(2,1)S(1)}, bf16[128,256]{1,0:T(8,128)(2,1)S(1)}, u32[]{:S(2)}, u32[]{:S(2)}) %collective-permute-start.3) | collective-permute-done | bytes 65568 | tf_op jit(solution)/shard_map/ppermute | solution.py:49
  20.6 7.4 %wide_bases.1 = (bf16[3,1024,1024]{2,1,0:T(8,128)(2,1)}, f32[8,128]{1,0:T(8,128)S(1)}) custom-call(f32[3,1024,1024]{2,1,0:T(8,128)} %refs_0_.6, bf16[4,128,256]{2,1,0:T(8,128)(2,1)S(1)} %join.4.refs_5_.refs_1_.refs_0_), custom_call_target="tpu_custom_call" | custom-call | bytes 21600000 | tf_op jit(solution)/shard_map/wide_bases/pallas_call | solution.py:91
  29.6 2.9 %collective-permute-start.8 = (bf16[16,128,256]{2,1,0:T(8,128)(2,1)S(1)}, bf16[16,128,256]{2,1,0:T(8,128)(2,1)S(1)}, u32[]{:S(2)}, u32[]{:S(2)}) collective-permute-start(bf16[16,128,256]{2,1,0:T(8,128)(2,1)S(1)} %join.5.refs_3_), channel_id=1, source_target_pairs={{0,1},{1,0},{2,3},{3,2},{4,5},{5,4},{6,7},{7,6},{8,9},{9,8},{10,11... | collective-permute-start | bytes 3145736 | tf_op jit(solution)/shard_map/ppermute | solution.py:49
  32.5 2.3 %collective-permute-done.8.refs_4_ = bf16[16,128,256]{2,1,0:T(8,128)(2,1)S(1)} collective-permute-done((bf16[16,128,256]{2,1,0:T(8,128)(2,1)S(1)}, bf16[16,128,256]{2,1,0:T(8,128)(2,1)S(1)}, u32[]{:S(2)}, u32[]{:S(2)}) %collective-permute-start.8) | collective-permute-done | bytes 1048608 | tf_op jit(solution)/shard_map/ppermute | solution.py:49
  35.7 2.1 %collective-permute-start.9 = (bf16[112,512]{1,0:T(8,128)(2,1)S(1)}, bf16[112,512]{1,0:T(8,128)(2,1)S(1)}, u32[]{:S(2)}, u32[]{:S(2)}) collective-permute-start(bf16[112,512]{1,0:T(8,128)(2,1)S(1)} %get-tuple-element.106.refs_2_), channel_id=1, source_target_pairs={{0,2},{1,3},{2,0},{3,1},{4,6},{5,7},{6,4},{7,5},{8,10},{9,11},{10,... | collective-permute-start | bytes 344072 | tf_op jit(solution)/shard_map/ppermute | solution.py:49
  41.2 2.9 %collective-permute-done.10 = bf16[112,512]{1,0:T(8,128)(2,1)S(1)} collective-permute-done((bf16[112,512]{1,0:T(8,128)(2,1)S(1)}, bf16[112,512]{1,0:T(8,128)(2,1)S(1)}, u32[]{:S(2)}, u32[]{:S(2)}) %collective-permute-start.10) | collective-permute-done | bytes 114720 | tf_op jit(solution)/shard_map/ppermute | solution.py:49
  47.6 7.5 %attend.1 = (bf16[448,256]{1,0:T(8,128)(2,1)S(1)}, bf16[896,256]{1,0:T(8,128)(2,1)S(1)}, bf16[896,256]{1,0:T(8,128)(2,1)S(1)}, f32[448,256]{1,0:T(8,128)S(1)}, f32[448,128]{1,0:T(8,128)S(1)}) custom-call(bf16[448,256]{1,0:T(8,128)(2,1)S(1)} %get-tuple-element.101.refs_1_.refs_0_.refs_7_, bf16[256,256]{1,0:T(8,128)(2,1)S(1)} %get-tuple-element.105.refs_1_.refs_4_, ...), custom_call_target="tpu_custom_call" | custom-call | bytes 28800000 | tf_op jit(solution)/shard_map/attend/pallas_call | solution.py:91
  55.1 3.3 %feed.1 = (bf16[448,256]{1,0:T(8,128)(2,1)}, bf16[448,256]{1,0:T(8,128)(2,1)S(1)}, f32[448,256]{1,0:T(8,128)S(1)}, f32[256,1024]{1,0:T(8,128)S(1)}, f32[256,1024...) custom-call(f32[448,256]{1,0:T(8,128)S(1)} %get-tuple-element.109.refs_0_.refs_4_, ...), custom_call_target="tpu_custom_call" | custom-call | bytes 12600000 | tf_op jit(solution)/shard_map/feed/pallas_call | solution.py:91
  58.5 1.8 %early_turn.1 = (f32[16,64,256]{2,1,0:T(8,128)S(1)}, f32[16,64,256]{2,1,0:T(8,128)S(1)}) custom-call(f32[256,1024]{1,0:T(8,128)S(1)} %get-tuple-element.118.refs_0_, f32[256,1024]{1,0:T(8,128)S(1)} %get-tuple-element.119.refs_1_, bf16[4,256,256]{2,1,0:T(8,128)(2,1)S(1)} %get-tuple-element.120.refs_2_.refs_3_.refs_9_, ...), custom_call_target="tpu_custom_call" | custom-call | bytes 7200000 | tf_op jit(solution)/shard_map/early_turn/pallas_call | solution.py:91
  60.6 4.5 %attend_back.2 = (bf16[448,128]{1,0:T(8,128)(2,1)S(1)}, f32[448,256]{1,0:T(8,128)S(1)}, f32[448,256]{1,0:T(8,128)S(1)}, f32[256,128]{1,0:T(8,128)S(1)}, f32[1,128]{1,0:T(1,128)S(1)}) custom-call(bf16[448,256]{1,0:T(8,128)(2,1)S(1)} %get-tuple-element.113.refs_0_, bf16[896,256]{1,0:T(8,128)(2,1)S(1)} %get-tuple-element.114.refs_1_, ...), custom_call_target="tpu_custom_call" | custom-call | bytes 18000000 | tf_op jit(solution)/shard_map/attend_back/pallas_call | solution.py:91
  65.7 4.5 %attend_back.3 = (bf16[448,128]{1,0:T(8,128)(2,1)S(1)}, f32[448,256]{1,0:T(8,128)S(1)}, f32[448,256]{1,0:T(8,128)S(1)}, f32[256,128]{1,0:T(8,128)S(1)}, f32[1,128]{1,0:T(1,128)S(1)}) custom-call(bf16[448,256]{1,0:T(8,128)(2,1)S(1)} %get-tuple-element.113.refs_0_, bf16[896,256]{1,0:T(8,128)(2,1)S(1)} %get-tuple-element.114.refs_1_, ...), custom_call_target="tpu_custom_call" | custom-call | bytes 18000000 | tf_op jit(solution)/shard_map/attend_back/pallas_call | solution.py:91
  77.3 4.8 %collective-permute-done.19.refs_1_ = bf16[8,64,256]{2,1,0:T(8,128)(2,1)S(1)} collective-permute-done((bf16[8,64,256]{2,1,0:T(8,128)(2,1)S(1)}, bf16[8,64,256]{2,1,0:T(8,128)(2,1)S(1)}, u32[]{:S(2)}, u32[]{:S(2)}) %collective-permute-start.19) | collective-permute-done | bytes 262176 | tf_op jit(solution)/shard_map/ppermute | solution.py:49
  82.2 1.8 %collective-permute-done.17.refs_2_ = bf16[112,512]{1,0:T(8,128)(2,1)S(1)} collective-permute-done((bf16[112,512]{1,0:T(8,128)(2,1)S(1)}, bf16[112,512]{1,0:T(8,128)(2,1)S(1)}, u32[]{:S(2)}, u32[]{:S(2)}) %collective-permute-start.17) | collective-permute-done | bytes 114720 | tf_op jit(solution)/shard_map/ppermute | solution.py:49
  84.0 1.8 %keys_back.1 = (f32[16,64,256]{2,1,0:T(8,128)S(1)}, f32[16,64,256]{2,1,0:T(8,128)S(1)}, bf16[112,256]{1,0:T(8,128)(2,1)S(1)}, f32[4,256]{1,0:T(4,128)S(1)}) custom-call(f32[112,512]{1,0:T(8,128)S(1)} %get-tuple-element.133.refs_5_.refs_2_.refs_1_.refs_0_, bf16[112,512]{1,0:T(8,128)(2,1)S(1)} %collective-permute-done.16.refs_1_, ...), custom_call_target="tpu_custom_call" | custom-call | bytes 7200000 | tf_op jit(solution)/shard_map/keys_back/pallas_call | solution.py:91
  89.9 1.7 %collective-permute-start.25 = (bf16[320,256]{1,0:T(8,128)(2,1)S(1)}, bf16[320,256]{1,0:T(8,128)(2,1)S(1)}, u32[]{:S(2)}, u32[]{:S(2)}) collective-permute-start(bf16[320,256]{1,0:T(8,128)(2,1)S(1)} %get-tuple-element.164), channel_id=1, source_target_pairs={{0,4},{1,5},{2,6},{3,7},{4,0},{5,1},{6,2},{7,3},{8,12},{9,13},{10,... | collective-permute-start | bytes 491528 | tf_op jit(solution)/shard_map/ppermute | solution.py:49
  93.4 8.7 %collective-permute-done.27 = bf16[4,64,256]{2,1,0:T(8,128)(2,1)S(1)} collective-permute-done((bf16[4,64,256]{2,1,0:T(8,128)(2,1)S(1)}, bf16[4,64,256]{2,1,0:T(8,128)(2,1)S(1)}, u32[]{:S(2)}, u32[]{:S(2)}) %collective-permute-start.27) | collective-permute-done | bytes 131104 | tf_op jit(solution)/shard_map/ppermute | solution.py:49
  102.3 2.3 %collective-permute-start.29 = (bf16[192,256]{1,0:T(8,128)(2,1)S(1)}, bf16[192,256]{1,0:T(8,128)(2,1)S(1)}, u32[]{:S(2)}, u32[]{:S(2)}) collective-permute-start(bf16[192,256]{1,0:T(8,128)(2,1)S(1)} %get-tuple-element.170), channel_id=1, source_target_pairs={{0,16},{8,24},{16,0},{24,8},{1,17},{9,25},{17,1},{25,9},{2,18},{10... | collective-permute-start | bytes 294920 | tf_op jit(solution)/shard_map/ppermute | solution.py:49
  104.6 2.0 %collective-permute-start.30 = (bf16[192,256]{1,0:T(8,128)(2,1)S(1)}, bf16[192,256]{1,0:T(8,128)(2,1)S(1)}, u32[]{:S(2)}, u32[]{:S(2)}) collective-permute-start(bf16[192,256]{1,0:T(8,128)(2,1)S(1)} %get-tuple-element.171), channel_id=1, source_target_pairs={{0,24},{8,16},{16,8},{24,0},{1,25},{9,17},{17,9},{25,1},{2,26},{10... | collective-permute-start | bytes 294920 | tf_op jit(solution)/shard_map/ppermute | solution.py:49
  107.8 5.0 %collective-permute-done.29.refs_2_ = bf16[192,256]{1,0:T(8,128)(2,1)S(1)} collective-permute-done((bf16[192,256]{1,0:T(8,128)(2,1)S(1)}, bf16[192,256]{1,0:T(8,128)(2,1)S(1)}, u32[]{:S(2)}, u32[]{:S(2)}) %collective-permute-start.29) | collective-permute-done | bytes 98336 | tf_op jit(solution)/shard_map/ppermute | solution.py:49
  118.5 4.2 %collective-permute-done.32 = bf16[128,256]{1,0:T(8,128)(2,1)S(1)} collective-permute-done((bf16[128,256]{1,0:T(8,128)(2,1)S(1)}, bf16[128,256]{1,0:T(8,128)(2,1)S(1)}, u32[]{:S(2)}, u32[]{:S(2)}) %collective-permute-start.32) | collective-permute-done | bytes 65568 | tf_op jit(solution)/shard_map/ppermute | solution.py:49
  133.2 2.2 %collective-permute-done.35.refs_2_ = bf16[4,128,256]{2,1,0:T(8,128)(2,1)S(1)} collective-permute-done((bf16[4,128,256]{2,1,0:T(8,128)(2,1)S(1)}, bf16[4,128,256]{2,1,0:T(8,128)(2,1)S(1)}, u32[]{:S(2)}, u32[]{:S(2)}) %collective-permute-start.35) | collective-permute-done | bytes 262176 | tf_op jit(solution)/shard_map/ppermute | solution.py:49
  135.7 1.8 %collective-permute-start.37 = (f32[128,256]{1,0:T(8,128)S(1)}, f32[128,256]{1,0:T(8,128)S(1)}, u32[]{:S(2)}, u32[]{:S(2)}) collective-permute-start(f32[128,256]{1,0:T(8,128)S(1)} %get-tuple-element.180), channel_id=1, source_target_pairs={{0,1},{1,0},{2,3},{3,2},{4,5},{5,4},{6,7},{7,6},{8,9},{9,8},{10,11... | collective-permute-start | bytes 393224 | tf_op jit(solution)/shard_map/ppermute | solution.py:49
  (120 shorter events, 52.9 us)
Async XLA Ops:
  4.7 7.3 %collective-permute-start.3 = (bf16[128,256]{1,0:T(8,128)(2,1)S(1)}, bf16[128,256]{1,0:T(8,128)(2,1)S(1)}, u32[]{:S(2)}, u32[]{:S(2)}) collective-permute-start(bf16[128,256]{1,0:T(8,128)(2,1)S(1)} %pack.1), channel_id=1, source_target_pairs={{0,16},{8,24},{16,0},{24,8},{1,17},{9,25},{17,1},{25,9},{2,18},{10... | collective-permute-start | bytes 196616 | tf_op jit(solution)/shard_map/ppermute | solution.py:49
  13.4 16.1 %collective-permute-start.5 = (bf16[4,128,256]{2,1,0:T(8,128)(2,1)S(1)}, bf16[4,128,256]{2,1,0:T(8,128)(2,1)S(1)}, u32[]{:S(2)}, u32[]{:S(2)}) collective-permute-start(bf16[4,128,256]{2,1,0:T(8,128)(2,1)S(1)} %join.4.refs_5_.refs_1_.refs_0_), channel_id=1, source_target_pairs={{0,2},{1,3},{2,0},{3,1},{4,6},{5,7},{6,4},{7,5},{8,10},{9,11},{10,... | collective-permute-start | bytes 786440 | tf_op jit(solution)/shard_map/ppermute | solution.py:49
  15.0 14.5 %collective-permute-start.6 = (bf16[4,128,256]{2,1,0:T(8,128)(2,1)S(1)}, bf16[4,128,256]{2,1,0:T(8,128)(2,1)S(1)}, u32[]{:S(2)}, u32[]{:S(2)}) collective-permute-start(bf16[4,128,256]{2,1,0:T(8,128)(2,1)S(1)} %join.4.refs_5_.refs_1_.refs_0_), channel_id=1, source_target_pairs={{0,4},{1,5},{2,6},{3,7},{4,0},{5,1},{6,2},{7,3},{8,12},{9,13},{10,... | collective-permute-start | bytes 786440 | tf_op jit(solution)/shard_map/ppermute | solution.py:49
  16.5 13.0 %collective-permute-start.7 = (bf16[4,128,256]{2,1,0:T(8,128)(2,1)S(1)}, bf16[4,128,256]{2,1,0:T(8,128)(2,1)S(1)}, u32[]{:S(2)}, u32[]{:S(2)}) collective-permute-start(bf16[4,128,256]{2,1,0:T(8,128)(2,1)S(1)} %join.4.refs_5_.refs_1_.refs_0_), channel_id=1, source_target_pairs={{0,6},{1,7},{2,4},{3,5},{4,2},{5,3},{6,0},{7,1},{8,14},{9,15},{10,... | collective-permute-start | bytes 786440 | tf_op jit(solution)/shard_map/ppermute | solution.py:49
  17.7 10.3 %collective-permute-start = (bf16[64,256]{1,0:T(8,128)(2,1)S(1)}, bf16[64,256]{1,0:T(8,128)(2,1)S(1)}, u32[]{:S(2)}, u32[]{:S(2)}) collective-permute-start(bf16[64,256]{1,0:T(8,128)(2,1)S(1)} %get-tuple-element.193), channel_id=1, source_target_pairs={{0,1},{1,2},{2,3},{3,4},{4,5},{5,6},{6,7},{8,9},{9,10},{10,11},{11... | collective-permute-start | bytes 98312 | tf_op jit(solution)/shard_map/ppermute | solution.py:857
  19.1 9.0 %collective-permute-start.1 = (bf16[64,256]{1,0:T(8,128)(2,1)S(1)}, bf16[64,256]{1,0:T(8,128)(2,1)S(1)}, u32[]{:S(2)}, u32[]{:S(2)}) collective-permute-start(bf16[64,256]{1,0:T(8,128)(2,1)S(1)} %get-tuple-element.192), channel_id=1, source_target_pairs={{1,0},{2,1},{3,2},{4,3},{5,4},{6,5},{7,6},{9,8},{10,9},{11,10},{12... | collective-permute-start | bytes 98312 | tf_op jit(solution)/shard_map/ppermute | solution.py:858
  37.7 6.4 %collective-permute-start.10 = (bf16[112,512]{1,0:T(8,128)(2,1)S(1)}, bf16[112,512]{1,0:T(8,128)(2,1)S(1)}, u32[]{:S(2)}, u32[]{:S(2)}) collective-permute-start(bf16[112,512]{1,0:T(8,128)(2,1)S(1)} %get-tuple-element.106.refs_2_), channel_id=1, source_target_pairs={{0,4},{1,5},{2,6},{3,7},{4,0},{5,1},{6,2},{7,3},{8,12},{9,13},{10,... | collective-permute-start | bytes 344072 | tf_op jit(solution)/shard_map/ppermute | solution.py:49
  39.2 6.5 %collective-permute-start.11 = (bf16[112,512]{1,0:T(8,128)(2,1)S(1)}, bf16[112,512]{1,0:T(8,128)(2,1)S(1)}, u32[]{:S(2)}, u32[]{:S(2)}) collective-permute-start(bf16[112,512]{1,0:T(8,128)(2,1)S(1)} %get-tuple-element.106.refs_2_), channel_id=1, source_target_pairs={{0,6},{1,7},{2,4},{3,5},{4,2},{5,3},{6,0},{7,1},{8,14},{9,15},{10,... | collective-permute-start | bytes 344072 | tf_op jit(solution)/shard_map/ppermute | solution.py:49
  65.1 6.3 %collective-permute-start.14 = (f32[448,256]{1,0:T(8,128)S(1)}, f32[448,256]{1,0:T(8,128)S(1)}, u32[]{:S(2)}, u32[]{:S(2)}) collective-permute-start(f32[448,256]{1,0:T(8,128)S(1)} %get-tuple-element.130), channel_id=1, source_target_pairs={{0,1},{1,0},{2,3},{3,2},{4,5},{5,4},{6,7},{7,6},{8,9},{9,8},{10,11... | collective-permute-start | bytes 1376264 | tf_op jit(solution)/shard_map/ppermute | solution.py:49
  70.5 11.6 %collective-permute-start.19 = (bf16[8,64,256]{2,1,0:T(8,128)(2,1)S(1)}, bf16[8,64,256]{2,1,0:T(8,128)(2,1)S(1)}, u32[]{:S(2)}, u32[]{:S(2)}) collective-permute-start(bf16[8,64,256]{2,1,0:T(8,128)(2,1)S(1)} %get-tuple-element.146), channel_id=1, source_target_pairs={{0,4},{1,5},{2,6},{3,7},{4,0},{5,1},{6,2},{7,3},{8,12},{9,13},{10,... | collective-permute-start | bytes 786440 | tf_op jit(solution)/shard_map/ppermute | solution.py:49
  72.3 9.9 %collective-permute-start.16 = (bf16[112,512]{1,0:T(8,128)(2,1)S(1)}, bf16[112,512]{1,0:T(8,128)(2,1)S(1)}, u32[]{:S(2)}, u32[]{:S(2)}) collective-permute-start(bf16[112,512]{1,0:T(8,128)(2,1)S(1)} %get-tuple-element.134), channel_id=1, source_target_pairs={{0,2},{1,3},{2,0},{3,1},{4,6},{5,7},{6,4},{7,5},{8,10},{9,11},{10,... | collective-permute-start | bytes 344072 | tf_op jit(solution)/shard_map/ppermute | solution.py:49
  73.0 11.0 %collective-permute-start.17 = (bf16[112,512]{1,0:T(8,128)(2,1)S(1)}, bf16[112,512]{1,0:T(8,128)(2,1)S(1)}, u32[]{:S(2)}, u32[]{:S(2)}) collective-permute-start(bf16[112,512]{1,0:T(8,128)(2,1)S(1)} %get-tuple-element.135), channel_id=1, source_target_pairs={{0,4},{1,5},{2,6},{3,7},{4,0},{5,1},{6,2},{7,3},{8,12},{9,13},{10,... | collective-permute-start | bytes 344072 | tf_op jit(solution)/shard_map/ppermute | solution.py:49
  74.7 9.3 %collective-permute-start.18 = (bf16[112,512]{1,0:T(8,128)(2,1)S(1)}, bf16[112,512]{1,0:T(8,128)(2,1)S(1)}, u32[]{:S(2)}, u32[]{:S(2)}) collective-permute-start(bf16[112,512]{1,0:T(8,128)(2,1)S(1)} %get-tuple-element.136), channel_id=1, source_target_pairs={{0,6},{1,7},{2,4},{3,5},{4,2},{5,3},{6,0},{7,1},{8,14},{9,15},{10,... | collective-permute-start | bytes 344072 | tf_op jit(solution)/shard_map/ppermute | solution.py:49
  89.2 12.9 %collective-permute-start.24 = (bf16[320,256]{1,0:T(8,128)(2,1)S(1)}, bf16[320,256]{1,0:T(8,128)(2,1)S(1)}, u32[]{:S(2)}, u32[]{:S(2)}) collective-permute-start(bf16[320,256]{1,0:T(8,128)(2,1)S(1)} %get-tuple-element.163), channel_id=1, source_target_pairs={{0,2},{1,3},{2,0},{3,1},{4,6},{5,7},{6,4},{7,5},{8,10},{9,11},{10,... | collective-permute-start | bytes 491528 | tf_op jit(solution)/shard_map/ppermute | solution.py:49
  89.9 12.2 %collective-permute-start.25 = (bf16[320,256]{1,0:T(8,128)(2,1)S(1)}, bf16[320,256]{1,0:T(8,128)(2,1)S(1)}, u32[]{:S(2)}, u32[]{:S(2)}) collective-permute-start(bf16[320,256]{1,0:T(8,128)(2,1)S(1)} %get-tuple-element.164), channel_id=1, source_target_pairs={{0,4},{1,5},{2,6},{3,7},{4,0},{5,1},{6,2},{7,3},{8,12},{9,13},{10,... | collective-permute-start | bytes 491528 | tf_op jit(solution)/shard_map/ppermute | solution.py:49
  91.6 10.5 %collective-permute-start.26 = (bf16[320,256]{1,0:T(8,128)(2,1)S(1)}, bf16[320,256]{1,0:T(8,128)(2,1)S(1)}, u32[]{:S(2)}, u32[]{:S(2)}) collective-permute-start(bf16[320,256]{1,0:T(8,128)(2,1)S(1)} %get-tuple-element.165), channel_id=1, source_target_pairs={{0,6},{1,7},{2,4},{3,5},{4,2},{5,3},{6,0},{7,1},{8,14},{9,15},{10,... | collective-permute-start | bytes 491528 | tf_op jit(solution)/shard_map/ppermute | solution.py:49
  92.8 9.3 %collective-permute-start.27 = (bf16[4,64,256]{2,1,0:T(8,128)(2,1)S(1)}, bf16[4,64,256]{2,1,0:T(8,128)(2,1)S(1)}, u32[]{:S(2)}, u32[]{:S(2)}) collective-permute-start(bf16[4,64,256]{2,1,0:T(8,128)(2,1)S(1)} %get-tuple-element.167), channel_id=1, source_target_pairs={{0,2},{1,3},{2,0},{3,1},{4,6},{5,7},{6,4},{7,5},{8,10},{9,11},{10,... | collective-permute-start | bytes 393224 | tf_op jit(solution)/shard_map/ppermute | solution.py:49
  102.3 10.5 %collective-permute-start.29 = (bf16[192,256]{1,0:T(8,128)(2,1)S(1)}, bf16[192,256]{1,0:T(8,128)(2,1)S(1)}, u32[]{:S(2)}, u32[]{:S(2)}) collective-permute-start(bf16[192,256]{1,0:T(8,128)(2,1)S(1)} %get-tuple-element.170), channel_id=1, source_target_pairs={{0,16},{8,24},{16,0},{24,8},{1,17},{9,25},{17,1},{25,9},{2,18},{10... | collective-permute-start | bytes 294920 | tf_op jit(solution)/shard_map/ppermute | solution.py:49
  104.6 8.2 %collective-permute-start.30 = (bf16[192,256]{1,0:T(8,128)(2,1)S(1)}, bf16[192,256]{1,0:T(8,128)(2,1)S(1)}, u32[]{:S(2)}, u32[]{:S(2)}) collective-permute-start(bf16[192,256]{1,0:T(8,128)(2,1)S(1)} %get-tuple-element.171), channel_id=1, source_target_pairs={{0,24},{8,16},{16,8},{24,0},{1,25},{9,17},{17,9},{25,1},{2,26},{10... | collective-permute-start | bytes 294920 | tf_op jit(solution)/shard_map/ppermute | solution.py:49
  115.1 7.6 %collective-permute-start.32 = (bf16[128,256]{1,0:T(8,128)(2,1)S(1)}, bf16[128,256]{1,0:T(8,128)(2,1)S(1)}, u32[]{:S(2)}, u32[]{:S(2)}) collective-permute-start(bf16[128,256]{1,0:T(8,128)(2,1)S(1)} %get-tuple-element.176), channel_id=1, source_target_pairs={{0,16},{8,24},{16,0},{24,8},{1,17},{9,25},{17,1},{25,9},{2,18},{10... | collective-permute-start | bytes 196616 | tf_op jit(solution)/shard_map/ppermute | solution.py:49
  116.4 6.3 %collective-permute-start.33 = (bf16[128,256]{1,0:T(8,128)(2,1)S(1)}, bf16[128,256]{1,0:T(8,128)(2,1)S(1)}, u32[]{:S(2)}, u32[]{:S(2)}) collective-permute-start(bf16[128,256]{1,0:T(8,128)(2,1)S(1)} %get-tuple-element.176), channel_id=1, source_target_pairs={{0,24},{8,16},{16,8},{24,0},{1,25},{9,17},{17,9},{25,1},{2,26},{10... | collective-permute-start | bytes 196616 | tf_op jit(solution)/shard_map/ppermute | solution.py:49
  122.7 10.4 %collective-permute-start.34 = (bf16[4,128,256]{2,1,0:T(8,128)(2,1)S(1)}, bf16[4,128,256]{2,1,0:T(8,128)(2,1)S(1)}, u32[]{:S(2)}, u32[]{:S(2)}) collective-permute-start(bf16[4,128,256]{2,1,0:T(8,128)(2,1)S(1)} %join.6.refs_1_.refs_0_), channel_id=1, source_target_pairs={{0,2},{1,3},{2,0},{3,1},{4,6},{5,7},{6,4},{7,5},{8,10},{9,11},{10,... | collective-permute-start | bytes 786440 | tf_op jit(solution)/shard_map/ppermute | solution.py:49
  123.4 11.9 %collective-permute-start.35 = (bf16[4,128,256]{2,1,0:T(8,128)(2,1)S(1)}, bf16[4,128,256]{2,1,0:T(8,128)(2,1)S(1)}, u32[]{:S(2)}, u32[]{:S(2)}) collective-permute-start(bf16[4,128,256]{2,1,0:T(8,128)(2,1)S(1)} %join.6.refs_1_.refs_0_), channel_id=1, source_target_pairs={{0,4},{1,5},{2,6},{3,7},{4,0},{5,1},{6,2},{7,3},{8,12},{9,13},{10,... | collective-permute-start | bytes 786440 | tf_op jit(solution)/shard_map/ppermute | solution.py:49
  125.1 10.2 %collective-permute-start.36 = (bf16[4,128,256]{2,1,0:T(8,128)(2,1)S(1)}, bf16[4,128,256]{2,1,0:T(8,128)(2,1)S(1)}, u32[]{:S(2)}, u32[]{:S(2)}) collective-permute-start(bf16[4,128,256]{2,1,0:T(8,128)(2,1)S(1)} %join.6.refs_1_.refs_0_), channel_id=1, source_target_pairs={{0,6},{1,7},{2,4},{3,5},{4,2},{5,3},{6,0},{7,1},{8,14},{9,15},{10,... | collective-permute-start | bytes 786440 | tf_op jit(solution)/shard_map/ppermute | solution.py:49
  (30 other events, 356.1 us)

commit v6 on v5

--- a/solution.py
+++ b/solution.py
@@ -218,36 +218,41 @@
         to_chunk(rows_ref, ref, width, index)
 
 
-def own_rows(matrix_ref, out_ref, tall):
-    count = device_count()
-    rank = lax.axis_index("img") * lax.axis_size("row") + lax.axis_index("row")
+def left_block(matrix_ref, out_ref):
+    lines, ranks = lax.axis_size("img"), lax.axis_size("row")
     size = matrix_ref.shape[0]
-    rows, pad = size // count, out_ref.shape[0] // 2
-    place = lax.broadcasted_iota(jnp.int32, (128, 1), 0)
-    mine = jnp.where(place < rows, place + rank * rows, -1)
-    other = place - pad
-    other = jnp.where((other >= 0) & (other < rows), other + (rank ^ 1) * rows, mine)
-    pick = (lax.broadcasted_iota(jnp.int32, (128, size), 1) == other).astype(f32).astype(bf16)
-    tall[0:size, :] = contract(pick, matrix_ref[...], 1, 0).T
-
-    def body(block):
-        put_rows(tall, size + block * rows, slice(None), get_rows(tall, source(block) * rows, rows, slice(None)))
-
-    each_block(count, body)
-    out_ref[...] = tall[size : 2 * size, :].T[0 : out_ref.shape[0]]
-
-
-def narrow_bases_kernel(narrow_ref, pair_ref, narrow_out, turned_out, pair_out, own_ref, tall):
+    rows = size // (lines * ranks)
+    img, row = lax.axis_index("img"), lax.axis_index("row")
+
+    def one_hot(count, axis, start_of):
+        shape = (count * rows, size) if axis == 0 else (size, count * rows)
+        place = lax.broadcasted_iota(jnp.int32, tuple(n if d == axis else 1 for d, n in enumerate(shape)), axis)
+        block = place >> (rows.bit_length() - 1)
+        target = start_of(block) * rows + (place & (rows - 1))
+        return (lax.broadcasted_iota(jnp.int32, shape, 1 - axis) == target).astype(f32).astype(bf16)
+
+    def owner(block):
+        rel = jnp.zeros_like(block)
+        for stride, count in reversed(rel_digits()):
+            rel = rel + (block & (count - 1)) * stride
+            block = block >> (count.bit_length() - 1)
+        return img * ranks + (rel ^ row)
+
+    mine = contract(one_hot(ranks, 0, owner), matrix_ref[...], 1, 0).astype(bf16)
+    out_ref[...] = contract(mine, one_hot(lines, 1, lambda block: (block ^ img) * ranks + row), 1, 0)
+
+
+def narrow_bases_kernel(narrow_ref, pair_ref, narrow_out, turned_out, pair_out, own_ref):
     narrow_out[...] = narrow_ref[...].astype(bf16)
     pair_out[...] = pair_ref[...].astype(bf16)
     for index, j in enumerate((0, 2, 3, 5)):
         turned_out[index] = narrow_ref[j].T.astype(bf16)
-        own_rows(narrow_out.at[j], own_ref.at[index], tall)
-
-
-def own_wide_kernel(wide_ref, own_ref, tall):
+        left_block(narrow_out.at[j], own_ref.at[index])
+
+
+def own_wide_kernel(wide_ref, own_ref):
     for index in range(2):
-        own_rows(wide_ref.at[index + 1], own_ref.at[index], tall)
+        left_block(wide_ref.at[index + 1], own_ref.at[index])
 
 
 def wide_bases_kernel(wide_ref, wide_out, token, buffer, sems):
@@ -430,17 +435,19 @@
         cols = head_columns(head)
         mine = lane // 32 == head % 4
         keys = jnp.where(mine, k_ref[:, cols], 0)
-        values = jnp.where(mine, v_ref[:, cols], 0)
+        ones = jnp.where(lane // 32 == (head + 2) % 4, 1.0, 0.0).astype(bf16)
+        values = jnp.where(mine, v_ref[:, cols], ones)
 
         def block(start):
             rows = pl.ds(start, step)
             scores = contract(q_ref[rows, cols], keys, 1, 1) * scale + mask
             top = jnp.max(scores, axis=1, keepdims=True)
-            exponent = jnp.exp2(scores - top)
-            total = jnp.sum(exponent, axis=1, keepdims=True)
-            probs = (exponent * (1.0 / total)).astype(bf16)
-            out = contract(probs, values, 1, 0)
-            o_ref[rows, cols] = jnp.where(mine, out, o_ref[rows, cols])
+            out = contract(jnp.exp2(scores - top).astype(bf16), values, 1, 0)
+            if isinstance(head, int):
+                total = out[:, (head + 2) % 4 * 32 : (head + 2) % 4 * 32 + 1]
+            else:
+                total = jnp.sum(jnp.where(lane == (head + 2) % 4 * 32, out, 0.0), axis=1, keepdims=True)
+            o_ref[rows, cols] = jnp.where(mine, out * (1.0 / total), o_ref[rows, cols])
             log_ref[rows, :] = jnp.where(lane == head, top + jnp.log2(total), log_ref[rows, :])
 
         over_blocks(block, tokens, step)
@@ -615,52 +622,44 @@
     return high, (value - high.astype(f32)).astype(bf16)
 
 
-def split_with_vectors_kernel(count, terms, first, early, *refs):
-    vec_terms = 2 if first else 1
-    early_refs = refs[terms + vec_terms : terms + vec_terms + early]
-    outs = refs[terms + vec_terms + early :]
-    rows = refs[0].shape[0]
+def sum_three(keeps, pieces):
+    late, vec, early = [ref[...] for ref in keeps]
+    rows, more = late.shape[0], vec.shape[0]
+    vecs = [vec]
+    for ref in pieces:
+        late = late + ref[0:rows, :].astype(f32)
+        vecs.append(ref[rows : rows + more, :].astype(f32))
+        early = early + ref[rows + more :, :].astype(f32)
+    return late, pair_total(vecs), early
+
+
+def split_three_kernel(count, pieces, first, *refs):
     if first:
-        total = total_of(refs[:terms])
-        vec = refs[terms][...] + refs[terms + 1][...]
+        late, vec, early = [refs[k][...] + refs[k + 1][...] for k in (0, 2, 4)]
+        outs = refs[6:]
     else:
-        total = refs[0][...]
-        for ref in refs[1:terms]:
-            total = total + ref[0:rows, :].astype(f32)
-        vec = pair_total([refs[terms][...]] + [vector_part(ref, rows) for ref in refs[1:terms]])
-    rows = total.shape[0] // count
-    outs[0][...] = total[:rows]
-    high, rest = two_parts(vec)
-    outs[1][...] = high.astype(f32) + rest.astype(f32)
-    sends = outs[2:]
-    if early:
-        early_total = total_of(early_refs)
-        more = early_total.shape[0] // count
-        outs[2][...] = early_total[:more]
-        sends = outs[3:]
-    for index, ref in enumerate(sends, 1):
-        ref[0:rows, :] = total[index * rows : (index + 1) * rows].astype(bf16)
-        ref[rows : rows + 32, :] = high
-        ref[rows + 32 : rows + 64, :] = rest
-        if early:
-            ref[rows + 64 :, :] = early_total[index * more : (index + 1) * more].astype(bf16)
-
-
-def vector_part(ref, rows):
-    return ref[rows : rows + 32, :].astype(f32) + ref[rows + 32 : rows + 64, :].astype(f32)
-
-
-def split_with_vectors(terms, vec_terms, early_terms, count, first, after=()):
-    rows = terms[0].shape[0] // count
-    width = terms[0].shape[1]
-    more = early_terms[0].shape[0] // count if early_terms else 0
-    outs = [((rows, width), f32), ((32, width), f32)]
-    outs += [((more, width), f32)] if early_terms else []
-    outs += [((rows + 64 + more, width), bf16)] * (count - 1)
-    body = functools.partial(split_with_vectors_kernel, count, len(terms), first, len(early_terms))
-    args = list(terms) + list(vec_terms) + list(early_terms)
-    found = run("split_with_vectors", body, outs, args, micros=0.6, after=after)
-    return found[: len(outs) - count + 1], found[len(outs) - count + 1 :]
+        late, vec, early = sum_three(refs[:3], refs[3 : 3 + pieces])
+        outs = refs[3 + pieces :]
+    rows, more, rest = late.shape[0] // count, vec.shape[0], early.shape[0] // count
+    low = vec.astype(bf16)
+    outs[0][...] = late[:rows]
+    outs[1][...] = low.astype(f32)
+    outs[2][...] = early[:rest]
+    for index in range(1, count):
+        ref = outs[2 + index]
+        ref[0:rows, :] = late[index * rows : (index + 1) * rows].astype(bf16)
+        ref[rows : rows + more, :] = low
+        ref[rows + more :, :] = early[index * rest : (index + 1) * rest].astype(bf16)
+
+
+def split_three(args, count, first, after=()):
+    late, vec, early = args[0:6:2] if first else args[0:3]
+    rows, more, rest, width = late.shape[0] // count, vec.shape[0], early.shape[0] // count, late.shape[1]
+    outs = [((rows, width), f32), ((more, width), f32), ((rest, width), f32)]
+    outs += [((rows + more + rest, width), bf16)] * (count - 1)
+    body = functools.partial(split_three_kernel, count, len(args) - 3, first)
+    found = run("split_three", body, outs, list(args), micros=0.6, after=after)
+    return list(found[:3]), found[3:]
 
 
 def row_parts():
@@ -749,58 +748,44 @@
 
 
 def adam_kernel(terms, *refs):
-    (own_vec, own_early, first_ref, second_ref, vec_ref, vec_first, vec_second, vec_ema,
+    (first_ref, second_ref, vec_ref, vec_first, vec_second, vec_ema,
      moment_ref, square_ref, step_ref, vec_out, vec_first_out, vec_second_out, vec_ema_out) = refs[terms:]
-    rows = refs[0].shape[0]
-    late, early = refs[0][...], own_early[...]
-    for ref in refs[1:terms]:
-        late = late + ref[0:rows, :].astype(f32)
-        early = early + ref[rows + 64 :, :].astype(f32)
+    late, vec, early = sum_three(refs[:3], refs[3:terms])
+    rows = late.shape[0]
     for total, at in ((late, slice(0, rows)), (early, slice(rows, rows + early.shape[0]))):
         step = moments_of(total, first_ref[at, :], second_ref[at, :], moment_ref.at[at, :], square_ref.at[at, :])
         step_ref[at, :] = step.astype(bf16)
-    vec = pair_total([own_vec[...]] + [vector_part(ref, rows) for ref in refs[1:terms]])
     vec = vec[0 : vec_ref.shape[0]]
     new = vec_ref[...] - VECTOR_RATE * moments_of(vec, vec_first[...], vec_second[...], vec_first_out, vec_second_out)
     vec_out[...] = new
     vec_ema_out[...] = EMA_KEEP * vec_ema[...] + (1.0 - EMA_KEEP) * new
 
 
-def step_sides(width, chunks, own_narrow, own_wide):
-    lefts = {0: (own_narrow, 0), 1: (own_narrow, 1), 2: (own_narrow, 2), 3: (own_narrow, 3), 4: (own_wide, 0), 5: (own_wide, 1)}
-    found = []
-    values = chunks[...].astype(f32)
-    for j, first, rows, blocks in both_groups(width):
-        left_ref, index = lefts[j]
-        half = left_ref.shape[2] // 2
-        left = left_ref[index][:, 0:half].astype(bf16)
-        sides = []
-        for col in range(blocks):
-            part = values[:, first + col * rows : first + (col + 1) * rows, :]
-            sides.append(contract(left, part.reshape(half, width).astype(bf16), 1, 0))
-        found.append(sides)
-    return found
-
-
 def both_groups(width):
     late, count = layout(width, LATE)
     return late + [(j, first + count, rows, blocks) for j, first, rows, blocks in layout(width, EARLY)[0]]
 
 
-def near_kernel(width, chunks, own_narrow, own_wide, keep_ref, send_ref):
-    for (j, first, rows, blocks), sides in zip(both_groups(width), step_sides(width, chunks, own_narrow, own_wide)):
-        pad = sides[0].shape[0] // 2
-        for col, side in enumerate(sides):
+def products_kernel(width, chunks, own_narrow, own_wide, keep_ref, send_ref):
+    lefts = {0: (own_narrow, 0), 1: (own_narrow, 1), 2: (own_narrow, 2), 3: (own_narrow, 3), 4: (own_wide, 0), 5: (own_wide, 1)}
+    half = keep_ref.shape[0]
+    values = chunks[...].astype(f32)
+    for j, first, rows, blocks in both_groups(width):
+        left = lefts[j][0][lefts[j][1]].astype(bf16)
+        for col in range(blocks):
             at = slice(first + col * rows, first + (col + 1) * rows)
-            keep_ref[at, :] = side[0:rows]
-            send_ref[at, :] = side[pad : pad + rows]
+            part = values[:, at, :].reshape(left.shape[1], width).astype(bf16)
+            side = contract(left, part, 1, 0).reshape(2 * half, rows, width)
+            keep_ref[:, at, :] = side[:half]
+            send_ref[:, at, :] = side[half:]
 
 
 def finish_kernel(
-    width, keep_ref, got_ref, narrow_ref, pair_ref, wide_ref, weights_ref, ema_ref, weights_out, ema_out, chunk
+    width, terms, *refs
 ):
+    narrow_ref, pair_ref, wide_ref, weights_ref, ema_ref, weights_out, ema_out, chunk = refs[terms:]
     rights = {0: narrow_ref.at[1], 1: pair_ref, 2: narrow_ref.at[4], 3: wide_ref.at[0], 4: narrow_ref.at[6], 5: narrow_ref.at[7]}
-    sides = keep_ref[...] + got_ref[...]
+    sides = total_of(refs[:terms])
     for j, first, rows, blocks in both_groups(width):
         parts = [sides[first + col * rows : first + (col + 1) * rows] for col in range(blocks)]
         side = parts[0] if blocks == 1 else jnp.concatenate(parts, axis=1)
@@ -817,7 +802,8 @@
     from_chunk(chunk, ema_out, width)
 
 
-def packed_moments_kernel(width, moment_ref, square_ref, first_out, second_out):
+def packed_moments_kernel(width, moment_ref, square_ref, first_out, second_out, token):
+    token[...] = jnp.zeros_like(token)
     from_chunk(moment_ref, first_out, width)
     from_chunk(square_ref, second_out, width)
 
@@ -916,9 +902,13 @@
     narrow, narrow_turned, pair, own_narrow = run(
         "narrow_bases",
         narrow_bases_kernel,
-        [((8, width, width), bf16), ((4, width, width), bf16), ((2 * width, 2 * width), bf16), ((4, 32, width), f32)],
+        [
+            ((8, width, width), bf16),
+            ((4, width, width), bf16),
+            ((2 * width, 2 * width), bf16),
+            ((4, width // lines, width // ranks), f32),
+        ],
         [basis_narrow, basis_pair],
-        scratch=[((2 * width, 128), f32)],
         micros=1.5,
         after=[own_kv],
     )
@@ -953,17 +943,6 @@
         mib=12,
         micros=3.5,
     )
-    half = (shards // 2, early_rows, width)
-    early_keep, early_send = run(
-        "early_turn",
-        early_turn_kernel,
-        [(half, f32), (half, f32)],
-        [up_grad, down_grad, narrow_turned, narrow, wide],
-        scratch=[((width, FF), f32), ((FF, width), f32)],
-        mib=10,
-        micros=2.0,
-    )
-
     def back(group, after):
         return run(
             "attend_back",
@@ -989,31 +968,35 @@
             after=after,
         )
 
-    pairs = one_by_one(xy_parts + [img_part])
-    place = 0
-
-    def early_pair(after=()):
-        nonlocal early_terms, place
-        keep, send = split_sum(early_terms, 2, after=after)
-        early_terms = [keep, swap(send, *pairs[place][:2])]
-        place += 1
-        return keep
-
-    early_terms = [early_keep, swap(early_send, "row", 1)]
-    dq_left, left_keep, left_send, query_left, left_sum = back(0, [early_keep])
-    token = early_pair([query_left])
+    dq_left, left_keep, left_send, query_left, left_sum = back(0, [dx1])
     left_got = swap(left_send, "row", 1)
-    dq_right, right_keep, right_send, query_right, right_sum = back(1, [token])
+    dq_right, right_keep, right_send, query_right, right_sum = back(1, [query_left])
     right_got = swap(right_send, "row", 1)
+    half = (shards // 2, early_rows, width)
+    early_keep, early_send = run(
+        "early_turn",
+        early_turn_kernel,
+        [(half, f32), (half, f32)],
+        [up_grad, down_grad, narrow_turned, narrow, wide],
+        scratch=[((width, FF), f32), ((FF, width), f32)],
+        mib=10,
+        micros=2.0,
+        after=[query_right],
+    )
+    early_got = swap(early_send, "row", 1)
     axis, stride, size = xy_parts[0]
-    dkv_keep, *dkv_sends = run(
+    dkv_keep, *sends = run(
         "split_heads",
         functools.partial(split_heads_kernel, size),
         [((keys // 2 // size, 2 * width), f32)] + [((keys // 2 // size, 2 * width), bf16)] * (size - 1),
         [left_keep, left_got, right_keep, right_got],
         micros=0.8,
-    )
-    token = early_pair([dkv_keep])
+        after=[early_keep],
+    )
+    dkv_terms = [dkv_keep] + [swap(x, axis, j * stride) for j, x in enumerate(sends, 1)]
+    for axis, stride, size in xy_parts[1:]:
+        keep, *sends = split_sum(dkv_terms, size)
+        dkv_terms = [keep] + [swap(x, axis, j * stride) for j, x in enumerate(sends, 1)]
     old_chunk, ema_chunk, first_chunk, second_chunk = run(
         "moments",
         functools.partial(moments_kernel, width),
@@ -1021,10 +1004,6 @@
         [jnp.concatenate([weights, weight_ema, first_moment, second_moment], axis=0)],
         after=[dkv_keep],
     )
-    dkv_terms = [dkv_keep] + [swap(x, axis, j * stride) for j, x in enumerate(dkv_sends, 1)]
-    for axis, stride, size in xy_parts[1:]:
-        keep, *sends = split_sum(dkv_terms, size)
-        dkv_terms = [keep] + [swap(x, axis, j * stride) for j, x in enumerate(sends, 1)]
     query_turn, out_turn = run(
         "middle_turn",
         middle_turn_kernel,
@@ -1041,7 +1020,7 @@
         list(dkv_terms) + [kn, c, vec, w_keyval, blocks, narrow_turned, narrow, pair, wide, query_turn, out_turn],
         scratch=[((4 * width, width), f32), ((width, 2 * width), f32)],
         micros=2.0,
-        after=[token, old_chunk],
+        after=[old_chunk],
     )
     late_got = swap(late_send, "row", 1)
     dx0, head, tail, vec_grads = run(
@@ -1055,35 +1034,12 @@
         scratch=[frame],
         micros=2.0,
     )
-    vec_terms = [vec_grads, swap(vec_grads, "row", 1)]
     grad_up, grad_down = border(head, tail)
-    while place < len(pairs) - (lines.bit_length() - 1):
-        early_pair([dc])
-    late_terms = [late_keep.reshape(-1, width), late_got.reshape(-1, width)]
-    early_keep, early_got = [t.reshape(-1, width) for t in early_terms]
-    parts = xy_parts + [img_part]
-    for index, (axis, stride, size) in enumerate(parts):
-        riders = [early_keep, early_got] if index == len(parts) - 1 else []
-        keeps, sends = split_with_vectors(late_terms, vec_terms, riders, size, index == 0, [dx0])
-        late_terms = [keeps[0]] + [swap(x, axis, j * stride) for j, x in enumerate(sends, 1)]
-        vec_terms = [keeps[1]]
-    moments, squares, step, new_vectors, vec_moment, vec_square, new_vec_ema = run(
-        "adam",
-        functools.partial(adam_kernel, len(late_terms)),
-        [((chunk, width), f32), ((chunk, width), f32), ((chunk, width), bf16)] + [(vectors.shape, f32)] * 4,
-        late_terms + vec_terms + [keeps[2], first_chunk, second_chunk, vec, vec_first, vec_second, vec_ema],
-        micros=0.8,
-    )
-    step_near = join([step[None]] + [swap(step, "img", j)[None] for j in range(1, lines)])
-    (own_wide,) = run(
-        "own_wide",
-        own_wide_kernel,
-        [((2, 2 * max(16, FF // shards), FF), f32)],
-        [wide],
-        scratch=[((2 * FF, 128), f32)],
-        micros=1.5,
-        after=[step_near],
-    )
+    args = [late_keep, late_got, vec_grads, swap(vec_grads, "row", 1), early_keep, early_got]
+    args = [x.reshape(-1, width) for x in args]
+    for index, (axis, stride, size) in enumerate(xy_parts + [img_part]):
+        keeps, sends = split_three(args, size, index == 0, [grad_up, grad_down] if index else [])
+        args = keeps + [swap(x, axis, j * stride) for j, x in enumerate(sends, 1)]
     grad_input, input_done = run(
         "input_grad",
         functools.partial(input_grad_kernel, rows),
@@ -1091,31 +1047,49 @@
         [dx0, grad_up, grad_down, vec],
         scratch=[frame],
         micros=1.5,
-        after=[own_wide],
-    )
-    for axis, stride, size in gather_groups:
-        pieces = [step_near] + [swap(step_near, axis, j * stride) for j in range(1, size)]
-        step_near = join(pieces, [input_done])
-    side_keep, side_send = run(
-        "near",
-        functools.partial(near_kernel, width),
-        [((chunk, width), f32), ((chunk, width), f32)],
-        [step_near, own_narrow, own_wide],
-        micros=2.0,
-    )
-    side_got = swap(side_send, "row", 1)
-    new_first, new_second = run(
+        after=[keeps[1]],
+    )
+    moments, squares, step, new_vectors, vec_moment, vec_square, new_vec_ema = run(
+        "adam",
+        functools.partial(adam_kernel, len(args)),
+        [((chunk, width), f32), ((chunk, width), f32), ((chunk, width), bf16)] + [(vectors.shape, f32)] * 4,
+        args + [first_chunk, second_chunk, vec, vec_first, vec_second, vec_ema],
+        micros=0.8,
+        after=[input_done],
+    )
+    (own_wide,) = run(
+        "own_wide",
+        own_wide_kernel,
+        [((2, FF // lines, FF // ranks), f32)],
+        [wide],
+        micros=1.5,
+        after=[step],
+    )
+    new_first, new_second, packed_done = run(
         "packed_moments",
         functools.partial(packed_moments_kernel, width),
-        [((1, per), f32), ((1, per), f32)],
+        [((1, per), f32), ((1, per), f32), ((8, 128), f32)],
         [moments, squares],
-        after=[side_keep],
-    )
+        after=[own_wide],
+    )
+    steps = join([step[None]] + [swap(step, "img", j)[None] for j in range(1, lines)], [packed_done])
+    half = (ranks // 2, chunk, width)
+    keep, send = run(
+        "products",
+        functools.partial(products_kernel, width),
+        [(half, f32), (half, f32)],
+        [steps, own_narrow, own_wide],
+        micros=1.0,
+    )
+    terms = [keep.reshape(-1, width), swap(send, "row", 1).reshape(-1, width)]
+    for index, (axis, stride, size) in enumerate(xy_parts):
+        part, *sends = split_sum(terms, size)
+        terms = [part] + [swap(x, axis, j * stride) for j, x in enumerate(sends, 1)]
     new_weights, new_ema = run(
         "finish",
-        functools.partial(finish_kernel, width),
+        functools.partial(finish_kernel, width, len(terms)),
         [((1, per), f32)] * 2,
-        [side_keep, side_got, narrow, pair, wide, old_chunk, ema_chunk],
+        list(terms) + [narrow, pair, wide, old_chunk, ema_chunk],
         scratch=[((chunk, width), f32)],
         micros=1.5,
     )

time: 140 us -> 130 us (0.929)
  waiting for transfers between devices: 46.6 us -> 40.3 us
  starting transfers between devices: 46.4 us -> 43 us
    ppermute x34 -> x32, waiting for transfers between devices: 45.1 us -> 37 us  [swap(): return lax.ppermute(x, axis, [(i, i ^ step) for i in range(count)])]
    ppermute x34 -> x32, starting transfers between devices: 41 us -> 37.5 us  [swap(): return lax.ppermute(x, axis, [(i, i ^ step) for i in range(count)])]
    ppermute x2, waiting for transfers between devices: 1.48 us -> 3.3 us  [border(): lax.ppermute(head, 'row', [(i + 1, i) for i in range(ranks - 1)])]
    pallas_call x29 -> x27, Pallas kernels: 43.6 us -> 42.7 us  [run(): pl.pallas_call(without, out_shape=tuple((jax.ShapeDtypeStruct(shape, dtyp...]
  transfers between devices with their start and end apart: 38 -> 36, of which waited for: 19 -> 21; matrix products, arithmetic and copies ran while one was open for 1% -> 1% of each run, Pallas kernels for 18% -> 15%
where the time goes in v6:
time: 130 us; the launch traced here: 129 us
  starting transfers between devices  43 us (33%)
  Pallas kernels  42.7 us (33%)
  waiting for transfers between devices  40.3 us (31%)
  local copies, waits for them, and re-layouts  1.8 us (1%)
    pallas_call x27, Pallas kernels, run(): pl.pallas_call(without, out_shape=tuple((jax.ShapeDtypeStruct(shape, dtyp...  42.7 us
    ppermute x32, starting transfers between devices, swap(): return lax.ppermute(x, axis, [(i, i ^ step) for i in range(count)])  37.5 us
    ppermute x32, waiting for transfers between devices, swap(): return lax.ppermute(x, axis, [(i, i ^ step) for i in range(count)])  37 us
    ppermute x2, waiting for transfers between devices, border(): lax.ppermute(head, 'row', [(i + 1, i) for i in range(ranks - 1)])  3.3 us
    ppermute x2, starting transfers between devices, border(): lax.ppermute(head, 'row', [(i + 1, i) for i in range(ranks - 1)])  2.85 us
    ppermute x2, starting transfers between devices, border(): up = lax.ppermute(tail, 'row', [(i, i + 1) for i in range(ranks - 1)])  2.68 us
  transfers between devices with their start and end apart: 36, of which 21 were waited for; matrix products, arithmetic and copies ran while one was open for 1% of the time, Pallas kernels for 15%

profile of v6, /device:TPU:0, one launch (start us, length us, event | category | flops | bytes accessed | tf_op | source)
XLA Modules:
  0.0 129.5 jit_solution(6588089768299475110)
XLA Ops:
  1.6 3.1 %collective-permute-start.2 = (bf16[128,256]{1,0:T(8,128)(2,1)S(1)}, bf16[128,256]{1,0:T(8,128)(2,1)S(1)}, u32[]{:S(2)}, u32[]{:S(2)}) collective-permute-start(bf16[128,256]{1,0:T(8,128)(2,1)S(1)} %pack.1), channel_id=1, source_target_pairs={{0,8},{8,0},{16,24},{24,16},{1,9},{9,1},{17,25},{25,17},{2,10},{10... | collective-permute-start | bytes 196616 | tf_op jit(solution)/shard_map/ppermute | solution.py:49
  4.7 2.6 %collective-permute-start.3 = (bf16[128,256]{1,0:T(8,128)(2,1)S(1)}, bf16[128,256]{1,0:T(8,128)(2,1)S(1)}, u32[]{:S(2)}, u32[]{:S(2)}) collective-permute-start(bf16[128,256]{1,0:T(8,128)(2,1)S(1)} %pack.1), channel_id=1, source_target_pairs={{0,16},{8,24},{16,0},{24,8},{1,17},{9,25},{17,1},{25,9},{2,18},{10... | collective-permute-start | bytes 196616 | tf_op jit(solution)/shard_map/ppermute | solution.py:49
  7.3 4.7 %collective-permute-done.3 = bf16[128,256]{1,0:T(8,128)(2,1)S(1)} collective-permute-done((bf16[128,256]{1,0:T(8,128)(2,1)S(1)}, bf16[128,256]{1,0:T(8,128)(2,1)S(1)}, u32[]{:S(2)}, u32[]{:S(2)}) %collective-permute-start.3) | collective-permute-done | bytes 65568 | tf_op jit(solution)/shard_map/ppermute | solution.py:49
  20.6 7.4 %wide_bases.1 = (bf16[3,1024,1024]{2,1,0:T(8,128)(2,1)}, f32[8,128]{1,0:T(8,128)S(1)}) custom-call(f32[3,1024,1024]{2,1,0:T(8,128)} %refs_0_.6, bf16[4,128,256]{2,1,0:T(8,128)(2,1)S(1)} %join.3.refs_5_.refs_1_.refs_0_), custom_call_target="tpu_custom_call" | custom-call | bytes 21600000 | tf_op jit(solution)/shard_map/wide_bases/pallas_call | solution.py:91
  29.6 2.9 %collective-permute-start.8 = (bf16[16,128,256]{2,1,0:T(8,128)(2,1)S(1)}, bf16[16,128,256]{2,1,0:T(8,128)(2,1)S(1)}, u32[]{:S(2)}, u32[]{:S(2)}) collective-permute-start(bf16[16,128,256]{2,1,0:T(8,128)(2,1)S(1)} %join.4.refs_3_), channel_id=1, source_target_pairs={{0,1},{1,0},{2,3},{3,2},{4,5},{5,4},{6,7},{7,6},{8,9},{9,8},{10,11... | collective-permute-start | bytes 3145736 | tf_op jit(solution)/shard_map/ppermute | solution.py:49
  32.5 2.3 %collective-permute-done.8.refs_4_ = bf16[16,128,256]{2,1,0:T(8,128)(2,1)S(1)} collective-permute-done((bf16[16,128,256]{2,1,0:T(8,128)(2,1)S(1)}, bf16[16,128,256]{2,1,0:T(8,128)(2,1)S(1)}, u32[]{:S(2)}, u32[]{:S(2)}) %collective-permute-start.8) | collective-permute-done | bytes 1048608 | tf_op jit(solution)/shard_map/ppermute | solution.py:49
  35.7 2.1 %collective-permute-start.9 = (bf16[112,512]{1,0:T(8,128)(2,1)S(1)}, bf16[112,512]{1,0:T(8,128)(2,1)S(1)}, u32[]{:S(2)}, u32[]{:S(2)}) collective-permute-start(bf16[112,512]{1,0:T(8,128)(2,1)S(1)} %get-tuple-element.108.refs_2_), channel_id=1, source_target_pairs={{0,2},{1,3},{2,0},{3,1},{4,6},{5,7},{6,4},{7,5},{8,10},{9,11},{10,... | collective-permute-start | bytes 344072 | tf_op jit(solution)/shard_map/ppermute | solution.py:49
  41.2 2.9 %collective-permute-done.10 = bf16[112,512]{1,0:T(8,128)(2,1)S(1)} collective-permute-done((bf16[112,512]{1,0:T(8,128)(2,1)S(1)}, bf16[112,512]{1,0:T(8,128)(2,1)S(1)}, u32[]{:S(2)}, u32[]{:S(2)}) %collective-permute-start.10) | collective-permute-done | bytes 114720 | tf_op jit(solution)/shard_map/ppermute | solution.py:49
  47.6 6.3 %attend.1 = (bf16[448,256]{1,0:T(8,128)(2,1)S(1)}, bf16[896,256]{1,0:T(8,128)(2,1)S(1)}, bf16[896,256]{1,0:T(8,128)(2,1)S(1)}, f32[448,256]{1,0:T(8,128)S(1)}, f32[448,128]{1,0:T(8,128)S(1)}) custom-call(bf16[448,256]{1,0:T(8,128)(2,1)S(1)} %get-tuple-element.103.refs_1_.refs_0_.refs_7_, bf16[256,256]{1,0:T(8,128)(2,1)S(1)} %get-tuple-element.107.refs_1_.refs_4_, ...), custom_call_target="tpu_custom_call" | custom-call | bytes 28800000 | tf_op jit(solution)/shard_map/attend/pallas_call | solution.py:91
  54.0 3.3 %feed.1 = (bf16[448,256]{1,0:T(8,128)(2,1)}, bf16[448,256]{1,0:T(8,128)(2,1)S(1)}, f32[448,256]{1,0:T(8,128)S(1)}, f32[256,1024]{1,0:T(8,128)S(1)}, f32[256,1024...) custom-call(f32[448,256]{1,0:T(8,128)S(1)} %get-tuple-element.111.refs_0_.refs_4_, ...), custom_call_target="tpu_custom_call" | custom-call | bytes 12600000 | tf_op jit(solution)/shard_map/feed/pallas_call | solution.py:91
  57.2 4.6 %attend_back.2 = (bf16[448,128]{1,0:T(8,128)(2,1)S(1)}, f32[448,256]{1,0:T(8,128)S(1)}, f32[448,256]{1,0:T(8,128)S(1)}, f32[256,128]{1,0:T(8,128)S(1)}, f32[1,128]{1,0:T(1,128)S(1)}) custom-call(bf16[448,256]{1,0:T(8,128)(2,1)S(1)} %get-tuple-element.115.refs_0_, bf16[896,256]{1,0:T(8,128)(2,1)S(1)} %get-tuple-element.116.refs_1_, ...), custom_call_target="tpu_custom_call" | custom-call | bytes 18000000 | tf_op jit(solution)/shard_map/attend_back/pallas_call | solution.py:91
  61.8 4.6 %attend_back.3 = (bf16[448,128]{1,0:T(8,128)(2,1)S(1)}, f32[448,256]{1,0:T(8,128)S(1)}, f32[448,256]{1,0:T(8,128)S(1)}, f32[256,128]{1,0:T(8,128)S(1)}, f32[1,128]{1,0:T(1,128)S(1)}) custom-call(bf16[448,256]{1,0:T(8,128)(2,1)S(1)} %get-tuple-element.115.refs_0_, bf16[896,256]{1,0:T(8,128)(2,1)S(1)} %get-tuple-element.116.refs_1_, ...), custom_call_target="tpu_custom_call" | custom-call | bytes 18000000 | tf_op jit(solution)/shard_map/attend_back/pallas_call | solution.py:91
  67.1 1.8 %early_turn.1 = (f32[16,64,256]{2,1,0:T(8,128)S(1)}, f32[16,64,256]{2,1,0:T(8,128)S(1)}) custom-call(f32[256,1024]{1,0:T(8,128)S(1)} %get-tuple-element.128.refs_0_, f32[256,1024]{1,0:T(8,128)S(1)} %get-tuple-element.129.refs_1_, bf16[4,256,256]{2,1,0:T(8,128)(2,1)S(1)} %get-tuple-element.130.refs_2_.refs_3_.refs_9_, ...), custom_call_target="tpu_custom_call" | custom-call | bytes 7200000 | tf_op jit(solution)/shard_map/early_turn/pallas_call | solution.py:91
  69.8 1.7 %collective-permute-start.16 = (bf16[112,512]{1,0:T(8,128)(2,1)S(1)}, bf16[112,512]{1,0:T(8,128)(2,1)S(1)}, u32[]{:S(2)}, u32[]{:S(2)}) collective-permute-start(bf16[112,512]{1,0:T(8,128)(2,1)S(1)} %get-tuple-element.137), channel_id=1, source_target_pairs={{0,4},{1,5},{2,6},{3,7},{4,0},{5,1},{6,2},{7,3},{8,12},{9,13},{10,... | collective-permute-start | bytes 344072 | tf_op jit(solution)/shard_map/ppermute | solution.py:49
  77.2 1.8 %keys_back.1 = (f32[16,64,256]{2,1,0:T(8,128)S(1)}, f32[16,64,256]{2,1,0:T(8,128)S(1)}, bf16[112,256]{1,0:T(8,128)(2,1)S(1)}, f32[4,256]{1,0:T(4,128)S(1)}) custom-call(f32[112,512]{1,0:T(8,128)S(1)} %get-tuple-element.135.refs_5_.refs_1_.refs_0_, bf16[112,512]{1,0:T(8,128)(2,1)S(1)} %collective-permute-done.15.refs_1_, ...), custom_call_target="tpu_custom_call" | custom-call | bytes 7200000 | tf_op jit(solution)/shard_map/keys_back/pallas_call | solution.py:91
  88.8 3.3 %collective-permute-done.19.refs_7_.refs_2_ = bf16[64,256]{1,0:T(8,128)(2,1)S(1)} collective-permute-done((bf16[64,256]{1,0:T(8,128)(2,1)S(1)}, bf16[64,256]{1,0:T(8,128)(2,1)S(1)}, u32[]{:S(2)}, u32[]{:S(2)}) %collective-permute-start.19) | collective-permute-done | bytes 32800 | tf_op jit(solution)/shard_map/ppermute | solution.py:844
  92.1 5.3 %collective-permute-done.24.refs_4_ = bf16[544,256]{1,0:T(8,128)(2,1)S(1)} collective-permute-done((bf16[544,256]{1,0:T(8,128)(2,1)S(1)}, bf16[544,256]{1,0:T(8,128)(2,1)S(1)}, u32[]{:S(2)}, u32[]{:S(2)}) %collective-permute-start.24) | collective-permute-done | bytes 278560 | tf_op jit(solution)/shard_map/ppermute | solution.py:49
  98.8 2.3 %collective-permute-start.27 = (bf16[160,256]{1,0:T(8,128)(2,1)S(1)}, bf16[160,256]{1,0:T(8,128)(2,1)S(1)}, u32[]{:S(2)}, u32[]{:S(2)}) collective-permute-start(bf16[160,256]{1,0:T(8,128)(2,1)S(1)} %get-tuple-element.172), channel_id=1, source_target_pairs={{0,16},{8,24},{16,0},{24,8},{1,17},{9,25},{17,1},{25,9},{2,18},{10... | collective-permute-start | bytes 245768 | tf_op jit(solution)/shard_map/ppermute | solution.py:49
  101.2 2.0 %collective-permute-start.28 = (bf16[160,256]{1,0:T(8,128)(2,1)S(1)}, bf16[160,256]{1,0:T(8,128)(2,1)S(1)}, u32[]{:S(2)}, u32[]{:S(2)}) collective-permute-start(bf16[160,256]{1,0:T(8,128)(2,1)S(1)} %get-tuple-element.173), channel_id=1, source_target_pairs={{0,24},{8,16},{16,8},{24,0},{1,25},{9,17},{17,9},{25,1},{2,26},{10... | collective-permute-start | bytes 245768 | tf_op jit(solution)/shard_map/ppermute | solution.py:49
  104.8 3.6 %collective-permute-done.27.refs_4_ = bf16[160,256]{1,0:T(8,128)(2,1)S(1)} collective-permute-done((bf16[160,256]{1,0:T(8,128)(2,1)S(1)}, bf16[160,256]{1,0:T(8,128)(2,1)S(1)}, u32[]{:S(2)}, u32[]{:S(2)}) %collective-permute-start.27) | collective-permute-done | bytes 81952 | tf_op jit(solution)/shard_map/ppermute | solution.py:49
  118.6 1.9 %collective-permute-done.32 = f32[4,128,256]{2,1,0:T(8,128)S(1)} collective-permute-done((f32[4,128,256]{2,1,0:T(8,128)S(1)}, f32[4,128,256]{2,1,0:T(8,128)S(1)}, u32[]{:S(2)}, u32[]{:S(2)}) %collective-permute-start.32) | collective-permute-done | bytes 524320 | tf_op jit(solution)/shard_map/ppermute | solution.py:49
  120.5 1.8 %collective-permute-start.33 = (bf16[128,256]{1,0:T(8,128)(2,1)S(1)}, bf16[128,256]{1,0:T(8,128)(2,1)S(1)}, u32[]{:S(2)}, u32[]{:S(2)}) collective-permute-start(bf16[128,256]{1,0:T(8,128)(2,1)S(1)} %get-tuple-element.184), channel_id=1, source_target_pairs={{0,2},{1,3},{2,0},{3,1},{4,6},{5,7},{6,4},{7,5},{8,10},{9,11},{10,... | collective-permute-start | bytes 196616 | tf_op jit(solution)/shard_map/ppermute | solution.py:49
  122.3 1.7 %collective-permute-start.35 = (bf16[128,256]{1,0:T(8,128)(2,1)S(1)}, bf16[128,256]{1,0:T(8,128)(2,1)S(1)}, u32[]{:S(2)}, u32[]{:S(2)}) collective-permute-start(bf16[128,256]{1,0:T(8,128)(2,1)S(1)} %get-tuple-element.186), channel_id=1, source_target_pairs={{0,6},{1,7},{2,4},{3,5},{4,2},{5,3},{6,0},{7,1},{8,14},{9,15},{10,... | collective-permute-start | bytes 196616 | tf_op jit(solution)/shard_map/ppermute | solution.py:49
  124.9 2.9 %collective-permute-done.34.refs_2_ = bf16[128,256]{1,0:T(8,128)(2,1)S(1)} collective-permute-done((bf16[128,256]{1,0:T(8,128)(2,1)S(1)}, bf16[128,256]{1,0:T(8,128)(2,1)S(1)}, u32[]{:S(2)}, u32[]{:S(2)}) %collective-permute-start.34) | collective-permute-done | bytes 65568 | tf_op jit(solution)/shard_map/ppermute | solution.py:49
  (114 shorter events, 51.5 us)
Async XLA Ops:
  1.6 5.7 %collective-permute-start.2 = (bf16[128,256]{1,0:T(8,128)(2,1)S(1)}, bf16[128,256]{1,0:T(8,128)(2,1)S(1)}, u32[]{:S(2)}, u32[]{:S(2)}) collective-permute-start(bf16[128,256]{1,0:T(8,128)(2,1)S(1)} %pack.1), channel_id=1, source_target_pairs={{0,8},{8,0},{16,24},{24,16},{1,9},{9,1},{17,25},{25,17},{2,10},{10... | collective-permute-start | bytes 196616 | tf_op jit(solution)/shard_map/ppermute | solution.py:49
  4.7 7.3 %collective-permute-start.3 = (bf16[128,256]{1,0:T(8,128)(2,1)S(1)}, bf16[128,256]{1,0:T(8,128)(2,1)S(1)}, u32[]{:S(2)}, u32[]{:S(2)}) collective-permute-start(bf16[128,256]{1,0:T(8,128)(2,1)S(1)} %pack.1), channel_id=1, source_target_pairs={{0,16},{8,24},{16,0},{24,8},{1,17},{9,25},{17,1},{25,9},{2,18},{10... | collective-permute-start | bytes 196616 | tf_op jit(solution)/shard_map/ppermute | solution.py:49
  7.3 6.1 %collective-permute-start.4 = (bf16[128,256]{1,0:T(8,128)(2,1)S(1)}, bf16[128,256]{1,0:T(8,128)(2,1)S(1)}, u32[]{:S(2)}, u32[]{:S(2)}) collective-permute-start(bf16[128,256]{1,0:T(8,128)(2,1)S(1)} %pack.1), channel_id=1, source_target_pairs={{0,24},{8,16},{16,8},{24,0},{1,25},{9,17},{17,9},{25,1},{2,26},{10... | collective-permute-start | bytes 196616 | tf_op jit(solution)/shard_map/ppermute | solution.py:49
  13.4 16.1 %collective-permute-start.5 = (bf16[4,128,256]{2,1,0:T(8,128)(2,1)S(1)}, bf16[4,128,256]{2,1,0:T(8,128)(2,1)S(1)}, u32[]{:S(2)}, u32[]{:S(2)}) collective-permute-start(bf16[4,128,256]{2,1,0:T(8,128)(2,1)S(1)} %join.3.refs_5_.refs_1_.refs_0_), channel_id=1, source_target_pairs={{0,2},{1,3},{2,0},{3,1},{4,6},{5,7},{6,4},{7,5},{8,10},{9,11},{10,... | collective-permute-start | bytes 786440 | tf_op jit(solution)/shard_map/ppermute | solution.py:49
  15.0 14.5 %collective-permute-start.6 = (bf16[4,128,256]{2,1,0:T(8,128)(2,1)S(1)}, bf16[4,128,256]{2,1,0:T(8,128)(2,1)S(1)}, u32[]{:S(2)}, u32[]{:S(2)}) collective-permute-start(bf16[4,128,256]{2,1,0:T(8,128)(2,1)S(1)} %join.3.refs_5_.refs_1_.refs_0_), channel_id=1, source_target_pairs={{0,4},{1,5},{2,6},{3,7},{4,0},{5,1},{6,2},{7,3},{8,12},{9,13},{10,... | collective-permute-start | bytes 786440 | tf_op jit(solution)/shard_map/ppermute | solution.py:49
  16.5 13.0 %collective-permute-start.7 = (bf16[4,128,256]{2,1,0:T(8,128)(2,1)S(1)}, bf16[4,128,256]{2,1,0:T(8,128)(2,1)S(1)}, u32[]{:S(2)}, u32[]{:S(2)}) collective-permute-start(bf16[4,128,256]{2,1,0:T(8,128)(2,1)S(1)} %join.3.refs_5_.refs_1_.refs_0_), channel_id=1, source_target_pairs={{0,6},{1,7},{2,4},{3,5},{4,2},{5,3},{6,0},{7,1},{8,14},{9,15},{10,... | collective-permute-start | bytes 786440 | tf_op jit(solution)/shard_map/ppermute | solution.py:49
  17.7 10.3 %collective-permute-start = (bf16[64,256]{1,0:T(8,128)(2,1)S(1)}, bf16[64,256]{1,0:T(8,128)(2,1)S(1)}, u32[]{:S(2)}, u32[]{:S(2)}) collective-permute-start(bf16[64,256]{1,0:T(8,128)(2,1)S(1)} %get-tuple-element.197), channel_id=1, source_target_pairs={{0,1},{1,2},{2,3},{3,4},{4,5},{5,6},{6,7},{8,9},{9,10},{10,11},{11... | collective-permute-start | bytes 98312 | tf_op jit(solution)/shard_map/ppermute | solution.py:843
  19.1 9.0 %collective-permute-start.1 = (bf16[64,256]{1,0:T(8,128)(2,1)S(1)}, bf16[64,256]{1,0:T(8,128)(2,1)S(1)}, u32[]{:S(2)}, u32[]{:S(2)}) collective-permute-start(bf16[64,256]{1,0:T(8,128)(2,1)S(1)} %get-tuple-element.196), channel_id=1, source_target_pairs={{1,0},{2,1},{3,2},{4,3},{5,4},{6,5},{7,6},{9,8},{10,9},{11,10},{12... | collective-permute-start | bytes 98312 | tf_op jit(solution)/shard_map/ppermute | solution.py:844
  35.7 5.5 %collective-permute-start.9 = (bf16[112,512]{1,0:T(8,128)(2,1)S(1)}, bf16[112,512]{1,0:T(8,128)(2,1)S(1)}, u32[]{:S(2)}, u32[]{:S(2)}) collective-permute-start(bf16[112,512]{1,0:T(8,128)(2,1)S(1)} %get-tuple-element.108.refs_2_), channel_id=1, source_target_pairs={{0,2},{1,3},{2,0},{3,1},{4,6},{5,7},{6,4},{7,5},{8,10},{9,11},{10,... | collective-permute-start | bytes 344072 | tf_op jit(solution)/shard_map/ppermute | solution.py:49
  37.7 6.4 %collective-permute-start.10 = (bf16[112,512]{1,0:T(8,128)(2,1)S(1)}, bf16[112,512]{1,0:T(8,128)(2,1)S(1)}, u32[]{:S(2)}, u32[]{:S(2)}) collective-permute-start(bf16[112,512]{1,0:T(8,128)(2,1)S(1)} %get-tuple-element.108.refs_2_), channel_id=1, source_target_pairs={{0,4},{1,5},{2,6},{3,7},{4,0},{5,1},{6,2},{7,3},{8,12},{9,13},{10,... | collective-permute-start | bytes 344072 | tf_op jit(solution)/shard_map/ppermute | solution.py:49
  39.2 6.5 %collective-permute-start.11 = (bf16[112,512]{1,0:T(8,128)(2,1)S(1)}, bf16[112,512]{1,0:T(8,128)(2,1)S(1)}, u32[]{:S(2)}, u32[]{:S(2)}) collective-permute-start(bf16[112,512]{1,0:T(8,128)(2,1)S(1)} %get-tuple-element.108.refs_2_), channel_id=1, source_target_pairs={{0,6},{1,7},{2,4},{3,5},{4,2},{5,3},{6,0},{7,1},{8,14},{9,15},{10,... | collective-permute-start | bytes 344072 | tf_op jit(solution)/shard_map/ppermute | solution.py:49
  69.1 6.1 %collective-permute-start.15 = (bf16[112,512]{1,0:T(8,128)(2,1)S(1)}, bf16[112,512]{1,0:T(8,128)(2,1)S(1)}, u32[]{:S(2)}, u32[]{:S(2)}) collective-permute-start(bf16[112,512]{1,0:T(8,128)(2,1)S(1)} %get-tuple-element.136), channel_id=1, source_target_pairs={{0,2},{1,3},{2,0},{3,1},{4,6},{5,7},{6,4},{7,5},{8,10},{9,11},{10,... | collective-permute-start | bytes 344072 | tf_op jit(solution)/shard_map/ppermute | solution.py:49
  69.8 6.6 %collective-permute-start.16 = (bf16[112,512]{1,0:T(8,128)(2,1)S(1)}, bf16[112,512]{1,0:T(8,128)(2,1)S(1)}, u32[]{:S(2)}, u32[]{:S(2)}) collective-permute-start(bf16[112,512]{1,0:T(8,128)(2,1)S(1)} %get-tuple-element.137), channel_id=1, source_target_pairs={{0,4},{1,5},{2,6},{3,7},{4,0},{5,1},{6,2},{7,3},{8,12},{9,13},{10,... | collective-permute-start | bytes 344072 | tf_op jit(solution)/shard_map/ppermute | solution.py:49
  71.5 5.7 %collective-permute-start.17 = (bf16[112,512]{1,0:T(8,128)(2,1)S(1)}, bf16[112,512]{1,0:T(8,128)(2,1)S(1)}, u32[]{:S(2)}, u32[]{:S(2)}) collective-permute-start(bf16[112,512]{1,0:T(8,128)(2,1)S(1)} %get-tuple-element.138), channel_id=1, source_target_pairs={{0,6},{1,7},{2,4},{3,5},{4,2},{5,3},{6,0},{7,1},{8,14},{9,15},{10,... | collective-permute-start | bytes 344072 | tf_op jit(solution)/shard_map/ppermute | solution.py:49
  73.2 9.1 %collective-permute-start.22 = (f32[16,64,256]{2,1,0:T(8,128)S(1)}, f32[16,64,256]{2,1,0:T(8,128)S(1)}, u32[]{:S(2)}, u32[]{:S(2)}) collective-permute-start(f32[16,64,256]{2,1,0:T(8,128)S(1)} %get-tuple-element.160), channel_id=1, source_target_pairs={{0,1},{1,0},{2,3},{3,2},{4,5},{5,4},{6,7},{7,6},{8,9},{9,8},{10,11... | collective-permute-start | bytes 3145736 | tf_op jit(solution)/shard_map/ppermute | solution.py:49
  82.6 9.6 %collective-permute-start.23 = (bf16[544,256]{1,0:T(8,128)(2,1)S(1)}, bf16[544,256]{1,0:T(8,128)(2,1)S(1)}, u32[]{:S(2)}, u32[]{:S(2)}) collective-permute-start(bf16[544,256]{1,0:T(8,128)(2,1)S(1)} %get-tuple-element.164), channel_id=1, source_target_pairs={{0,2},{1,3},{2,0},{3,1},{4,6},{5,7},{6,4},{7,5},{8,10},{9,11},{10,... | collective-permute-start | bytes 835592 | tf_op jit(solution)/shard_map/ppermute | solution.py:49
  84.0 13.4 %collective-permute-start.24 = (bf16[544,256]{1,0:T(8,128)(2,1)S(1)}, bf16[544,256]{1,0:T(8,128)(2,1)S(1)}, u32[]{:S(2)}, u32[]{:S(2)}) collective-permute-start(bf16[544,256]{1,0:T(8,128)(2,1)S(1)} %get-tuple-element.165), channel_id=1, source_target_pairs={{0,4},{1,5},{2,6},{3,7},{4,0},{5,1},{6,2},{7,3},{8,12},{9,13},{10,... | collective-permute-start | bytes 835592 | tf_op jit(solution)/shard_map/ppermute | solution.py:49
  84.9 13.7 %collective-permute-start.25 = (bf16[544,256]{1,0:T(8,128)(2,1)S(1)}, bf16[544,256]{1,0:T(8,128)(2,1)S(1)}, u32[]{:S(2)}, u32[]{:S(2)}) collective-permute-start(bf16[544,256]{1,0:T(8,128)(2,1)S(1)} %get-tuple-element.166), channel_id=1, source_target_pairs={{0,6},{1,7},{2,4},{3,5},{4,2},{5,3},{6,0},{7,1},{8,14},{9,15},{10,... | collective-permute-start | bytes 835592 | tf_op jit(solution)/shard_map/ppermute | solution.py:49
  98.7 6.1 %collective-permute-start.26 = (bf16[160,256]{1,0:T(8,128)(2,1)S(1)}, bf16[160,256]{1,0:T(8,128)(2,1)S(1)}, u32[]{:S(2)}, u32[]{:S(2)}) collective-permute-start(bf16[160,256]{1,0:T(8,128)(2,1)S(1)} %get-tuple-element.171), channel_id=1, source_target_pairs={{0,8},{8,0},{16,24},{24,16},{1,9},{9,1},{17,25},{25,17},{2,10},{10... | collective-permute-start | bytes 245768 | tf_op jit(solution)/shard_map/ppermute | solution.py:49
  98.8 9.6 %collective-permute-start.27 = (bf16[160,256]{1,0:T(8,128)(2,1)S(1)}, bf16[160,256]{1,0:T(8,128)(2,1)S(1)}, u32[]{:S(2)}, u32[]{:S(2)}) collective-permute-start(bf16[160,256]{1,0:T(8,128)(2,1)S(1)} %get-tuple-element.172), channel_id=1, source_target_pairs={{0,16},{8,24},{16,0},{24,8},{1,17},{9,25},{17,1},{25,9},{2,18},{10... | collective-permute-start | bytes 245768 | tf_op jit(solution)/shard_map/ppermute | solution.py:49
  101.2 7.2 %collective-permute-start.28 = (bf16[160,256]{1,0:T(8,128)(2,1)S(1)}, bf16[160,256]{1,0:T(8,128)(2,1)S(1)}, u32[]{:S(2)}, u32[]{:S(2)}) collective-permute-start(bf16[160,256]{1,0:T(8,128)(2,1)S(1)} %get-tuple-element.173), channel_id=1, source_target_pairs={{0,24},{8,16},{16,8},{24,0},{1,25},{9,17},{17,9},{25,1},{2,26},{10... | collective-permute-start | bytes 245768 | tf_op jit(solution)/shard_map/ppermute | solution.py:49
  109.1 6.8 %collective-permute-start.29 = (bf16[128,256]{1,0:T(8,128)(2,1)S(1)}, bf16[128,256]{1,0:T(8,128)(2,1)S(1)}, u32[]{:S(2)}, u32[]{:S(2)}) collective-permute-start(bf16[128,256]{1,0:T(8,128)(2,1)S(1)} %get-tuple-element.177.refs_1_), channel_id=1, source_target_pairs={{0,8},{8,0},{16,24},{24,16},{1,9},{9,1},{17,25},{25,17},{2,10},{10... | collective-permute-start | bytes 196616 | tf_op jit(solution)/shard_map/ppermute | solution.py:49
  110.7 6.8 %collective-permute-start.30 = (bf16[128,256]{1,0:T(8,128)(2,1)S(1)}, bf16[128,256]{1,0:T(8,128)(2,1)S(1)}, u32[]{:S(2)}, u32[]{:S(2)}) collective-permute-start(bf16[128,256]{1,0:T(8,128)(2,1)S(1)} %get-tuple-element.177.refs_1_), channel_id=1, source_target_pairs={{0,16},{8,24},{16,0},{24,8},{1,17},{9,25},{17,1},{25,9},{2,18},{10... | collective-permute-start | bytes 196616 | tf_op jit(solution)/shard_map/ppermute | solution.py:49
  112.0 6.2 %collective-permute-start.31 = (bf16[128,256]{1,0:T(8,128)(2,1)S(1)}, bf16[128,256]{1,0:T(8,128)(2,1)S(1)}, u32[]{:S(2)}, u32[]{:S(2)}) collective-permute-start(bf16[128,256]{1,0:T(8,128)(2,1)S(1)} %get-tuple-element.177.refs_1_), channel_id=1, source_target_pairs={{0,24},{8,16},{16,8},{24,0},{1,25},{9,17},{17,9},{25,1},{2,26},{10... | collective-permute-start | bytes 196616 | tf_op jit(solution)/shard_map/ppermute | solution.py:49
  (28 other events, 293.5 us)

commit v7 on v6

--- a/solution.py
+++ b/solution.py
@@ -255,37 +255,22 @@
         left_block(wide_ref.at[index + 1], own_ref.at[index])
 
 
-def wide_bases_kernel(wide_ref, wide_out, token, buffer, sems):
-    count, size = wide_ref.shape[0], wide_ref.shape[1]
-    rows, depth = buffer.shape[1], buffer.shape[0]
-    each = size // rows
-    total = count * each
-
-    def copy(index):
-        at = wide_ref.at[index // each, pl.ds(index % each * rows, rows)]
-        return pltpu.make_async_copy(at, buffer.at[index % depth], sems.at[index % depth])
-
-    for index in range(depth):
-        copy(index).start()
-    for index in range(total):
-        copy(index).wait()
-        first = index % each * rows
-        wide_out[index // each, first : first + rows, :] = buffer[index % depth].astype(bf16)
-        if index + depth < total:
-            copy(index + depth).start()
+def wide_bases_kernel(wide_ref, wide_out, token):
+    for index in range(wide_ref.shape[0]):
+        wide_out[index] = wide_ref[index].astype(bf16)
     token[...] = jnp.zeros_like(token)
 
 
 def join_kernel(*refs):
     start = 0
-    for ref in refs[:-1]:
+    for ref in refs[-2::-1]:
         refs[-1][start : start + ref.shape[0]] = ref[...]
         start += ref.shape[0]
 
 
 def join(pieces, after=()):
     shape = (sum(x.shape[0] for x in pieces),) + pieces[0].shape[1:]
-    return run("join", join_kernel, [(shape, pieces[0].dtype)], list(pieces), micros=0.4, after=after)[0]
+    return run("join", join_kernel, [(shape, pieces[0].dtype)], list(pieces)[::-1], micros=0.4, after=after)[0]
 
 
 def unpack(pieces, group, mats, base=0):
@@ -419,7 +404,7 @@
 
 
 def attend_kernel(
-    step, unroll, h1_ref, query_ref, vec_ref, near_ref, far_ref, mask_ref, q_ref, k_ref, v_ref, o_ref, log_ref
+    step, unroll, h1_ref, query_ref, vec_ref, near_ref, far_ref, mask_ref, q_ref, k_ref, v_ref, o_ref, stat_ref, *kept
 ):
     tokens = h1_ref.shape[0]
     half = near_ref.shape[0]
@@ -442,13 +427,18 @@
             rows = pl.ds(start, step)
             scores = contract(q_ref[rows, cols], keys, 1, 1) * scale + mask
             top = jnp.max(scores, axis=1, keepdims=True)
-            out = contract(jnp.exp2(scores - top).astype(bf16), values, 1, 0)
+            exponent = jnp.exp2(scores - top).astype(bf16)
+            if kept:
+                kept[0][head] = exponent
+            out = contract(exponent, values, 1, 0)
             if isinstance(head, int):
                 total = out[:, (head + 2) % 4 * 32 : (head + 2) % 4 * 32 + 1]
             else:
                 total = jnp.sum(jnp.where(lane == (head + 2) % 4 * 32, out, 0.0), axis=1, keepdims=True)
-            o_ref[rows, cols] = jnp.where(mine, out * (1.0 / total), o_ref[rows, cols])
-            log_ref[rows, :] = jnp.where(lane == head, top + jnp.log2(total), log_ref[rows, :])
+            inverse = 1.0 / total
+            o_ref[rows, cols] = jnp.where(mine, out * inverse, o_ref[rows, cols])
+            stat = inverse if kept else top + jnp.log2(total)
+            stat_ref[rows, :] = jnp.where(lane == head, stat, stat_ref[rows, :])
 
         over_blocks(block, tokens, step)
 
@@ -530,8 +520,51 @@
     out_ref[...] = rotate(turned_ref[2], out_grad[...], narrow_ref[4])
 
 
+def back_outputs(dq_wide, dkv, h1_ref, dq_ref, keep_ref, send_ref, query_grad, bias_ref):
+    dq = dq_wide[...].astype(bf16)
+    dq_ref[...] = dq
+    bias_ref[...] = col_sum(dq.astype(f32))
+    half = keep_ref.shape[0]
+    keep_ref[...] = dkv[:, 0:half].T
+    send_ref[...] = dkv[:, half:].T
+    query_grad[...] = contract(turned(h1_ref[...]), dq, 1, 0)
+
+
+def inner_sum(grad, out, mine):
+    return jnp.sum(jnp.where(mine, grad.astype(f32) * out, 0.0), axis=1, keepdims=True)
+
+
+def attend_back_kept_kernel(
+    group, q_ref, k_ref, v_ref, o_ref, stat_ref, kept_ref, g_ref, h1_ref,
+    dq_ref, keep_ref, send_ref, query_grad, bias_ref, dq_wide, dkv, dss, qt, gt,
+):
+    scale = 32**-0.5
+    lane = lax.broadcasted_iota(jnp.int32, (1, 128), 1)
+    cols = slice(group * 128, group * 128 + 128)
+    grad = g_ref[:, cols]
+    stats = [stat_ref[:, group * 4 + head : group * 4 + head + 1] for head in range(4)]
+    spread_stats = stats[3]
+    for head in range(3):
+        spread_stats = jnp.where(lane // 32 == head, stats[head], spread_stats)
+    qt[...] = turned(q_ref[:, cols])
+    gt[...] = (grad.astype(f32) * spread_stats).T.astype(bf16)
+    for head in range(4):
+        mine = lane // 32 == head
+        keys = jnp.where(mine, k_ref[:, cols], 0)
+        values = jnp.where(mine, v_ref[:, cols], 0)
+        inner = inner_sum(grad, o_ref[:, cols], mine)
+        exponent = kept_ref[group * 4 + head]
+        slope = (contract(grad, values, 1, 1) - inner) * stats[head]
+        dss[...] = (exponent.astype(f32) * slope).astype(bf16)
+        out = contract(dss[...], keys, 1, 0) * scale
+        dq_wide[...] = jnp.where(mine, out, dq_wide[...])
+        dkv[head_rows(head), :] = contract(qt[head_rows(head), :], dss[...], 1, 0) * scale
+        dkv[head_rows(head, 128), :] = contract(gt[head_rows(head), :], exponent, 1, 0)
+    back_outputs(dq_wide, dkv, h1_ref, dq_ref, keep_ref, send_ref, query_grad, bias_ref)
+
+
 def attend_back_kernel(
-    step, unroll, group, q_ref, k_ref, v_ref, mask_ref, o_ref, log_ref, g_ref, h1_ref,
+    step, group, q_ref, k_ref, v_ref, mask_ref, o_ref, stat_ref, g_ref, h1_ref,
     dq_ref, keep_ref, send_ref, query_grad, bias_ref, dq_wide, dkv, ps, dss, qt, gt,
 ):
     tokens = q_ref.shape[0]
@@ -550,11 +583,8 @@
         def block(start):
             rows = pl.ds(start, step)
             grad = g_ref[rows, cols]
-            inner = jnp.sum(jnp.where(mine, grad.astype(f32) * o_ref[rows, cols], 0.0), axis=1, keepdims=True)
-            if isinstance(head, int):
-                log = log_ref[rows, group * 4 + head : group * 4 + head + 1]
-            else:
-                log = jnp.sum(jnp.where(lane == head + group * 4, log_ref[rows, :], 0.0), axis=1, keepdims=True)
+            inner = inner_sum(grad, o_ref[rows, cols], mine)
+            log = jnp.sum(jnp.where(lane == head + group * 4, stat_ref[rows, :], 0.0), axis=1, keepdims=True)
             scores = contract(q_ref[rows, cols], keys, 1, 1)
             probs = jnp.exp2(scores * (scale * LOG2E) + mask - log)
             grad_scores = (probs * (contract(grad, values, 1, 1) - inner)).astype(bf16)
@@ -567,14 +597,8 @@
         dkv[head_rows(head), :] = contract(qt[head_rows(head), :], dss[...], 1, 0) * scale
         dkv[head_rows(head, 128), :] = contract(gt[head_rows(head), :], ps[...], 1, 0)
 
-    over_heads(one_head, 0, 4, unroll)
-    dq = dq_wide[...].astype(bf16)
-    dq_ref[...] = dq
-    bias_ref[...] = col_sum(dq.astype(f32))
-    half = keep_ref.shape[0]
-    keep_ref[...] = dkv[:, 0:half].T
-    send_ref[...] = dkv[:, half:].T
-    query_grad[...] = contract(turned(h1_ref[...]), dq, 1, 0)
+    over_heads(one_head, 0, 4, False)
+    back_outputs(dq_wide, dkv, h1_ref, dq_ref, keep_ref, send_ref, query_grad, bias_ref)
 
 
 def total_of(refs):
@@ -870,11 +894,7 @@
         wide_bases_kernel,
         [((3, FF, FF), bf16), ((8, 128), f32)],
         [basis_wide],
-        scratch=[((12, width, FF), f32)],
         micros=6.0,
-        mib=48,
-        raw=(0,),
-        sems=12,
         after=[line],
     )
     all_near = line
@@ -917,10 +937,11 @@
 
     unroll = keys <= 1024
     step = tokens if unroll else 32
-    q, k, v, o, log = run(
+    q, k, v, o, stat, *kept = run(
         "attend",
         functools.partial(attend_kernel, step, unroll),
-        [((tokens, width), bf16), ((keys, width), bf16), ((keys, width), bf16), ((tokens, width), f32), ((tokens, 128), f32)],
+        [((tokens, width), bf16), ((keys, width), bf16), ((keys, width), bf16), ((tokens, width), f32), ((tokens, 128), f32)]
+        + ([((HEADS, tokens, keys), bf16)] if unroll else []),
         [h1, w_query, vec, kv_near, kv_far, mask],
         mib=8 if unroll else 44,
         micros=8.0,
@@ -944,9 +965,14 @@
         micros=3.5,
     )
     def back(group, after):
+        if kept:
+            body, args, more = functools.partial(attend_back_kept_kernel, group), [q, k, v, o, stat, kept[0]], []
+        else:
+            body, args = functools.partial(attend_back_kernel, step, group), [q, k, v, mask, o, stat]
+            more = [((tokens, keys), bf16)]
         return run(
             "attend_back",
-            functools.partial(attend_back_kernel, step, unroll, group),
+            body,
             [
                 ((tokens, 128), bf16),
                 ((keys // 2, width), f32),
@@ -954,16 +980,11 @@
                 ((width, 128), f32),
                 ((1, 128), f32),
             ],
-            [q, k, v, mask, o, log, do, h1],
-            scratch=[
-                ((tokens, 128), f32),
-                ((width, keys), f32),
-                ((tokens, keys), bf16),
-                ((tokens, keys), bf16),
-                ((128, tokens), bf16),
-                ((128, tokens), bf16),
-            ],
-            mib=14 if unroll else 60,
+            args + [do, h1],
+            scratch=[((tokens, 128), f32), ((width, keys), f32)]
+            + more
+            + [((tokens, keys), bf16), ((128, tokens), bf16), ((128, tokens), bf16)],
+            mib=14 if kept else 60,
             micros=5.0,
             after=after,
         )

time: 130 us -> 124 us (0.954)
  Pallas kernels: 42.7 us -> 34.2 us
  local copies, waits for them, and re-layouts: 1.8 us -> 6.61 us
  starting transfers between devices: 43 us -> 41.6 us
    pallas_call x27, Pallas kernels: 42.7 us -> 34.2 us  [run(): pl.pallas_call(without, out_shape=tuple((jax.ShapeDtypeStruct(shape, dtyp...]
    unnamed x35 -> x33, local copies, waits for them, and re-layouts: 1.01 us -> 5.82 us
  transfers between devices with their start and end apart: 36 -> 36, of which waited for: 21 -> 22; matrix products, arithmetic and copies ran while one was open for 1% -> 1% of each run, Pallas kernels for 15% -> 11%
where the time goes in v7:
time: 124 us
  starting transfers between devices  41.6 us (34%)
  waiting for transfers between devices  39.6 us (32%)
  Pallas kernels  34.2 us (28%)
  local copies, waits for them, and re-layouts  6.61 us (5%)
    ppermute x32, starting transfers between devices, swap(): return lax.ppermute(x, axis, [(i, i ^ step) for i in range(count)])  36.3 us
    ppermute x32, waiting for transfers between devices, swap(): return lax.ppermute(x, axis, [(i, i ^ step) for i in range(count)])  36.3 us
    pallas_call x27, Pallas kernels, run(): pl.pallas_call(without, out_shape=tuple((jax.ShapeDtypeStruct(shape, dtyp...  34.2 us
    unnamed x33, local copies, waits for them, and re-layouts  5.82 us
    ppermute x2, waiting for transfers between devices, border(): lax.ppermute(head, 'row', [(i + 1, i) for i in range(ranks - 1)])  3.3 us
    ppermute x2, starting transfers between devices, border(): up = lax.ppermute(tail, 'row', [(i, i + 1) for i in range(ranks - 1)])  2.68 us
    ppermute x2, starting transfers between devices, border(): lax.ppermute(head, 'row', [(i + 1, i) for i in range(ranks - 1)])  2.58 us
  transfers between devices with their start and end apart: 36, of which 22 were waited for; matrix products, arithmetic and copies ran while one was open for 1% of the time, Pallas kernels for 11%

profile of v7, /device:TPU:0, one launch (start us, length us, event | category | flops | bytes accessed | tf_op | source)
XLA Modules:
  0.0 123.6 jit_solution(3578532386333949031)
XLA Ops:
  1.6 5.1 %collective-permute-start.2 = (bf16[128,256]{1,0:T(8,128)(2,1)S(1)}, bf16[128,256]{1,0:T(8,128)(2,1)S(1)}, u32[]{:S(2)}, u32[]{:S(2)}) collective-permute-start(bf16[128,256]{1,0:T(8,128)(2,1)S(1)} %pack.1), channel_id=1, source_target_pairs={{0,24},{8,16},{16,8},{24,0},{1,25},{9,17},{17,9},{25,1},{2,26},{10... | collective-permute-start | bytes 196616 | tf_op jit(solution)/shard_map/ppermute | solution.py:49
  7.4 1.9 %collective-permute-done.2 = bf16[128,256]{1,0:T(8,128)(2,1)S(1)} collective-permute-done((bf16[128,256]{1,0:T(8,128)(2,1)S(1)}, bf16[128,256]{1,0:T(8,128)(2,1)S(1)}, u32[]{:S(2)}, u32[]{:S(2)}) %collective-permute-start.2) | collective-permute-done | bytes 65568 | tf_op jit(solution)/shard_map/ppermute | solution.py:49
  9.3 3.0 %collective-permute-done.3 = bf16[128,256]{1,0:T(8,128)(2,1)S(1)} collective-permute-done((bf16[128,256]{1,0:T(8,128)(2,1)S(1)}, bf16[128,256]{1,0:T(8,128)(2,1)S(1)}, u32[]{:S(2)}, u32[]{:S(2)}) %collective-permute-start.3) | collective-permute-done | bytes 65568 | tf_op jit(solution)/shard_map/ppermute | solution.py:49
  12.4 2.5 %collective-permute-start.5 = (bf16[4,128,256]{2,1,0:T(8,128)(2,1)S(1)}, bf16[4,128,256]{2,1,0:T(8,128)(2,1)S(1)}, u32[]{:S(2)}, u32[]{:S(2)}) collective-permute-start(bf16[4,128,256]{2,1,0:T(8,128)(2,1)S(1)} %join.3.refs_5_.refs_1_.refs_3_), channel_id=1, source_target_pairs={{0,6},{1,7},{2,4},{3,5},{4,2},{5,3},{6,0},{7,1},{8,14},{9,15},{10,... | collective-permute-start | bytes 786440 | tf_op jit(solution)/shard_map/ppermute | solution.py:49
  19.3 4.6 %copy-done = f32[3,1024,1024]{2,1,0:T(8,128)S(1)} copy-done((f32[3,1024,1024]{2,1,0:T(8,128)S(1)}, f32[3,1024,1024]{2,1,0:T(8,128)}, u32[]{:S(2)}) %copy-start) | copy-done | bytes 12582936
  29.2 2.3 %collective-permute-done.8.refs_4_ = bf16[16,128,256]{2,1,0:T(8,128)(2,1)S(1)} collective-permute-done((bf16[16,128,256]{2,1,0:T(8,128)(2,1)S(1)}, bf16[16,128,256]{2,1,0:T(8,128)(2,1)S(1)}, u32[]{:S(2)}, u32[]{:S(2)}) %collective-permute-start.8) | collective-permute-done | bytes 1048608 | tf_op jit(solution)/shard_map/ppermute | solution.py:49
  32.4 2.1 %collective-permute-start.9 = (bf16[112,512]{1,0:T(8,128)(2,1)S(1)}, bf16[112,512]{1,0:T(8,128)(2,1)S(1)}, u32[]{:S(2)}, u32[]{:S(2)}) collective-permute-start(bf16[112,512]{1,0:T(8,128)(2,1)S(1)} %get-tuple-element.109.refs_2_), channel_id=1, source_target_pairs={{0,2},{1,3},{2,0},{3,1},{4,6},{5,7},{6,4},{7,5},{8,10},{9,11},{10,... | collective-permute-start | bytes 344072 | tf_op jit(solution)/shard_map/ppermute | solution.py:49
  37.9 2.9 %collective-permute-done.10 = bf16[112,512]{1,0:T(8,128)(2,1)S(1)} collective-permute-done((bf16[112,512]{1,0:T(8,128)(2,1)S(1)}, bf16[112,512]{1,0:T(8,128)(2,1)S(1)}, u32[]{:S(2)}, u32[]{:S(2)}) %collective-permute-start.10) | collective-permute-done | bytes 114720 | tf_op jit(solution)/shard_map/ppermute | solution.py:49
  44.3 6.3 %attend.1 = (bf16[448,256]{1,0:T(8,128)(2,1)S(1)}, bf16[896,256]{1,0:T(8,128)(2,1)S(1)}, bf16[896,256]{1,0:T(8,128)(2,1)S(1)}, f32[448,256]{1,0:T(8,128)S(1)}, f...) custom-call(bf16[448,256]{1,0:T(8,128)(2,1)S(1)} %get-tuple-element.104.refs_1_.refs_0_.refs_7_, ...), custom_call_target="tpu_custom_call" | custom-call | bytes 28800000 | tf_op jit(solution)/shard_map/attend/pallas_call | solution.py:91
  50.6 3.3 %feed.1 = (bf16[448,256]{1,0:T(8,128)(2,1)}, bf16[448,256]{1,0:T(8,128)(2,1)S(1)}, f32[448,256]{1,0:T(8,128)S(1)}, f32[256,1024]{1,0:T(8,128)S(1)}, f32[256,1024...) custom-call(f32[448,256]{1,0:T(8,128)S(1)} %get-tuple-element.112.refs_0_.refs_3_, ...), custom_call_target="tpu_custom_call" | custom-call | bytes 12600000 | tf_op jit(solution)/shard_map/feed/pallas_call | solution.py:91
  53.9 3.6 %attend_back.2 = (bf16[448,128]{1,0:T(8,128)(2,1)S(1)}, f32[448,256]{1,0:T(8,128)S(1)}, f32[448,256]{1,0:T(8,128)S(1)}, f32[256,128]{1,0:T(8,128)S(1)}, f32[1,128]{1,0:T(1,128)S(1)}) custom-call(bf16[448,256]{1,0:T(8,128)(2,1)S(1)} %get-tuple-element.116.refs_0_, bf16[896,256]{1,0:T(8,128)(2,1)S(1)} %get-tuple-element.117.refs_1_, ...), custom_call_target="tpu_custom_call" | custom-call | bytes 18000000 | tf_op jit(solution)/shard_map/attend_back/pallas_call | solution.py:91
  57.6 3.6 %attend_back.3 = (bf16[448,128]{1,0:T(8,128)(2,1)S(1)}, f32[448,256]{1,0:T(8,128)S(1)}, f32[448,256]{1,0:T(8,128)S(1)}, f32[256,128]{1,0:T(8,128)S(1)}, f32[1,128]{1,0:T(1,128)S(1)}) custom-call(bf16[448,256]{1,0:T(8,128)(2,1)S(1)} %get-tuple-element.116.refs_0_, bf16[896,256]{1,0:T(8,128)(2,1)S(1)} %get-tuple-element.117.refs_1_, ...), custom_call_target="tpu_custom_call" | custom-call | bytes 18000000 | tf_op jit(solution)/shard_map/attend_back/pallas_call | solution.py:91
  61.8 1.8 %early_turn.1 = (f32[16,64,256]{2,1,0:T(8,128)S(1)}, f32[16,64,256]{2,1,0:T(8,128)S(1)}) custom-call(f32[256,1024]{1,0:T(8,128)S(1)} %get-tuple-element.130.refs_0_, f32[256,1024]{1,0:T(8,128)S(1)} %get-tuple-element.131.refs_1_, bf16[4,256,256]{2,1,0:T(8,128)(2,1)S(1)} %get-tuple-element.132.refs_2_.refs_3_.refs_9_, ...), custom_call_target="tpu_custom_call" | custom-call | bytes 7200000 | tf_op jit(solution)/shard_map/early_turn/pallas_call | solution.py:91
  72.0 1.8 %keys_back.1 = (f32[16,64,256]{2,1,0:T(8,128)S(1)}, f32[16,64,256]{2,1,0:T(8,128)S(1)}, bf16[112,256]{1,0:T(8,128)(2,1)S(1)}, f32[4,256]{1,0:T(4,128)S(1)}) custom-call(f32[112,512]{1,0:T(8,128)S(1)} %get-tuple-element.137.refs_5_.refs_1_.refs_0_, bf16[112,512]{1,0:T(8,128)(2,1)S(1)} %collective-permute-done.15.refs_1_, ...), custom_call_target="tpu_custom_call" | custom-call | bytes 7200000 | tf_op jit(solution)/shard_map/keys_back/pallas_call | solution.py:91
  74.0 1.9 %cells_back.1 = (f32[448,256]{1,0:T(8,128)S(1)}, bf16[64,256]{1,0:T(8,128)(2,1)S(1)}, bf16[64,256]{1,0:T(8,128)(2,1)S(1)}, f32[32,256]{1,0:T(8,128)S(1)}) custom-call(s32[8,128]{1,0:T(8,128)S(1)} %get-tuple-element.105.refs_0_, bf16[448,128]{1,0:T(8,128)(2,1)S(1)} %get-tuple-element.123.refs_1_, bf16[448,128]{1,0:T(8,128)(2,1)S(1)} %get-tuple-element.125.refs_2_, ...), custom_call_target="tpu_custom_call" | custom-call | bytes 7200000 | tf_op jit(solution)/shard_map/cells_back/pallas_call | solution.py:91
  83.8 3.3 %collective-permute-done.19.refs_7_.refs_2_ = bf16[64,256]{1,0:T(8,128)(2,1)S(1)} collective-permute-done((bf16[64,256]{1,0:T(8,128)(2,1)S(1)}, bf16[64,256]{1,0:T(8,128)(2,1)S(1)}, u32[]{:S(2)}, u32[]{:S(2)}) %collective-permute-start.19) | collective-permute-done | bytes 32800 | tf_op jit(solution)/shard_map/ppermute | solution.py:868
  87.1 5.3 %collective-permute-done.24.refs_4_ = bf16[544,256]{1,0:T(8,128)(2,1)S(1)} collective-permute-done((bf16[544,256]{1,0:T(8,128)(2,1)S(1)}, bf16[544,256]{1,0:T(8,128)(2,1)S(1)}, u32[]{:S(2)}, u32[]{:S(2)}) %collective-permute-start.24) | collective-permute-done | bytes 278560 | tf_op jit(solution)/shard_map/ppermute | solution.py:49
  94.9 2.2 %collective-permute-start.27 = (bf16[160,256]{1,0:T(8,128)(2,1)S(1)}, bf16[160,256]{1,0:T(8,128)(2,1)S(1)}, u32[]{:S(2)}, u32[]{:S(2)}) collective-permute-start(bf16[160,256]{1,0:T(8,128)(2,1)S(1)} %get-tuple-element.174), channel_id=1, source_target_pairs={{0,16},{8,24},{16,0},{24,8},{1,17},{9,25},{17,1},{25,9},{2,18},{10... | collective-permute-start | bytes 245768 | tf_op jit(solution)/shard_map/ppermute | solution.py:49
  99.8 4.2 %collective-permute-done.27.refs_4_ = bf16[160,256]{1,0:T(8,128)(2,1)S(1)} collective-permute-done((bf16[160,256]{1,0:T(8,128)(2,1)S(1)}, bf16[160,256]{1,0:T(8,128)(2,1)S(1)}, u32[]{:S(2)}, u32[]{:S(2)}) %collective-permute-start.27) | collective-permute-done | bytes 81952 | tf_op jit(solution)/shard_map/ppermute | solution.py:49
  104.7 2.0 %collective-permute-start.29 = (bf16[128,256]{1,0:T(8,128)(2,1)S(1)}, bf16[128,256]{1,0:T(8,128)(2,1)S(1)}, u32[]{:S(2)}, u32[]{:S(2)}) collective-permute-start(bf16[128,256]{1,0:T(8,128)(2,1)S(1)} %get-tuple-element.179.refs_1_), channel_id=1, source_target_pairs={{0,24},{8,16},{16,8},{24,0},{1,25},{9,17},{17,9},{25,1},{2,26},{10... | collective-permute-start | bytes 196616 | tf_op jit(solution)/shard_map/ppermute | solution.py:49
  112.9 1.9 %collective-permute-done.32 = f32[4,128,256]{2,1,0:T(8,128)S(1)} collective-permute-done((f32[4,128,256]{2,1,0:T(8,128)S(1)}, f32[4,128,256]{2,1,0:T(8,128)S(1)}, u32[]{:S(2)}, u32[]{:S(2)}) %collective-permute-start.32) | collective-permute-done | bytes 524320 | tf_op jit(solution)/shard_map/ppermute | solution.py:49
  116.5 1.9 %collective-permute-start.35 = (bf16[128,256]{1,0:T(8,128)(2,1)S(1)}, bf16[128,256]{1,0:T(8,128)(2,1)S(1)}, u32[]{:S(2)}, u32[]{:S(2)}) collective-permute-start(bf16[128,256]{1,0:T(8,128)(2,1)S(1)} %get-tuple-element.188), channel_id=1, source_target_pairs={{0,6},{1,7},{2,4},{3,5},{4,2},{5,3},{6,0},{7,1},{8,14},{9,15},{10,... | collective-permute-start | bytes 196616 | tf_op jit(solution)/shard_map/ppermute | solution.py:49
  119.2 2.6 %collective-permute-done.34.refs_2_ = bf16[128,256]{1,0:T(8,128)(2,1)S(1)} collective-permute-done((bf16[128,256]{1,0:T(8,128)(2,1)S(1)}, bf16[128,256]{1,0:T(8,128)(2,1)S(1)}, u32[]{:S(2)}, u32[]{:S(2)}) %collective-permute-start.34) | collective-permute-done | bytes 65568 | tf_op jit(solution)/shard_map/ppermute | solution.py:49
  121.9 1.7 %finish.1 = (f32[1,32768]{1,0:T(1,128)}, f32[1,32768]{1,0:T(1,128)}) custom-call(f32[128,256]{1,0:T(8,128)S(1)} %get-tuple-element.185.refs_0_, bf16[128,256]{1,0:T(8,128)(2,1)S(1)} %collective-permute-done.33.refs_1_, bf16[128,256]{1,0:T(8,128)(2,1)S(1)} %collective-permute-done.34.refs_2_, bf16[128,256]{1,0:T(8,128)(2,1)S(1)} %collective-permute-done.35.refs_3_, ...), custom_call_target="tpu_custom_call" | custom-call | bytes 5400000 | tf_op jit(solution)/shard_map/finish/pallas_call | solution.py:91
  (111 shorter events, 50.5 us)
Async XLA Ops:
  1.6 7.7 %collective-permute-start.2 = (bf16[128,256]{1,0:T(8,128)(2,1)S(1)}, bf16[128,256]{1,0:T(8,128)(2,1)S(1)}, u32[]{:S(2)}, u32[]{:S(2)}) collective-permute-start(bf16[128,256]{1,0:T(8,128)(2,1)S(1)} %pack.1), channel_id=1, source_target_pairs={{0,24},{8,16},{16,8},{24,0},{1,25},{9,17},{17,9},{25,1},{2,26},{10... | collective-permute-start | bytes 196616 | tf_op jit(solution)/shard_map/ppermute | solution.py:49
  6.7 5.6 %collective-permute-start.3 = (bf16[128,256]{1,0:T(8,128)(2,1)S(1)}, bf16[128,256]{1,0:T(8,128)(2,1)S(1)}, u32[]{:S(2)}, u32[]{:S(2)}) collective-permute-start(bf16[128,256]{1,0:T(8,128)(2,1)S(1)} %pack.1), channel_id=1, source_target_pairs={{0,16},{8,24},{16,0},{24,8},{1,17},{9,25},{17,1},{25,9},{2,18},{10... | collective-permute-start | bytes 196616 | tf_op jit(solution)/shard_map/ppermute | solution.py:49
  6.7 5.6 %collective-permute-start.4 = (bf16[128,256]{1,0:T(8,128)(2,1)S(1)}, bf16[128,256]{1,0:T(8,128)(2,1)S(1)}, u32[]{:S(2)}, u32[]{:S(2)}) collective-permute-start(bf16[128,256]{1,0:T(8,128)(2,1)S(1)} %pack.1), channel_id=1, source_target_pairs={{0,8},{8,0},{16,24},{24,16},{1,9},{9,1},{17,25},{25,17},{2,10},{10... | collective-permute-start | bytes 196616 | tf_op jit(solution)/shard_map/ppermute | solution.py:49
  12.4 13.8 %collective-permute-start.5 = (bf16[4,128,256]{2,1,0:T(8,128)(2,1)S(1)}, bf16[4,128,256]{2,1,0:T(8,128)(2,1)S(1)}, u32[]{:S(2)}, u32[]{:S(2)}) collective-permute-start(bf16[4,128,256]{2,1,0:T(8,128)(2,1)S(1)} %join.3.refs_5_.refs_1_.refs_3_), channel_id=1, source_target_pairs={{0,6},{1,7},{2,4},{3,5},{4,2},{5,3},{6,0},{7,1},{8,14},{9,15},{10,... | collective-permute-start | bytes 786440 | tf_op jit(solution)/shard_map/ppermute | solution.py:49
  14.9 11.9 %collective-permute-start.6 = (bf16[4,128,256]{2,1,0:T(8,128)(2,1)S(1)}, bf16[4,128,256]{2,1,0:T(8,128)(2,1)S(1)}, u32[]{:S(2)}, u32[]{:S(2)}) collective-permute-start(bf16[4,128,256]{2,1,0:T(8,128)(2,1)S(1)} %join.3.refs_5_.refs_1_.refs_3_), channel_id=1, source_target_pairs={{0,4},{1,5},{2,6},{3,7},{4,0},{5,1},{6,2},{7,3},{8,12},{9,13},{10,... | collective-permute-start | bytes 786440 | tf_op jit(solution)/shard_map/ppermute | solution.py:49
  15.4 12.1 %collective-permute-start.7 = (bf16[4,128,256]{2,1,0:T(8,128)(2,1)S(1)}, bf16[4,128,256]{2,1,0:T(8,128)(2,1)S(1)}, u32[]{:S(2)}, u32[]{:S(2)}) collective-permute-start(bf16[4,128,256]{2,1,0:T(8,128)(2,1)S(1)} %join.3.refs_5_.refs_1_.refs_3_), channel_id=1, source_target_pairs={{0,2},{1,3},{2,0},{3,1},{4,6},{5,7},{6,4},{7,5},{8,10},{9,11},{10,... | collective-permute-start | bytes 786440 | tf_op jit(solution)/shard_map/ppermute | solution.py:49
  16.7 7.8 %collective-permute-start = (bf16[64,256]{1,0:T(8,128)(2,1)S(1)}, bf16[64,256]{1,0:T(8,128)(2,1)S(1)}, u32[]{:S(2)}, u32[]{:S(2)}) collective-permute-start(bf16[64,256]{1,0:T(8,128)(2,1)S(1)} %get-tuple-element.199), channel_id=1, source_target_pairs={{0,1},{1,2},{2,3},{3,4},{4,5},{5,6},{6,7},{8,9},{9,10},{10,11},{11... | collective-permute-start | bytes 98312 | tf_op jit(solution)/shard_map/ppermute | solution.py:867
  18.0 6.5 %collective-permute-start.1 = (bf16[64,256]{1,0:T(8,128)(2,1)S(1)}, bf16[64,256]{1,0:T(8,128)(2,1)S(1)}, u32[]{:S(2)}, u32[]{:S(2)}) collective-permute-start(bf16[64,256]{1,0:T(8,128)(2,1)S(1)} %get-tuple-element.198), channel_id=1, source_target_pairs={{1,0},{2,1},{3,2},{4,3},{5,4},{6,5},{7,6},{9,8},{10,9},{11,10},{12... | collective-permute-start | bytes 98312 | tf_op jit(solution)/shard_map/ppermute | solution.py:868
  32.4 5.5 %collective-permute-start.9 = (bf16[112,512]{1,0:T(8,128)(2,1)S(1)}, bf16[112,512]{1,0:T(8,128)(2,1)S(1)}, u32[]{:S(2)}, u32[]{:S(2)}) collective-permute-start(bf16[112,512]{1,0:T(8,128)(2,1)S(1)} %get-tuple-element.109.refs_2_), channel_id=1, source_target_pairs={{0,2},{1,3},{2,0},{3,1},{4,6},{5,7},{6,4},{7,5},{8,10},{9,11},{10,... | collective-permute-start | bytes 344072 | tf_op jit(solution)/shard_map/ppermute | solution.py:49
  34.4 6.4 %collective-permute-start.10 = (bf16[112,512]{1,0:T(8,128)(2,1)S(1)}, bf16[112,512]{1,0:T(8,128)(2,1)S(1)}, u32[]{:S(2)}, u32[]{:S(2)}) collective-permute-start(bf16[112,512]{1,0:T(8,128)(2,1)S(1)} %get-tuple-element.109.refs_2_), channel_id=1, source_target_pairs={{0,4},{1,5},{2,6},{3,7},{4,0},{5,1},{6,2},{7,3},{8,12},{9,13},{10,... | collective-permute-start | bytes 344072 | tf_op jit(solution)/shard_map/ppermute | solution.py:49
  36.0 6.5 %collective-permute-start.11 = (bf16[112,512]{1,0:T(8,128)(2,1)S(1)}, bf16[112,512]{1,0:T(8,128)(2,1)S(1)}, u32[]{:S(2)}, u32[]{:S(2)}) collective-permute-start(bf16[112,512]{1,0:T(8,128)(2,1)S(1)} %get-tuple-element.109.refs_2_), channel_id=1, source_target_pairs={{0,6},{1,7},{2,4},{3,5},{4,2},{5,3},{6,0},{7,1},{8,14},{9,15},{10,... | collective-permute-start | bytes 344072 | tf_op jit(solution)/shard_map/ppermute | solution.py:49
  63.9 6.1 %collective-permute-start.15 = (bf16[112,512]{1,0:T(8,128)(2,1)S(1)}, bf16[112,512]{1,0:T(8,128)(2,1)S(1)}, u32[]{:S(2)}, u32[]{:S(2)}) collective-permute-start(bf16[112,512]{1,0:T(8,128)(2,1)S(1)} %get-tuple-element.138), channel_id=1, source_target_pairs={{0,2},{1,3},{2,0},{3,1},{4,6},{5,7},{6,4},{7,5},{8,10},{9,11},{10,... | collective-permute-start | bytes 344072 | tf_op jit(solution)/shard_map/ppermute | solution.py:49
  64.6 6.6 %collective-permute-start.16 = (bf16[112,512]{1,0:T(8,128)(2,1)S(1)}, bf16[112,512]{1,0:T(8,128)(2,1)S(1)}, u32[]{:S(2)}, u32[]{:S(2)}) collective-permute-start(bf16[112,512]{1,0:T(8,128)(2,1)S(1)} %get-tuple-element.139), channel_id=1, source_target_pairs={{0,4},{1,5},{2,6},{3,7},{4,0},{5,1},{6,2},{7,3},{8,12},{9,13},{10,... | collective-permute-start | bytes 344072 | tf_op jit(solution)/shard_map/ppermute | solution.py:49
  66.3 5.7 %collective-permute-start.17 = (bf16[112,512]{1,0:T(8,128)(2,1)S(1)}, bf16[112,512]{1,0:T(8,128)(2,1)S(1)}, u32[]{:S(2)}, u32[]{:S(2)}) collective-permute-start(bf16[112,512]{1,0:T(8,128)(2,1)S(1)} %get-tuple-element.140), channel_id=1, source_target_pairs={{0,6},{1,7},{2,4},{3,5},{4,2},{5,3},{6,0},{7,1},{8,14},{9,15},{10,... | collective-permute-start | bytes 344072 | tf_op jit(solution)/shard_map/ppermute | solution.py:49
  67.9 9.4 %collective-permute-start.22 = (f32[16,64,256]{2,1,0:T(8,128)S(1)}, f32[16,64,256]{2,1,0:T(8,128)S(1)}, u32[]{:S(2)}, u32[]{:S(2)}) collective-permute-start(f32[16,64,256]{2,1,0:T(8,128)S(1)} %get-tuple-element.162), channel_id=1, source_target_pairs={{0,1},{1,0},{2,3},{3,2},{4,5},{5,4},{6,7},{7,6},{8,9},{9,8},{10,11... | collective-permute-start | bytes 3145736 | tf_op jit(solution)/shard_map/ppermute | solution.py:49
  77.5 9.6 %collective-permute-start.23 = (bf16[544,256]{1,0:T(8,128)(2,1)S(1)}, bf16[544,256]{1,0:T(8,128)(2,1)S(1)}, u32[]{:S(2)}, u32[]{:S(2)}) collective-permute-start(bf16[544,256]{1,0:T(8,128)(2,1)S(1)} %get-tuple-element.166), channel_id=1, source_target_pairs={{0,2},{1,3},{2,0},{3,1},{4,6},{5,7},{6,4},{7,5},{8,10},{9,11},{10,... | collective-permute-start | bytes 835592 | tf_op jit(solution)/shard_map/ppermute | solution.py:49
  79.0 13.4 %collective-permute-start.24 = (bf16[544,256]{1,0:T(8,128)(2,1)S(1)}, bf16[544,256]{1,0:T(8,128)(2,1)S(1)}, u32[]{:S(2)}, u32[]{:S(2)}) collective-permute-start(bf16[544,256]{1,0:T(8,128)(2,1)S(1)} %get-tuple-element.167), channel_id=1, source_target_pairs={{0,4},{1,5},{2,6},{3,7},{4,0},{5,1},{6,2},{7,3},{8,12},{9,13},{10,... | collective-permute-start | bytes 835592 | tf_op jit(solution)/shard_map/ppermute | solution.py:49
  79.9 13.7 %collective-permute-start.25 = (bf16[544,256]{1,0:T(8,128)(2,1)S(1)}, bf16[544,256]{1,0:T(8,128)(2,1)S(1)}, u32[]{:S(2)}, u32[]{:S(2)}) collective-permute-start(bf16[544,256]{1,0:T(8,128)(2,1)S(1)} %get-tuple-element.168), channel_id=1, source_target_pairs={{0,6},{1,7},{2,4},{3,5},{4,2},{5,3},{6,0},{7,1},{8,14},{9,15},{10,... | collective-permute-start | bytes 835592 | tf_op jit(solution)/shard_map/ppermute | solution.py:49
  93.7 6.1 %collective-permute-start.26 = (bf16[160,256]{1,0:T(8,128)(2,1)S(1)}, bf16[160,256]{1,0:T(8,128)(2,1)S(1)}, u32[]{:S(2)}, u32[]{:S(2)}) collective-permute-start(bf16[160,256]{1,0:T(8,128)(2,1)S(1)} %get-tuple-element.173), channel_id=1, source_target_pairs={{0,8},{8,0},{16,24},{24,16},{1,9},{9,1},{17,25},{25,17},{2,10},{10... | collective-permute-start | bytes 245768 | tf_op jit(solution)/shard_map/ppermute | solution.py:49
  94.9 9.1 %collective-permute-start.27 = (bf16[160,256]{1,0:T(8,128)(2,1)S(1)}, bf16[160,256]{1,0:T(8,128)(2,1)S(1)}, u32[]{:S(2)}, u32[]{:S(2)}) collective-permute-start(bf16[160,256]{1,0:T(8,128)(2,1)S(1)} %get-tuple-element.174), channel_id=1, source_target_pairs={{0,16},{8,24},{16,0},{24,8},{1,17},{9,25},{17,1},{25,9},{2,18},{10... | collective-permute-start | bytes 245768 | tf_op jit(solution)/shard_map/ppermute | solution.py:49
  97.1 6.9 %collective-permute-start.28 = (bf16[160,256]{1,0:T(8,128)(2,1)S(1)}, bf16[160,256]{1,0:T(8,128)(2,1)S(1)}, u32[]{:S(2)}, u32[]{:S(2)}) collective-permute-start(bf16[160,256]{1,0:T(8,128)(2,1)S(1)} %get-tuple-element.175), channel_id=1, source_target_pairs={{0,24},{8,16},{16,8},{24,0},{1,25},{9,17},{17,9},{25,1},{2,26},{10... | collective-permute-start | bytes 245768 | tf_op jit(solution)/shard_map/ppermute | solution.py:49
  104.7 6.8 %collective-permute-start.29 = (bf16[128,256]{1,0:T(8,128)(2,1)S(1)}, bf16[128,256]{1,0:T(8,128)(2,1)S(1)}, u32[]{:S(2)}, u32[]{:S(2)}) collective-permute-start(bf16[128,256]{1,0:T(8,128)(2,1)S(1)} %get-tuple-element.179.refs_1_), channel_id=1, source_target_pairs={{0,24},{8,16},{16,8},{24,0},{1,25},{9,17},{17,9},{25,1},{2,26},{10... | collective-permute-start | bytes 196616 | tf_op jit(solution)/shard_map/ppermute | solution.py:49
  106.7 5.9 %collective-permute-start.30 = (bf16[128,256]{1,0:T(8,128)(2,1)S(1)}, bf16[128,256]{1,0:T(8,128)(2,1)S(1)}, u32[]{:S(2)}, u32[]{:S(2)}) collective-permute-start(bf16[128,256]{1,0:T(8,128)(2,1)S(1)} %get-tuple-element.179.refs_1_), channel_id=1, source_target_pairs={{0,16},{8,24},{16,0},{24,8},{1,17},{9,25},{17,1},{25,9},{2,18},{10... | collective-permute-start | bytes 196616 | tf_op jit(solution)/shard_map/ppermute | solution.py:49
  116.3 5.5 %collective-permute-start.34 = (bf16[128,256]{1,0:T(8,128)(2,1)S(1)}, bf16[128,256]{1,0:T(8,128)(2,1)S(1)}, u32[]{:S(2)}, u32[]{:S(2)}) collective-permute-start(bf16[128,256]{1,0:T(8,128)(2,1)S(1)} %get-tuple-element.187), channel_id=1, source_target_pairs={{0,4},{1,5},{2,6},{3,7},{4,0},{5,1},{6,2},{7,3},{8,12},{9,13},{10,... | collective-permute-start | bytes 196616 | tf_op jit(solution)/shard_map/ppermute | solution.py:49
  (27 other events, 224.0 us)

commit v8 on v7

--- a/solution.py
+++ b/solution.py
@@ -343,7 +343,7 @@
 
 def keys_kernel(
     tile_rows, cols, size_ref, h1_ref, vec_ref, near_ref, far_ref,
-    reduce_ref, keyval_ref, query_ref, out_ref, blocks_ref, c_ref, kn_ref, kv_ref,
+    reduce_ref, keyval_ref, query_ref, out_ref, blocks_ref, c_ref, kn_ref,
     reduce_wide, keyval_wide, query_wide, out_wide,
 ):
     unpack((near_ref, far_ref), LATE, (reduce_wide, keyval_wide, query_wide, out_wide))
@@ -360,9 +360,6 @@
     unit, _ = norm_parts(c)
     kn = (unit * vec_ref[14:15, :] + vec_ref[15:16, :]).astype(bf16)
     kn_ref[...] = kn
-    kv = contract(kn, keyval_ref[...], 1, 0)
-    kv_ref[:, 0:256] = kv[:, 0:256].astype(bf16)
-    kv_ref[:, 256:512] = (kv[:, 256:512] + vec_ref[16:17, :]).astype(bf16)
 
 
 def over_heads(body, first, last, unroll):
@@ -404,13 +401,15 @@
 
 
 def attend_kernel(
-    step, unroll, h1_ref, query_ref, vec_ref, near_ref, far_ref, mask_ref, q_ref, k_ref, v_ref, o_ref, stat_ref, *kept
+    step, unroll, h1_ref, query_ref, keyval_ref, vec_ref, near_ref, far_ref, mask_ref,
+    kn_ref, q_ref, k_ref, v_ref, o_ref, stat_ref, *kept
 ):
     tokens = h1_ref.shape[0]
     half = near_ref.shape[0]
-    for start, ref in ((0, near_ref), (half, far_ref)):
-        k_ref[start : start + half, :] = ref[:, 0:256]
-        v_ref[start : start + half, :] = ref[:, 256:512]
+    kn_ref[0:half, :] = near_ref[...]
+    kn_ref[half:, :] = far_ref[...]
+    k_ref[...] = contract(kn_ref[...], keyval_ref[:, 0:256], 1, 0).astype(bf16)
+    v_ref[...] = (contract(kn_ref[...], keyval_ref[:, 256:512], 1, 0) + vec_ref[16:17, :]).astype(bf16)
     q_ref[...] = (contract(h1_ref[...], query_ref[...], 1, 0) + vec_ref[12:13, :]).astype(bf16)
     scale = 32**-0.5 * LOG2E
     lane = lax.broadcasted_iota(jnp.int32, (1, 128), 1)
@@ -514,20 +513,47 @@
     share_out(keep_ref, send_ref, layout(256, EARLY)[0], (up, down))
 
 
-def middle_turn_kernel(query_left, query_right, out_grad, turned_ref, narrow_ref, query_ref, out_ref):
-    query_grad = jnp.concatenate([query_left[...], query_right[...]], axis=1)
-    query_ref[...] = rotate(turned_ref[0], query_grad, narrow_ref[1])
+def middle_turn_kernel(
+    h1_ref, dq_left, dq_right, out_grad, kn_ref, dkv_left, dkv_right, turned_ref, narrow_ref, pair_ref,
+    query_ref, out_ref, keyval_ref, sums_ref, grad,
+):
+    dq = jnp.concatenate([dq_left[...], dq_right[...]], axis=1)
+    query_ref[...] = rotate(turned_ref[0], contract(turned(h1_ref[...]), dq, 1, 0), narrow_ref[1])
     out_ref[...] = rotate(turned_ref[2], out_grad[...], narrow_ref[4])
-
-
-def back_outputs(dq_wide, dkv, h1_ref, dq_ref, keep_ref, send_ref, query_grad, bias_ref):
-    dq = dq_wide[...].astype(bf16)
-    dq_ref[...] = dq
-    bias_ref[...] = col_sum(dq.astype(f32))
-    half = keep_ref.shape[0]
-    keep_ref[...] = dkv[:, 0:half].T
-    send_ref[...] = dkv[:, half:].T
-    query_grad[...] = contract(turned(h1_ref[...]), dq, 1, 0)
+    sums_ref[0:1, :] = col_sum(dq.astype(f32))
+    sums_ref[2:8, :] = jnp.zeros((6, 256), f32)
+    ones = jnp.ones((8, kn_ref.shape[0]), bf16)
+    for group, ref in enumerate((dkv_left, dkv_right)):
+        high, rest = two_parts(ref[...])
+        found = contract(high, kn_ref[...], 1, 0) + contract(rest, kn_ref[...], 1, 0)
+        grad[group * 128 : group * 128 + 128, :] = found[0:128]
+        grad[256 + group * 128 : 256 + group * 128 + 128, :] = found[128:256]
+        sums = contract(ones, high[128:256, :], 1, 1) + contract(ones, rest[128:256, :], 1, 1)
+        sums_ref[1:2, group * 128 : group * 128 + 128] = sums[0:1]
+    keyval_ref[...] = rotate_turned(grad[...], narrow_ref[2], pair_ref[...])
+
+
+def back_outputs(group, dq_wide, dkv, keyval_ref, earlier, dq_ref, outs):
+    dq_ref[...] = dq_wide[...].astype(bf16)
+    keys = dkv.shape[1]
+    span = keys if keys <= 1024 else keys // 8
+    for start in range(0, keys, span):
+        at = slice(start, start + span)
+        high, rest = two_parts(dkv[:, at])
+        total = earlier[0][:, at] if earlier else None
+        for base, first in ((0, group * 128), (128, 256 + group * 128)):
+            matrix = keyval_ref[:, first : first + 128]
+            for part in (high, rest):
+                term = contract(matrix, part[base : base + 128, :], 1, 0)
+                total = term if total is None else total + term
+        half = keys // 2
+        if not earlier:
+            outs[0][:, at] = total
+        elif span == keys:
+            outs[0][...] = total[:, 0:half].T
+            outs[1][...] = total[:, half:].T
+        else:
+            outs[start // half][start % half : start % half + span, :] = total.T
 
 
 def inner_sum(grad, out, mine):
@@ -535,9 +561,9 @@
 
 
 def attend_back_kept_kernel(
-    group, q_ref, k_ref, v_ref, o_ref, stat_ref, kept_ref, g_ref, h1_ref,
-    dq_ref, keep_ref, send_ref, query_grad, bias_ref, dq_wide, dkv, dss, qt, gt,
+    group, q_ref, k_ref, v_ref, o_ref, stat_ref, kept_ref, g_ref, keyval_ref, *refs
 ):
+    earlier, (dq_ref, dkv, *outs), (dq_wide, dss, qt, gt) = refs[:group], refs[group:-4], refs[-4:]
     scale = 32**-0.5
     lane = lax.broadcasted_iota(jnp.int32, (1, 128), 1)
     cols = slice(group * 128, group * 128 + 128)
@@ -560,13 +586,13 @@
         dq_wide[...] = jnp.where(mine, out, dq_wide[...])
         dkv[head_rows(head), :] = contract(qt[head_rows(head), :], dss[...], 1, 0) * scale
         dkv[head_rows(head, 128), :] = contract(gt[head_rows(head), :], exponent, 1, 0)
-    back_outputs(dq_wide, dkv, h1_ref, dq_ref, keep_ref, send_ref, query_grad, bias_ref)
+    back_outputs(group, dq_wide, dkv, keyval_ref, earlier, dq_ref, outs)
 
 
 def attend_back_kernel(
-    step, group, q_ref, k_ref, v_ref, mask_ref, o_ref, stat_ref, g_ref, h1_ref,
-    dq_ref, keep_ref, send_ref, query_grad, bias_ref, dq_wide, dkv, ps, dss, qt, gt,
+    step, group, q_ref, k_ref, v_ref, mask_ref, o_ref, stat_ref, g_ref, keyval_ref, *refs
 ):
+    earlier, (dq_ref, dkv, *outs), (dq_wide, ps, dss, qt, gt) = refs[:group], refs[group:-5], refs[-5:]
     tokens = q_ref.shape[0]
     scale = 32**-0.5
     lane = lax.broadcasted_iota(jnp.int32, (1, 128), 1)
@@ -598,7 +624,7 @@
         dkv[head_rows(head, 128), :] = contract(gt[head_rows(head), :], ps[...], 1, 0)
 
     over_heads(one_head, 0, 4, False)
-    back_outputs(dq_wide, dkv, h1_ref, dq_ref, keep_ref, send_ref, query_grad, bias_ref)
+    back_outputs(group, dq_wide, dkv, keyval_ref, earlier, dq_ref, outs)
 
 
 def total_of(refs):
@@ -621,18 +647,6 @@
     tail = terms[0].shape[1:]
     outs = [((rows,) + tail, f32)] + [((rows,) + tail, bf16)] * (count - 1)
     return run("split_sum", functools.partial(split_kernel, count, len(terms)), outs, terms, micros=0.6, after=after)
-
-
-def split_heads_kernel(count, left_keep, left_got, right_keep, right_got, *outs):
-    rows = outs[0].shape[0]
-    for index in range(count):
-        at = slice(index * rows, (index + 1) * rows)
-        left = left_keep[at, :] + left_got[at, :]
-        right = right_keep[at, :] + right_got[at, :]
-        parts = (left[:, 0:128], right[:, 0:128], left[:, 128:256], right[:, 128:256])
-        for place, part in enumerate(parts):
-            cols = slice(place * 128, place * 128 + 128)
-            outs[index][:, cols] = part if index == 0 else part.astype(bf16)
 
 
 def pair_total(values):
@@ -700,31 +714,24 @@
     return x
 
 
-def keys_back_kernel(
-    terms, *refs
-):
-    (kn_ref, c_ref, vec_ref, keyval_ref, blocks_ref, turned_ref, narrow_ref, pair_ref, wide_ref, query, out,
-     keep_ref, send_ref, dc_ref, sums_ref, reduce, keyval) = refs[terms:]
-    dkv = total_of(refs[:terms])
-    high, rest = two_parts(dkv)
-    dkn = contract(high, keyval_ref[...], 1, 1) + contract(rest, keyval_ref[...], 1, 1)
+def keys_back_kernel(terms, *refs):
+    (c_ref, vec_ref, blocks_ref, narrow_ref, wide_ref, query, out, keyval,
+     keep_ref, send_ref, dc_ref, sums_ref, reduce) = refs[terms:]
+    dkn = total_of(refs[:terms])
     unit, inverse = norm_parts(c_ref[...])
     back, gain_sum, bias_sum = norm_back(dkn, unit, inverse, vec_ref[14:15, :])
     dc = back.astype(bf16)
     dc_ref[...] = dc
-    knt = turned(kn_ref[...])
-    keyval[...] = rotate(turned_ref[1], contract(knt, high, 1, 0) + contract(knt, rest, 1, 0), pair_ref[...])
     reduce[...] = rotate_turned(contract(turned(dc), blocks_ref[...], 1, 0), wide_ref[2], narrow_ref[7])
     share_out(keep_ref, send_ref, layout(256, LATE)[0], (reduce, keyval, query, out))
     sums_ref[0:1, :] = col_sum(dc.astype(f32))
     sums_ref[1:2, :] = gain_sum
     sums_ref[2:3, :] = bias_sum
-    sums_ref[3:4, :] = col_sum(dkv[:, 256:512])
 
 
 def cells_back_kernel(
     tile_rows, cols, size_ref, dq_left, dq_right, dc_ref, query_ref, reduce_ref, x0_ref, dx1_ref, vec_ref, tile_ref, up_ref, down_ref,
-    feed_sums, key_sums, left_sum, right_sum, dx0_ref, head_ref, tail_ref, sums_ref, frame,
+    feed_sums, key_sums, query_sums, dx0_ref, head_ref, tail_ref, sums_ref, frame,
 ):
     tokens = x0_ref.shape[0]
     dh1 = contract(dq_left[...], query_ref[:, 0:128], 1, 1) + contract(dq_right[...], query_ref[:, 128:256], 1, 1)
@@ -748,9 +755,9 @@
     sums_ref[9:10, :] = col_sum(dx0)
     sums_ref[10:11, :] = gain_sum
     sums_ref[11:12, :] = bias_sum
-    sums_ref[12:13, 0:128] = left_sum[...]
-    sums_ref[12:13, 128:256] = right_sum[...]
-    sums_ref[13:17, :] = key_sums[...]
+    sums_ref[12:13, :] = query_sums[0:1, :]
+    sums_ref[13:16, :] = key_sums[...]
+    sums_ref[16:17, :] = query_sums[1:2, :]
 
 
 def input_grad_kernel(tile_rows, dx0_ref, up_ref, down_ref, vec_ref, out_ref, token, frame):
@@ -902,7 +909,7 @@
         pieces = [all_near] + [swap(all_near, axis, j * stride) for j in range(1, size)]
         all_near = join(pieces, after=[wide_done, vec])
     all_far = swap(all_near, "row", 1)
-    w_reduce, w_keyval, w_query, w_out, blocks, c, kn, own_kv = run(
+    w_reduce, w_keyval, w_query, w_out, blocks, c, kn = run(
         "keys",
         functools.partial(keys_kernel, rows, cols),
         [
@@ -913,7 +920,6 @@
             ((own_keys, 4 * width), bf16),
             ((own_keys, width), f32),
             ((own_keys, width), bf16),
-            ((own_keys, 2 * width), bf16),
         ],
         [sizes, h1, vec, all_near, all_far],
         scratch=[((4 * width, width), f32), ((width, 2 * width), f32), ((width, width), f32), ((width, width), f32)],
@@ -930,19 +936,20 @@
         ],
         [basis_narrow, basis_pair],
         micros=1.5,
-        after=[own_kv],
-    )
-    kv_near = side_by_side(own_kv, gather_groups)
-    kv_far = swap(kv_near, "row", 1)
+        after=[kn],
+    )
+    kn_near = side_by_side(kn, gather_groups)
+    kn_far = swap(kn_near, "row", 1)
 
     unroll = keys <= 1024
     step = tokens if unroll else 32
-    q, k, v, o, stat, *kept = run(
+    kn_all, q, k, v, o, stat, *kept = run(
         "attend",
         functools.partial(attend_kernel, step, unroll),
-        [((tokens, width), bf16), ((keys, width), bf16), ((keys, width), bf16), ((tokens, width), f32), ((tokens, 128), f32)]
+        [((keys, width), bf16), ((tokens, width), bf16), ((keys, width), bf16), ((keys, width), bf16)]
+        + [((tokens, width), f32), ((tokens, 128), f32)]
         + ([((HEADS, tokens, keys), bf16)] if unroll else []),
-        [h1, w_query, vec, kv_near, kv_far, mask],
+        [h1, w_query, w_keyval, vec, kn_near, kn_far, mask],
         mib=8 if unroll else 44,
         micros=8.0,
         after=[own_narrow],
@@ -964,35 +971,29 @@
         mib=12,
         micros=3.5,
     )
-    def back(group, after):
+    def back(group, earlier):
         if kept:
             body, args, more = functools.partial(attend_back_kept_kernel, group), [q, k, v, o, stat, kept[0]], []
         else:
             body, args = functools.partial(attend_back_kernel, step, group), [q, k, v, mask, o, stat]
             more = [((tokens, keys), bf16)]
+        halves = [((keys // 2, width), f32)] * 2 if earlier else [((width, keys), f32)]
         return run(
             "attend_back",
             body,
-            [
-                ((tokens, 128), bf16),
-                ((keys // 2, width), f32),
-                ((keys // 2, width), f32),
-                ((width, 128), f32),
-                ((1, 128), f32),
-            ],
-            args + [do, h1],
-            scratch=[((tokens, 128), f32), ((width, keys), f32)]
+            [((tokens, 128), bf16), ((width, keys), f32)] + halves,
+            args + [do, w_keyval] + earlier,
+            scratch=[((tokens, 128), f32)]
             + more
             + [((tokens, keys), bf16), ((128, tokens), bf16), ((128, tokens), bf16)],
             mib=14 if kept else 60,
             micros=5.0,
-            after=after,
+            after=[dx1],
         )
 
-    dq_left, left_keep, left_send, query_left, left_sum = back(0, [dx1])
-    left_got = swap(left_send, "row", 1)
-    dq_right, right_keep, right_send, query_right, right_sum = back(1, [query_left])
-    right_got = swap(right_send, "row", 1)
+    dq_left, dkv_left, dkn_left = back(0, [])
+    dq_right, dkv_right, dkn_keep, dkn_send = back(1, [dkn_left])
+    dkn_got = swap(dkn_send, "row", 1)
     half = (shards // 2, early_rows, width)
     early_keep, early_send = run(
         "early_turn",
@@ -1002,44 +1003,37 @@
         scratch=[((width, FF), f32), ((FF, width), f32)],
         mib=10,
         micros=2.0,
-        after=[query_right],
+        after=[dq_right],
     )
     early_got = swap(early_send, "row", 1)
-    axis, stride, size = xy_parts[0]
-    dkv_keep, *sends = run(
-        "split_heads",
-        functools.partial(split_heads_kernel, size),
-        [((keys // 2 // size, 2 * width), f32)] + [((keys // 2 // size, 2 * width), bf16)] * (size - 1),
-        [left_keep, left_got, right_keep, right_got],
-        micros=0.8,
-        after=[early_keep],
-    )
-    dkv_terms = [dkv_keep] + [swap(x, axis, j * stride) for j, x in enumerate(sends, 1)]
-    for axis, stride, size in xy_parts[1:]:
-        keep, *sends = split_sum(dkv_terms, size)
-        dkv_terms = [keep] + [swap(x, axis, j * stride) for j, x in enumerate(sends, 1)]
+    dkn_terms = [dkn_keep, dkn_got]
+    for axis, stride, size in xy_parts:
+        part, *sends = split_sum(dkn_terms, size, [early_keep])
+        dkn_terms = [part] + [swap(x, axis, j * stride) for j, x in enumerate(sends, 1)]
     old_chunk, ema_chunk, first_chunk, second_chunk = run(
         "moments",
         functools.partial(moments_kernel, width),
         [((chunk, width), f32)] * 4,
         [jnp.concatenate([weights, weight_ema, first_moment, second_moment], axis=0)],
-        after=[dkv_keep],
-    )
-    query_turn, out_turn = run(
+        after=[part],
+    )
+    query_turn, out_turn, keyval_turn, query_sums = run(
         "middle_turn",
         middle_turn_kernel,
-        [((width, width), f32), ((width, width), f32)],
-        [query_left, query_right, out_grad, narrow_turned, narrow],
-        micros=0.7,
-        after=[dkv_keep],
+        [((width, width), f32), ((width, width), f32), ((width, 2 * width), f32), ((8, width), f32)],
+        [h1, dq_left, dq_right, out_grad, kn_all, dkv_left, dkv_right, narrow_turned, narrow, pair],
+        scratch=[((2 * width, width), f32)],
+        micros=1.5,
+        mib=12 if kept else 40,
+        after=[part],
     )
     half = (shards // 2, late_rows, width)
     late_keep, late_send, dc, key_sums = run(
         "keys_back",
-        functools.partial(keys_back_kernel, len(dkv_terms)),
-        [(half, f32), (half, f32), ((own_keys, width), bf16), ((4, width), f32)],
-        list(dkv_terms) + [kn, c, vec, w_keyval, blocks, narrow_turned, narrow, pair, wide, query_turn, out_turn],
-        scratch=[((4 * width, width), f32), ((width, 2 * width), f32)],
+        functools.partial(keys_back_kernel, len(dkn_terms)),
+        [(half, f32), (half, f32), ((own_keys, width), bf16), ((3, width), f32)],
+        list(dkn_terms) + [c, vec, blocks, narrow, wide, query_turn, out_turn, keyval_turn],
+        scratch=[((4 * width, width), f32)],
         micros=2.0,
         after=[old_chunk],
     )
@@ -1050,7 +1044,7 @@
         [((tokens, width), f32), ((64, width), bf16), ((64, width), bf16), ((32, width), f32)],
         [
             sizes, dq_left, dq_right, dc, w_query, w_reduce, x0, dx1, vec, tile, up_halo, down_halo,
-            feed_sums, key_sums, left_sum, right_sum,
+            feed_sums, key_sums, query_sums,
         ],
         scratch=[frame],
         micros=2.0,

time: 124 us -> 120 us (0.968)
  waiting for transfers between devices: 39.6 us -> 35.1 us
  Pallas kernels: 34.2 us -> 35.7 us
    ppermute x32 -> x31, waiting for transfers between devices: 36.3 us -> 32 us  [swap(): return lax.ppermute(x, axis, [(i, i ^ step) for i in range(count)])]
    pallas_call x27, Pallas kernels: 34.2 us -> 35.7 us  [run(): pl.pallas_call(without, out_shape=tuple((jax.ShapeDtypeStruct(shape, dtyp...]
    ppermute x32 -> x31, starting transfers between devices: 36.3 us -> 35.9 us  [swap(): return lax.ppermute(x, axis, [(i, i ^ step) for i in range(count)])]
  transfers between devices with their start and end apart: 36 -> 35, of which waited for: 22 -> 19; matrix products, arithmetic and copies ran while one was open for 1% -> 1% of each run, Pallas kernels for 11% -> 12%
where the time goes in v8:
time: 120 us
  starting transfers between devices  41.2 us (34%)
  Pallas kernels  35.7 us (30%)
  waiting for transfers between devices  35.1 us (29%)
  local copies, waits for them, and re-layouts  6.6 us (6%)
    ppermute x31, starting transfers between devices, swap(): return lax.ppermute(x, axis, [(i, i ^ step) for i in range(count)])  35.9 us
    pallas_call x27, Pallas kernels, run(): pl.pallas_call(without, out_shape=tuple((jax.ShapeDtypeStruct(shape, dtyp...  35.7 us
    ppermute x31, waiting for transfers between devices, swap(): return lax.ppermute(x, axis, [(i, i ^ step) for i in range(count)])  32 us
    unnamed x33, local copies, waits for them, and re-layouts  5.82 us
    ppermute x2, waiting for transfers between devices, border(): lax.ppermute(head, 'row', [(i + 1, i) for i in range(ranks - 1)])  3.16 us
    ppermute x2, starting transfers between devices, border(): up = lax.ppermute(tail, 'row', [(i, i + 1) for i in range(ranks - 1)])  2.68 us
    ppermute x2, starting transfers between devices, border(): lax.ppermute(head, 'row', [(i + 1, i) for i in range(ranks - 1)])  2.58 us
  transfers between devices with their start and end apart: 35, of which 19 were waited for; matrix products, arithmetic and copies ran while one was open for 1% of the time, Pallas kernels for 12%

profile of v8, /device:TPU:0, one launch (start us, length us, event | category | flops | bytes accessed | tf_op | source)
XLA Modules:
  0.0 120.1 jit_solution(14807168634129335140)
XLA Ops:
  1.6 5.1 %collective-permute-start.2 = (bf16[128,256]{1,0:T(8,128)(2,1)S(1)}, bf16[128,256]{1,0:T(8,128)(2,1)S(1)}, u32[]{:S(2)}, u32[]{:S(2)}) collective-permute-start(bf16[128,256]{1,0:T(8,128)(2,1)S(1)} %pack.1), channel_id=1, source_target_pairs={{0,24},{8,16},{16,8},{24,0},{1,25},{9,17},{17,9},{25,1},{2,26},{10... | collective-permute-start | bytes 196616 | tf_op jit(solution)/shard_map/ppermute | solution.py:49
  7.4 1.9 %collective-permute-done.2 = bf16[128,256]{1,0:T(8,128)(2,1)S(1)} collective-permute-done((bf16[128,256]{1,0:T(8,128)(2,1)S(1)}, bf16[128,256]{1,0:T(8,128)(2,1)S(1)}, u32[]{:S(2)}, u32[]{:S(2)}) %collective-permute-start.2) | collective-permute-done | bytes 65568 | tf_op jit(solution)/shard_map/ppermute | solution.py:49
  9.3 3.0 %collective-permute-done.3 = bf16[128,256]{1,0:T(8,128)(2,1)S(1)} collective-permute-done((bf16[128,256]{1,0:T(8,128)(2,1)S(1)}, bf16[128,256]{1,0:T(8,128)(2,1)S(1)}, u32[]{:S(2)}, u32[]{:S(2)}) %collective-permute-start.3) | collective-permute-done | bytes 65568 | tf_op jit(solution)/shard_map/ppermute | solution.py:49
  12.4 2.5 %collective-permute-start.5 = (bf16[4,128,256]{2,1,0:T(8,128)(2,1)S(1)}, bf16[4,128,256]{2,1,0:T(8,128)(2,1)S(1)}, u32[]{:S(2)}, u32[]{:S(2)}) collective-permute-start(bf16[4,128,256]{2,1,0:T(8,128)(2,1)S(1)} %join.3.refs_5_.refs_1_.refs_3_), channel_id=1, source_target_pairs={{0,6},{1,7},{2,4},{3,5},{4,2},{5,3},{6,0},{7,1},{8,14},{9,15},{10,... | collective-permute-start | bytes 786440 | tf_op jit(solution)/shard_map/ppermute | solution.py:49
  19.3 4.6 %copy-done = f32[3,1024,1024]{2,1,0:T(8,128)S(1)} copy-done((f32[3,1024,1024]{2,1,0:T(8,128)S(1)}, f32[3,1024,1024]{2,1,0:T(8,128)}, u32[]{:S(2)}) %copy-start) | copy-done | bytes 12582936
  29.2 2.3 %collective-permute-done.8.refs_4_ = bf16[16,128,256]{2,1,0:T(8,128)(2,1)S(1)} collective-permute-done((bf16[16,128,256]{2,1,0:T(8,128)(2,1)S(1)}, bf16[16,128,256]{2,1,0:T(8,128)(2,1)S(1)}, u32[]{:S(2)}, u32[]{:S(2)}) %collective-permute-start.8) | collective-permute-done | bytes 1048608 | tf_op jit(solution)/shard_map/ppermute | solution.py:49
  32.3 2.1 %collective-permute-start.9 = (bf16[112,256]{1,0:T(8,128)(2,1)S(1)}, bf16[112,256]{1,0:T(8,128)(2,1)S(1)}, u32[]{:S(2)}, u32[]{:S(2)}) collective-permute-start(bf16[112,256]{1,0:T(8,128)(2,1)S(1)} %get-tuple-element.109.refs_2_), channel_id=1, source_target_pairs={{0,2},{1,3},{2,0},{3,1},{4,6},{5,7},{6,4},{7,5},{8,10},{9,11},{10,... | collective-permute-start | bytes 172040 | tf_op jit(solution)/shard_map/ppermute | solution.py:49
  38.5 2.4 %collective-permute-done.11 = bf16[112,256]{1,0:T(8,128)(2,1)S(1)} collective-permute-done((bf16[112,256]{1,0:T(8,128)(2,1)S(1)}, bf16[112,256]{1,0:T(8,128)(2,1)S(1)}, u32[]{:S(2)}, u32[]{:S(2)}) %collective-permute-start.11) | collective-permute-done | bytes 57376 | tf_op jit(solution)/shard_map/ppermute | solution.py:49
  42.4 6.2 %attend.1 = (bf16[896,256]{1,0:T(8,128)(2,1)S(1)}, bf16[448,256]{1,0:T(8,128)(2,1)S(1)}, bf16[896,256]{1,0:T(8,128)(2,1)S(1)}, bf16[896,256]{1,0:T(8,128)(2,1)S(...) custom-call(bf16[448,256]{1,0:T(8,128)(2,1)S(1)} %get-tuple-element.103.refs_1_.refs_0_, ...), custom_call_target="tpu_custom_call" | custom-call | bytes 28800000 | tf_op jit(solution)/shard_map/attend/pallas_call | solution.py:91
  48.7 3.3 %feed.1 = (bf16[448,256]{1,0:T(8,128)(2,1)}, bf16[448,256]{1,0:T(8,128)(2,1)S(1)}, f32[448,256]{1,0:T(8,128)S(1)}, f32[256,1024]{1,0:T(8,128)S(1)}, f32[256,1024...) custom-call(f32[448,256]{1,0:T(8,128)S(1)} %get-tuple-element.112.refs_0_.refs_3_, ...), custom_call_target="tpu_custom_call" | custom-call | bytes 12600000 | tf_op jit(solution)/shard_map/feed/pallas_call | solution.py:91
  51.9 3.8 %attend_back.2 = (bf16[448,128]{1,0:T(8,128)(2,1)S(1)}, f32[256,896]{1,0:T(8,128)S(1)}, f32[256,896]{1,0:T(8,128)S(1)}) custom-call(bf16[448,256]{1,0:T(8,128)(2,1)S(1)} %get-tuple-element.116.refs_0_, bf16[896,256]{1,0:T(8,128)(2,1)S(1)} %get-tuple-element.117.refs_1_, bf16[896,256]{1,0:T(8,128)(2,1)S(1)} %get-tuple-element.118.refs_2_, ...), custom_call_target="tpu_custom_call" | custom-call | bytes 18000000 | tf_op jit(solution)/shard_map/attend_back/pallas_call | solution.py:91
  55.7 4.0 %attend_back.3 = (bf16[448,128]{1,0:T(8,128)(2,1)S(1)}, f32[256,896]{1,0:T(8,128)S(1)}, f32[448,256]{1,0:T(8,128)S(1)}, f32[448,256]{1,0:T(8,128)S(1)}) custom-call(bf16[448,256]{1,0:T(8,128)(2,1)S(1)} %get-tuple-element.116.refs_0_, bf16[896,256]{1,0:T(8,128)(2,1)S(1)} %get-tuple-element.117.refs_1_, bf16[896,256]{1,0:T(8,128)(2,1)S(1)} %get-tuple-element.118.refs_2_, ...), custom_call_target="tpu_custom_call" | custom-call | bytes 18000000 | tf_op jit(solution)/shard_map/attend_back/pallas_call | solution.py:91
  60.0 1.8 %early_turn.1 = (f32[16,64,256]{2,1,0:T(8,128)S(1)}, f32[16,64,256]{2,1,0:T(8,128)S(1)}) custom-call(f32[256,1024]{1,0:T(8,128)S(1)} %get-tuple-element.128.refs_0_, f32[256,1024]{1,0:T(8,128)S(1)} %get-tuple-element.129.refs_1_, bf16[4,256,256]{2,1,0:T(8,128)(2,1)S(1)} %get-tuple-element.130.refs_2_.refs_7_, ...), custom_call_target="tpu_custom_call" | custom-call | bytes 7200000 | tf_op jit(solution)/shard_map/early_turn/pallas_call | solution.py:91
  63.6 1.9 %collective-permute-start.16 = (bf16[112,256]{1,0:T(8,128)(2,1)S(1)}, bf16[112,256]{1,0:T(8,128)(2,1)S(1)}, u32[]{:S(2)}, u32[]{:S(2)}) collective-permute-start(bf16[112,256]{1,0:T(8,128)(2,1)S(1)} %get-tuple-element.137), channel_id=1, source_target_pairs={{0,6},{1,7},{2,4},{3,5},{4,2},{5,3},{6,0},{7,1},{8,14},{9,15},{10,... | collective-permute-start | bytes 172040 | tf_op jit(solution)/shard_map/ppermute | solution.py:49
  66.4 1.9 %middle_turn.1 = (f32[256,256]{1,0:T(8,128)S(1)}, f32[256,256]{1,0:T(8,128)S(1)}, f32[256,512]{1,0:T(8,128)S(1)}, f32[8,256]{1,0:T(8,128)S(1)}) custom-call(bf16[448,256]{1,0:T(8,128)(2,1)S(1)} %get-tuple-element.103.refs_1_.refs_0_, bf16[448,128]{1,0:T(8,128)(2,1)S(1)} %get-tuple-element.123.refs_1_, ...), custom_call_target="tpu_custom_call" | custom-call | bytes 5400000 | tf_op jit(solution)/shard_map/middle_turn/pallas_call | solution.py:91
  68.9 1.8 %keys_back.1 = (f32[16,64,256]{2,1,0:T(8,128)S(1)}, f32[16,64,256]{2,1,0:T(8,128)S(1)}, bf16[112,256]{1,0:T(8,128)(2,1)S(1)}, f32[3,256]{1,0:T(4,128)S(1)}) custom-call(f32[112,256]{1,0:T(8,128)S(1)} %get-tuple-element.134.refs_10_.refs_1_.refs_0_, bf16[112,256]{1,0:T(8,128)(2,1)S(1)} %collective-permute-done.14.refs_1_, ...), custom_call_target="tpu_custom_call" | custom-call | bytes 7200000 | tf_op jit(solution)/shard_map/keys_back/pallas_call | solution.py:91
  80.4 3.2 %collective-permute-done.18.refs_7_.refs_2_ = bf16[64,256]{1,0:T(8,128)(2,1)S(1)} collective-permute-done((bf16[64,256]{1,0:T(8,128)(2,1)S(1)}, bf16[64,256]{1,0:T(8,128)(2,1)S(1)}, u32[]{:S(2)}, u32[]{:S(2)}) %collective-permute-start.18) | collective-permute-done | bytes 32800 | tf_op jit(solution)/shard_map/ppermute | solution.py:875
  83.6 5.3 %collective-permute-done.23.refs_4_ = bf16[544,256]{1,0:T(8,128)(2,1)S(1)} collective-permute-done((bf16[544,256]{1,0:T(8,128)(2,1)S(1)}, bf16[544,256]{1,0:T(8,128)(2,1)S(1)}, u32[]{:S(2)}, u32[]{:S(2)}) %collective-permute-start.23) | collective-permute-done | bytes 278560 | tf_op jit(solution)/shard_map/ppermute | solution.py:49
  91.4 2.2 %collective-permute-start.26 = (bf16[160,256]{1,0:T(8,128)(2,1)S(1)}, bf16[160,256]{1,0:T(8,128)(2,1)S(1)}, u32[]{:S(2)}, u32[]{:S(2)}) collective-permute-start(bf16[160,256]{1,0:T(8,128)(2,1)S(1)} %get-tuple-element.172), channel_id=1, source_target_pairs={{0,16},{8,24},{16,0},{24,8},{1,17},{9,25},{17,1},{25,9},{2,18},{10... | collective-permute-start | bytes 245768 | tf_op jit(solution)/shard_map/ppermute | solution.py:49
  96.3 4.2 %collective-permute-done.26.refs_4_ = bf16[160,256]{1,0:T(8,128)(2,1)S(1)} collective-permute-done((bf16[160,256]{1,0:T(8,128)(2,1)S(1)}, bf16[160,256]{1,0:T(8,128)(2,1)S(1)}, u32[]{:S(2)}, u32[]{:S(2)}) %collective-permute-start.26) | collective-permute-done | bytes 81952 | tf_op jit(solution)/shard_map/ppermute | solution.py:49
  101.3 2.0 %collective-permute-start.28 = (bf16[128,256]{1,0:T(8,128)(2,1)S(1)}, bf16[128,256]{1,0:T(8,128)(2,1)S(1)}, u32[]{:S(2)}, u32[]{:S(2)}) collective-permute-start(bf16[128,256]{1,0:T(8,128)(2,1)S(1)} %get-tuple-element.177.refs_1_), channel_id=1, source_target_pairs={{0,24},{8,16},{16,8},{24,0},{1,25},{9,17},{17,9},{25,1},{2,26},{10... | collective-permute-start | bytes 196616 | tf_op jit(solution)/shard_map/ppermute | solution.py:49
  109.5 1.9 %collective-permute-done.31 = f32[4,128,256]{2,1,0:T(8,128)S(1)} collective-permute-done((f32[4,128,256]{2,1,0:T(8,128)S(1)}, f32[4,128,256]{2,1,0:T(8,128)S(1)}, u32[]{:S(2)}, u32[]{:S(2)}) %collective-permute-start.31) | collective-permute-done | bytes 524320 | tf_op jit(solution)/shard_map/ppermute | solution.py:49
  112.9 2.1 %collective-permute-start.34 = (bf16[128,256]{1,0:T(8,128)(2,1)S(1)}, bf16[128,256]{1,0:T(8,128)(2,1)S(1)}, u32[]{:S(2)}, u32[]{:S(2)}) collective-permute-start(bf16[128,256]{1,0:T(8,128)(2,1)S(1)} %get-tuple-element.186), channel_id=1, source_target_pairs={{0,6},{1,7},{2,4},{3,5},{4,2},{5,3},{6,0},{7,1},{8,14},{9,15},{10,... | collective-permute-start | bytes 196616 | tf_op jit(solution)/shard_map/ppermute | solution.py:49
  115.8 2.6 %collective-permute-done.33.refs_2_ = bf16[128,256]{1,0:T(8,128)(2,1)S(1)} collective-permute-done((bf16[128,256]{1,0:T(8,128)(2,1)S(1)}, bf16[128,256]{1,0:T(8,128)(2,1)S(1)}, u32[]{:S(2)}, u32[]{:S(2)}) %collective-permute-start.33) | collective-permute-done | bytes 65568 | tf_op jit(solution)/shard_map/ppermute | solution.py:49
  (109 shorter events, 47.0 us)
Async XLA Ops:
  1.6 7.7 %collective-permute-start.2 = (bf16[128,256]{1,0:T(8,128)(2,1)S(1)}, bf16[128,256]{1,0:T(8,128)(2,1)S(1)}, u32[]{:S(2)}, u32[]{:S(2)}) collective-permute-start(bf16[128,256]{1,0:T(8,128)(2,1)S(1)} %pack.1), channel_id=1, source_target_pairs={{0,24},{8,16},{16,8},{24,0},{1,25},{9,17},{17,9},{25,1},{2,26},{10... | collective-permute-start | bytes 196616 | tf_op jit(solution)/shard_map/ppermute | solution.py:49
  6.7 5.6 %collective-permute-start.3 = (bf16[128,256]{1,0:T(8,128)(2,1)S(1)}, bf16[128,256]{1,0:T(8,128)(2,1)S(1)}, u32[]{:S(2)}, u32[]{:S(2)}) collective-permute-start(bf16[128,256]{1,0:T(8,128)(2,1)S(1)} %pack.1), channel_id=1, source_target_pairs={{0,16},{8,24},{16,0},{24,8},{1,17},{9,25},{17,1},{25,9},{2,18},{10... | collective-permute-start | bytes 196616 | tf_op jit(solution)/shard_map/ppermute | solution.py:49
  6.7 5.6 %collective-permute-start.4 = (bf16[128,256]{1,0:T(8,128)(2,1)S(1)}, bf16[128,256]{1,0:T(8,128)(2,1)S(1)}, u32[]{:S(2)}, u32[]{:S(2)}) collective-permute-start(bf16[128,256]{1,0:T(8,128)(2,1)S(1)} %pack.1), channel_id=1, source_target_pairs={{0,8},{8,0},{16,24},{24,16},{1,9},{9,1},{17,25},{25,17},{2,10},{10... | collective-permute-start | bytes 196616 | tf_op jit(solution)/shard_map/ppermute | solution.py:49
  12.4 13.8 %collective-permute-start.5 = (bf16[4,128,256]{2,1,0:T(8,128)(2,1)S(1)}, bf16[4,128,256]{2,1,0:T(8,128)(2,1)S(1)}, u32[]{:S(2)}, u32[]{:S(2)}) collective-permute-start(bf16[4,128,256]{2,1,0:T(8,128)(2,1)S(1)} %join.3.refs_5_.refs_1_.refs_3_), channel_id=1, source_target_pairs={{0,6},{1,7},{2,4},{3,5},{4,2},{5,3},{6,0},{7,1},{8,14},{9,15},{10,... | collective-permute-start | bytes 786440 | tf_op jit(solution)/shard_map/ppermute | solution.py:49
  14.9 11.9 %collective-permute-start.6 = (bf16[4,128,256]{2,1,0:T(8,128)(2,1)S(1)}, bf16[4,128,256]{2,1,0:T(8,128)(2,1)S(1)}, u32[]{:S(2)}, u32[]{:S(2)}) collective-permute-start(bf16[4,128,256]{2,1,0:T(8,128)(2,1)S(1)} %join.3.refs_5_.refs_1_.refs_3_), channel_id=1, source_target_pairs={{0,4},{1,5},{2,6},{3,7},{4,0},{5,1},{6,2},{7,3},{8,12},{9,13},{10,... | collective-permute-start | bytes 786440 | tf_op jit(solution)/shard_map/ppermute | solution.py:49
  15.4 12.1 %collective-permute-start.7 = (bf16[4,128,256]{2,1,0:T(8,128)(2,1)S(1)}, bf16[4,128,256]{2,1,0:T(8,128)(2,1)S(1)}, u32[]{:S(2)}, u32[]{:S(2)}) collective-permute-start(bf16[4,128,256]{2,1,0:T(8,128)(2,1)S(1)} %join.3.refs_5_.refs_1_.refs_3_), channel_id=1, source_target_pairs={{0,2},{1,3},{2,0},{3,1},{4,6},{5,7},{6,4},{7,5},{8,10},{9,11},{10,... | collective-permute-start | bytes 786440 | tf_op jit(solution)/shard_map/ppermute | solution.py:49
  16.7 7.8 %collective-permute-start = (bf16[64,256]{1,0:T(8,128)(2,1)S(1)}, bf16[64,256]{1,0:T(8,128)(2,1)S(1)}, u32[]{:S(2)}, u32[]{:S(2)}) collective-permute-start(bf16[64,256]{1,0:T(8,128)(2,1)S(1)} %get-tuple-element.197), channel_id=1, source_target_pairs={{0,1},{1,2},{2,3},{3,4},{4,5},{5,6},{6,7},{8,9},{9,10},{10,11},{11... | collective-permute-start | bytes 98312 | tf_op jit(solution)/shard_map/ppermute | solution.py:874
  18.0 6.5 %collective-permute-start.1 = (bf16[64,256]{1,0:T(8,128)(2,1)S(1)}, bf16[64,256]{1,0:T(8,128)(2,1)S(1)}, u32[]{:S(2)}, u32[]{:S(2)}) collective-permute-start(bf16[64,256]{1,0:T(8,128)(2,1)S(1)} %get-tuple-element.196), channel_id=1, source_target_pairs={{1,0},{2,1},{3,2},{4,3},{5,4},{6,5},{7,6},{9,8},{10,9},{11,10},{12... | collective-permute-start | bytes 98312 | tf_op jit(solution)/shard_map/ppermute | solution.py:875
  35.9 5.1 %collective-permute-start.11 = (bf16[112,256]{1,0:T(8,128)(2,1)S(1)}, bf16[112,256]{1,0:T(8,128)(2,1)S(1)}, u32[]{:S(2)}, u32[]{:S(2)}) collective-permute-start(bf16[112,256]{1,0:T(8,128)(2,1)S(1)} %get-tuple-element.109.refs_2_), channel_id=1, source_target_pairs={{0,6},{1,7},{2,4},{3,5},{4,2},{5,3},{6,0},{7,1},{8,14},{9,15},{10,... | collective-permute-start | bytes 172040 | tf_op jit(solution)/shard_map/ppermute | solution.py:49
  61.9 6.4 %collective-permute-start.14 = (bf16[112,256]{1,0:T(8,128)(2,1)S(1)}, bf16[112,256]{1,0:T(8,128)(2,1)S(1)}, u32[]{:S(2)}, u32[]{:S(2)}) collective-permute-start(bf16[112,256]{1,0:T(8,128)(2,1)S(1)} %get-tuple-element.135), channel_id=1, source_target_pairs={{0,2},{1,3},{2,0},{3,1},{4,6},{5,7},{6,4},{7,5},{8,10},{9,11},{10,... | collective-permute-start | bytes 172040 | tf_op jit(solution)/shard_map/ppermute | solution.py:49
  63.4 5.4 %collective-permute-start.15 = (bf16[112,256]{1,0:T(8,128)(2,1)S(1)}, bf16[112,256]{1,0:T(8,128)(2,1)S(1)}, u32[]{:S(2)}, u32[]{:S(2)}) collective-permute-start(bf16[112,256]{1,0:T(8,128)(2,1)S(1)} %get-tuple-element.136), channel_id=1, source_target_pairs={{0,4},{1,5},{2,6},{3,7},{4,0},{5,1},{6,2},{7,3},{8,12},{9,13},{10,... | collective-permute-start | bytes 172040 | tf_op jit(solution)/shard_map/ppermute | solution.py:49
  63.6 5.2 %collective-permute-start.16 = (bf16[112,256]{1,0:T(8,128)(2,1)S(1)}, bf16[112,256]{1,0:T(8,128)(2,1)S(1)}, u32[]{:S(2)}, u32[]{:S(2)}) collective-permute-start(bf16[112,256]{1,0:T(8,128)(2,1)S(1)} %get-tuple-element.137), channel_id=1, source_target_pairs={{0,6},{1,7},{2,4},{3,5},{4,2},{5,3},{6,0},{7,1},{8,14},{9,15},{10,... | collective-permute-start | bytes 172040 | tf_op jit(solution)/shard_map/ppermute | solution.py:49
  66.0 7.9 %collective-permute-start.21 = (f32[16,64,256]{2,1,0:T(8,128)S(1)}, f32[16,64,256]{2,1,0:T(8,128)S(1)}, u32[]{:S(2)}, u32[]{:S(2)}) collective-permute-start(f32[16,64,256]{2,1,0:T(8,128)S(1)} %get-tuple-element.160), channel_id=1, source_target_pairs={{0,1},{1,0},{2,3},{3,2},{4,5},{5,4},{6,7},{7,6},{8,9},{9,8},{10,11... | collective-permute-start | bytes 3145736 | tf_op jit(solution)/shard_map/ppermute | solution.py:49
  74.1 9.5 %collective-permute-start.22 = (bf16[544,256]{1,0:T(8,128)(2,1)S(1)}, bf16[544,256]{1,0:T(8,128)(2,1)S(1)}, u32[]{:S(2)}, u32[]{:S(2)}) collective-permute-start(bf16[544,256]{1,0:T(8,128)(2,1)S(1)} %get-tuple-element.164), channel_id=1, source_target_pairs={{0,2},{1,3},{2,0},{3,1},{4,6},{5,7},{6,4},{7,5},{8,10},{9,11},{10,... | collective-permute-start | bytes 835592 | tf_op jit(solution)/shard_map/ppermute | solution.py:49
  75.4 13.5 %collective-permute-start.23 = (bf16[544,256]{1,0:T(8,128)(2,1)S(1)}, bf16[544,256]{1,0:T(8,128)(2,1)S(1)}, u32[]{:S(2)}, u32[]{:S(2)}) collective-permute-start(bf16[544,256]{1,0:T(8,128)(2,1)S(1)} %get-tuple-element.165), channel_id=1, source_target_pairs={{0,4},{1,5},{2,6},{3,7},{4,0},{5,1},{6,2},{7,3},{8,12},{9,13},{10,... | collective-permute-start | bytes 835592 | tf_op jit(solution)/shard_map/ppermute | solution.py:49
  76.4 13.7 %collective-permute-start.24 = (bf16[544,256]{1,0:T(8,128)(2,1)S(1)}, bf16[544,256]{1,0:T(8,128)(2,1)S(1)}, u32[]{:S(2)}, u32[]{:S(2)}) collective-permute-start(bf16[544,256]{1,0:T(8,128)(2,1)S(1)} %get-tuple-element.166), channel_id=1, source_target_pairs={{0,6},{1,7},{2,4},{3,5},{4,2},{5,3},{6,0},{7,1},{8,14},{9,15},{10,... | collective-permute-start | bytes 835592 | tf_op jit(solution)/shard_map/ppermute | solution.py:49
  90.3 6.1 %collective-permute-start.25 = (bf16[160,256]{1,0:T(8,128)(2,1)S(1)}, bf16[160,256]{1,0:T(8,128)(2,1)S(1)}, u32[]{:S(2)}, u32[]{:S(2)}) collective-permute-start(bf16[160,256]{1,0:T(8,128)(2,1)S(1)} %get-tuple-element.171), channel_id=1, source_target_pairs={{0,8},{8,0},{16,24},{24,16},{1,9},{9,1},{17,25},{25,17},{2,10},{10... | collective-permute-start | bytes 245768 | tf_op jit(solution)/shard_map/ppermute | solution.py:49
  91.4 9.1 %collective-permute-start.26 = (bf16[160,256]{1,0:T(8,128)(2,1)S(1)}, bf16[160,256]{1,0:T(8,128)(2,1)S(1)}, u32[]{:S(2)}, u32[]{:S(2)}) collective-permute-start(bf16[160,256]{1,0:T(8,128)(2,1)S(1)} %get-tuple-element.172), channel_id=1, source_target_pairs={{0,16},{8,24},{16,0},{24,8},{1,17},{9,25},{17,1},{25,9},{2,18},{10... | collective-permute-start | bytes 245768 | tf_op jit(solution)/shard_map/ppermute | solution.py:49
  93.6 6.9 %collective-permute-start.27 = (bf16[160,256]{1,0:T(8,128)(2,1)S(1)}, bf16[160,256]{1,0:T(8,128)(2,1)S(1)}, u32[]{:S(2)}, u32[]{:S(2)}) collective-permute-start(bf16[160,256]{1,0:T(8,128)(2,1)S(1)} %get-tuple-element.173), channel_id=1, source_target_pairs={{0,24},{8,16},{16,8},{24,0},{1,25},{9,17},{17,9},{25,1},{2,26},{10... | collective-permute-start | bytes 245768 | tf_op jit(solution)/shard_map/ppermute | solution.py:49
  101.3 6.8 %collective-permute-start.28 = (bf16[128,256]{1,0:T(8,128)(2,1)S(1)}, bf16[128,256]{1,0:T(8,128)(2,1)S(1)}, u32[]{:S(2)}, u32[]{:S(2)}) collective-permute-start(bf16[128,256]{1,0:T(8,128)(2,1)S(1)} %get-tuple-element.177.refs_1_), channel_id=1, source_target_pairs={{0,24},{8,16},{16,8},{24,0},{1,25},{9,17},{17,9},{25,1},{2,26},{10... | collective-permute-start | bytes 196616 | tf_op jit(solution)/shard_map/ppermute | solution.py:49
  103.3 5.9 %collective-permute-start.29 = (bf16[128,256]{1,0:T(8,128)(2,1)S(1)}, bf16[128,256]{1,0:T(8,128)(2,1)S(1)}, u32[]{:S(2)}, u32[]{:S(2)}) collective-permute-start(bf16[128,256]{1,0:T(8,128)(2,1)S(1)} %get-tuple-element.177.refs_1_), channel_id=1, source_target_pairs={{0,16},{8,24},{16,0},{24,8},{1,17},{9,25},{17,1},{25,9},{2,18},{10... | collective-permute-start | bytes 196616 | tf_op jit(solution)/shard_map/ppermute | solution.py:49
  104.1 5.0 %collective-permute-start.30 = (bf16[128,256]{1,0:T(8,128)(2,1)S(1)}, bf16[128,256]{1,0:T(8,128)(2,1)S(1)}, u32[]{:S(2)}, u32[]{:S(2)}) collective-permute-start(bf16[128,256]{1,0:T(8,128)(2,1)S(1)} %get-tuple-element.177.refs_1_), channel_id=1, source_target_pairs={{0,8},{8,0},{16,24},{24,16},{1,9},{9,1},{17,25},{25,17},{2,10},{10... | collective-permute-start | bytes 196616 | tf_op jit(solution)/shard_map/ppermute | solution.py:49
  112.9 5.5 %collective-permute-start.33 = (bf16[128,256]{1,0:T(8,128)(2,1)S(1)}, bf16[128,256]{1,0:T(8,128)(2,1)S(1)}, u32[]{:S(2)}, u32[]{:S(2)}) collective-permute-start(bf16[128,256]{1,0:T(8,128)(2,1)S(1)} %get-tuple-element.185), channel_id=1, source_target_pairs={{0,4},{1,5},{2,6},{3,7},{4,0},{5,1},{6,2},{7,3},{8,12},{9,13},{10,... | collective-permute-start | bytes 196616 | tf_op jit(solution)/shard_map/ppermute | solution.py:49
  112.9 5.5 %collective-permute-start.34 = (bf16[128,256]{1,0:T(8,128)(2,1)S(1)}, bf16[128,256]{1,0:T(8,128)(2,1)S(1)}, u32[]{:S(2)}, u32[]{:S(2)}) collective-permute-start(bf16[128,256]{1,0:T(8,128)(2,1)S(1)} %get-tuple-element.186), channel_id=1, source_target_pairs={{0,6},{1,7},{2,4},{3,5},{4,2},{5,3},{6,0},{7,1},{8,14},{9,15},{10,... | collective-permute-start | bytes 196616 | tf_op jit(solution)/shard_map/ppermute | solution.py:49
  (26 other events, 213.3 us)

commit v9 on v8

--- a/solution.py
+++ b/solution.py
@@ -514,46 +514,35 @@
 
 
 def middle_turn_kernel(
-    h1_ref, dq_left, dq_right, out_grad, kn_ref, dkv_left, dkv_right, turned_ref, narrow_ref, pair_ref,
-    query_ref, out_ref, keyval_ref, sums_ref, grad,
+    h1_ref, dq_ref, out_grad, kn_ref, dkv_ref, turned_ref, narrow_ref, pair_ref, query_ref, out_ref, keyval_ref, sums_ref
 ):
-    dq = jnp.concatenate([dq_left[...], dq_right[...]], axis=1)
+    dq = dq_ref[...]
     query_ref[...] = rotate(turned_ref[0], contract(turned(h1_ref[...]), dq, 1, 0), narrow_ref[1])
     out_ref[...] = rotate(turned_ref[2], out_grad[...], narrow_ref[4])
     sums_ref[0:1, :] = col_sum(dq.astype(f32))
     sums_ref[2:8, :] = jnp.zeros((6, 256), f32)
+    high, rest = two_parts(dkv_ref[...])
     ones = jnp.ones((8, kn_ref.shape[0]), bf16)
-    for group, ref in enumerate((dkv_left, dkv_right)):
-        high, rest = two_parts(ref[...])
-        found = contract(high, kn_ref[...], 1, 0) + contract(rest, kn_ref[...], 1, 0)
-        grad[group * 128 : group * 128 + 128, :] = found[0:128]
-        grad[256 + group * 128 : 256 + group * 128 + 128, :] = found[128:256]
-        sums = contract(ones, high[128:256, :], 1, 1) + contract(ones, rest[128:256, :], 1, 1)
-        sums_ref[1:2, group * 128 : group * 128 + 128] = sums[0:1]
-    keyval_ref[...] = rotate_turned(grad[...], narrow_ref[2], pair_ref[...])
-
-
-def back_outputs(group, dq_wide, dkv, keyval_ref, earlier, dq_ref, outs):
+    sums = contract(ones, high[256:512, :], 1, 1) + contract(ones, rest[256:512, :], 1, 1)
+    sums_ref[1:2, :] = sums[0:1]
+    grad = contract(high, kn_ref[...], 1, 0) + contract(rest, kn_ref[...], 1, 0)
+    keyval_ref[...] = rotate_turned(grad, narrow_ref[2], pair_ref[...])
+
+
+def back_outputs(dq_wide, dkv, keyval_ref, dq_ref, keep_ref, send_ref):
     dq_ref[...] = dq_wide[...].astype(bf16)
     keys = dkv.shape[1]
+    half = keys // 2
     span = keys if keys <= 1024 else keys // 8
     for start in range(0, keys, span):
-        at = slice(start, start + span)
-        high, rest = two_parts(dkv[:, at])
-        total = earlier[0][:, at] if earlier else None
-        for base, first in ((0, group * 128), (128, 256 + group * 128)):
-            matrix = keyval_ref[:, first : first + 128]
-            for part in (high, rest):
-                term = contract(matrix, part[base : base + 128, :], 1, 0)
-                total = term if total is None else total + term
-        half = keys // 2
-        if not earlier:
-            outs[0][:, at] = total
-        elif span == keys:
-            outs[0][...] = total[:, 0:half].T
-            outs[1][...] = total[:, half:].T
+        high, rest = two_parts(dkv[:, start : start + span])
+        total = contract(keyval_ref[...], high, 1, 0) + contract(keyval_ref[...], rest, 1, 0)
+        if span == keys:
+            keep_ref[...] = total[:, 0:half].T
+            send_ref[...] = total[:, half:].T
         else:
-            outs[start // half][start % half : start % half + span, :] = total.T
+            out = (keep_ref, send_ref)[start // half]
+            out[start % half : start % half + span, :] = total.T
 
 
 def inner_sum(grad, out, mine):
@@ -561,48 +550,51 @@
 
 
 def attend_back_kept_kernel(
-    group, q_ref, k_ref, v_ref, o_ref, stat_ref, kept_ref, g_ref, keyval_ref, *refs
+    q_ref, k_ref, v_ref, o_ref, stat_ref, kept_ref, g_ref, keyval_ref,
+    dq_ref, dkv, keep_ref, send_ref, dq_wide, dss, qt, gt,
 ):
-    earlier, (dq_ref, dkv, *outs), (dq_wide, dss, qt, gt) = refs[:group], refs[group:-4], refs[-4:]
     scale = 32**-0.5
+    width = q_ref.shape[1]
     lane = lax.broadcasted_iota(jnp.int32, (1, 128), 1)
-    cols = slice(group * 128, group * 128 + 128)
-    grad = g_ref[:, cols]
-    stats = [stat_ref[:, group * 4 + head : group * 4 + head + 1] for head in range(4)]
-    spread_stats = stats[3]
-    for head in range(3):
-        spread_stats = jnp.where(lane // 32 == head, stats[head], spread_stats)
-    qt[...] = turned(q_ref[:, cols])
-    gt[...] = (grad.astype(f32) * spread_stats).T.astype(bf16)
-    for head in range(4):
-        mine = lane // 32 == head
-        keys = jnp.where(mine, k_ref[:, cols], 0)
-        values = jnp.where(mine, v_ref[:, cols], 0)
-        inner = inner_sum(grad, o_ref[:, cols], mine)
-        exponent = kept_ref[group * 4 + head]
-        slope = (contract(grad, values, 1, 1) - inner) * stats[head]
-        dss[...] = (exponent.astype(f32) * slope).astype(bf16)
-        out = contract(dss[...], keys, 1, 0) * scale
-        dq_wide[...] = jnp.where(mine, out, dq_wide[...])
-        dkv[head_rows(head), :] = contract(qt[head_rows(head), :], dss[...], 1, 0) * scale
-        dkv[head_rows(head, 128), :] = contract(gt[head_rows(head), :], exponent, 1, 0)
-    back_outputs(group, dq_wide, dkv, keyval_ref, earlier, dq_ref, outs)
+    qt[...] = turned(q_ref[...])
+    for group in range(2):
+        cols = slice(group * 128, group * 128 + 128)
+        grad = g_ref[:, cols]
+        stats = [stat_ref[:, group * 4 + head : group * 4 + head + 1] for head in range(4)]
+        spread_stats = stats[3]
+        for head in range(3):
+            spread_stats = jnp.where(lane // 32 == head, stats[head], spread_stats)
+        gt[cols, :] = (grad.astype(f32) * spread_stats).T.astype(bf16)
+        for head in range(4):
+            mine = lane // 32 == head
+            keys = jnp.where(mine, k_ref[:, cols], 0)
+            values = jnp.where(mine, v_ref[:, cols], 0)
+            inner = inner_sum(grad, o_ref[:, cols], mine)
+            rows = head_rows(group * 4 + head)
+            exponent = kept_ref[group * 4 + head]
+            slope = (contract(grad, values, 1, 1) - inner) * stats[head]
+            dss[...] = (exponent.astype(f32) * slope).astype(bf16)
+            out = contract(dss[...], keys, 1, 0) * scale
+            dq_wide[:, cols] = jnp.where(mine, out, dq_wide[:, cols])
+            dkv[rows, :] = contract(qt[rows, :], dss[...], 1, 0) * scale
+            dkv[head_rows(group * 4 + head, width), :] = contract(gt[rows, :], exponent, 1, 0)
+    back_outputs(dq_wide, dkv, keyval_ref, dq_ref, keep_ref, send_ref)
 
 
 def attend_back_kernel(
-    step, group, q_ref, k_ref, v_ref, mask_ref, o_ref, stat_ref, g_ref, keyval_ref, *refs
+    step, q_ref, k_ref, v_ref, mask_ref, o_ref, stat_ref, g_ref, keyval_ref,
+    dq_ref, dkv, keep_ref, send_ref, dq_wide, dss, qt, gt, ps,
 ):
-    earlier, (dq_ref, dkv, *outs), (dq_wide, ps, dss, qt, gt) = refs[:group], refs[group:-5], refs[-5:]
-    tokens = q_ref.shape[0]
+    tokens, width = q_ref.shape
     scale = 32**-0.5
     lane = lax.broadcasted_iota(jnp.int32, (1, 128), 1)
     mask = mask_ref[...]
-    cols = slice(group * 128, group * 128 + 128)
-    qt[...] = turned(q_ref[:, cols])
-    gt[...] = turned(g_ref[:, cols])
+    qt[...] = turned(q_ref[...])
+    gt[...] = turned(g_ref[...])
 
     def one_head(head):
-        mine = lane // 32 == head
+        cols = head_columns(head)
+        mine = lane // 32 == head % 4
         keys = jnp.where(mine, k_ref[:, cols], 0)
         values = jnp.where(mine, v_ref[:, cols], 0)
 
@@ -610,21 +602,21 @@
             rows = pl.ds(start, step)
             grad = g_ref[rows, cols]
             inner = inner_sum(grad, o_ref[rows, cols], mine)
-            log = jnp.sum(jnp.where(lane == head + group * 4, stat_ref[rows, :], 0.0), axis=1, keepdims=True)
+            log = jnp.sum(jnp.where(lane == head, stat_ref[rows, :], 0.0), axis=1, keepdims=True)
             scores = contract(q_ref[rows, cols], keys, 1, 1)
             probs = jnp.exp2(scores * (scale * LOG2E) + mask - log)
             grad_scores = (probs * (contract(grad, values, 1, 1) - inner)).astype(bf16)
             ps[rows, :] = probs.astype(bf16)
             dss[rows, :] = grad_scores
             out = contract(grad_scores, keys, 1, 0) * scale
-            dq_wide[rows, :] = jnp.where(mine, out, dq_wide[rows, :])
+            dq_wide[rows, cols] = jnp.where(mine, out, dq_wide[rows, cols])
 
         over_blocks(block, tokens, step)
         dkv[head_rows(head), :] = contract(qt[head_rows(head), :], dss[...], 1, 0) * scale
-        dkv[head_rows(head, 128), :] = contract(gt[head_rows(head), :], ps[...], 1, 0)
-
-    over_heads(one_head, 0, 4, False)
-    back_outputs(group, dq_wide, dkv, keyval_ref, earlier, dq_ref, outs)
+        dkv[head_rows(head, width), :] = contract(gt[head_rows(head), :], ps[...], 1, 0)
+
+    over_heads(one_head, 0, HEADS, False)
+    back_outputs(dq_wide, dkv, keyval_ref, dq_ref, keep_ref, send_ref)
 
 
 def total_of(refs):
@@ -730,11 +722,11 @@
 
 
 def cells_back_kernel(
-    tile_rows, cols, size_ref, dq_left, dq_right, dc_ref, query_ref, reduce_ref, x0_ref, dx1_ref, vec_ref, tile_ref, up_ref, down_ref,
+    tile_rows, cols, size_ref, dq_ref, dc_ref, query_ref, reduce_ref, x0_ref, dx1_ref, vec_ref, tile_ref, up_ref, down_ref,
     feed_sums, key_sums, query_sums, dx0_ref, head_ref, tail_ref, sums_ref, frame,
 ):
     tokens = x0_ref.shape[0]
-    dh1 = contract(dq_left[...], query_ref[:, 0:128], 1, 1) + contract(dq_right[...], query_ref[:, 128:256], 1, 1)
+    dh1 = contract(dq_ref[...], query_ref[...], 1, 1)
     for corner in range(4):
         pick = picked_cells((tokens, dc_ref.shape[0]), 0, size_ref, corner, tile_rows, cols)
         placed = contract(pick, dc_ref[...], 1, 0).astype(bf16)
@@ -797,7 +789,7 @@
     return late + [(j, first + count, rows, blocks) for j, first, rows, blocks in layout(width, EARLY)[0]]
 
 
-def products_kernel(width, chunks, own_narrow, own_wide, keep_ref, send_ref):
+def products_kernel(width, chunks, own_narrow, own_wide, keep_ref, send_ref, whole):
     lefts = {0: (own_narrow, 0), 1: (own_narrow, 1), 2: (own_narrow, 2), 3: (own_narrow, 3), 4: (own_wide, 0), 5: (own_wide, 1)}
     half = keep_ref.shape[0]
     values = chunks[...].astype(f32)
@@ -808,7 +800,8 @@
             part = values[:, at, :].reshape(left.shape[1], width).astype(bf16)
             side = contract(left, part, 1, 0).reshape(2 * half, rows, width)
             keep_ref[:, at, :] = side[:half]
-            send_ref[:, at, :] = side[half:]
+            whole[:, at, :] = side[half:]
+    send_ref[...] = whole[...].astype(bf16)
 
 
 def finish_kernel(
@@ -971,28 +964,20 @@
         mib=12,
         micros=3.5,
     )
-    def back(group, earlier):
-        if kept:
-            body, args, more = functools.partial(attend_back_kept_kernel, group), [q, k, v, o, stat, kept[0]], []
-        else:
-            body, args = functools.partial(attend_back_kernel, step, group), [q, k, v, mask, o, stat]
-            more = [((tokens, keys), bf16)]
-        halves = [((keys // 2, width), f32)] * 2 if earlier else [((width, keys), f32)]
-        return run(
-            "attend_back",
-            body,
-            [((tokens, 128), bf16), ((width, keys), f32)] + halves,
-            args + [do, w_keyval] + earlier,
-            scratch=[((tokens, 128), f32)]
-            + more
-            + [((tokens, keys), bf16), ((128, tokens), bf16), ((128, tokens), bf16)],
-            mib=14 if kept else 60,
-            micros=5.0,
-            after=[dx1],
-        )
-
-    dq_left, dkv_left, dkn_left = back(0, [])
-    dq_right, dkv_right, dkn_keep, dkn_send = back(1, [dkn_left])
+    if kept:
+        body, args, more = attend_back_kept_kernel, [q, k, v, o, stat, kept[0]], []
+    else:
+        body, args = functools.partial(attend_back_kernel, step), [q, k, v, mask, o, stat]
+        more = [((tokens, keys), bf16)]
+    dq, dkv, dkn_keep, dkn_send = run(
+        "attend_back",
+        body,
+        [((tokens, width), bf16), ((2 * width, keys), f32), ((keys // 2, width), f32), ((keys // 2, width), f32)],
+        args + [do, w_keyval],
+        scratch=[((tokens, width), f32), ((tokens, keys), bf16), ((width, tokens), bf16), ((width, tokens), bf16)] + more,
+        mib=16 if kept else 60,
+        micros=8.0,
+    )
     dkn_got = swap(dkn_send, "row", 1)
     half = (shards // 2, early_rows, width)
     early_keep, early_send = run(
@@ -1003,13 +988,13 @@
         scratch=[((width, FF), f32), ((FF, width), f32)],
         mib=10,
         micros=2.0,
-        after=[dq_right],
+        after=[dq],
     )
     early_got = swap(early_send, "row", 1)
     dkn_terms = [dkn_keep, dkn_got]
     for axis, stride, size in xy_parts:
         part, *sends = split_sum(dkn_terms, size, [early_keep])
-        dkn_terms = [part] + [swap(x, axis, j * stride) for j, x in enumerate(sends, 1)]
+        dkn_terms = [part] + [swap(x, axis, j * stride) for j, x in enumerate(sends, 1)][::-1]
     old_chunk, ema_chunk, first_chunk, second_chunk = run(
         "moments",
         functools.partial(moments_kernel, width),
@@ -1021,8 +1006,7 @@
         "middle_turn",
         middle_turn_kernel,
         [((width, width), f32), ((width, width), f32), ((width, 2 * width), f32), ((8, width), f32)],
-        [h1, dq_left, dq_right, out_grad, kn_all, dkv_left, dkv_right, narrow_turned, narrow, pair],
-        scratch=[((2 * width, width), f32)],
+        [h1, dq, out_grad, kn_all, dkv, narrow_turned, narrow, pair],
         micros=1.5,
         mib=12 if kept else 40,
         after=[part],
@@ -1043,7 +1027,7 @@
         functools.partial(cells_back_kernel, rows, cols),
         [((tokens, width), f32), ((64, width), bf16), ((64, width), bf16), ((32, width), f32)],
         [
-            sizes, dq_left, dq_right, dc, w_query, w_reduce, x0, dx1, vec, tile, up_halo, down_halo,
+            sizes, dq, dc, w_query, w_reduce, x0, dx1, vec, tile, up_halo, down_halo,
             feed_sums, key_sums, query_sums,
         ],
         scratch=[frame],
@@ -1092,8 +1076,9 @@
     keep, send = run(
         "products",
         functools.partial(products_kernel, width),
-        [(half, f32), (half, f32)],
+        [(half, f32), (half, bf16)],
         [steps, own_narrow, own_wide],
+        scratch=[(half, f32)],
         micros=1.0,
     )
     terms = [keep.reshape(-1, width), swap(send, "row", 1).reshape(-1, width)]

time: 120 us -> 119 us (level)
    pallas_call x27 -> x26, Pallas kernels: 35.7 us -> 35 us  [run(): pl.pallas_call(without, out_shape=tuple((jax.ShapeDtypeStruct(shape, dtyp...]
where the time goes in v9:
time: 119 us; the launch traced here: 118 us
  starting transfers between devices  41.2 us (35%)
  Pallas kernels  35 us (29%)
  waiting for transfers between devices  34 us (29%)
  local copies, waits for them, and re-layouts  6.6 us (6%)
    ppermute x31, starting transfers between devices, swap(): return lax.ppermute(x, axis, [(i, i ^ step) for i in range(count)])  35.9 us
    pallas_call x26, Pallas kernels, run(): pl.pallas_call(without, out_shape=tuple((jax.ShapeDtypeStruct(shape, dtyp...  35 us
    ppermute x31, waiting for transfers between devices, swap(): return lax.ppermute(x, axis, [(i, i ^ step) for i in range(count)])  30.8 us
    unnamed x33, local copies, waits for them, and re-layouts  5.82 us
    ppermute x2, waiting for transfers between devices, border(): lax.ppermute(head, 'row', [(i + 1, i) for i in range(ranks - 1)])  3.14 us
    ppermute x2, starting transfers between devices, border(): up = lax.ppermute(tail, 'row', [(i, i + 1) for i in range(ranks - 1)])  2.68 us
    ppermute x2, starting transfers between devices, border(): lax.ppermute(head, 'row', [(i + 1, i) for i in range(ranks - 1)])  2.58 us
  transfers between devices with their start and end apart: 35, of which 19 were waited for; matrix products, arithmetic and copies ran while one was open for 1% of the time, Pallas kernels for 12%

profile of v9, /device:TPU:0, one launch (start us, length us, event | category | flops | bytes accessed | tf_op | source)
XLA Modules:
  0.0 118.3 jit_solution(6302574052381016127)
XLA Ops:
  1.6 5.1 %collective-permute-start.2 = (bf16[128,256]{1,0:T(8,128)(2,1)S(1)}, bf16[128,256]{1,0:T(8,128)(2,1)S(1)}, u32[]{:S(2)}, u32[]{:S(2)}) collective-permute-start(bf16[128,256]{1,0:T(8,128)(2,1)S(1)} %pack.1), channel_id=1, source_target_pairs={{0,24},{8,16},{16,8},{24,0},{1,25},{9,17},{17,9},{25,1},{2,26},{10... | collective-permute-start | bytes 196616 | tf_op jit(solution)/shard_map/ppermute | solution.py:49
  7.4 1.9 %collective-permute-done.2 = bf16[128,256]{1,0:T(8,128)(2,1)S(1)} collective-permute-done((bf16[128,256]{1,0:T(8,128)(2,1)S(1)}, bf16[128,256]{1,0:T(8,128)(2,1)S(1)}, u32[]{:S(2)}, u32[]{:S(2)}) %collective-permute-start.2) | collective-permute-done | bytes 65568 | tf_op jit(solution)/shard_map/ppermute | solution.py:49
  9.3 3.0 %collective-permute-done.3 = bf16[128,256]{1,0:T(8,128)(2,1)S(1)} collective-permute-done((bf16[128,256]{1,0:T(8,128)(2,1)S(1)}, bf16[128,256]{1,0:T(8,128)(2,1)S(1)}, u32[]{:S(2)}, u32[]{:S(2)}) %collective-permute-start.3) | collective-permute-done | bytes 65568 | tf_op jit(solution)/shard_map/ppermute | solution.py:49
  12.4 2.5 %collective-permute-start.5 = (bf16[4,128,256]{2,1,0:T(8,128)(2,1)S(1)}, bf16[4,128,256]{2,1,0:T(8,128)(2,1)S(1)}, u32[]{:S(2)}, u32[]{:S(2)}) collective-permute-start(bf16[4,128,256]{2,1,0:T(8,128)(2,1)S(1)} %join.3.refs_5_.refs_1_.refs_3_), channel_id=1, source_target_pairs={{0,6},{1,7},{2,4},{3,5},{4,2},{5,3},{6,0},{7,1},{8,14},{9,15},{10,... | collective-permute-start | bytes 786440 | tf_op jit(solution)/shard_map/ppermute | solution.py:49
  19.3 4.6 %copy-done = f32[3,1024,1024]{2,1,0:T(8,128)S(1)} copy-done((f32[3,1024,1024]{2,1,0:T(8,128)S(1)}, f32[3,1024,1024]{2,1,0:T(8,128)}, u32[]{:S(2)}) %copy-start) | copy-done | bytes 12582936
  29.2 2.3 %collective-permute-done.8.refs_4_ = bf16[16,128,256]{2,1,0:T(8,128)(2,1)S(1)} collective-permute-done((bf16[16,128,256]{2,1,0:T(8,128)(2,1)S(1)}, bf16[16,128,256]{2,1,0:T(8,128)(2,1)S(1)}, u32[]{:S(2)}, u32[]{:S(2)}) %collective-permute-start.8) | collective-permute-done | bytes 1048608 | tf_op jit(solution)/shard_map/ppermute | solution.py:49
  32.3 2.1 %collective-permute-start.9 = (bf16[112,256]{1,0:T(8,128)(2,1)S(1)}, bf16[112,256]{1,0:T(8,128)(2,1)S(1)}, u32[]{:S(2)}, u32[]{:S(2)}) collective-permute-start(bf16[112,256]{1,0:T(8,128)(2,1)S(1)} %get-tuple-element.106.refs_2_), channel_id=1, source_target_pairs={{0,2},{1,3},{2,0},{3,1},{4,6},{5,7},{6,4},{7,5},{8,10},{9,11},{10,... | collective-permute-start | bytes 172040 | tf_op jit(solution)/shard_map/ppermute | solution.py:49
  36.8 1.8 %collective-permute-done.10 = bf16[112,256]{1,0:T(8,128)(2,1)S(1)} collective-permute-done((bf16[112,256]{1,0:T(8,128)(2,1)S(1)}, bf16[112,256]{1,0:T(8,128)(2,1)S(1)}, u32[]{:S(2)}, u32[]{:S(2)}) %collective-permute-start.10) | collective-permute-done | bytes 57376 | tf_op jit(solution)/shard_map/ppermute | solution.py:49
  38.5 2.4 %collective-permute-done.11 = bf16[112,256]{1,0:T(8,128)(2,1)S(1)} collective-permute-done((bf16[112,256]{1,0:T(8,128)(2,1)S(1)}, bf16[112,256]{1,0:T(8,128)(2,1)S(1)}, u32[]{:S(2)}, u32[]{:S(2)}) %collective-permute-start.11) | collective-permute-done | bytes 57376 | tf_op jit(solution)/shard_map/ppermute | solution.py:49
  42.4 6.2 %attend.1 = (bf16[896,256]{1,0:T(8,128)(2,1)S(1)}, bf16[448,256]{1,0:T(8,128)(2,1)S(1)}, bf16[896,256]{1,0:T(8,128)(2,1)S(1)}, bf16[896,256]{1,0:T(8,128)(2,1)S(...) custom-call(bf16[448,256]{1,0:T(8,128)(2,1)S(1)} %get-tuple-element.100.refs_1_.refs_0_, ...), custom_call_target="tpu_custom_call" | custom-call | bytes 28800000 | tf_op jit(solution)/shard_map/attend/pallas_call | solution.py:91
  48.7 3.3 %feed.1 = (bf16[448,256]{1,0:T(8,128)(2,1)}, bf16[448,256]{1,0:T(8,128)(2,1)S(1)}, f32[448,256]{1,0:T(8,128)S(1)}, f32[256,1024]{1,0:T(8,128)S(1)}, f32[256,1024...) custom-call(f32[448,256]{1,0:T(8,128)S(1)} %get-tuple-element.109.refs_0_.refs_3_, ...), custom_call_target="tpu_custom_call" | custom-call | bytes 12600000 | tf_op jit(solution)/shard_map/feed/pallas_call | solution.py:91
  51.9 7.0 %attend_back.1 = (bf16[448,256]{1,0:T(8,128)(2,1)S(1)}, f32[512,896]{1,0:T(8,128)S(1)}, f32[448,256]{1,0:T(8,128)S(1)}, f32[448,256]{1,0:T(8,128)S(1)}) custom-call(bf16[448,256]{1,0:T(8,128)(2,1)S(1)} %get-tuple-element.113.refs_0_, bf16[896,256]{1,0:T(8,128)(2,1)S(1)} %get-tuple-element.114.refs_1_, bf16[896,256]{1,0:T(8,128)(2,1)S(1)} %get-tuple-element.115.refs_2_, ...), custom_call_target="tpu_custom_call" | custom-call | bytes 28800000 | tf_op jit(solution)/shard_map/attend_back/pallas_call | solution.py:91
  59.2 1.8 %early_turn.1 = (f32[16,64,256]{2,1,0:T(8,128)S(1)}, f32[16,64,256]{2,1,0:T(8,128)S(1)}) custom-call(f32[256,1024]{1,0:T(8,128)S(1)} %get-tuple-element.122.refs_0_, f32[256,1024]{1,0:T(8,128)S(1)} %get-tuple-element.123.refs_1_, bf16[4,256,256]{2,1,0:T(8,128)(2,1)S(1)} %get-tuple-element.124.refs_2_.refs_5_, ...), custom_call_target="tpu_custom_call" | custom-call | bytes 7200000 | tf_op jit(solution)/shard_map/early_turn/pallas_call | solution.py:91
  62.3 1.8 %collective-permute-start.15 = (bf16[112,256]{1,0:T(8,128)(2,1)S(1)}, bf16[112,256]{1,0:T(8,128)(2,1)S(1)}, u32[]{:S(2)}, u32[]{:S(2)}) collective-permute-start(bf16[112,256]{1,0:T(8,128)(2,1)S(1)} %get-tuple-element.130), channel_id=1, source_target_pairs={{0,4},{1,5},{2,6},{3,7},{4,0},{5,1},{6,2},{7,3},{8,12},{9,13},{10,... | collective-permute-start | bytes 172040 | tf_op jit(solution)/shard_map/ppermute | solution.py:49
  65.6 2.1 %middle_turn.1 = (f32[256,256]{1,0:T(8,128)S(1)}, f32[256,256]{1,0:T(8,128)S(1)}, f32[256,512]{1,0:T(8,128)S(1)}, f32[8,256]{1,0:T(8,128)S(1)}) custom-call(bf16[448,256]{1,0:T(8,128)(2,1)S(1)} %get-tuple-element.100.refs_1_.refs_0_, bf16[448,256]{1,0:T(8,128)(2,1)S(1)} %get-tuple-element.119.refs_5_.refs_1_, f32[256,256]{1,0:T(8,128)S(1)} %get-tuple-element.134.refs_2_, ...), custom_call_target="tpu_custom_call" | custom-call | bytes 5400000 | tf_op jit(solution)/shard_map/middle_turn/pallas_call | solution.py:91
  70.0 1.8 %cells_back.1 = (f32[448,256]{1,0:T(8,128)S(1)}, bf16[64,256]{1,0:T(8,128)(2,1)S(1)}, bf16[64,256]{1,0:T(8,128)(2,1)S(1)}, f32[32,256]{1,0:T(8,128)S(1)}) custom-call(s32[8,128]{1,0:T(8,128)S(1)} %get-tuple-element.101.refs_0_, bf16[448,256]{1,0:T(8,128)(2,1)S(1)} %get-tuple-element.119.refs_5_.refs_1_, bf16[112,256]{1,0:T(8,128)(2,1)S(1)} %get-tuple-element.142.refs_2_, ...), custom_call_target="tpu_custom_call" | custom-call | bytes 7200000 | tf_op jit(solution)/shard_map/cells_back/pallas_call | solution.py:91
  74.9 2.0 %collective-permute-start.24 = (bf16[544,256]{1,0:T(8,128)(2,1)S(1)}, bf16[544,256]{1,0:T(8,128)(2,1)S(1)}, u32[]{:S(2)}, u32[]{:S(2)}) collective-permute-start(bf16[544,256]{1,0:T(8,128)(2,1)S(1)} %get-tuple-element.160), channel_id=1, source_target_pairs={{0,6},{1,7},{2,4},{3,5},{4,2},{5,3},{6,0},{7,1},{8,14},{9,15},{10,... | collective-permute-start | bytes 835592 | tf_op jit(solution)/shard_map/ppermute | solution.py:49
  79.6 3.1 %collective-permute-done.18.refs_7_.refs_2_ = bf16[64,256]{1,0:T(8,128)(2,1)S(1)} collective-permute-done((bf16[64,256]{1,0:T(8,128)(2,1)S(1)}, bf16[64,256]{1,0:T(8,128)(2,1)S(1)}, u32[]{:S(2)}, u32[]{:S(2)}) %collective-permute-start.18) | collective-permute-done | bytes 32800 | tf_op jit(solution)/shard_map/ppermute | solution.py:868
  82.9 6.2 %collective-permute-done.23.refs_4_ = bf16[544,256]{1,0:T(8,128)(2,1)S(1)} collective-permute-done((bf16[544,256]{1,0:T(8,128)(2,1)S(1)}, bf16[544,256]{1,0:T(8,128)(2,1)S(1)}, u32[]{:S(2)}, u32[]{:S(2)}) %collective-permute-start.23) | collective-permute-done | bytes 278560 | tf_op jit(solution)/shard_map/ppermute | solution.py:49
  90.4 2.2 %collective-permute-start.26 = (bf16[160,256]{1,0:T(8,128)(2,1)S(1)}, bf16[160,256]{1,0:T(8,128)(2,1)S(1)}, u32[]{:S(2)}, u32[]{:S(2)}) collective-permute-start(bf16[160,256]{1,0:T(8,128)(2,1)S(1)} %get-tuple-element.166), channel_id=1, source_target_pairs={{0,16},{8,24},{16,0},{24,8},{1,17},{9,25},{17,1},{25,9},{2,18},{10... | collective-permute-start | bytes 245768 | tf_op jit(solution)/shard_map/ppermute | solution.py:49
  95.3 4.4 %collective-permute-done.26.refs_4_ = bf16[160,256]{1,0:T(8,128)(2,1)S(1)} collective-permute-done((bf16[160,256]{1,0:T(8,128)(2,1)S(1)}, bf16[160,256]{1,0:T(8,128)(2,1)S(1)}, u32[]{:S(2)}, u32[]{:S(2)}) %collective-permute-start.26) | collective-permute-done | bytes 81952 | tf_op jit(solution)/shard_map/ppermute | solution.py:49
  100.4 2.1 %collective-permute-start.28 = (bf16[128,256]{1,0:T(8,128)(2,1)S(1)}, bf16[128,256]{1,0:T(8,128)(2,1)S(1)}, u32[]{:S(2)}, u32[]{:S(2)}) collective-permute-start(bf16[128,256]{1,0:T(8,128)(2,1)S(1)} %get-tuple-element.171.refs_1_), channel_id=1, source_target_pairs={{0,24},{8,16},{16,8},{24,0},{1,25},{9,17},{17,9},{25,1},{2,26},{10... | collective-permute-start | bytes 196616 | tf_op jit(solution)/shard_map/ppermute | solution.py:49
  111.4 2.5 %collective-permute-start.34 = (bf16[128,256]{1,0:T(8,128)(2,1)S(1)}, bf16[128,256]{1,0:T(8,128)(2,1)S(1)}, u32[]{:S(2)}, u32[]{:S(2)}) collective-permute-start(bf16[128,256]{1,0:T(8,128)(2,1)S(1)} %get-tuple-element.180), channel_id=1, source_target_pairs={{0,6},{1,7},{2,4},{3,5},{4,2},{5,3},{6,0},{7,1},{8,14},{9,15},{10,... | collective-permute-start | bytes 196616 | tf_op jit(solution)/shard_map/ppermute | solution.py:49
  116.6 1.7 %finish.1 = (f32[1,32768]{1,0:T(1,128)}, f32[1,32768]{1,0:T(1,128)}) custom-call(f32[128,256]{1,0:T(8,128)S(1)} %get-tuple-element.177.refs_0_, bf16[128,256]{1,0:T(8,128)(2,1)S(1)} %collective-permute-done.32.refs_1_, bf16[128,256]{1,0:T(8,128)(2,1)S(1)} %collective-permute-done.33.refs_2_, bf16[128,256]{1,0:T(8,128)(2,1)S(1)} %collective-permute-done.34.refs_3_, ...), custom_call_target="tpu_custom_call" | custom-call | bytes 5400000 | tf_op jit(solution)/shard_map/finish/pallas_call | solution.py:91
  (108 shorter events, 43.3 us)
Async XLA Ops:
  1.6 7.7 %collective-permute-start.2 = (bf16[128,256]{1,0:T(8,128)(2,1)S(1)}, bf16[128,256]{1,0:T(8,128)(2,1)S(1)}, u32[]{:S(2)}, u32[]{:S(2)}) collective-permute-start(bf16[128,256]{1,0:T(8,128)(2,1)S(1)} %pack.1), channel_id=1, source_target_pairs={{0,24},{8,16},{16,8},{24,0},{1,25},{9,17},{17,9},{25,1},{2,26},{10... | collective-permute-start | bytes 196616 | tf_op jit(solution)/shard_map/ppermute | solution.py:49
  6.7 5.6 %collective-permute-start.3 = (bf16[128,256]{1,0:T(8,128)(2,1)S(1)}, bf16[128,256]{1,0:T(8,128)(2,1)S(1)}, u32[]{:S(2)}, u32[]{:S(2)}) collective-permute-start(bf16[128,256]{1,0:T(8,128)(2,1)S(1)} %pack.1), channel_id=1, source_target_pairs={{0,16},{8,24},{16,0},{24,8},{1,17},{9,25},{17,1},{25,9},{2,18},{10... | collective-permute-start | bytes 196616 | tf_op jit(solution)/shard_map/ppermute | solution.py:49
  6.7 5.6 %collective-permute-start.4 = (bf16[128,256]{1,0:T(8,128)(2,1)S(1)}, bf16[128,256]{1,0:T(8,128)(2,1)S(1)}, u32[]{:S(2)}, u32[]{:S(2)}) collective-permute-start(bf16[128,256]{1,0:T(8,128)(2,1)S(1)} %pack.1), channel_id=1, source_target_pairs={{0,8},{8,0},{16,24},{24,16},{1,9},{9,1},{17,25},{25,17},{2,10},{10... | collective-permute-start | bytes 196616 | tf_op jit(solution)/shard_map/ppermute | solution.py:49
  12.4 13.8 %collective-permute-start.5 = (bf16[4,128,256]{2,1,0:T(8,128)(2,1)S(1)}, bf16[4,128,256]{2,1,0:T(8,128)(2,1)S(1)}, u32[]{:S(2)}, u32[]{:S(2)}) collective-permute-start(bf16[4,128,256]{2,1,0:T(8,128)(2,1)S(1)} %join.3.refs_5_.refs_1_.refs_3_), channel_id=1, source_target_pairs={{0,6},{1,7},{2,4},{3,5},{4,2},{5,3},{6,0},{7,1},{8,14},{9,15},{10,... | collective-permute-start | bytes 786440 | tf_op jit(solution)/shard_map/ppermute | solution.py:49
  14.9 11.9 %collective-permute-start.6 = (bf16[4,128,256]{2,1,0:T(8,128)(2,1)S(1)}, bf16[4,128,256]{2,1,0:T(8,128)(2,1)S(1)}, u32[]{:S(2)}, u32[]{:S(2)}) collective-permute-start(bf16[4,128,256]{2,1,0:T(8,128)(2,1)S(1)} %join.3.refs_5_.refs_1_.refs_3_), channel_id=1, source_target_pairs={{0,4},{1,5},{2,6},{3,7},{4,0},{5,1},{6,2},{7,3},{8,12},{9,13},{10,... | collective-permute-start | bytes 786440 | tf_op jit(solution)/shard_map/ppermute | solution.py:49
  15.4 12.1 %collective-permute-start.7 = (bf16[4,128,256]{2,1,0:T(8,128)(2,1)S(1)}, bf16[4,128,256]{2,1,0:T(8,128)(2,1)S(1)}, u32[]{:S(2)}, u32[]{:S(2)}) collective-permute-start(bf16[4,128,256]{2,1,0:T(8,128)(2,1)S(1)} %join.3.refs_5_.refs_1_.refs_3_), channel_id=1, source_target_pairs={{0,2},{1,3},{2,0},{3,1},{4,6},{5,7},{6,4},{7,5},{8,10},{9,11},{10,... | collective-permute-start | bytes 786440 | tf_op jit(solution)/shard_map/ppermute | solution.py:49
  16.7 7.8 %collective-permute-start = (bf16[64,256]{1,0:T(8,128)(2,1)S(1)}, bf16[64,256]{1,0:T(8,128)(2,1)S(1)}, u32[]{:S(2)}, u32[]{:S(2)}) collective-permute-start(bf16[64,256]{1,0:T(8,128)(2,1)S(1)} %get-tuple-element.191), channel_id=1, source_target_pairs={{0,1},{1,2},{2,3},{3,4},{4,5},{5,6},{6,7},{8,9},{9,10},{10,11},{11... | collective-permute-start | bytes 98312 | tf_op jit(solution)/shard_map/ppermute | solution.py:867
  18.0 6.5 %collective-permute-start.1 = (bf16[64,256]{1,0:T(8,128)(2,1)S(1)}, bf16[64,256]{1,0:T(8,128)(2,1)S(1)}, u32[]{:S(2)}, u32[]{:S(2)}) collective-permute-start(bf16[64,256]{1,0:T(8,128)(2,1)S(1)} %get-tuple-element.190), channel_id=1, source_target_pairs={{1,0},{2,1},{3,2},{4,3},{5,4},{6,5},{7,6},{9,8},{10,9},{11,10},{12... | collective-permute-start | bytes 98312 | tf_op jit(solution)/shard_map/ppermute | solution.py:868
  35.9 5.1 %collective-permute-start.11 = (bf16[112,256]{1,0:T(8,128)(2,1)S(1)}, bf16[112,256]{1,0:T(8,128)(2,1)S(1)}, u32[]{:S(2)}, u32[]{:S(2)}) collective-permute-start(bf16[112,256]{1,0:T(8,128)(2,1)S(1)} %get-tuple-element.106.refs_2_), channel_id=1, source_target_pairs={{0,6},{1,7},{2,4},{3,5},{4,2},{5,3},{6,0},{7,1},{8,14},{9,15},{10,... | collective-permute-start | bytes 172040 | tf_op jit(solution)/shard_map/ppermute | solution.py:49
  61.1 6.6 %collective-permute-start.14 = (bf16[112,256]{1,0:T(8,128)(2,1)S(1)}, bf16[112,256]{1,0:T(8,128)(2,1)S(1)}, u32[]{:S(2)}, u32[]{:S(2)}) collective-permute-start(bf16[112,256]{1,0:T(8,128)(2,1)S(1)} %get-tuple-element.129), channel_id=1, source_target_pairs={{0,6},{1,7},{2,4},{3,5},{4,2},{5,3},{6,0},{7,1},{8,14},{9,15},{10,... | collective-permute-start | bytes 172040 | tf_op jit(solution)/shard_map/ppermute | solution.py:49
  62.3 5.4 %collective-permute-start.15 = (bf16[112,256]{1,0:T(8,128)(2,1)S(1)}, bf16[112,256]{1,0:T(8,128)(2,1)S(1)}, u32[]{:S(2)}, u32[]{:S(2)}) collective-permute-start(bf16[112,256]{1,0:T(8,128)(2,1)S(1)} %get-tuple-element.130), channel_id=1, source_target_pairs={{0,4},{1,5},{2,6},{3,7},{4,0},{5,1},{6,2},{7,3},{8,12},{9,13},{10,... | collective-permute-start | bytes 172040 | tf_op jit(solution)/shard_map/ppermute | solution.py:49
  65.2 8.0 %collective-permute-start.21 = (f32[16,64,256]{2,1,0:T(8,128)S(1)}, f32[16,64,256]{2,1,0:T(8,128)S(1)}, u32[]{:S(2)}, u32[]{:S(2)}) collective-permute-start(f32[16,64,256]{2,1,0:T(8,128)S(1)} %get-tuple-element.154), channel_id=1, source_target_pairs={{0,1},{1,0},{2,3},{3,2},{4,5},{5,4},{6,7},{7,6},{8,9},{9,8},{10,11... | collective-permute-start | bytes 3145736 | tf_op jit(solution)/shard_map/ppermute | solution.py:49
  73.4 9.5 %collective-permute-start.22 = (bf16[544,256]{1,0:T(8,128)(2,1)S(1)}, bf16[544,256]{1,0:T(8,128)(2,1)S(1)}, u32[]{:S(2)}, u32[]{:S(2)}) collective-permute-start(bf16[544,256]{1,0:T(8,128)(2,1)S(1)} %get-tuple-element.158), channel_id=1, source_target_pairs={{0,2},{1,3},{2,0},{3,1},{4,6},{5,7},{6,4},{7,5},{8,10},{9,11},{10,... | collective-permute-start | bytes 835592 | tf_op jit(solution)/shard_map/ppermute | solution.py:49
  74.7 14.4 %collective-permute-start.23 = (bf16[544,256]{1,0:T(8,128)(2,1)S(1)}, bf16[544,256]{1,0:T(8,128)(2,1)S(1)}, u32[]{:S(2)}, u32[]{:S(2)}) collective-permute-start(bf16[544,256]{1,0:T(8,128)(2,1)S(1)} %get-tuple-element.159), channel_id=1, source_target_pairs={{0,4},{1,5},{2,6},{3,7},{4,0},{5,1},{6,2},{7,3},{8,12},{9,13},{10,... | collective-permute-start | bytes 835592 | tf_op jit(solution)/shard_map/ppermute | solution.py:49
  74.9 14.2 %collective-permute-start.24 = (bf16[544,256]{1,0:T(8,128)(2,1)S(1)}, bf16[544,256]{1,0:T(8,128)(2,1)S(1)}, u32[]{:S(2)}, u32[]{:S(2)}) collective-permute-start(bf16[544,256]{1,0:T(8,128)(2,1)S(1)} %get-tuple-element.160), channel_id=1, source_target_pairs={{0,6},{1,7},{2,4},{3,5},{4,2},{5,3},{6,0},{7,1},{8,14},{9,15},{10,... | collective-permute-start | bytes 835592 | tf_op jit(solution)/shard_map/ppermute | solution.py:49
  89.2 6.1 %collective-permute-start.25 = (bf16[160,256]{1,0:T(8,128)(2,1)S(1)}, bf16[160,256]{1,0:T(8,128)(2,1)S(1)}, u32[]{:S(2)}, u32[]{:S(2)}) collective-permute-start(bf16[160,256]{1,0:T(8,128)(2,1)S(1)} %get-tuple-element.165), channel_id=1, source_target_pairs={{0,8},{8,0},{16,24},{24,16},{1,9},{9,1},{17,25},{25,17},{2,10},{10... | collective-permute-start | bytes 245768 | tf_op jit(solution)/shard_map/ppermute | solution.py:49
  90.4 9.3 %collective-permute-start.26 = (bf16[160,256]{1,0:T(8,128)(2,1)S(1)}, bf16[160,256]{1,0:T(8,128)(2,1)S(1)}, u32[]{:S(2)}, u32[]{:S(2)}) collective-permute-start(bf16[160,256]{1,0:T(8,128)(2,1)S(1)} %get-tuple-element.166), channel_id=1, source_target_pairs={{0,16},{8,24},{16,0},{24,8},{1,17},{9,25},{17,1},{25,9},{2,18},{10... | collective-permute-start | bytes 245768 | tf_op jit(solution)/shard_map/ppermute | solution.py:49
  92.6 7.1 %collective-permute-start.27 = (bf16[160,256]{1,0:T(8,128)(2,1)S(1)}, bf16[160,256]{1,0:T(8,128)(2,1)S(1)}, u32[]{:S(2)}, u32[]{:S(2)}) collective-permute-start(bf16[160,256]{1,0:T(8,128)(2,1)S(1)} %get-tuple-element.167), channel_id=1, source_target_pairs={{0,24},{8,16},{16,8},{24,0},{1,25},{9,17},{17,9},{25,1},{2,26},{10... | collective-permute-start | bytes 245768 | tf_op jit(solution)/shard_map/ppermute | solution.py:49
  100.4 6.8 %collective-permute-start.28 = (bf16[128,256]{1,0:T(8,128)(2,1)S(1)}, bf16[128,256]{1,0:T(8,128)(2,1)S(1)}, u32[]{:S(2)}, u32[]{:S(2)}) collective-permute-start(bf16[128,256]{1,0:T(8,128)(2,1)S(1)} %get-tuple-element.171.refs_1_), channel_id=1, source_target_pairs={{0,24},{8,16},{16,8},{24,0},{1,25},{9,17},{17,9},{25,1},{2,26},{10... | collective-permute-start | bytes 196616 | tf_op jit(solution)/shard_map/ppermute | solution.py:49
  102.5 5.9 %collective-permute-start.29 = (bf16[128,256]{1,0:T(8,128)(2,1)S(1)}, bf16[128,256]{1,0:T(8,128)(2,1)S(1)}, u32[]{:S(2)}, u32[]{:S(2)}) collective-permute-start(bf16[128,256]{1,0:T(8,128)(2,1)S(1)} %get-tuple-element.171.refs_1_), channel_id=1, source_target_pairs={{0,16},{8,24},{16,0},{24,8},{1,17},{9,25},{17,1},{25,9},{2,18},{10... | collective-permute-start | bytes 196616 | tf_op jit(solution)/shard_map/ppermute | solution.py:49
  103.4 5.0 %collective-permute-start.30 = (bf16[128,256]{1,0:T(8,128)(2,1)S(1)}, bf16[128,256]{1,0:T(8,128)(2,1)S(1)}, u32[]{:S(2)}, u32[]{:S(2)}) collective-permute-start(bf16[128,256]{1,0:T(8,128)(2,1)S(1)} %get-tuple-element.171.refs_1_), channel_id=1, source_target_pairs={{0,8},{8,0},{16,24},{24,16},{1,9},{9,1},{17,25},{25,17},{2,10},{10... | collective-permute-start | bytes 196616 | tf_op jit(solution)/shard_map/ppermute | solution.py:49
  110.3 4.5 %collective-permute-start.32 = (bf16[128,256]{1,0:T(8,128)(2,1)S(1)}, bf16[128,256]{1,0:T(8,128)(2,1)S(1)}, u32[]{:S(2)}, u32[]{:S(2)}) collective-permute-start(bf16[128,256]{1,0:T(8,128)(2,1)S(1)} %get-tuple-element.178), channel_id=1, source_target_pairs={{0,2},{1,3},{2,0},{3,1},{4,6},{5,7},{6,4},{7,5},{8,10},{9,11},{10,... | collective-permute-start | bytes 196616 | tf_op jit(solution)/shard_map/ppermute | solution.py:49
  110.9 5.0 %collective-permute-start.33 = (bf16[128,256]{1,0:T(8,128)(2,1)S(1)}, bf16[128,256]{1,0:T(8,128)(2,1)S(1)}, u32[]{:S(2)}, u32[]{:S(2)}) collective-permute-start(bf16[128,256]{1,0:T(8,128)(2,1)S(1)} %get-tuple-element.179), channel_id=1, source_target_pairs={{0,4},{1,5},{2,6},{3,7},{4,0},{5,1},{6,2},{7,3},{8,12},{9,13},{10,... | collective-permute-start | bytes 196616 | tf_op jit(solution)/shard_map/ppermute | solution.py:49
  111.4 5.2 %collective-permute-start.34 = (bf16[128,256]{1,0:T(8,128)(2,1)S(1)}, bf16[128,256]{1,0:T(8,128)(2,1)S(1)}, u32[]{:S(2)}, u32[]{:S(2)}) collective-permute-start(bf16[128,256]{1,0:T(8,128)(2,1)S(1)} %get-tuple-element.180), channel_id=1, source_target_pairs={{0,6},{1,7},{2,4},{3,5},{4,2},{5,3},{6,0},{7,1},{8,14},{9,15},{10,... | collective-permute-start | bytes 196616 | tf_op jit(solution)/shard_map/ppermute | solution.py:49
  (26 other events, 212.8 us)

commit v10 on v9

--- a/solution.py
+++ b/solution.py
@@ -268,13 +268,30 @@
         start += ref.shape[0]
 
 
+def join_apart_kernel(rows, *refs):
+    first, second = refs[-2:]
+    start = 0
+    for ref in refs[-3::-1]:
+        first[start : start + ref.shape[0]] = ref[:, 0:rows]
+        second[start : start + ref.shape[0]] = ref[:, rows:]
+        start += ref.shape[0]
+
+
+def join_apart(pieces, rows, after):
+    count, all_rows, width = sum(x.shape[0] for x in pieces), pieces[0].shape[1], pieces[0].shape[2]
+    outs = [((count, rows, width), bf16), ((count, all_rows - rows, width), bf16)]
+    return run("join", functools.partial(join_apart_kernel, rows), outs, list(pieces)[::-1], micros=0.4, after=after)
+
+
 def join(pieces, after=()):
     shape = (sum(x.shape[0] for x in pieces),) + pieces[0].shape[1:]
     return run("join", join_kernel, [(shape, pieces[0].dtype)], list(pieces)[::-1], micros=0.4, after=after)[0]
 
 
-def unpack(pieces, group, mats, base=0):
-    parts = [(j, first + base, rows, blocks) for j, first, rows, blocks in layout(256, group)[0]]
+def unpack(pieces, group, mats):
+    parts, start = [], min(part[1] for part in both_groups(256) if part[0] in group)
+    for j in group:
+        parts += [(j, first - start, rows, blocks) for k, first, rows, blocks in both_groups(256) if k == j]
     done = 0
     for piece in pieces:
 
@@ -283,6 +300,13 @@
 
         each_block(piece.shape[0], body)
         done += piece.shape[0]
+
+
+def weights_kernel(group, near_ref, far_ref, *refs):
+    count = len(group)
+    unpack((near_ref, far_ref), group, refs[count:])
+    for out_ref, ref in zip(refs[:count], refs[count:]):
+        out_ref[...] = ref[...].astype(bf16)
 
 
 def shifted_frame(frame_ref, tile_ref, up_ref, down_ref):
@@ -343,14 +367,10 @@
 
 def keys_kernel(
     tile_rows, cols, size_ref, h1_ref, vec_ref, near_ref, far_ref,
-    reduce_ref, keyval_ref, query_ref, out_ref, blocks_ref, c_ref, kn_ref,
-    reduce_wide, keyval_wide, query_wide, out_wide,
+    reduce_ref, blocks_ref, c_ref, kn_ref, reduce_wide,
 ):
-    unpack((near_ref, far_ref), LATE, (reduce_wide, keyval_wide, query_wide, out_wide))
+    unpack((near_ref, far_ref), (5,), (reduce_wide,))
     reduce_ref[...] = reduce_wide[...].astype(bf16)
-    keyval_ref[...] = keyval_wide[...].astype(bf16)
-    query_ref[...] = query_wide[...].astype(bf16)
-    out_ref[...] = out_wide[...].astype(bf16)
     keys = c_ref.shape[0]
     for corner in range(4):
         pick = picked_cells((keys, h1_ref.shape[0]), 1, size_ref, corner, tile_rows, cols)
@@ -445,12 +465,9 @@
 
 
 def feed_kernel(
-    o_ref, x0_ref, out_ref, near_ref, far_ref, vec_ref, dy_ref,
-    y_ref, do_ref, dx1_ref, up_grad, down_grad, out_grad, sums_ref, up_ref, down_ref, up_wide, down_wide,
+    o_ref, x0_ref, out_ref, up_ref, down_ref, vec_ref, dy_ref,
+    y_ref, do_ref, dx1_ref, up_grad, down_grad, out_grad, sums_ref,
 ):
-    unpack((near_ref, far_ref), EARLY, (up_wide, down_wide), layout(256, LATE)[1])
-    up_ref[...] = up_wide[...].astype(bf16)
-    down_ref[...] = down_wide[...].astype(bf16)
     o = o_ref[...].astype(bf16)
     x1 = x0_ref[...] + (contract(o, out_ref[...], 1, 0) + vec_ref[17:18, :])
     unit, inverse = norm_parts(x1)
@@ -900,22 +917,22 @@
     all_near = line
     for axis, stride, size in gather_groups:
         pieces = [all_near] + [swap(all_near, axis, j * stride) for j in range(1, size)]
-        all_near = join(pieces, after=[wide_done, vec])
-    all_far = swap(all_near, "row", 1)
-    w_reduce, w_keyval, w_query, w_out, blocks, c, kn = run(
+        if stride * size == ranks:
+            near, rest_near = join_apart(pieces, width * 4 // shards, [wide_done, vec])
+        else:
+            all_near = join(pieces, after=[wide_done, vec])
+    far, rest_far = swap(near, "row", 1), swap(rest_near, "row", 1)
+    w_reduce, blocks, c, kn = run(
         "keys",
         functools.partial(keys_kernel, rows, cols),
         [
             ((4 * width, width), bf16),
-            ((width, 2 * width), bf16),
-            ((width, width), bf16),
-            ((width, width), bf16),
             ((own_keys, 4 * width), bf16),
             ((own_keys, width), f32),
             ((own_keys, width), bf16),
         ],
-        [sizes, h1, vec, all_near, all_far],
-        scratch=[((4 * width, width), f32), ((width, 2 * width), f32), ((width, width), f32), ((width, width), f32)],
+        [sizes, h1, vec, near, far],
+        scratch=[((4 * width, width), f32)],
         micros=1.5,
     )
     narrow, narrow_turned, pair, own_narrow = run(
@@ -931,6 +948,16 @@
         micros=1.5,
         after=[kn],
     )
+    group = (1, 0, 2, 3, 4)
+    w_keyval, w_query, w_out, w_up, w_down = run(
+        "weights",
+        functools.partial(weights_kernel, group),
+        [(matrix_shapes(width, FF)[j], bf16) for j in group],
+        [rest_near, rest_far],
+        scratch=[(matrix_shapes(width, FF)[j], f32) for j in group],
+        micros=1.0,
+        after=[kn],
+    )
     kn_near = side_by_side(kn, gather_groups)
     kn_far = swap(kn_near, "row", 1)
 
@@ -959,8 +986,7 @@
             ((width, width), f32),
             (vectors.shape, f32),
         ],
-        [o, x0, w_out, all_near, all_far, vec, dy],
-        scratch=[((width, FF), bf16), ((FF, width), bf16), ((width, FF), f32), ((FF, width), f32)],
+        [o, x0, w_out, w_up, w_down, vec, dy],
         mib=12,
         micros=3.5,
     )

time: 119 us -> 117 us (0.983)
  waiting for transfers between devices: 34 us -> 32.4 us
    ppermute x31 -> x32, waiting for transfers between devices: 30.8 us -> 29.2 us  [swap(): return lax.ppermute(x, axis, [(i, i ^ step) for i in range(count)])]
    pallas_call x26 -> x27, Pallas kernels: 35 us -> 35.2 us  [run(): pl.pallas_call(without, out_shape=tuple((jax.ShapeDtypeStruct(shape, dtyp...]
    ppermute x31 -> x32, starting transfers between devices: 35.9 us -> 36.1 us  [swap(): return lax.ppermute(x, axis, [(i, i ^ step) for i in range(count)])]
  transfers between devices with their start and end apart: 35 -> 36, of which waited for: 19 -> 19; matrix products, arithmetic and copies ran while one was open for 1% -> 1% of each run, Pallas kernels for 12% -> 13%
where the time goes in v10:
time: 117 us
  starting transfers between devices  41.4 us (35%)
  Pallas kernels  35.2 us (30%)
  waiting for transfers between devices  32.4 us (28%)
  local copies, waits for them, and re-layouts  6.6 us (6%)
    ppermute x32, starting transfers between devices, swap(): return lax.ppermute(x, axis, [(i, i ^ step) for i in range(count)])  36.1 us
    pallas_call x27, Pallas kernels, run(): pl.pallas_call(without, out_shape=tuple((jax.ShapeDtypeStruct(shape, dtyp...  35.2 us
    ppermute x32, waiting for transfers between devices, swap(): return lax.ppermute(x, axis, [(i, i ^ step) for i in range(count)])  29.2 us
    unnamed x33, local copies, waits for them, and re-layouts  5.82 us
    ppermute x2, waiting for transfers between devices, border(): lax.ppermute(head, 'row', [(i + 1, i) for i in range(ranks - 1)])  3.14 us
    ppermute x2, starting transfers between devices, border(): up = lax.ppermute(tail, 'row', [(i, i + 1) for i in range(ranks - 1)])  2.68 us
    ppermute x2, starting transfers between devices, border(): lax.ppermute(head, 'row', [(i + 1, i) for i in range(ranks - 1)])  2.58 us
  transfers between devices with their start and end apart: 36, of which 19 were waited for; matrix products, arithmetic and copies ran while one was open for 1% of the time, Pallas kernels for 13%

profile of v10, /device:TPU:0, one launch (start us, length us, event | category | flops | bytes accessed | tf_op | source)
XLA Modules:
  0.0 117.2 jit_solution(11620540176069588482)
XLA Ops:
  1.6 5.1 %collective-permute-start.2 = (bf16[128,256]{1,0:T(8,128)(2,1)S(1)}, bf16[128,256]{1,0:T(8,128)(2,1)S(1)}, u32[]{:S(2)}, u32[]{:S(2)}) collective-permute-start(bf16[128,256]{1,0:T(8,128)(2,1)S(1)} %pack.1), channel_id=1, source_target_pairs={{0,24},{8,16},{16,8},{24,0},{1,25},{9,17},{17,9},{25,1},{2,26},{10... | collective-permute-start | bytes 196616 | tf_op jit(solution)/shard_map/ppermute | solution.py:49
  7.4 1.9 %collective-permute-done.2 = bf16[128,256]{1,0:T(8,128)(2,1)S(1)} collective-permute-done((bf16[128,256]{1,0:T(8,128)(2,1)S(1)}, bf16[128,256]{1,0:T(8,128)(2,1)S(1)}, u32[]{:S(2)}, u32[]{:S(2)}) %collective-permute-start.2) | collective-permute-done | bytes 65568 | tf_op jit(solution)/shard_map/ppermute | solution.py:49
  9.3 3.0 %collective-permute-done.3 = bf16[128,256]{1,0:T(8,128)(2,1)S(1)} collective-permute-done((bf16[128,256]{1,0:T(8,128)(2,1)S(1)}, bf16[128,256]{1,0:T(8,128)(2,1)S(1)}, u32[]{:S(2)}, u32[]{:S(2)}) %collective-permute-start.3) | collective-permute-done | bytes 65568 | tf_op jit(solution)/shard_map/ppermute | solution.py:49
  12.4 2.5 %collective-permute-start.5 = (bf16[4,128,256]{2,1,0:T(8,128)(2,1)S(1)}, bf16[4,128,256]{2,1,0:T(8,128)(2,1)S(1)}, u32[]{:S(2)}, u32[]{:S(2)}) collective-permute-start(bf16[4,128,256]{2,1,0:T(8,128)(2,1)S(1)} %join.3.refs_5_.refs_1_.refs_3_), channel_id=1, source_target_pairs={{0,6},{1,7},{2,4},{3,5},{4,2},{5,3},{6,0},{7,1},{8,14},{9,15},{10,... | collective-permute-start | bytes 786440 | tf_op jit(solution)/shard_map/ppermute | solution.py:49
  19.3 4.6 %copy-done = f32[3,1024,1024]{2,1,0:T(8,128)S(1)} copy-done((f32[3,1024,1024]{2,1,0:T(8,128)S(1)}, f32[3,1024,1024]{2,1,0:T(8,128)}, u32[]{:S(2)}) %copy-start) | copy-done | bytes 12582936
  27.5 1.7 %collective-permute-start.9 = (bf16[16,32,256]{2,1,0:T(8,128)(2,1)S(1)}, bf16[16,32,256]{2,1,0:T(8,128)(2,1)S(1)}, u32[]{:S(2)}, u32[]{:S(2)}) collective-permute-start(bf16[16,32,256]{2,1,0:T(8,128)(2,1)S(1)} %get-tuple-element.109.refs_3_), channel_id=1, source_target_pairs={{0,1},{1,0},{2,3},{3,2},{4,5},{5,4},{6,7},{7,6},{8,9},{9,8},{10,11... | collective-permute-start | bytes 786440 | tf_op jit(solution)/shard_map/ppermute | solution.py:49
  31.1 2.1 %collective-permute-start.10 = (bf16[112,256]{1,0:T(8,128)(2,1)S(1)}, bf16[112,256]{1,0:T(8,128)(2,1)S(1)}, u32[]{:S(2)}, u32[]{:S(2)}) collective-permute-start(bf16[112,256]{1,0:T(8,128)(2,1)S(1)} %get-tuple-element.110.refs_2_), channel_id=1, source_target_pairs={{0,2},{1,3},{2,0},{3,1},{4,6},{5,7},{6,4},{7,5},{8,10},{9,11},{10,... | collective-permute-start | bytes 172040 | tf_op jit(solution)/shard_map/ppermute | solution.py:49
  35.5 1.8 %collective-permute-done.11 = bf16[112,256]{1,0:T(8,128)(2,1)S(1)} collective-permute-done((bf16[112,256]{1,0:T(8,128)(2,1)S(1)}, bf16[112,256]{1,0:T(8,128)(2,1)S(1)}, u32[]{:S(2)}, u32[]{:S(2)}) %collective-permute-start.11) | collective-permute-done | bytes 57376 | tf_op jit(solution)/shard_map/ppermute | solution.py:49
  37.3 2.4 %collective-permute-done.12 = bf16[112,256]{1,0:T(8,128)(2,1)S(1)} collective-permute-done((bf16[112,256]{1,0:T(8,128)(2,1)S(1)}, bf16[112,256]{1,0:T(8,128)(2,1)S(1)}, u32[]{:S(2)}, u32[]{:S(2)}) %collective-permute-start.12) | collective-permute-done | bytes 57376 | tf_op jit(solution)/shard_map/ppermute | solution.py:49
  41.2 6.2 %attend.1 = (bf16[896,256]{1,0:T(8,128)(2,1)S(1)}, bf16[448,256]{1,0:T(8,128)(2,1)S(1)}, bf16[896,256]{1,0:T(8,128)(2,1)S(1)}, bf16[896,256]{1,0:T(8,128)(2,1)S(...) custom-call(bf16[448,256]{1,0:T(8,128)(2,1)S(1)} %get-tuple-element.104.refs_1_.refs_0_, ...), custom_call_target="tpu_custom_call" | custom-call | bytes 28800000 | tf_op jit(solution)/shard_map/attend/pallas_call | solution.py:91
  47.4 3.2 %feed.1 = (bf16[448,256]{1,0:T(8,128)(2,1)}, bf16[448,256]{1,0:T(8,128)(2,1)S(1)}, f32[448,256]{1,0:T(8,128)S(1)}, f32[256,1024]{1,0:T(8,128)S(1)}, f32[256,1024...) custom-call(f32[448,256]{1,0:T(8,128)S(1)} %get-tuple-element.115.refs_0_.refs_3_, ...), custom_call_target="tpu_custom_call" | custom-call | bytes 12600000 | tf_op jit(solution)/shard_map/feed/pallas_call | solution.py:91
  50.7 7.0 %attend_back.1 = (bf16[448,256]{1,0:T(8,128)(2,1)S(1)}, f32[512,896]{1,0:T(8,128)S(1)}, f32[448,256]{1,0:T(8,128)S(1)}, f32[448,256]{1,0:T(8,128)S(1)}) custom-call(bf16[448,256]{1,0:T(8,128)(2,1)S(1)} %get-tuple-element.121.refs_0_, bf16[896,256]{1,0:T(8,128)(2,1)S(1)} %get-tuple-element.122.refs_1_, bf16[896,256]{1,0:T(8,128)(2,1)S(1)} %get-tuple-element.123.refs_2_, ...), custom_call_target="tpu_custom_call" | custom-call | bytes 28800000 | tf_op jit(solution)/shard_map/attend_back/pallas_call | solution.py:91
  58.1 1.8 %early_turn.1 = (f32[16,64,256]{2,1,0:T(8,128)S(1)}, f32[16,64,256]{2,1,0:T(8,128)S(1)}) custom-call(f32[256,1024]{1,0:T(8,128)S(1)} %get-tuple-element.130.refs_0_, f32[256,1024]{1,0:T(8,128)S(1)} %get-tuple-element.131.refs_1_, bf16[4,256,256]{2,1,0:T(8,128)(2,1)S(1)} %get-tuple-element.132.refs_2_.refs_5_, ...), custom_call_target="tpu_custom_call" | custom-call | bytes 7200000 | tf_op jit(solution)/shard_map/early_turn/pallas_call | solution.py:91
  61.1 1.8 %collective-permute-start.16 = (bf16[112,256]{1,0:T(8,128)(2,1)S(1)}, bf16[112,256]{1,0:T(8,128)(2,1)S(1)}, u32[]{:S(2)}, u32[]{:S(2)}) collective-permute-start(bf16[112,256]{1,0:T(8,128)(2,1)S(1)} %get-tuple-element.138), channel_id=1, source_target_pairs={{0,4},{1,5},{2,6},{3,7},{4,0},{5,1},{6,2},{7,3},{8,12},{9,13},{10,... | collective-permute-start | bytes 172040 | tf_op jit(solution)/shard_map/ppermute | solution.py:49
  64.4 2.1 %middle_turn.1 = (f32[256,256]{1,0:T(8,128)S(1)}, f32[256,256]{1,0:T(8,128)S(1)}, f32[256,512]{1,0:T(8,128)S(1)}, f32[8,256]{1,0:T(8,128)S(1)}) custom-call(bf16[448,256]{1,0:T(8,128)(2,1)S(1)} %get-tuple-element.104.refs_1_.refs_0_, bf16[448,256]{1,0:T(8,128)(2,1)S(1)} %get-tuple-element.127.refs_5_.refs_1_, f32[256,256]{1,0:T(8,128)S(1)} %get-tuple-element.142.refs_2_, ...), custom_call_target="tpu_custom_call" | custom-call | bytes 5400000 | tf_op jit(solution)/shard_map/middle_turn/pallas_call | solution.py:91
  67.1 1.8 %keys_back.1 = (f32[16,64,256]{2,1,0:T(8,128)S(1)}, f32[16,64,256]{2,1,0:T(8,128)S(1)}, bf16[112,256]{1,0:T(8,128)(2,1)S(1)}, f32[3,256]{1,0:T(4,128)S(1)}) custom-call(f32[112,256]{1,0:T(8,128)S(1)} %get-tuple-element.136.refs_8_.refs_1_.refs_0_, bf16[112,256]{1,0:T(8,128)(2,1)S(1)} %collective-permute-done.15.refs_1_, ...), custom_call_target="tpu_custom_call" | custom-call | bytes 7200000 | tf_op jit(solution)/shard_map/keys_back/pallas_call | solution.py:91
  73.8 2.0 %collective-permute-start.25 = (bf16[544,256]{1,0:T(8,128)(2,1)S(1)}, bf16[544,256]{1,0:T(8,128)(2,1)S(1)}, u32[]{:S(2)}, u32[]{:S(2)}) collective-permute-start(bf16[544,256]{1,0:T(8,128)(2,1)S(1)} %get-tuple-element.168), channel_id=1, source_target_pairs={{0,6},{1,7},{2,4},{3,5},{4,2},{5,3},{6,0},{7,1},{8,14},{9,15},{10,... | collective-permute-start | bytes 835592 | tf_op jit(solution)/shard_map/ppermute | solution.py:49
  78.5 3.1 %collective-permute-done.19.refs_7_.refs_2_ = bf16[64,256]{1,0:T(8,128)(2,1)S(1)} collective-permute-done((bf16[64,256]{1,0:T(8,128)(2,1)S(1)}, bf16[64,256]{1,0:T(8,128)(2,1)S(1)}, u32[]{:S(2)}, u32[]{:S(2)}) %collective-permute-start.19) | collective-permute-done | bytes 32800 | tf_op jit(solution)/shard_map/ppermute | solution.py:885
  81.8 6.2 %collective-permute-done.24.refs_4_ = bf16[544,256]{1,0:T(8,128)(2,1)S(1)} collective-permute-done((bf16[544,256]{1,0:T(8,128)(2,1)S(1)}, bf16[544,256]{1,0:T(8,128)(2,1)S(1)}, u32[]{:S(2)}, u32[]{:S(2)}) %collective-permute-start.24) | collective-permute-done | bytes 278560 | tf_op jit(solution)/shard_map/ppermute | solution.py:49
  89.3 2.2 %collective-permute-start.27 = (bf16[160,256]{1,0:T(8,128)(2,1)S(1)}, bf16[160,256]{1,0:T(8,128)(2,1)S(1)}, u32[]{:S(2)}, u32[]{:S(2)}) collective-permute-start(bf16[160,256]{1,0:T(8,128)(2,1)S(1)} %get-tuple-element.174), channel_id=1, source_target_pairs={{0,16},{8,24},{16,0},{24,8},{1,17},{9,25},{17,1},{25,9},{2,18},{10... | collective-permute-start | bytes 245768 | tf_op jit(solution)/shard_map/ppermute | solution.py:49
  94.2 4.4 %collective-permute-done.27.refs_4_ = bf16[160,256]{1,0:T(8,128)(2,1)S(1)} collective-permute-done((bf16[160,256]{1,0:T(8,128)(2,1)S(1)}, bf16[160,256]{1,0:T(8,128)(2,1)S(1)}, u32[]{:S(2)}, u32[]{:S(2)}) %collective-permute-start.27) | collective-permute-done | bytes 81952 | tf_op jit(solution)/shard_map/ppermute | solution.py:49
  99.3 2.1 %collective-permute-start.29 = (bf16[128,256]{1,0:T(8,128)(2,1)S(1)}, bf16[128,256]{1,0:T(8,128)(2,1)S(1)}, u32[]{:S(2)}, u32[]{:S(2)}) collective-permute-start(bf16[128,256]{1,0:T(8,128)(2,1)S(1)} %get-tuple-element.179.refs_1_), channel_id=1, source_target_pairs={{0,24},{8,16},{16,8},{24,0},{1,25},{9,17},{17,9},{25,1},{2,26},{10... | collective-permute-start | bytes 196616 | tf_op jit(solution)/shard_map/ppermute | solution.py:49
  110.3 2.5 %collective-permute-start.35 = (bf16[128,256]{1,0:T(8,128)(2,1)S(1)}, bf16[128,256]{1,0:T(8,128)(2,1)S(1)}, u32[]{:S(2)}, u32[]{:S(2)}) collective-permute-start(bf16[128,256]{1,0:T(8,128)(2,1)S(1)} %get-tuple-element.188), channel_id=1, source_target_pairs={{0,6},{1,7},{2,4},{3,5},{4,2},{5,3},{6,0},{7,1},{8,14},{9,15},{10,... | collective-permute-start | bytes 196616 | tf_op jit(solution)/shard_map/ppermute | solution.py:49
  115.5 1.7 %finish.1 = (f32[1,32768]{1,0:T(1,128)}, f32[1,32768]{1,0:T(1,128)}) custom-call(f32[128,256]{1,0:T(8,128)S(1)} %get-tuple-element.185.refs_0_, bf16[128,256]{1,0:T(8,128)(2,1)S(1)} %collective-permute-done.33.refs_1_, bf16[128,256]{1,0:T(8,128)(2,1)S(1)} %collective-permute-done.34.refs_2_, bf16[128,256]{1,0:T(8,128)(2,1)S(1)} %collective-permute-done.35.refs_3_, ...), custom_call_target="tpu_custom_call" | custom-call | bytes 5400000 | tf_op jit(solution)/shard_map/finish/pallas_call | solution.py:91
  (111 shorter events, 42.8 us)
Async XLA Ops:
  1.6 7.7 %collective-permute-start.2 = (bf16[128,256]{1,0:T(8,128)(2,1)S(1)}, bf16[128,256]{1,0:T(8,128)(2,1)S(1)}, u32[]{:S(2)}, u32[]{:S(2)}) collective-permute-start(bf16[128,256]{1,0:T(8,128)(2,1)S(1)} %pack.1), channel_id=1, source_target_pairs={{0,24},{8,16},{16,8},{24,0},{1,25},{9,17},{17,9},{25,1},{2,26},{10... | collective-permute-start | bytes 196616 | tf_op jit(solution)/shard_map/ppermute | solution.py:49
  6.7 5.6 %collective-permute-start.3 = (bf16[128,256]{1,0:T(8,128)(2,1)S(1)}, bf16[128,256]{1,0:T(8,128)(2,1)S(1)}, u32[]{:S(2)}, u32[]{:S(2)}) collective-permute-start(bf16[128,256]{1,0:T(8,128)(2,1)S(1)} %pack.1), channel_id=1, source_target_pairs={{0,16},{8,24},{16,0},{24,8},{1,17},{9,25},{17,1},{25,9},{2,18},{10... | collective-permute-start | bytes 196616 | tf_op jit(solution)/shard_map/ppermute | solution.py:49
  6.7 5.6 %collective-permute-start.4 = (bf16[128,256]{1,0:T(8,128)(2,1)S(1)}, bf16[128,256]{1,0:T(8,128)(2,1)S(1)}, u32[]{:S(2)}, u32[]{:S(2)}) collective-permute-start(bf16[128,256]{1,0:T(8,128)(2,1)S(1)} %pack.1), channel_id=1, source_target_pairs={{0,8},{8,0},{16,24},{24,16},{1,9},{9,1},{17,25},{25,17},{2,10},{10... | collective-permute-start | bytes 196616 | tf_op jit(solution)/shard_map/ppermute | solution.py:49
  12.4 13.8 %collective-permute-start.5 = (bf16[4,128,256]{2,1,0:T(8,128)(2,1)S(1)}, bf16[4,128,256]{2,1,0:T(8,128)(2,1)S(1)}, u32[]{:S(2)}, u32[]{:S(2)}) collective-permute-start(bf16[4,128,256]{2,1,0:T(8,128)(2,1)S(1)} %join.3.refs_5_.refs_1_.refs_3_), channel_id=1, source_target_pairs={{0,6},{1,7},{2,4},{3,5},{4,2},{5,3},{6,0},{7,1},{8,14},{9,15},{10,... | collective-permute-start | bytes 786440 | tf_op jit(solution)/shard_map/ppermute | solution.py:49
  14.9 11.9 %collective-permute-start.6 = (bf16[4,128,256]{2,1,0:T(8,128)(2,1)S(1)}, bf16[4,128,256]{2,1,0:T(8,128)(2,1)S(1)}, u32[]{:S(2)}, u32[]{:S(2)}) collective-permute-start(bf16[4,128,256]{2,1,0:T(8,128)(2,1)S(1)} %join.3.refs_5_.refs_1_.refs_3_), channel_id=1, source_target_pairs={{0,4},{1,5},{2,6},{3,7},{4,0},{5,1},{6,2},{7,3},{8,12},{9,13},{10,... | collective-permute-start | bytes 786440 | tf_op jit(solution)/shard_map/ppermute | solution.py:49
  15.4 12.1 %collective-permute-start.7 = (bf16[4,128,256]{2,1,0:T(8,128)(2,1)S(1)}, bf16[4,128,256]{2,1,0:T(8,128)(2,1)S(1)}, u32[]{:S(2)}, u32[]{:S(2)}) collective-permute-start(bf16[4,128,256]{2,1,0:T(8,128)(2,1)S(1)} %join.3.refs_5_.refs_1_.refs_3_), channel_id=1, source_target_pairs={{0,2},{1,3},{2,0},{3,1},{4,6},{5,7},{6,4},{7,5},{8,10},{9,11},{10,... | collective-permute-start | bytes 786440 | tf_op jit(solution)/shard_map/ppermute | solution.py:49
  16.7 7.8 %collective-permute-start = (bf16[64,256]{1,0:T(8,128)(2,1)S(1)}, bf16[64,256]{1,0:T(8,128)(2,1)S(1)}, u32[]{:S(2)}, u32[]{:S(2)}) collective-permute-start(bf16[64,256]{1,0:T(8,128)(2,1)S(1)} %get-tuple-element.199), channel_id=1, source_target_pairs={{0,1},{1,2},{2,3},{3,4},{4,5},{5,6},{6,7},{8,9},{9,10},{10,11},{11... | collective-permute-start | bytes 98312 | tf_op jit(solution)/shard_map/ppermute | solution.py:884
  18.0 6.5 %collective-permute-start.1 = (bf16[64,256]{1,0:T(8,128)(2,1)S(1)}, bf16[64,256]{1,0:T(8,128)(2,1)S(1)}, u32[]{:S(2)}, u32[]{:S(2)}) collective-permute-start(bf16[64,256]{1,0:T(8,128)(2,1)S(1)} %get-tuple-element.198), channel_id=1, source_target_pairs={{1,0},{2,1},{3,2},{4,3},{5,4},{6,5},{7,6},{9,8},{10,9},{11,10},{12... | collective-permute-start | bytes 98312 | tf_op jit(solution)/shard_map/ppermute | solution.py:885
  29.2 11.4 %collective-permute-start.8 = (bf16[16,96,256]{2,1,0:T(8,128)(2,1)S(1)}, bf16[16,96,256]{2,1,0:T(8,128)(2,1)S(1)}, u32[]{:S(2)}, u32[]{:S(2)}) collective-permute-start(bf16[16,96,256]{2,1,0:T(8,128)(2,1)S(1)} %get-tuple-element.107.refs_0_), channel_id=1, source_target_pairs={{0,1},{1,0},{2,3},{3,2},{4,5},{5,4},{6,7},{7,6},{8,9},{9,8},{10,11... | collective-permute-start | bytes 2359304 | tf_op jit(solution)/shard_map/ppermute | solution.py:49
  34.6 5.1 %collective-permute-start.12 = (bf16[112,256]{1,0:T(8,128)(2,1)S(1)}, bf16[112,256]{1,0:T(8,128)(2,1)S(1)}, u32[]{:S(2)}, u32[]{:S(2)}) collective-permute-start(bf16[112,256]{1,0:T(8,128)(2,1)S(1)} %get-tuple-element.110.refs_2_), channel_id=1, source_target_pairs={{0,6},{1,7},{2,4},{3,5},{4,2},{5,3},{6,0},{7,1},{8,14},{9,15},{10,... | collective-permute-start | bytes 172040 | tf_op jit(solution)/shard_map/ppermute | solution.py:49
  60.0 6.6 %collective-permute-start.15 = (bf16[112,256]{1,0:T(8,128)(2,1)S(1)}, bf16[112,256]{1,0:T(8,128)(2,1)S(1)}, u32[]{:S(2)}, u32[]{:S(2)}) collective-permute-start(bf16[112,256]{1,0:T(8,128)(2,1)S(1)} %get-tuple-element.137), channel_id=1, source_target_pairs={{0,6},{1,7},{2,4},{3,5},{4,2},{5,3},{6,0},{7,1},{8,14},{9,15},{10,... | collective-permute-start | bytes 172040 | tf_op jit(solution)/shard_map/ppermute | solution.py:49
  61.1 5.5 %collective-permute-start.16 = (bf16[112,256]{1,0:T(8,128)(2,1)S(1)}, bf16[112,256]{1,0:T(8,128)(2,1)S(1)}, u32[]{:S(2)}, u32[]{:S(2)}) collective-permute-start(bf16[112,256]{1,0:T(8,128)(2,1)S(1)} %get-tuple-element.138), channel_id=1, source_target_pairs={{0,4},{1,5},{2,6},{3,7},{4,0},{5,1},{6,2},{7,3},{8,12},{9,13},{10,... | collective-permute-start | bytes 172040 | tf_op jit(solution)/shard_map/ppermute | solution.py:49
  64.0 8.0 %collective-permute-start.22 = (f32[16,64,256]{2,1,0:T(8,128)S(1)}, f32[16,64,256]{2,1,0:T(8,128)S(1)}, u32[]{:S(2)}, u32[]{:S(2)}) collective-permute-start(f32[16,64,256]{2,1,0:T(8,128)S(1)} %get-tuple-element.162), channel_id=1, source_target_pairs={{0,1},{1,0},{2,3},{3,2},{4,5},{5,4},{6,7},{7,6},{8,9},{9,8},{10,11... | collective-permute-start | bytes 3145736 | tf_op jit(solution)/shard_map/ppermute | solution.py:49
  72.3 9.5 %collective-permute-start.23 = (bf16[544,256]{1,0:T(8,128)(2,1)S(1)}, bf16[544,256]{1,0:T(8,128)(2,1)S(1)}, u32[]{:S(2)}, u32[]{:S(2)}) collective-permute-start(bf16[544,256]{1,0:T(8,128)(2,1)S(1)} %get-tuple-element.166), channel_id=1, source_target_pairs={{0,2},{1,3},{2,0},{3,1},{4,6},{5,7},{6,4},{7,5},{8,10},{9,11},{10,... | collective-permute-start | bytes 835592 | tf_op jit(solution)/shard_map/ppermute | solution.py:49
  73.6 14.4 %collective-permute-start.24 = (bf16[544,256]{1,0:T(8,128)(2,1)S(1)}, bf16[544,256]{1,0:T(8,128)(2,1)S(1)}, u32[]{:S(2)}, u32[]{:S(2)}) collective-permute-start(bf16[544,256]{1,0:T(8,128)(2,1)S(1)} %get-tuple-element.167), channel_id=1, source_target_pairs={{0,4},{1,5},{2,6},{3,7},{4,0},{5,1},{6,2},{7,3},{8,12},{9,13},{10,... | collective-permute-start | bytes 835592 | tf_op jit(solution)/shard_map/ppermute | solution.py:49
  73.8 14.2 %collective-permute-start.25 = (bf16[544,256]{1,0:T(8,128)(2,1)S(1)}, bf16[544,256]{1,0:T(8,128)(2,1)S(1)}, u32[]{:S(2)}, u32[]{:S(2)}) collective-permute-start(bf16[544,256]{1,0:T(8,128)(2,1)S(1)} %get-tuple-element.168), channel_id=1, source_target_pairs={{0,6},{1,7},{2,4},{3,5},{4,2},{5,3},{6,0},{7,1},{8,14},{9,15},{10,... | collective-permute-start | bytes 835592 | tf_op jit(solution)/shard_map/ppermute | solution.py:49
  88.1 6.1 %collective-permute-start.26 = (bf16[160,256]{1,0:T(8,128)(2,1)S(1)}, bf16[160,256]{1,0:T(8,128)(2,1)S(1)}, u32[]{:S(2)}, u32[]{:S(2)}) collective-permute-start(bf16[160,256]{1,0:T(8,128)(2,1)S(1)} %get-tuple-element.173), channel_id=1, source_target_pairs={{0,8},{8,0},{16,24},{24,16},{1,9},{9,1},{17,25},{25,17},{2,10},{10... | collective-permute-start | bytes 245768 | tf_op jit(solution)/shard_map/ppermute | solution.py:49
  89.3 9.3 %collective-permute-start.27 = (bf16[160,256]{1,0:T(8,128)(2,1)S(1)}, bf16[160,256]{1,0:T(8,128)(2,1)S(1)}, u32[]{:S(2)}, u32[]{:S(2)}) collective-permute-start(bf16[160,256]{1,0:T(8,128)(2,1)S(1)} %get-tuple-element.174), channel_id=1, source_target_pairs={{0,16},{8,24},{16,0},{24,8},{1,17},{9,25},{17,1},{25,9},{2,18},{10... | collective-permute-start | bytes 245768 | tf_op jit(solution)/shard_map/ppermute | solution.py:49
  91.5 7.1 %collective-permute-start.28 = (bf16[160,256]{1,0:T(8,128)(2,1)S(1)}, bf16[160,256]{1,0:T(8,128)(2,1)S(1)}, u32[]{:S(2)}, u32[]{:S(2)}) collective-permute-start(bf16[160,256]{1,0:T(8,128)(2,1)S(1)} %get-tuple-element.175), channel_id=1, source_target_pairs={{0,24},{8,16},{16,8},{24,0},{1,25},{9,17},{17,9},{25,1},{2,26},{10... | collective-permute-start | bytes 245768 | tf_op jit(solution)/shard_map/ppermute | solution.py:49
  99.3 6.8 %collective-permute-start.29 = (bf16[128,256]{1,0:T(8,128)(2,1)S(1)}, bf16[128,256]{1,0:T(8,128)(2,1)S(1)}, u32[]{:S(2)}, u32[]{:S(2)}) collective-permute-start(bf16[128,256]{1,0:T(8,128)(2,1)S(1)} %get-tuple-element.179.refs_1_), channel_id=1, source_target_pairs={{0,24},{8,16},{16,8},{24,0},{1,25},{9,17},{17,9},{25,1},{2,26},{10... | collective-permute-start | bytes 196616 | tf_op jit(solution)/shard_map/ppermute | solution.py:49
  101.4 5.9 %collective-permute-start.30 = (bf16[128,256]{1,0:T(8,128)(2,1)S(1)}, bf16[128,256]{1,0:T(8,128)(2,1)S(1)}, u32[]{:S(2)}, u32[]{:S(2)}) collective-permute-start(bf16[128,256]{1,0:T(8,128)(2,1)S(1)} %get-tuple-element.179.refs_1_), channel_id=1, source_target_pairs={{0,16},{8,24},{16,0},{24,8},{1,17},{9,25},{17,1},{25,9},{2,18},{10... | collective-permute-start | bytes 196616 | tf_op jit(solution)/shard_map/ppermute | solution.py:49
  102.3 5.0 %collective-permute-start.31 = (bf16[128,256]{1,0:T(8,128)(2,1)S(1)}, bf16[128,256]{1,0:T(8,128)(2,1)S(1)}, u32[]{:S(2)}, u32[]{:S(2)}) collective-permute-start(bf16[128,256]{1,0:T(8,128)(2,1)S(1)} %get-tuple-element.179.refs_1_), channel_id=1, source_target_pairs={{0,8},{8,0},{16,24},{24,16},{1,9},{9,1},{17,25},{25,17},{2,10},{10... | collective-permute-start | bytes 196616 | tf_op jit(solution)/shard_map/ppermute | solution.py:49
  109.8 5.0 %collective-permute-start.34 = (bf16[128,256]{1,0:T(8,128)(2,1)S(1)}, bf16[128,256]{1,0:T(8,128)(2,1)S(1)}, u32[]{:S(2)}, u32[]{:S(2)}) collective-permute-start(bf16[128,256]{1,0:T(8,128)(2,1)S(1)} %get-tuple-element.187), channel_id=1, source_target_pairs={{0,4},{1,5},{2,6},{3,7},{4,0},{5,1},{6,2},{7,3},{8,12},{9,13},{10,... | collective-permute-start | bytes 196616 | tf_op jit(solution)/shard_map/ppermute | solution.py:49
  110.3 5.2 %collective-permute-start.35 = (bf16[128,256]{1,0:T(8,128)(2,1)S(1)}, bf16[128,256]{1,0:T(8,128)(2,1)S(1)}, u32[]{:S(2)}, u32[]{:S(2)}) collective-permute-start(bf16[128,256]{1,0:T(8,128)(2,1)S(1)} %get-tuple-element.188), channel_id=1, source_target_pairs={{0,6},{1,7},{2,4},{3,5},{4,2},{5,3},{6,0},{7,1},{8,14},{9,15},{10,... | collective-permute-start | bytes 196616 | tf_op jit(solution)/shard_map/ppermute | solution.py:49
  (27 other events, 212.5 us)

commit v11 on v10

--- a/solution.py
+++ b/solution.py
@@ -948,6 +948,13 @@
         micros=1.5,
         after=[kn],
     )
+    old_chunk, ema_chunk, first_chunk, second_chunk = run(
+        "moments",
+        functools.partial(moments_kernel, width),
+        [((chunk, width), f32)] * 4,
+        [jnp.concatenate([weights, weight_ema, first_moment, second_moment], axis=0)],
+        after=[kn],
+    )
     group = (1, 0, 2, 3, 4)
     w_keyval, w_query, w_out, w_up, w_down = run(
         "weights",
@@ -972,7 +979,7 @@
         [h1, w_query, w_keyval, vec, kn_near, kn_far, mask],
         mib=8 if unroll else 44,
         micros=8.0,
-        after=[own_narrow],
+        after=[own_narrow, old_chunk],
     )
     y, do, dx1, up_grad, down_grad, out_grad, feed_sums = run(
         "feed",
@@ -1021,13 +1028,6 @@
     for axis, stride, size in xy_parts:
         part, *sends = split_sum(dkn_terms, size, [early_keep])
         dkn_terms = [part] + [swap(x, axis, j * stride) for j, x in enumerate(sends, 1)][::-1]
-    old_chunk, ema_chunk, first_chunk, second_chunk = run(
-        "moments",
-        functools.partial(moments_kernel, width),
-        [((chunk, width), f32)] * 4,
-        [jnp.concatenate([weights, weight_ema, first_moment, second_moment], axis=0)],
-        after=[part],
-    )
     query_turn, out_turn, keyval_turn, query_sums = run(
         "middle_turn",
         middle_turn_kernel,
@@ -1045,7 +1045,6 @@
         list(dkn_terms) + [c, vec, blocks, narrow, wide, query_turn, out_turn, keyval_turn],
         scratch=[((4 * width, width), f32)],
         micros=2.0,
-        after=[old_chunk],
     )
     late_got = swap(late_send, "row", 1)
     dx0, head, tail, vec_grads = run(

time: 117 us -> 119 us (1.017)
    ppermute x2, starting transfers between devices: 2.68 us -> 4.43 us  [border(): up = lax.ppermute(tail, 'row', [(i, i + 1) for i in range(ranks - 1)])]
    ppermute x32, starting transfers between devices: 36.1 us -> 34.8 us  [swap(): return lax.ppermute(x, axis, [(i, i ^ step) for i in range(count)])]
  transfers between devices with their start and end apart: 36 -> 36, of which waited for: 19 -> 15; matrix products, arithmetic and copies ran while one was open for 1% -> 1% of each run, Pallas kernels for 13% -> 13%
where the time goes in v11:
time: 119 us
  starting transfers between devices  41.9 us (35%)
  Pallas kernels  35.4 us (30%)
  waiting for transfers between devices  33.1 us (28%)
  local copies, waits for them, and re-layouts  6.56 us (6%)
    pallas_call x27, Pallas kernels, run(): pl.pallas_call(without, out_shape=tuple((jax.ShapeDtypeStruct(shape, dtyp...  35.4 us
    ppermute x32, starting transfers between devices, swap(): return lax.ppermute(x, axis, [(i, i ^ step) for i in range(count)])  34.8 us
    ppermute x32, waiting for transfers between devices, swap(): return lax.ppermute(x, axis, [(i, i ^ step) for i in range(count)])  29.8 us
    unnamed x33, local copies, waits for them, and re-layouts  5.77 us
    ppermute x2, starting transfers between devices, border(): up = lax.ppermute(tail, 'row', [(i, i + 1) for i in range(ranks - 1)])  4.43 us
    ppermute x2, waiting for transfers between devices, border(): lax.ppermute(head, 'row', [(i + 1, i) for i in range(ranks - 1)])  3.29 us
    ppermute x2, starting transfers between devices, border(): lax.ppermute(head, 'row', [(i + 1, i) for i in range(ranks - 1)])  2.57 us
  transfers between devices with their start and end apart: 36, of which 15 were waited for; matrix products, arithmetic and copies ran while one was open for 1% of the time, Pallas kernels for 13%

profile of v11, /device:TPU:0, one launch (start us, length us, event | category | flops | bytes accessed | tf_op | source)
XLA Modules:
  0.0 118.6 jit_solution(810294596246044744)
XLA Ops:
  1.6 3.1 %collective-permute-start.4 = (bf16[128,256]{1,0:T(8,128)(2,1)S(1)}, bf16[128,256]{1,0:T(8,128)(2,1)S(1)}, u32[]{:S(2)}, u32[]{:S(2)}) collective-permute-start(bf16[128,256]{1,0:T(8,128)(2,1)S(1)} %pack.1), channel_id=1, source_target_pairs={{0,8},{8,0},{16,24},{24,16},{1,9},{9,1},{17,25},{25,17},{2,10},{10... | collective-permute-start | bytes 196616 | tf_op jit(solution)/shard_map/ppermute | solution.py:49
  4.7 2.6 %collective-permute-start.3 = (bf16[128,256]{1,0:T(8,128)(2,1)S(1)}, bf16[128,256]{1,0:T(8,128)(2,1)S(1)}, u32[]{:S(2)}, u32[]{:S(2)}) collective-permute-start(bf16[128,256]{1,0:T(8,128)(2,1)S(1)} %pack.1), channel_id=1, source_target_pairs={{0,16},{8,24},{16,0},{24,8},{1,17},{9,25},{17,1},{25,9},{2,18},{10... | collective-permute-start | bytes 196616 | tf_op jit(solution)/shard_map/ppermute | solution.py:49
  7.3 4.7 %collective-permute-done.3 = bf16[128,256]{1,0:T(8,128)(2,1)S(1)} collective-permute-done((bf16[128,256]{1,0:T(8,128)(2,1)S(1)}, bf16[128,256]{1,0:T(8,128)(2,1)S(1)}, u32[]{:S(2)}, u32[]{:S(2)}) %collective-permute-start.3) | collective-permute-done | bytes 65568 | tf_op jit(solution)/shard_map/ppermute | solution.py:49
  19.0 3.0 %collective-permute-start = (bf16[64,256]{1,0:T(8,128)(2,1)S(1)}, bf16[64,256]{1,0:T(8,128)(2,1)S(1)}, u32[]{:S(2)}, u32[]{:S(2)}) collective-permute-start(bf16[64,256]{1,0:T(8,128)(2,1)S(1)} %get-tuple-element.199), channel_id=1, source_target_pairs={{0,1},{1,2},{2,3},{3,4},{4,5},{5,6},{6,7},{8,9},{9,10},{10,11},{11... | collective-permute-start | bytes 98312 | tf_op jit(solution)/shard_map/ppermute | solution.py:884
  22.1 4.6 %copy-done = f32[3,1024,1024]{2,1,0:T(8,128)S(1)} copy-done((f32[3,1024,1024]{2,1,0:T(8,128)S(1)}, f32[3,1024,1024]{2,1,0:T(8,128)}, u32[]{:S(2)}) %copy-start) | copy-done | bytes 12582936
  32.1 1.8 %collective-permute-start.12 = (bf16[112,256]{1,0:T(8,128)(2,1)S(1)}, bf16[112,256]{1,0:T(8,128)(2,1)S(1)}, u32[]{:S(2)}, u32[]{:S(2)}) collective-permute-start(bf16[112,256]{1,0:T(8,128)(2,1)S(1)} %get-tuple-element.110.refs_2_.refs_1_), channel_id=1, source_target_pairs={{0,6},{1,7},{2,4},{3,5},{4,2},{5,3},{6,0},{7,1},{8,14},{9,15},{10,... | collective-permute-start | bytes 172040 | tf_op jit(solution)/shard_map/ppermute | solution.py:49
  35.7 3.6 %collective-permute-done.10 = bf16[112,256]{1,0:T(8,128)(2,1)S(1)} collective-permute-done((bf16[112,256]{1,0:T(8,128)(2,1)S(1)}, bf16[112,256]{1,0:T(8,128)(2,1)S(1)}, u32[]{:S(2)}, u32[]{:S(2)}) %collective-permute-start.10) | collective-permute-done | bytes 57376 | tf_op jit(solution)/shard_map/ppermute | solution.py:49
  41.5 6.2 %attend.1 = (bf16[896,256]{1,0:T(8,128)(2,1)S(1)}, bf16[448,256]{1,0:T(8,128)(2,1)S(1)}, bf16[896,256]{1,0:T(8,128)(2,1)S(1)}, bf16[896,256]{1,0:T(8,128)(2,1)S(...) custom-call(bf16[448,256]{1,0:T(8,128)(2,1)S(1)} %get-tuple-element.104.refs_1_.refs_0_, ...), custom_call_target="tpu_custom_call" | custom-call | bytes 28800000 | tf_op jit(solution)/shard_map/attend/pallas_call | solution.py:91
  47.8 3.4 %feed.1 = (bf16[448,256]{1,0:T(8,128)(2,1)}, bf16[448,256]{1,0:T(8,128)(2,1)S(1)}, f32[448,256]{1,0:T(8,128)S(1)}, f32[256,1024]{1,0:T(8,128)S(1)}, f32[256,1024...) custom-call(f32[448,256]{1,0:T(8,128)S(1)} %get-tuple-element.116.refs_0_.refs_3_, ...), custom_call_target="tpu_custom_call" | custom-call | bytes 12600000 | tf_op jit(solution)/shard_map/feed/pallas_call | solution.py:91
  51.2 7.0 %attend_back.1 = (bf16[448,256]{1,0:T(8,128)(2,1)S(1)}, f32[512,896]{1,0:T(8,128)S(1)}, f32[448,256]{1,0:T(8,128)S(1)}, f32[448,256]{1,0:T(8,128)S(1)}) custom-call(bf16[448,256]{1,0:T(8,128)(2,1)S(1)} %get-tuple-element.122.refs_0_, bf16[896,256]{1,0:T(8,128)(2,1)S(1)} %get-tuple-element.123.refs_1_, bf16[896,256]{1,0:T(8,128)(2,1)S(1)} %get-tuple-element.124.refs_2_, ...), custom_call_target="tpu_custom_call" | custom-call | bytes 28800000 | tf_op jit(solution)/shard_map/attend_back/pallas_call | solution.py:91
  58.7 1.8 %early_turn.1 = (f32[16,64,256]{2,1,0:T(8,128)S(1)}, f32[16,64,256]{2,1,0:T(8,128)S(1)}) custom-call(f32[256,1024]{1,0:T(8,128)S(1)} %get-tuple-element.131.refs_0_, f32[256,1024]{1,0:T(8,128)S(1)} %get-tuple-element.132.refs_1_, bf16[4,256,256]{2,1,0:T(8,128)(2,1)S(1)} %get-tuple-element.133.refs_2_.refs_5_, ...), custom_call_target="tpu_custom_call" | custom-call | bytes 7200000 | tf_op jit(solution)/shard_map/early_turn/pallas_call | solution.py:91
  64.2 2.1 %middle_turn.1 = (f32[256,256]{1,0:T(8,128)S(1)}, f32[256,256]{1,0:T(8,128)S(1)}, f32[256,512]{1,0:T(8,128)S(1)}, f32[8,256]{1,0:T(8,128)S(1)}) custom-call(bf16[448,256]{1,0:T(8,128)(2,1)S(1)} %get-tuple-element.104.refs_1_.refs_0_, bf16[448,256]{1,0:T(8,128)(2,1)S(1)} %get-tuple-element.128.refs_5_.refs_1_, f32[256,256]{1,0:T(8,128)S(1)} %get-tuple-element.143.refs_2_, ...), custom_call_target="tpu_custom_call" | custom-call | bytes 5400000 | tf_op jit(solution)/shard_map/middle_turn/pallas_call | solution.py:91
  67.0 1.8 %keys_back.1 = (f32[16,64,256]{2,1,0:T(8,128)S(1)}, f32[16,64,256]{2,1,0:T(8,128)S(1)}, bf16[112,256]{1,0:T(8,128)(2,1)S(1)}, f32[3,256]{1,0:T(4,128)S(1)}) custom-call(f32[112,256]{1,0:T(8,128)S(1)} %get-tuple-element.137.refs_8_.refs_0_, bf16[112,256]{1,0:T(8,128)(2,1)S(1)} %collective-permute-done.15.refs_1_, ...), custom_call_target="tpu_custom_call" | custom-call | bytes 7200000 | tf_op jit(solution)/shard_map/keys_back/pallas_call | solution.py:91
  68.9 1.6 %cells_back.1 = (f32[448,256]{1,0:T(8,128)S(1)}, bf16[64,256]{1,0:T(8,128)(2,1)S(1)}, bf16[64,256]{1,0:T(8,128)(2,1)S(1)}, f32[32,256]{1,0:T(8,128)S(1)}) custom-call(s32[8,128]{1,0:T(8,128)S(1)} %get-tuple-element.108.refs_0_, bf16[448,256]{1,0:T(8,128)(2,1)S(1)} %get-tuple-element.128.refs_5_.refs_1_, bf16[112,256]{1,0:T(8,128)(2,1)S(1)} %get-tuple-element.150.refs_2_, ...), custom_call_target="tpu_custom_call" | custom-call | bytes 7200000 | tf_op jit(solution)/shard_map/cells_back/pallas_call | solution.py:91
  78.4 3.3 %collective-permute-done.19.refs_7_.refs_2_ = bf16[64,256]{1,0:T(8,128)(2,1)S(1)} collective-permute-done((bf16[64,256]{1,0:T(8,128)(2,1)S(1)}, bf16[64,256]{1,0:T(8,128)(2,1)S(1)}, u32[]{:S(2)}, u32[]{:S(2)}) %collective-permute-start.19) | collective-permute-done | bytes 32800 | tf_op jit(solution)/shard_map/ppermute | solution.py:885
  81.7 6.5 %collective-permute-done.24.refs_4_ = bf16[544,256]{1,0:T(8,128)(2,1)S(1)} collective-permute-done((bf16[544,256]{1,0:T(8,128)(2,1)S(1)}, bf16[544,256]{1,0:T(8,128)(2,1)S(1)}, u32[]{:S(2)}, u32[]{:S(2)}) %collective-permute-start.24) | collective-permute-done | bytes 278560 | tf_op jit(solution)/shard_map/ppermute | solution.py:49
  88.4 2.3 %collective-permute-start.27 = (bf16[160,256]{1,0:T(8,128)(2,1)S(1)}, bf16[160,256]{1,0:T(8,128)(2,1)S(1)}, u32[]{:S(2)}, u32[]{:S(2)}) collective-permute-start(bf16[160,256]{1,0:T(8,128)(2,1)S(1)} %get-tuple-element.174), channel_id=1, source_target_pairs={{0,16},{8,24},{16,0},{24,8},{1,17},{9,25},{17,1},{25,9},{2,18},{10... | collective-permute-start | bytes 245768 | tf_op jit(solution)/shard_map/ppermute | solution.py:49
  90.7 2.0 %collective-permute-start.28 = (bf16[160,256]{1,0:T(8,128)(2,1)S(1)}, bf16[160,256]{1,0:T(8,128)(2,1)S(1)}, u32[]{:S(2)}, u32[]{:S(2)}) collective-permute-start(bf16[160,256]{1,0:T(8,128)(2,1)S(1)} %get-tuple-element.175), channel_id=1, source_target_pairs={{0,24},{8,16},{16,8},{24,0},{1,25},{9,17},{17,9},{25,1},{2,26},{10... | collective-permute-start | bytes 245768 | tf_op jit(solution)/shard_map/ppermute | solution.py:49
  92.8 1.6 %input_grad.1 = (f32[448,256]{1,0:T(8,128)}, f32[8,128]{1,0:T(8,128)S(1)}) custom-call(f32[448,256]{1,0:T(8,128)S(1)} %get-tuple-element.156.refs_0_, bf16[64,256]{1,0:T(8,128)(2,1)S(1)} %collective-permute-done.18.refs_6_.refs_1_, bf16[64,256]{1,0:T(8,128)(2,1)S(1)} %collective-permute-done.19.refs_7_.refs_2_, ...), custom_call_target="tpu_custom_call" | custom-call | bytes 5400000 | tf_op jit(solution)/shard_map/input_grad/pallas_call | solution.py:91
  94.4 3.6 %collective-permute-done.27.refs_4_ = bf16[160,256]{1,0:T(8,128)(2,1)S(1)} collective-permute-done((bf16[160,256]{1,0:T(8,128)(2,1)S(1)}, bf16[160,256]{1,0:T(8,128)(2,1)S(1)}, u32[]{:S(2)}, u32[]{:S(2)}) %collective-permute-start.27) | collective-permute-done | bytes 81952 | tf_op jit(solution)/shard_map/ppermute | solution.py:49
  109.8 1.7 %collective-permute-start.33 = (bf16[128,256]{1,0:T(8,128)(2,1)S(1)}, bf16[128,256]{1,0:T(8,128)(2,1)S(1)}, u32[]{:S(2)}, u32[]{:S(2)}) collective-permute-start(bf16[128,256]{1,0:T(8,128)(2,1)S(1)} %get-tuple-element.186), channel_id=1, source_target_pairs={{0,2},{1,3},{2,0},{3,1},{4,6},{5,7},{6,4},{7,5},{8,10},{9,11},{10,... | collective-permute-start | bytes 196616 | tf_op jit(solution)/shard_map/ppermute | solution.py:49
  111.6 1.7 %collective-permute-start.35 = (bf16[128,256]{1,0:T(8,128)(2,1)S(1)}, bf16[128,256]{1,0:T(8,128)(2,1)S(1)}, u32[]{:S(2)}, u32[]{:S(2)}) collective-permute-start(bf16[128,256]{1,0:T(8,128)(2,1)S(1)} %get-tuple-element.188), channel_id=1, source_target_pairs={{0,6},{1,7},{2,4},{3,5},{4,2},{5,3},{6,0},{7,1},{8,14},{9,15},{10,... | collective-permute-start | bytes 196616 | tf_op jit(solution)/shard_map/ppermute | solution.py:49
  114.1 2.8 %collective-permute-done.34.refs_2_ = bf16[128,256]{1,0:T(8,128)(2,1)S(1)} collective-permute-done((bf16[128,256]{1,0:T(8,128)(2,1)S(1)}, bf16[128,256]{1,0:T(8,128)(2,1)S(1)}, u32[]{:S(2)}, u32[]{:S(2)}) %collective-permute-start.34) | collective-permute-done | bytes 65568 | tf_op jit(solution)/shard_map/ppermute | solution.py:49
  116.9 1.7 %finish.1 = (f32[1,32768]{1,0:T(1,128)}, f32[1,32768]{1,0:T(1,128)}) custom-call(f32[128,256]{1,0:T(8,128)S(1)} %get-tuple-element.185.refs_0_, bf16[128,256]{1,0:T(8,128)(2,1)S(1)} %collective-permute-done.33.refs_1_, bf16[128,256]{1,0:T(8,128)(2,1)S(1)} %collective-permute-done.34.refs_2_, bf16[128,256]{1,0:T(8,128)(2,1)S(1)} %collective-permute-done.35.refs_3_, ...), custom_call_target="tpu_custom_call" | custom-call | bytes 5400000 | tf_op jit(solution)/shard_map/finish/pallas_call | solution.py:91
  (111 shorter events, 42.8 us)
Async XLA Ops:
  1.6 5.7 %collective-permute-start.4 = (bf16[128,256]{1,0:T(8,128)(2,1)S(1)}, bf16[128,256]{1,0:T(8,128)(2,1)S(1)}, u32[]{:S(2)}, u32[]{:S(2)}) collective-permute-start(bf16[128,256]{1,0:T(8,128)(2,1)S(1)} %pack.1), channel_id=1, source_target_pairs={{0,8},{8,0},{16,24},{24,16},{1,9},{9,1},{17,25},{25,17},{2,10},{10... | collective-permute-start | bytes 196616 | tf_op jit(solution)/shard_map/ppermute | solution.py:49
  4.7 7.3 %collective-permute-start.3 = (bf16[128,256]{1,0:T(8,128)(2,1)S(1)}, bf16[128,256]{1,0:T(8,128)(2,1)S(1)}, u32[]{:S(2)}, u32[]{:S(2)}) collective-permute-start(bf16[128,256]{1,0:T(8,128)(2,1)S(1)} %pack.1), channel_id=1, source_target_pairs={{0,16},{8,24},{16,0},{24,8},{1,17},{9,25},{17,1},{25,9},{2,18},{10... | collective-permute-start | bytes 196616 | tf_op jit(solution)/shard_map/ppermute | solution.py:49
  7.3 6.1 %collective-permute-start.2 = (bf16[128,256]{1,0:T(8,128)(2,1)S(1)}, bf16[128,256]{1,0:T(8,128)(2,1)S(1)}, u32[]{:S(2)}, u32[]{:S(2)}) collective-permute-start(bf16[128,256]{1,0:T(8,128)(2,1)S(1)} %pack.1), channel_id=1, source_target_pairs={{0,24},{8,16},{16,8},{24,0},{1,25},{9,17},{17,9},{25,1},{2,26},{10... | collective-permute-start | bytes 196616 | tf_op jit(solution)/shard_map/ppermute | solution.py:49
  13.4 15.5 %collective-permute-start.7 = (bf16[4,128,256]{2,1,0:T(8,128)(2,1)S(1)}, bf16[4,128,256]{2,1,0:T(8,128)(2,1)S(1)}, u32[]{:S(2)}, u32[]{:S(2)}) collective-permute-start(bf16[4,128,256]{2,1,0:T(8,128)(2,1)S(1)} %join.3.refs_5_.refs_1_.refs_3_), channel_id=1, source_target_pairs={{0,2},{1,3},{2,0},{3,1},{4,6},{5,7},{6,4},{7,5},{8,10},{9,11},{10,... | collective-permute-start | bytes 786440 | tf_op jit(solution)/shard_map/ppermute | solution.py:49
  15.0 14.0 %collective-permute-start.6 = (bf16[4,128,256]{2,1,0:T(8,128)(2,1)S(1)}, bf16[4,128,256]{2,1,0:T(8,128)(2,1)S(1)}, u32[]{:S(2)}, u32[]{:S(2)}) collective-permute-start(bf16[4,128,256]{2,1,0:T(8,128)(2,1)S(1)} %join.3.refs_5_.refs_1_.refs_3_), channel_id=1, source_target_pairs={{0,4},{1,5},{2,6},{3,7},{4,0},{5,1},{6,2},{7,3},{8,12},{9,13},{10,... | collective-permute-start | bytes 786440 | tf_op jit(solution)/shard_map/ppermute | solution.py:49
  16.5 12.5 %collective-permute-start.5 = (bf16[4,128,256]{2,1,0:T(8,128)(2,1)S(1)}, bf16[4,128,256]{2,1,0:T(8,128)(2,1)S(1)}, u32[]{:S(2)}, u32[]{:S(2)}) collective-permute-start(bf16[4,128,256]{2,1,0:T(8,128)(2,1)S(1)} %join.3.refs_5_.refs_1_.refs_3_), channel_id=1, source_target_pairs={{0,6},{1,7},{2,4},{3,5},{4,2},{5,3},{6,0},{7,1},{8,14},{9,15},{10,... | collective-permute-start | bytes 786440 | tf_op jit(solution)/shard_map/ppermute | solution.py:49
  17.7 9.6 %collective-permute-start.1 = (bf16[64,256]{1,0:T(8,128)(2,1)S(1)}, bf16[64,256]{1,0:T(8,128)(2,1)S(1)}, u32[]{:S(2)}, u32[]{:S(2)}) collective-permute-start(bf16[64,256]{1,0:T(8,128)(2,1)S(1)} %get-tuple-element.198), channel_id=1, source_target_pairs={{1,0},{2,1},{3,2},{4,3},{5,4},{6,5},{7,6},{9,8},{10,9},{11,10},{12... | collective-permute-start | bytes 98312 | tf_op jit(solution)/shard_map/ppermute | solution.py:885
  19.0 8.3 %collective-permute-start = (bf16[64,256]{1,0:T(8,128)(2,1)S(1)}, bf16[64,256]{1,0:T(8,128)(2,1)S(1)}, u32[]{:S(2)}, u32[]{:S(2)}) collective-permute-start(bf16[64,256]{1,0:T(8,128)(2,1)S(1)} %get-tuple-element.199), channel_id=1, source_target_pairs={{0,1},{1,2},{2,3},{3,4},{4,5},{5,6},{6,7},{8,9},{9,10},{10,11},{11... | collective-permute-start | bytes 98312 | tf_op jit(solution)/shard_map/ppermute | solution.py:884
  30.2 10.9 %collective-permute-start.8 = (bf16[16,96,256]{2,1,0:T(8,128)(2,1)S(1)}, bf16[16,96,256]{2,1,0:T(8,128)(2,1)S(1)}, u32[]{:S(2)}, u32[]{:S(2)}) collective-permute-start(bf16[16,96,256]{2,1,0:T(8,128)(2,1)S(1)} %get-tuple-element.107.refs_0_), channel_id=1, source_target_pairs={{0,1},{1,0},{2,3},{3,2},{4,5},{5,4},{6,7},{7,6},{8,9},{9,8},{10,11... | collective-permute-start | bytes 2359304 | tf_op jit(solution)/shard_map/ppermute | solution.py:49
  32.1 7.2 %collective-permute-start.12 = (bf16[112,256]{1,0:T(8,128)(2,1)S(1)}, bf16[112,256]{1,0:T(8,128)(2,1)S(1)}, u32[]{:S(2)}, u32[]{:S(2)}) collective-permute-start(bf16[112,256]{1,0:T(8,128)(2,1)S(1)} %get-tuple-element.110.refs_2_.refs_1_), channel_id=1, source_target_pairs={{0,6},{1,7},{2,4},{3,5},{4,2},{5,3},{6,0},{7,1},{8,14},{9,15},{10,... | collective-permute-start | bytes 172040 | tf_op jit(solution)/shard_map/ppermute | solution.py:49
  33.9 5.4 %collective-permute-start.11 = (bf16[112,256]{1,0:T(8,128)(2,1)S(1)}, bf16[112,256]{1,0:T(8,128)(2,1)S(1)}, u32[]{:S(2)}, u32[]{:S(2)}) collective-permute-start(bf16[112,256]{1,0:T(8,128)(2,1)S(1)} %get-tuple-element.110.refs_2_.refs_1_), channel_id=1, source_target_pairs={{0,4},{1,5},{2,6},{3,7},{4,0},{5,1},{6,2},{7,3},{8,12},{9,13},{10,... | collective-permute-start | bytes 172040 | tf_op jit(solution)/shard_map/ppermute | solution.py:49
  60.6 5.7 %collective-permute-start.15 = (bf16[112,256]{1,0:T(8,128)(2,1)S(1)}, bf16[112,256]{1,0:T(8,128)(2,1)S(1)}, u32[]{:S(2)}, u32[]{:S(2)}) collective-permute-start(bf16[112,256]{1,0:T(8,128)(2,1)S(1)} %get-tuple-element.138), channel_id=1, source_target_pairs={{0,6},{1,7},{2,4},{3,5},{4,2},{5,3},{6,0},{7,1},{8,14},{9,15},{10,... | collective-permute-start | bytes 172040 | tf_op jit(solution)/shard_map/ppermute | solution.py:49
  64.2 7.8 %collective-permute-start.22 = (f32[16,64,256]{2,1,0:T(8,128)S(1)}, f32[16,64,256]{2,1,0:T(8,128)S(1)}, u32[]{:S(2)}, u32[]{:S(2)}) collective-permute-start(f32[16,64,256]{2,1,0:T(8,128)S(1)} %get-tuple-element.162), channel_id=1, source_target_pairs={{0,1},{1,0},{2,3},{3,2},{4,5},{5,4},{6,7},{7,6},{8,9},{9,8},{10,11... | collective-permute-start | bytes 3145736 | tf_op jit(solution)/shard_map/ppermute | solution.py:49
  72.1 9.6 %collective-permute-start.23 = (bf16[544,256]{1,0:T(8,128)(2,1)S(1)}, bf16[544,256]{1,0:T(8,128)(2,1)S(1)}, u32[]{:S(2)}, u32[]{:S(2)}) collective-permute-start(bf16[544,256]{1,0:T(8,128)(2,1)S(1)} %get-tuple-element.166), channel_id=1, source_target_pairs={{0,2},{1,3},{2,0},{3,1},{4,6},{5,7},{6,4},{7,5},{8,10},{9,11},{10,... | collective-permute-start | bytes 835592 | tf_op jit(solution)/shard_map/ppermute | solution.py:49
  73.6 14.6 %collective-permute-start.24 = (bf16[544,256]{1,0:T(8,128)(2,1)S(1)}, bf16[544,256]{1,0:T(8,128)(2,1)S(1)}, u32[]{:S(2)}, u32[]{:S(2)}) collective-permute-start(bf16[544,256]{1,0:T(8,128)(2,1)S(1)} %get-tuple-element.167), channel_id=1, source_target_pairs={{0,4},{1,5},{2,6},{3,7},{4,0},{5,1},{6,2},{7,3},{8,12},{9,13},{10,... | collective-permute-start | bytes 835592 | tf_op jit(solution)/shard_map/ppermute | solution.py:49
  74.4 13.8 %collective-permute-start.25 = (bf16[544,256]{1,0:T(8,128)(2,1)S(1)}, bf16[544,256]{1,0:T(8,128)(2,1)S(1)}, u32[]{:S(2)}, u32[]{:S(2)}) collective-permute-start(bf16[544,256]{1,0:T(8,128)(2,1)S(1)} %get-tuple-element.168), channel_id=1, source_target_pairs={{0,6},{1,7},{2,4},{3,5},{4,2},{5,3},{6,0},{7,1},{8,14},{9,15},{10,... | collective-permute-start | bytes 835592 | tf_op jit(solution)/shard_map/ppermute | solution.py:49
  88.3 6.1 %collective-permute-start.26 = (bf16[160,256]{1,0:T(8,128)(2,1)S(1)}, bf16[160,256]{1,0:T(8,128)(2,1)S(1)}, u32[]{:S(2)}, u32[]{:S(2)}) collective-permute-start(bf16[160,256]{1,0:T(8,128)(2,1)S(1)} %get-tuple-element.173), channel_id=1, source_target_pairs={{0,8},{8,0},{16,24},{24,16},{1,9},{9,1},{17,25},{25,17},{2,10},{10... | collective-permute-start | bytes 245768 | tf_op jit(solution)/shard_map/ppermute | solution.py:49
  88.4 9.6 %collective-permute-start.27 = (bf16[160,256]{1,0:T(8,128)(2,1)S(1)}, bf16[160,256]{1,0:T(8,128)(2,1)S(1)}, u32[]{:S(2)}, u32[]{:S(2)}) collective-permute-start(bf16[160,256]{1,0:T(8,128)(2,1)S(1)} %get-tuple-element.174), channel_id=1, source_target_pairs={{0,16},{8,24},{16,0},{24,8},{1,17},{9,25},{17,1},{25,9},{2,18},{10... | collective-permute-start | bytes 245768 | tf_op jit(solution)/shard_map/ppermute | solution.py:49
  90.7 7.2 %collective-permute-start.28 = (bf16[160,256]{1,0:T(8,128)(2,1)S(1)}, bf16[160,256]{1,0:T(8,128)(2,1)S(1)}, u32[]{:S(2)}, u32[]{:S(2)}) collective-permute-start(bf16[160,256]{1,0:T(8,128)(2,1)S(1)} %get-tuple-element.175), channel_id=1, source_target_pairs={{0,24},{8,16},{16,8},{24,0},{1,25},{9,17},{17,9},{25,1},{2,26},{10... | collective-permute-start | bytes 245768 | tf_op jit(solution)/shard_map/ppermute | solution.py:49
  98.7 6.8 %collective-permute-start.31 = (bf16[128,256]{1,0:T(8,128)(2,1)S(1)}, bf16[128,256]{1,0:T(8,128)(2,1)S(1)}, u32[]{:S(2)}, u32[]{:S(2)}) collective-permute-start(bf16[128,256]{1,0:T(8,128)(2,1)S(1)} %get-tuple-element.179.refs_1_), channel_id=1, source_target_pairs={{0,8},{8,0},{16,24},{24,16},{1,9},{9,1},{17,25},{25,17},{2,10},{10... | collective-permute-start | bytes 196616 | tf_op jit(solution)/shard_map/ppermute | solution.py:49
  100.2 6.8 %collective-permute-start.30 = (bf16[128,256]{1,0:T(8,128)(2,1)S(1)}, bf16[128,256]{1,0:T(8,128)(2,1)S(1)}, u32[]{:S(2)}, u32[]{:S(2)}) collective-permute-start(bf16[128,256]{1,0:T(8,128)(2,1)S(1)} %get-tuple-element.179.refs_1_), channel_id=1, source_target_pairs={{0,16},{8,24},{16,0},{24,8},{1,17},{9,25},{17,1},{25,9},{2,18},{10... | collective-permute-start | bytes 196616 | tf_op jit(solution)/shard_map/ppermute | solution.py:49
  101.6 6.2 %collective-permute-start.29 = (bf16[128,256]{1,0:T(8,128)(2,1)S(1)}, bf16[128,256]{1,0:T(8,128)(2,1)S(1)}, u32[]{:S(2)}, u32[]{:S(2)}) collective-permute-start(bf16[128,256]{1,0:T(8,128)(2,1)S(1)} %get-tuple-element.179.refs_1_), channel_id=1, source_target_pairs={{0,24},{8,16},{16,8},{24,0},{1,25},{9,17},{17,9},{25,1},{2,26},{10... | collective-permute-start | bytes 196616 | tf_op jit(solution)/shard_map/ppermute | solution.py:49
  111.4 5.5 %collective-permute-start.34 = (bf16[128,256]{1,0:T(8,128)(2,1)S(1)}, bf16[128,256]{1,0:T(8,128)(2,1)S(1)}, u32[]{:S(2)}, u32[]{:S(2)}) collective-permute-start(bf16[128,256]{1,0:T(8,128)(2,1)S(1)} %get-tuple-element.187), channel_id=1, source_target_pairs={{0,4},{1,5},{2,6},{3,7},{4,0},{5,1},{6,2},{7,3},{8,12},{9,13},{10,... | collective-permute-start | bytes 196616 | tf_op jit(solution)/shard_map/ppermute | solution.py:49
  111.6 5.3 %collective-permute-start.35 = (bf16[128,256]{1,0:T(8,128)(2,1)S(1)}, bf16[128,256]{1,0:T(8,128)(2,1)S(1)}, u32[]{:S(2)}, u32[]{:S(2)}) collective-permute-start(bf16[128,256]{1,0:T(8,128)(2,1)S(1)} %get-tuple-element.188), channel_id=1, source_target_pairs={{0,6},{1,7},{2,4},{3,5},{4,2},{5,3},{6,0},{7,1},{8,14},{9,15},{10,... | collective-permute-start | bytes 196616 | tf_op jit(solution)/shard_map/ppermute | solution.py:49
  (27 other events, 232.2 us)
